TPU v7x, 768 devices: a whole 4x8x12 slice. The times are simulated.
768 devices in a mesh: rows: 96 (over x, y, z_lo), feat: 8 (over z_hi, core).
Axes of the slice: x: 4, y: 8, z: 12 (z_hi: 4, z_lo: 3; z = z_hi * 3 + z_lo), core: 2. Of those that a mesh axis runs over, the one named last changes fastest.
Arguments:
- features: bfloat16 [49152, 768], P('rows', 'feat'), may hold values from -6 to 6
- tile_values: bfloat16 [10752, 128, 128], P('rows'), may hold values from -0.09375 to 0.09375
- dest_block: int32 [10752], P('rows'), may hold values from 0 to 3
- source_block: int32 [10752], P('rows'), may hold values from 0 to 383, as said below
- tile_count: int32 [672], P('rows'), may hold values from 1 to 16
- degree: int32 [49152], P('rows'), may hold values from 1 to 4
- self_weight: bfloat16 [768, 1024], P('feat'), may hold values from -0.21875 to 0.21875
- neighbour_weight: bfloat16 [768, 1024], P('feat'), may hold values from -0.21875 to 0.21875
- hidden_bias: bfloat16 [1024], P('feat'), may hold values from -3 to 3
- cotangent: bfloat16 [49152, 1024], P('rows', 'feat'), may hold values from -6 to 6
Outputs:
- activations: bfloat16 [49152, 1024], P('rows', 'feat')
- grad_features: bfloat16 [49152, 768], P('rows', 'feat')
- grad_self: float32 [768, 1024], P('feat')
- grad_neighbour: float32 [768, 1024], P('feat')
- grad_bias: float32 [1024], P('feat')
Inputs may be any that keep to these rules, and one draw needn't show every extreme that they name: `source_block`: tile k = (g * 7 + o) * 16 + s reads a block of row group (g + o - 3) mod 96.
All inputs are finite; a program needn't handle non-finite values.
Results may differ from a plain program's by a relative error of at most 0.02.
Values may be sent and summed in bfloat16 or wider, within the bound.
No kernel may reach another device: no remote copies, remote signals or barrier semaphores. Data moves between devices by JAX's collectives and lax.ppermute only.
A program may use at most 32 MiB of HBM per device.

v0:
```python
import jax
import jax.numpy as jnp
from jax import lax
from jax.sharding import PartitionSpec as P

REACH = 3
SLOTS = 16


def shifted(value, axis, steps):
    count = lax.axis_size(axis)
    pairs = [(source, (source + steps) % count) for source in range(count)]
    return lax.ppermute(value, axis, pairs)


def on_device(
    features,
    tile_values,
    dest_block,
    source_block,
    tile_count,
    degree,
    self_weight,
    neighbour_weight,
    hidden_bias,
    cotangent,
):
    node_dev, feat_width = features.shape
    block_size = tile_values.shape[1]
    block_count = node_dev // block_size
    groups = lax.axis_size("rows")
    position = lax.axis_index("rows")
    slot_ids = jnp.arange(SLOTS)
    block_ids = jnp.arange(block_count)
    highest = lax.Precision.HIGHEST

    def layout(offset):
        first_slot = offset * SLOTS
        tile_part = tile_values[first_slot : first_slot + SLOTS]
        live_mask = (slot_ids < tile_count[offset]).astype(jnp.float32)
        dest_hot = (
            dest_block[first_slot : first_slot + SLOTS][:, None] == block_ids[None, :]
        ).astype(jnp.float32) * live_mask[:, None]
        source = (position + offset - REACH) % groups
        source_local = source_block[first_slot : first_slot + SLOTS] - source * block_count
        source_hot = (source_local[:, None] == block_ids[None, :]).astype(jnp.float32)
        return (tile_part, dest_hot, source_hot)

    def gather_terms(offset, incoming):
        tile_part, dest_hot, source_hot = layout(offset)
        shaped = incoming.reshape(block_count, block_size, feat_width)
        picked = jnp.einsum(
            "sb,bnf->snf",
            source_hot.astype(jnp.bfloat16),
            shaped,
            preferred_element_type=jnp.float32,
        ).astype(jnp.bfloat16)
        products = jnp.einsum("sij,sjf->sif", tile_part, picked, preferred_element_type=jnp.float32)
        return jnp.einsum("sb,sif->bif", dest_hot, products, precision=highest)

    def scatter_terms(offset, back_blocks):
        tile_part, dest_hot, source_hot = layout(offset)
        rows_in = jnp.einsum(
            "sb,bif->sif",
            dest_hot.astype(jnp.bfloat16),
            back_blocks,
            preferred_element_type=jnp.float32,
        ).astype(jnp.bfloat16)
        products = jnp.einsum(
            "sij,sif->sjf", tile_part, rows_in, preferred_element_type=jnp.float32
        )
        return jnp.einsum("sb,sjf->bjf", source_hot, products, precision=highest)

    summed = gather_terms(REACH, features)
    for shift_by in range(-REACH, REACH + 1):
        if shift_by != 0:
            incoming = shifted(features, "rows", -shift_by)
            summed = summed + gather_terms(REACH + shift_by, incoming)
    degrees = degree.astype(jnp.float32)[:, None]
    aggregate = (summed.reshape(node_dev, feat_width) / degrees).astype(jnp.bfloat16)
    partial_pre = jnp.dot(features, self_weight, preferred_element_type=jnp.float32)
    partial_pre = partial_pre + jnp.dot(
        aggregate, neighbour_weight, preferred_element_type=jnp.float32
    )
    preact = lax.psum_scatter(
        partial_pre.astype(jnp.bfloat16), "feat", scatter_dimension=1, tiled=True
    ).astype(jnp.float32) + hidden_bias.astype(jnp.float32)
    gate_value = jax.nn.sigmoid(preact)
    activations = (preact * gate_value).astype(jnp.bfloat16)
    grad_pre = (
        cotangent.astype(jnp.float32) * gate_value * (1.0 + preact * (1.0 - gate_value))
    ).astype(jnp.bfloat16)
    grad_full = lax.all_gather(grad_pre, "feat", axis=1, tiled=True)
    contract_rows = (((0,), (0,)), ((), ()))
    self_part = lax.dot_general(
        features, grad_full, contract_rows, preferred_element_type=jnp.float32
    )
    neighbour_part = lax.dot_general(
        aggregate, grad_full, contract_rows, preferred_element_type=jnp.float32
    )
    bias_part = jnp.sum(grad_pre.astype(jnp.float32), axis=0)
    grad_self, grad_neighbour, grad_bias = lax.psum((self_part, neighbour_part, bias_part), "rows")
    contract_hidden = (((1,), (1,)), ((), ()))
    back_rows = (
        lax.dot_general(
            grad_full, neighbour_weight, contract_hidden, preferred_element_type=jnp.float32
        )
        / degrees
    ).astype(jnp.bfloat16)
    back_blocks = back_rows.reshape(block_count, block_size, feat_width)
    spread = scatter_terms(REACH, back_blocks)
    for shift_by in range(-REACH, REACH + 1):
        if shift_by != 0:
            outgoing = scatter_terms(REACH + shift_by, back_blocks)
            spread = spread + shifted(outgoing.astype(jnp.bfloat16), "rows", shift_by).astype(
                outgoing.dtype
            )
    self_term = lax.dot_general(
        grad_full, self_weight, contract_hidden, preferred_element_type=jnp.float32
    )
    grad_features = (self_term + spread.reshape(node_dev, feat_width)).astype(jnp.bfloat16)
    return (activations, grad_features, grad_self, grad_neighbour, grad_bias)


def solution(mesh):
    in_specs = (
        P("rows", "feat"),
        P("rows", None, None),
        P("rows"),
        P("rows"),
        P("rows"),
        P("rows"),
        P("feat", None),
        P("feat", None),
        P("feat"),
        P("rows", "feat"),
    )
    out_specs = (P("rows", "feat"), P("rows", "feat"), P("feat", None), P("feat", None), P("feat"))
    return jax.shard_map(
        on_device, mesh=mesh, in_specs=in_specs, out_specs=out_specs, check_vma=False
    )
```

profile of v0, /device:TPU:192, one launch (start us, length us, event | category | flops | bytes accessed | tf_op | source)
XLA Modules:
  0.0 1580.1 jit_solution(7201177499365676436)
XLA Ops:
  7.3 3.6 collective-permute-start
  10.9 7.3 collective-permute-start.1
  18.2 1.9 collective-permute-start.2
  20.1 10.3 collective-permute-start.3
  30.4 1.9 collective-permute-start.4
  46.2 2.9 collective-permute-start.5
  55.4 2.6 fusion.53
  62.0 2.6 fusion.51
  68.5 2.6 fusion.49
  75.0 2.6 fusion.47
  81.6 1.8 fusion.45
  83.4 1.8 convolution_add_fusion.5
  85.3 2.0 convolution_add_fusion.4
  94.0 44.4 %reduce-scatter.4.cloned.1.call-done = bf16[128,512]{1,0:T(8,128)(2,1)} async-done(((bf16[1024,512]{1,0:T(8,128)(2,1)}), bf16[128,512]{1,0:T(8,128)(2,1)}) %reduce-scatter.4.cloned.1.call-update) | async-done | bytes 131088
  141.3 292.3 %psum.23 = f32[128]{0:T(128)} all-reduce(f32[128]{0:T(128)S(1)} %get-tuple-element.7), channel_id=1, replica_groups=mesh['rows'=96,'feat'=8] {'rows'}, use_global_device_ids=true, to_apply=%region_4.5 | all-reduce | flops 128 | bytes 1024 | tf_op jit(solution)/shard_map/psum | solution.py:102
  442.4 1.9 collective-permute-start.11
  446.9 1.9 collective-permute-start.10
  451.4 1.9 collective-permute-start.9
  456.6 10.4 collective-permute-start.8
  469.6 4.5 collective-permute-start.7
  476.7 2.0 convolution_bitcast_fusion
  480.5 3.9 collective-permute-start.6
  489.1 1080.9 %all-reduce.3.cloned.1.call-done = (f32[96,1024]{1,0:T(8,128)}, f32[96,1024]{1,0:T(8,128)}) async-done(((f32[96,1024]{1,0:T(8,128)}, f32[96,1024]{1,0:T(8,128)}), (f32[96,1024]{1,0:T(8,128)}, f32[96,1024]{1,0:T(8,128)})) %all-reduce.3.cloned.1.call-update) | async-done | bytes 786448 | tf_op jit(solution)/shard_map/psum | solution.py:102
  1571.8 1.8 copy.112
  (187 shorter events, 75.2 us)
Async XLA Ops:
  7.2 131.2 %reduce-scatter.4.cloned.1.call-start = ((), (), s32[]{:S(2)}) async-start(), calls=%async_computation.2 | async-start | bytes 1179648
  7.3 39.0 %collective-permute-start = (bf16[512,96]{0,1:T(8,128)(2,1)}, bf16[512,96]{0,1:T(8,128)(2,1)S(1)}, u32[]{:S(2)}, u32[]{:S(2)}) collective-permute-start(bf16[512,96]{0,1:T(8,128)(2,1)} %param.10), channel_id=1, source_target_pairs={{0,24},{8,32},{16,40},{24,48},{32,56},{40,64},{48,72},{56,80},{64,... | collective-permute-start | bytes 294920 | tf_op jit(solution)/shard_map/ppermute | solution.py:13
  10.9 41.4 %collective-permute-start.1 = (bf16[512,96]{0,1:T(8,128)(2,1)}, bf16[512,96]{0,1:T(8,128)(2,1)S(1)}, u32[]{:S(2)}, u32[]{:S(2)}) collective-permute-start(bf16[512,96]{0,1:T(8,128)(2,1)} %param.10), channel_id=1, source_target_pairs={{0,16},{8,24},{16,32},{24,40},{32,48},{40,56},{48,64},{56,72},{64,... | collective-permute-start | bytes 294920 | tf_op jit(solution)/shard_map/ppermute | solution.py:13
  18.2 39.8 %collective-permute-start.2 = (bf16[512,96]{0,1:T(8,128)(2,1)}, bf16[512,96]{0,1:T(8,128)(2,1)}, u32[]{:S(2)}, u32[]{:S(2)}) collective-permute-start(bf16[512,96]{0,1:T(8,128)(2,1)} %param.10), channel_id=1, source_target_pairs={{0,8},{8,16},{16,24},{24,32},{32,40},{40,48},{48,56},{56,64},{64,7... | collective-permute-start | bytes 294920 | tf_op jit(solution)/shard_map/ppermute | solution.py:13
  20.1 44.4 %collective-permute-start.3 = (bf16[512,96]{0,1:T(8,128)(2,1)}, bf16[512,96]{0,1:T(8,128)(2,1)}, u32[]{:S(2)}, u32[]{:S(2)}) collective-permute-start(bf16[512,96]{0,1:T(8,128)(2,1)} %param.10), channel_id=1, source_target_pairs={{0,760},{8,0},{16,8},{24,16},{32,24},{40,32},{48,40},{56,48},{64,5... | collective-permute-start | bytes 294920 | tf_op jit(solution)/shard_map/ppermute | solution.py:13
  30.4 40.7 %collective-permute-start.4 = (bf16[512,96]{0,1:T(8,128)(2,1)}, bf16[512,96]{0,1:T(8,128)(2,1)}, u32[]{:S(2)}, u32[]{:S(2)}) collective-permute-start(bf16[512,96]{0,1:T(8,128)(2,1)} %param.10), channel_id=1, source_target_pairs={{0,752},{8,760},{16,0},{24,8},{32,16},{40,24},{48,32},{56,40},{64,... | collective-permute-start | bytes 294920 | tf_op jit(solution)/shard_map/ppermute | solution.py:13
  46.2 31.4 %collective-permute-start.5 = (bf16[512,96]{0,1:T(8,128)(2,1)}, bf16[512,96]{0,1:T(8,128)(2,1)}, u32[]{:S(2)}, u32[]{:S(2)}) collective-permute-start(bf16[512,96]{0,1:T(8,128)(2,1)} %param.10), channel_id=1, source_target_pairs={{0,744},{8,752},{16,760},{24,0},{32,8},{40,16},{48,24},{56,32},{64... | collective-permute-start | bytes 294920 | tf_op jit(solution)/shard_map/ppermute | solution.py:13
  91.7 344.8 %copy-start.27 = (s32[16]{0:T(128)S(1)}, s32[16]{0:T(128)}, u32[]{:S(2)}) copy-start(s32[16]{0:T(128)} %copy-done.26) | copy-start | bytes 196
  91.7 344.8 %copy-start.42 = (f32[16]{0:T(128)S(1)}, f32[16]{0:T(128)}, u32[]{:S(2)}) copy-start(f32[16]{0:T(128)} %copy-done.41) | copy-start | bytes 196
  91.7 345.1 %copy-start.25 = (s32[16]{0:T(128)S(1)}, s32[16]{0:T(128)}, u32[]{:S(2)}) copy-start(s32[16]{0:T(128)} %copy-done.24) | copy-start | bytes 196
  91.7 345.1 %copy-start.40 = (f32[16]{0:T(128)S(1)}, f32[16]{0:T(128)}, u32[]{:S(2)}) copy-start(f32[16]{0:T(128)} %copy-done.39) | copy-start | bytes 196
  91.7 345.4 %copy-start.23 = (s32[16]{0:T(128)S(1)}, s32[16]{0:T(128)}, u32[]{:S(2)}) copy-start(s32[16]{0:T(128)} %copy-done.22) | copy-start | bytes 196
  91.7 345.4 %copy-start.38 = (f32[16]{0:T(128)S(1)}, f32[16]{0:T(128)}, u32[]{:S(2)}) copy-start(f32[16]{0:T(128)} %copy-done.37) | copy-start | bytes 196
  91.7 345.7 %copy-start.21 = (s32[16]{0:T(128)S(1)}, s32[16]{0:T(128)}, u32[]{:S(2)}) copy-start(s32[16]{0:T(128)} %copy-done.20) | copy-start | bytes 196
  91.7 345.7 %copy-start.36 = (f32[16]{0:T(128)S(1)}, f32[16]{0:T(128)}, u32[]{:S(2)}) copy-start(f32[16]{0:T(128)} %copy-done.35) | copy-start | bytes 196
  93.1 344.7 %copy-start.34 = (f32[16]{0:T(128)S(1)}, f32[16]{0:T(128)}, u32[]{:S(2)}) copy-start(f32[16]{0:T(128)} %copy-done.33) | copy-start | bytes 196
  93.1 340.5 %all-gather.2.cloned.1.call-start = ((), (), s32[]{:S(2)}) async-start(), calls=%async_computation.1 | async-start | bytes 1179648 | tf_op jit(solution)/shard_map/all_gather | solution.py:93
  141.3 1428.8 %all-reduce.3.cloned.1.call-start = ((), (), s32[]{:S(2)}) async-start(), calls=%async_computation.3 | async-start | bytes 1572864 | tf_op jit(solution)/shard_map/psum | solution.py:102
  442.4 38.1 %collective-permute-start.11 = (bf16[4,128,96]{1,0,2:T(4,128)(2,1)}, bf16[4,128,96]{1,0,2:T(4,128)(2,1)S(1)}, u32[]{:S(2)}, u32[]{:S(2)}) collective-permute-start(bf16[4,128,96]{1,0,2:T(4,128)(2,1)} %convolution_convert_fusion), channel_id=1, source_target_pairs={{0,24},{8,32},{16,40},{24,48},{32,56},{40,64},{48,72},{56,80},{64,... | collective-permute-start | bytes 294920 | tf_op jit(solution)/shard_map/ppermute | solution.py:13
  446.9 38.9 %collective-permute-start.10 = (bf16[4,128,96]{1,0,2:T(4,128)(2,1)S(1)}, bf16[4,128,96]{1,0,2:T(4,128)(2,1)S(1)}, u32[]{:S(2)}, u32[]{:S(2)}) collective-permute-start(bf16[4,128,96]{1,0,2:T(4,128)(2,1)S(1)} %convolution_convert_fusion.1), channel_id=1, source_target_pairs={{0,16},{8,24},{16,32},{24,40},{32,48},{40,56},{48,64},{56,72},{64,... | collective-permute-start | bytes 294920 | tf_op jit(solution)/shard_map/ppermute | solution.py:13
  451.4 34.4 %collective-permute-start.9 = (bf16[4,128,96]{1,0,2:T(4,128)(2,1)S(1)}, bf16[4,128,96]{1,0,2:T(4,128)(2,1)S(1)}, u32[]{:S(2)}, u32[]{:S(2)}) collective-permute-start(bf16[4,128,96]{1,0,2:T(4,128)(2,1)S(1)} %convolution_convert_fusion.2), channel_id=1, source_target_pairs={{0,8},{8,16},{16,24},{24,32},{32,40},{40,48},{48,56},{56,64},{64,7... | collective-permute-start | bytes 294920 | tf_op jit(solution)/shard_map/ppermute | solution.py:13
  456.6 29.2 %collective-permute-start.8 = (bf16[4,128,96]{1,0,2:T(4,128)(2,1)}, bf16[4,128,96]{1,0,2:T(4,128)(2,1)S(1)}, u32[]{:S(2)}, u32[]{:S(2)}) collective-permute-start(bf16[4,128,96]{1,0,2:T(4,128)(2,1)} %convolution_convert_fusion.3), channel_id=1, source_target_pairs={{0,760},{8,0},{16,8},{24,16},{32,24},{40,32},{48,40},{56,48},{64,5... | collective-permute-start | bytes 294920 | tf_op jit(solution)/shard_map/ppermute | solution.py:13
  469.6 16.2 %collective-permute-start.7 = (bf16[4,128,96]{1,0,2:T(4,128)(2,1)S(1)}, bf16[4,128,96]{1,0,2:T(4,128)(2,1)S(1)}, u32[]{:S(2)}, u32[]{:S(2)}) collective-permute-start(bf16[4,128,96]{1,0,2:T(4,128)(2,1)S(1)} %convolution_convert_fusion.4), channel_id=1, source_target_pairs={{0,752},{8,760},{16,0},{24,8},{32,16},{40,24},{48,32},{56,40},{64,... | collective-permute-start | bytes 294920 | tf_op jit(solution)/shard_map/ppermute | solution.py:13
  480.5 6.5 collective-permute-start.6
  (36 other events, 1972.4 us)
Sparse Core Ops, SparseCore 0:
  93.2 45.2 reduce-scatter.3
  141.4 44.8 all-gather.1
  480.6 1089.3 all-reduce.2
where the time goes:
time: 1580 us
  waiting for transfers between devices  1130 us (72%)
  blocking collectives  292 us (18%)
  matrix products  58.7 us (4%)
  starting transfers between devices  52.8 us (3%)
  local copies, waits for them, and re-layouts  26.3 us (2%)
    psum x1, waiting for transfers between devices, on_device(): lax.psum((self_part, neighbour_part, bias_part), 'rows')  1080 us
    psum x1, blocking collectives, on_device(): lax.psum((self_part, neighbour_part, bias_part), 'rows')  292 us
    ppermute x12, starting transfers between devices, shifted(): return lax.ppermute(value, axis, pairs)  52.4 us
    unnamed x4, waiting for transfers between devices  44.5 us
  transfers between devices with their start and end apart: 15, of which 3 were waited for; matrix products, arithmetic and copies ran while one was open for 4% of the time, Pallas kernels for 0%

commit v1 on v0

--- a/solution.py
+++ b/solution.py
@@ -82,15 +82,20 @@
     partial_pre = partial_pre + jnp.dot(
         aggregate, neighbour_weight, preferred_element_type=jnp.float32
     )
-    preact = lax.psum_scatter(
-        partial_pre.astype(jnp.bfloat16), "feat", scatter_dimension=1, tiled=True
-    ).astype(jnp.float32) + hidden_bias.astype(jnp.float32)
+    hidden_dev = hidden_bias.shape[0]
+    feats = lax.axis_size("feat")
+    pieces = partial_pre.astype(jnp.bfloat16).reshape(node_dev, feats, hidden_dev)
+    pieces = lax.all_to_all(pieces.transpose(1, 0, 2), "feat", 0, 0)
+    preact = jnp.sum(pieces.astype(jnp.float32), axis=0) + hidden_bias.astype(jnp.float32)
     gate_value = jax.nn.sigmoid(preact)
     activations = (preact * gate_value).astype(jnp.bfloat16)
     grad_pre = (
         cotangent.astype(jnp.float32) * gate_value * (1.0 + preact * (1.0 - gate_value))
     ).astype(jnp.bfloat16)
-    grad_full = lax.all_gather(grad_pre, "feat", axis=1, tiled=True)
+    grad_full = lax.all_to_all(
+        jnp.broadcast_to(grad_pre[None], (feats,) + grad_pre.shape), "feat", 0, 0
+    )
+    grad_full = grad_full.transpose(1, 0, 2).reshape(node_dev, feats * hidden_dev)
     contract_rows = (((0,), (0,)), ((), ()))
     self_part = lax.dot_general(
         features, grad_full, contract_rows, preferred_element_type=jnp.float32
@@ -99,7 +104,19 @@
         aggregate, grad_full, contract_rows, preferred_element_type=jnp.float32
     )
     bias_part = jnp.sum(grad_pre.astype(jnp.float32), axis=0)
-    grad_self, grad_neighbour, grad_bias = lax.psum((self_part, neighbour_part, bias_part), "rows")
+    weight_part = jnp.concatenate([self_part, neighbour_part], axis=0).astype(jnp.bfloat16)
+    weight_part = weight_part.reshape(12, 16, feats, hidden_dev).transpose(0, 2, 1, 3)
+    weight_part = weight_part.reshape(groups, 16, hidden_dev)
+    bias_rows = jnp.broadcast_to(
+        bias_part.astype(jnp.bfloat16)[None, None], (groups, 16, hidden_dev)
+    )
+    sent = jnp.concatenate([weight_part, bias_rows], axis=1)
+    got = jnp.sum(lax.all_to_all(sent, "rows", 0, 0).astype(jnp.float32), axis=0)
+    grad_bias = got[16]
+    owned = jnp.broadcast_to(got[:16].astype(jnp.bfloat16)[None], (groups, 16, hidden_dev))
+    whole = lax.all_to_all(owned, "rows", 0, 0).reshape(12, feats, 16, hidden_dev)
+    whole = whole.transpose(0, 2, 1, 3).reshape(2, feat_width, feats * hidden_dev)
+    grad_self, grad_neighbour = whole[0].astype(jnp.float32), whole[1].astype(jnp.float32)
     contract_hidden = (((1,), (1,)), ((), ()))
     back_rows = (
         lax.dot_general(

time: 1580 us -> 255 us (0.16)
  the two profiles are of different devices: /device:TPU:192 before, /device:TPU:1 now
where the time goes in v1:
time: 255 us; the launch traced here: 253 us
  starting transfers between devices  128 us (50%)
  waiting for transfers between devices  54.7 us (21%)
  matrix products  45.1 us (18%)
  local copies, waits for them, and re-layouts  13.8 us (5%)
  other arithmetic  9.43 us (4%)
    ppermute x12, starting transfers between devices, shifted(): return lax.ppermute(value, axis, pairs)  69.5 us
    all_to_all x1, waiting for transfers between devices, on_device(): pieces = lax.all_to_all(pieces.transpose(1, 0, 2), 'feat', 0, 0)  25.3 us
    all_to_all x1, waiting for transfers between devices, on_device(): lax.all_to_all(jnp.broadcast_to(grad_pre[None], (feats,) + grad_pre.shape...  22.4 us
    all_to_all x1, starting transfers between devices, on_device(): lax.all_to_all(jnp.broadcast_to(grad_pre[None], (feats,) + grad_pre.shape...  20.9 us
    all_to_all x1, starting transfers between devices, on_device(): pieces = lax.all_to_all(pieces.transpose(1, 0, 2), 'feat', 0, 0)  16.3 us
    dot_general x7, matrix products, gather_terms(): jnp.einsum('sij,sjf->sif', tile_part, picked, preferred_element_type=jnp....  14.4 us
    all_to_all x1, starting transfers between devices, on_device(): lax.all_to_all(owned, 'rows', 0, 0).reshape(12, feats, 16, hidden_dev)  11.3 us
    all_to_all x1, starting transfers between devices, on_device(): lax.all_to_all(sent, 'rows', 0, 0).astype(jnp.float32)  10.4 us
  transfers between devices with their start and end apart: 16, of which 5 were waited for; matrix products, arithmetic and copies ran while one was open for 20% of the time, Pallas kernels for 0%

profile of v1, /device:TPU:1, one launch (start us, length us, event | category | flops | bytes accessed | tf_op | source)
XLA Modules:
  0.0 253.0 jit_solution(14473299046386047050)
XLA Ops:
  0.7 4.2 %collective-permute-start = (bf16[512,96]{0,1:T(8,128)(2,1)}, bf16[512,96]{0,1:T(8,128)(2,1)S(1)}, u32[]{:S(2)}, u32[]{:S(2)}) collective-permute-start(bf16[512,96]{0,1:T(8,128)(2,1)} %param.10), channel_id=1, source_target_pairs={{0,24},{8,32},{16,40},{24,48},{32,56},{40,64},{48,72},{56,80},{64,... | collective-permute-start | bytes 294920 | tf_op jit(solution)/shard_map/ppermute | solution.py:13
  4.8 5.8 %collective-permute-start.1 = (bf16[512,96]{0,1:T(8,128)(2,1)}, bf16[512,96]{0,1:T(8,128)(2,1)}, u32[]{:S(2)}, u32[]{:S(2)}) collective-permute-start(bf16[512,96]{0,1:T(8,128)(2,1)} %param.10), channel_id=1, source_target_pairs={{0,16},{8,24},{16,32},{24,40},{32,48},{40,56},{48,64},{56,72},{64,... | collective-permute-start | bytes 294920 | tf_op jit(solution)/shard_map/ppermute | solution.py:13
  10.7 1.9 collective-permute-start.2
  12.6 8.5 %collective-permute-start.3 = (bf16[512,96]{0,1:T(8,128)(2,1)}, bf16[512,96]{0,1:T(8,128)(2,1)}, u32[]{:S(2)}, u32[]{:S(2)}) collective-permute-start(bf16[512,96]{0,1:T(8,128)(2,1)} %param.10), channel_id=1, source_target_pairs={{0,760},{8,0},{16,8},{24,16},{32,24},{40,32},{48,40},{56,48},{64,5... | collective-permute-start | bytes 294920 | tf_op jit(solution)/shard_map/ppermute | solution.py:13
  21.1 1.9 collective-permute-start.4
  38.5 2.9 %collective-permute-start.5 = (bf16[512,96]{0,1:T(8,128)(2,1)S(1)}, bf16[512,96]{0,1:T(8,128)(2,1)}, u32[]{:S(2)}, u32[]{:S(2)}) collective-permute-start(bf16[512,96]{0,1:T(8,128)(2,1)S(1)} %copy-done.5), channel_id=1, source_target_pairs={{0,744},{8,752},{16,760},{24,0},{32,8},{40,16},{48,24},{56,32},{64... | collective-permute-start | bytes 294920 | tf_op jit(solution)/shard_map/ppermute | solution.py:13
  44.5 2.4 convolution_bitcast_fusion.11
  48.2 2.5 convolution_bitcast_fusion.10
  51.9 2.4 convolution_bitcast_fusion.9
  55.6 2.4 convolution_bitcast_fusion.8
  68.9 16.3 %all-to-all-start = ((bf16[8,512,128]{2,1,0:T(8,128)(2,1)}), bf16[8,512,128]{2,1,0:T(8,128)(2,1)S(1)}, u32[]{:S(2)}, u32[]{:S(2)}) async-start(bf16[8,512,128]{2,1,0:T(8,128)(2,1)} %bitcast.218), calls=%async_computation | async-start | bytes 2097152 | tf_op jit(solution)/shard_map/all_to_all | solution.py:88
  85.2 25.3 %all-to-all-done = bf16[8,512,128]{2,1,0:T(8,128)(2,1)S(1)} async-done(((bf16[8,512,128]{2,1,0:T(8,128)(2,1)}), bf16[8,512,128]{2,1,0:T(8,128)(2,1)S(1)}, u32[]{:S(2)}, u32[]{:S(2)}) %all-to-all-start) | async-done | bytes 1048608 | tf_op jit(solution)/shard_map/all_to_all | solution.py:88
  112.0 20.9 %all-to-all-start.1 = ((bf16[8,512,128]{1,2,0:T(8,128)(2,1)}), bf16[8,512,128]{1,2,0:T(8,128)(2,1)S(1)}, u32[]{:S(2)}, u32[]{:S(2)}) async-start(bf16[8,512,128]{1,2,0:T(8,128)(2,1)} %broadcast_in_dim.6), calls=%async_computation.1 | async-start | bytes 2097152 | tf_op jit(solution)/shard_map/all_to_all | solution.py:95
  133.7 22.4 %all-to-all-done.1 = bf16[8,512,128]{1,2,0:T(8,128)(2,1)S(1)} async-done(((bf16[8,512,128]{1,2,0:T(8,128)(2,1)}), bf16[8,512,128]{1,2,0:T(8,128)(2,1)S(1)}, u32[]{:S(2)}, u32[]{:S(2)}) %all-to-all-start.1) | async-done | bytes 1048608 | tf_op jit(solution)/shard_map/all_to_all | solution.py:95
  160.0 2.9 %collective-permute-start.11 = (bf16[4,128,96]{1,0,2:T(4,128)(2,1)S(1)}, bf16[4,128,96]{1,0,2:T(4,128)(2,1)S(1)}, u32[]{:S(2)}, u32[]{:S(2)}) collective-permute-start(bf16[4,128,96]{1,0,2:T(4,128)(2,1)S(1)} %convolution_convert_fusion.16), channel_id=1, source_target_pairs={{0,24},{8,32},{16,40},{24,48},{32,56},{40,64},{48,72},{56,80},{64,... | collective-permute-start | bytes 294920 | tf_op jit(solution)/shard_map/ppermute | solution.py:13
  165.0 20.6 %collective-permute-start.9 = (bf16[4,128,96]{1,0,2:T(4,128)(2,1)S(1)}, bf16[4,128,96]{1,0,2:T(4,128)(2,1)S(1)}, u32[]{:S(2)}, u32[]{:S(2)}) collective-permute-start(bf16[4,128,96]{1,0,2:T(4,128)(2,1)S(1)} %convolution_convert_fusion.18), channel_id=1, source_target_pairs={{0,8},{8,16},{16,24},{24,32},{32,40},{40,48},{48,56},{56,64},{64,7... | collective-permute-start | bytes 294920 | tf_op jit(solution)/shard_map/ppermute | solution.py:13
  188.7 10.4 %all-to-all-start.2 = ((bf16[96,32,128]{2,1,0:T(8,128)(2,1)}), bf16[96,32,128]{2,1,0:T(8,128)(2,1)S(1)}, u32[]{:S(2)}, u32[]{:S(2)}) async-start(bf16[96,32,128]{2,1,0:T(8,128)(2,1)} %pad_maximum_fusion), calls=%async_computation.2 | async-start | bytes 1572864 | tf_op jit(solution)/shard_map/all_to_all | solution.py:114
  199.9 8.3 %collective-permute-start.8 = (bf16[4,128,96]{1,0,2:T(4,128)(2,1)S(1)}, bf16[4,128,96]{1,0,2:T(4,128)(2,1)S(1)}, u32[]{:S(2)}, u32[]{:S(2)}) collective-permute-start(bf16[4,128,96]{1,0,2:T(4,128)(2,1)S(1)} %convolution_convert_fusion.19), channel_id=1, source_target_pairs={{0,760},{8,0},{16,8},{24,16},{32,24},{40,32},{48,40},{56,48},{64,5... | collective-permute-start | bytes 294920 | tf_op jit(solution)/shard_map/ppermute | solution.py:13
  210.8 1.9 collective-permute-start.7
  217.7 4.6 %all-to-all-done.2 = bf16[96,32,128]{2,1,0:T(8,128)(2,1)S(1)} async-done(((bf16[96,32,128]{2,1,0:T(8,128)(2,1)}), bf16[96,32,128]{2,1,0:T(8,128)(2,1)S(1)}, u32[]{:S(2)}, u32[]{:S(2)}) %all-to-all-start.2) | async-done | bytes 786464 | tf_op jit(solution)/shard_map/all_to_all | solution.py:114
  223.2 11.3 %all-to-all-start.3 = ((bf16[96,16,128]{2,1,0:T(8,128)(2,1)}), bf16[96,16,128]{2,1,0:T(8,128)(2,1)S(1)}, u32[]{:S(2)}, u32[]{:S(2)}) async-start(bf16[96,16,128]{2,1,0:T(8,128)(2,1)} %broadcast_in_dim.8), calls=%async_computation.3 | async-start | bytes 786432 | tf_op jit(solution)/shard_map/all_to_all | solution.py:117
  234.9 3.6 %collective-permute-start.10 = (bf16[4,128,96]{1,0,2:T(4,128)(2,1)S(1)}, bf16[4,128,96]{1,0,2:T(4,128)(2,1)S(1)}, u32[]{:S(2)}, u32[]{:S(2)}) collective-permute-start(bf16[4,128,96]{1,0,2:T(4,128)(2,1)S(1)} %convolution_convert_fusion.17), channel_id=1, source_target_pairs={{0,16},{8,24},{16,32},{24,40},{32,48},{40,56},{48,64},{56,72},{64,... | collective-permute-start | bytes 294920 | tf_op jit(solution)/shard_map/ppermute | solution.py:13
  238.5 6.9 %collective-permute-start.6 = (bf16[4,128,96]{1,0,2:T(4,128)(2,1)S(1)}, bf16[4,128,96]{1,0,2:T(4,128)(2,1)S(1)}, u32[]{:S(2)}, u32[]{:S(2)}) collective-permute-start(bf16[4,128,96]{1,0,2:T(4,128)(2,1)S(1)} %convolution_convert_fusion.21), channel_id=1, source_target_pairs={{0,744},{8,752},{16,760},{24,0},{32,8},{40,16},{48,24},{56,32},{64... | collective-permute-start | bytes 294920 | tf_op jit(solution)/shard_map/ppermute | solution.py:13
  249.8 1.8 all-to-all-done.3
  (119 shorter events, 59.3 us)
Async XLA Ops:
  0.6 66.6 %copy-start = (bf16[96,1024]{1,0:T(8,128)(2,1)S(1)}, bf16[96,1024]{1,0:T(8,128)(2,1)}, u32[]{:S(2)}) copy-start(bf16[96,1024]{1,0:T(8,128)(2,1)} %param.17) | copy-start | bytes 589828
  0.6 37.9 %copy-start.5 = (bf16[512,96]{0,1:T(8,128)(2,1)S(1)}, bf16[512,96]{0,1:T(8,128)(2,1)}, u32[]{:S(2)}) copy-start(bf16[512,96]{0,1:T(8,128)(2,1)} %param.10) | copy-start | bytes 294916
  0.7 37.9 %collective-permute-start = (bf16[512,96]{0,1:T(8,128)(2,1)}, bf16[512,96]{0,1:T(8,128)(2,1)S(1)}, u32[]{:S(2)}, u32[]{:S(2)}) collective-permute-start(bf16[512,96]{0,1:T(8,128)(2,1)} %param.10), channel_id=1, source_target_pairs={{0,24},{8,32},{16,40},{24,48},{32,56},{40,64},{48,72},{56,80},{64,... | collective-permute-start | bytes 294920 | tf_op jit(solution)/shard_map/ppermute | solution.py:13
  4.8 38.4 %collective-permute-start.1 = (bf16[512,96]{0,1:T(8,128)(2,1)}, bf16[512,96]{0,1:T(8,128)(2,1)}, u32[]{:S(2)}, u32[]{:S(2)}) collective-permute-start(bf16[512,96]{0,1:T(8,128)(2,1)} %param.10), channel_id=1, source_target_pairs={{0,16},{8,24},{16,32},{24,40},{32,48},{40,56},{48,64},{56,72},{64,... | collective-permute-start | bytes 294920 | tf_op jit(solution)/shard_map/ppermute | solution.py:13
  10.7 36.3 %collective-permute-start.2 = (bf16[512,96]{0,1:T(8,128)(2,1)}, bf16[512,96]{0,1:T(8,128)(2,1)}, u32[]{:S(2)}, u32[]{:S(2)}) collective-permute-start(bf16[512,96]{0,1:T(8,128)(2,1)} %param.10), channel_id=1, source_target_pairs={{0,8},{8,16},{16,24},{24,32},{32,40},{40,48},{48,56},{56,64},{64,7... | collective-permute-start | bytes 294920 | tf_op jit(solution)/shard_map/ppermute | solution.py:13
  12.6 38.1 %collective-permute-start.3 = (bf16[512,96]{0,1:T(8,128)(2,1)}, bf16[512,96]{0,1:T(8,128)(2,1)}, u32[]{:S(2)}, u32[]{:S(2)}) collective-permute-start(bf16[512,96]{0,1:T(8,128)(2,1)} %param.10), channel_id=1, source_target_pairs={{0,760},{8,0},{16,8},{24,16},{32,24},{40,32},{48,40},{56,48},{64,5... | collective-permute-start | bytes 294920 | tf_op jit(solution)/shard_map/ppermute | solution.py:13
  21.1 33.3 %collective-permute-start.4 = (bf16[512,96]{0,1:T(8,128)(2,1)}, bf16[512,96]{0,1:T(8,128)(2,1)}, u32[]{:S(2)}, u32[]{:S(2)}) collective-permute-start(bf16[512,96]{0,1:T(8,128)(2,1)} %param.10), channel_id=1, source_target_pairs={{0,752},{8,760},{16,0},{24,8},{32,16},{40,24},{48,32},{56,40},{64,... | collective-permute-start | bytes 294920 | tf_op jit(solution)/shard_map/ppermute | solution.py:13
  38.5 19.4 %collective-permute-start.5 = (bf16[512,96]{0,1:T(8,128)(2,1)S(1)}, bf16[512,96]{0,1:T(8,128)(2,1)}, u32[]{:S(2)}, u32[]{:S(2)}) collective-permute-start(bf16[512,96]{0,1:T(8,128)(2,1)S(1)} %copy-done.5), channel_id=1, source_target_pairs={{0,744},{8,752},{16,760},{24,0},{32,8},{40,16},{48,24},{56,32},{64... | collective-permute-start | bytes 294920 | tf_op jit(solution)/shard_map/ppermute | solution.py:13
  59.2 7.0 %copy-start.9 = (s32[16]{0:T(128)S(1)}, s32[16]{0:T(128)}, u32[]{:S(2)}) copy-start(s32[16]{0:T(128)} %get-tuple-element.11) | copy-start | bytes 196
  59.3 7.0 %copy-start.10 = (f32[16]{0:T(128)S(1)}, f32[16]{0:T(128)}, u32[]{:S(2)}) copy-start(f32[16]{0:T(128)} %compare_convert_fusion) | copy-start | bytes 196
  67.2 18.0 %copy-start.11 = (bf16[128]{0:T(256)(128)(2,1)S(1)}, bf16[128]{0:T(256)(128)(2,1)}, u32[]{:S(2)}) copy-start(bf16[128]{0:T(256)(128)(2,1)} %param.18) | copy-start | bytes 772
  67.3 43.4 %copy-start.7 = (bf16[512,128]{1,0:T(8,128)(2,1)S(1)}, bf16[512,128]{1,0:T(8,128)(2,1)}, u32[]{:S(2)}) copy-start(bf16[512,128]{1,0:T(8,128)(2,1)} %param.19) | copy-start | bytes 393220
  68.9 41.6 %all-to-all-start = ((bf16[8,512,128]{2,1,0:T(8,128)(2,1)}), bf16[8,512,128]{2,1,0:T(8,128)(2,1)S(1)}, u32[]{:S(2)}, u32[]{:S(2)}) async-start(bf16[8,512,128]{2,1,0:T(8,128)(2,1)} %bitcast.218), calls=%async_computation | async-start | bytes 2097152 | tf_op jit(solution)/shard_map/all_to_all | solution.py:88
  110.7 46.0 %copy-start.8 = (f32[16]{0:T(128)S(1)}, f32[16]{0:T(128)}, u32[]{:S(2)}) copy-start(f32[16]{0:T(128)} %compare_convert_fusion.2) | copy-start | bytes 196
  112.0 44.0 %all-to-all-start.1 = ((bf16[8,512,128]{1,2,0:T(8,128)(2,1)}), bf16[8,512,128]{1,2,0:T(8,128)(2,1)S(1)}, u32[]{:S(2)}, u32[]{:S(2)}) async-start(bf16[8,512,128]{1,2,0:T(8,128)(2,1)} %broadcast_in_dim.6), calls=%async_computation.1 | async-start | bytes 2097152 | tf_op jit(solution)/shard_map/all_to_all | solution.py:95
  160.0 78.5 %collective-permute-start.11 = (bf16[4,128,96]{1,0,2:T(4,128)(2,1)S(1)}, bf16[4,128,96]{1,0,2:T(4,128)(2,1)S(1)}, u32[]{:S(2)}, u32[]{:S(2)}) collective-permute-start(bf16[4,128,96]{1,0,2:T(4,128)(2,1)S(1)} %convolution_convert_fusion.16), channel_id=1, source_target_pairs={{0,24},{8,32},{16,40},{24,48},{32,56},{40,64},{48,72},{56,80},{64,... | collective-permute-start | bytes 294920 | tf_op jit(solution)/shard_map/ppermute | solution.py:13
  165.0 82.3 %collective-permute-start.9 = (bf16[4,128,96]{1,0,2:T(4,128)(2,1)S(1)}, bf16[4,128,96]{1,0,2:T(4,128)(2,1)S(1)}, u32[]{:S(2)}, u32[]{:S(2)}) collective-permute-start(bf16[4,128,96]{1,0,2:T(4,128)(2,1)S(1)} %convolution_convert_fusion.18), channel_id=1, source_target_pairs={{0,8},{8,16},{16,24},{24,32},{32,40},{40,48},{48,56},{56,64},{64,7... | collective-permute-start | bytes 294920 | tf_op jit(solution)/shard_map/ppermute | solution.py:13
  188.7 33.6 %all-to-all-start.2 = ((bf16[96,32,128]{2,1,0:T(8,128)(2,1)}), bf16[96,32,128]{2,1,0:T(8,128)(2,1)S(1)}, u32[]{:S(2)}, u32[]{:S(2)}) async-start(bf16[96,32,128]{2,1,0:T(8,128)(2,1)} %pad_maximum_fusion), calls=%async_computation.2 | async-start | bytes 1572864 | tf_op jit(solution)/shard_map/all_to_all | solution.py:114
  199.9 47.4 %collective-permute-start.8 = (bf16[4,128,96]{1,0,2:T(4,128)(2,1)S(1)}, bf16[4,128,96]{1,0,2:T(4,128)(2,1)S(1)}, u32[]{:S(2)}, u32[]{:S(2)}) collective-permute-start(bf16[4,128,96]{1,0,2:T(4,128)(2,1)S(1)} %convolution_convert_fusion.19), channel_id=1, source_target_pairs={{0,760},{8,0},{16,8},{24,16},{32,24},{40,32},{48,40},{56,48},{64,5... | collective-permute-start | bytes 294920 | tf_op jit(solution)/shard_map/ppermute | solution.py:13
  210.8 36.6 %collective-permute-start.7 = (bf16[4,128,96]{1,0,2:T(4,128)(2,1)S(1)}, bf16[4,128,96]{1,0,2:T(4,128)(2,1)S(1)}, u32[]{:S(2)}, u32[]{:S(2)}) collective-permute-start(bf16[4,128,96]{1,0,2:T(4,128)(2,1)S(1)} %convolution_convert_fusion.20), channel_id=1, source_target_pairs={{0,752},{8,760},{16,0},{24,8},{32,16},{40,24},{48,32},{56,40},{64,... | collective-permute-start | bytes 294920 | tf_op jit(solution)/shard_map/ppermute | solution.py:13
  216.8 31.5 %copy-start.6 = (bf16[96,1024]{1,0:T(8,128)(2,1)S(1)}, bf16[96,1024]{1,0:T(8,128)(2,1)}, u32[]{:S(2)}) copy-start(bf16[96,1024]{1,0:T(8,128)(2,1)} %param.16) | copy-start | bytes 589828
  223.2 28.4 %all-to-all-start.3 = ((bf16[96,16,128]{2,1,0:T(8,128)(2,1)}), bf16[96,16,128]{2,1,0:T(8,128)(2,1)S(1)}, u32[]{:S(2)}, u32[]{:S(2)}) async-start(bf16[96,16,128]{2,1,0:T(8,128)(2,1)} %broadcast_in_dim.8), calls=%async_computation.3 | async-start | bytes 786432 | tf_op jit(solution)/shard_map/all_to_all | solution.py:117
  234.9 12.5 %collective-permute-start.10 = (bf16[4,128,96]{1,0,2:T(4,128)(2,1)S(1)}, bf16[4,128,96]{1,0,2:T(4,128)(2,1)S(1)}, u32[]{:S(2)}, u32[]{:S(2)}) collective-permute-start(bf16[4,128,96]{1,0,2:T(4,128)(2,1)S(1)} %convolution_convert_fusion.17), channel_id=1, source_target_pairs={{0,16},{8,24},{16,32},{24,40},{32,48},{40,56},{48,64},{56,72},{64,... | collective-permute-start | bytes 294920 | tf_op jit(solution)/shard_map/ppermute | solution.py:13
  238.5 8.9 %collective-permute-start.6 = (bf16[4,128,96]{1,0,2:T(4,128)(2,1)S(1)}, bf16[4,128,96]{1,0,2:T(4,128)(2,1)S(1)}, u32[]{:S(2)}, u32[]{:S(2)}) collective-permute-start(bf16[4,128,96]{1,0,2:T(4,128)(2,1)S(1)} %convolution_convert_fusion.21), channel_id=1, source_target_pairs={{0,744},{8,752},{16,760},{24,0},{32,8},{40,16},{48,24},{56,32},{64... | collective-permute-start | bytes 294920 | tf_op jit(solution)/shard_map/ppermute | solution.py:13
  (4 other events, 18.2 us)

commit v2 on v0

v2 whole, which is shorter than its diff:
```python
import functools

import jax
import jax.numpy as jnp
from jax import lax
from jax.experimental import pallas as pl
from jax.experimental.pallas import tpu as pltpu
from jax.sharding import PartitionSpec as P

REACH = 3
SLOTS = 16
OFFS = 2 * REACH + 1
BLOCK = 128
GROUP = 4
CORES = 2
F32 = jnp.float32
BF16 = jnp.bfloat16
VMEM_BYTES = 40 * 1024 * 1024
VMEM = pl.BlockSpec(memory_space=pltpu.VMEM)
SMEM = pl.BlockSpec(memory_space=pltpu.SMEM)


def lanes(block):
    return pl.ds(pl.multiple_of(block * BLOCK, BLOCK), BLOCK)


def live_tiles(offset, count_ref, product, place_of, total_ref):
    count = count_ref[offset]
    spare = total_ref.shape[0] - 1

    def step(at, carry):
        products = []
        places = []
        for inner in range(GROUP):
            slot = at * GROUP + inner
            tile = offset * SLOTS + slot
            products.append(product(tile))
            places.append(jnp.where(slot < count, place_of(tile), spare))
        for place, value in zip(places, products):
            total_ref[place] += value
        return carry

    lax.fori_loop(0, (count + GROUP - 1) // GROUP, step, 0)


def gather_kernel(count_ref, dest_ref, source_ref, tiles_ref, degree_ref, *refs):
    inputs, out_ref, total_ref = refs[:OFFS], refs[OFFS], refs[OFFS + 1]
    blocks = total_ref.shape[0] - 1
    total_ref[...] = jnp.zeros_like(total_ref)
    for offset in range(OFFS):

        def product(tile, offset=offset):
            picked = inputs[offset][:, lanes(source_ref[tile] % blocks)]
            return lax.dot_general(
                picked, tiles_ref[tile], (((1,), (1,)), ((), ())), preferred_element_type=F32
            )

        live_tiles(offset, count_ref, product, lambda tile: dest_ref[tile], total_ref)
    for block in range(blocks):
        part = pl.ds(block * BLOCK, BLOCK)
        out_ref[:, part] = (total_ref[block] / degree_ref[:, part].astype(F32)).astype(BF16)


def middle_kernel(count_ref, dest_ref, source_ref, tiles_ref, degree_ref, *refs):
    inputs, refs = refs[:4], refs[4:]
    self_ref, neighbour_ref, bias_ref, cotangent_ref, refs = *refs[:4], refs[4:]
    act_ref, grad_ref, weight_ref, bias_out_ref, refs = *refs[:4], refs[4:]
    outs, refs = refs[:OFFS], refs[OFFS:]
    scaled_ref, total_ref = refs
    blocks = total_ref.shape[0] - 1
    half = inputs[0].shape[0]
    contract_first = (((0,), (0,)), ((), ()))
    pre = None
    for at, operand in enumerate(inputs):
        weights = (self_ref, neighbour_ref)[at // 2][pl.ds((at % 2) * half, half), :]
        term = lax.dot_general(
            weights, operand[...], contract_first, preferred_element_type=F32
        )
        pre = term if pre is None else pre + term
    preact = pre.T + bias_ref[...].astype(F32)
    gate_value = jax.nn.sigmoid(preact)
    act_ref[...] = (preact * gate_value).astype(BF16)
    grad = cotangent_ref[...].astype(F32) * gate_value * (1.0 + preact * (1.0 - gate_value))
    grad_pre = grad.astype(BF16)
    grad = grad_pre.astype(F32)
    bias_out_ref[...] = jnp.broadcast_to(
        jnp.sum(grad, axis=0, keepdims=True), bias_out_ref.shape
    ).astype(bias_out_ref.dtype)
    turned = grad.T
    grad_ref[...] = turned.astype(BF16)
    scaled = (turned / degree_ref[...].astype(F32)).astype(BF16)
    for block in range(blocks):
        scaled_ref[block] = scaled[:, block * BLOCK : (block + 1) * BLOCK]
    parts = half // 4
    for at, operand in enumerate(inputs):
        term = jnp.dot(operand[...], grad_pre, preferred_element_type=F32).astype(BF16)
        for piece in range(4):
            first = ((at % 2) * 4 + piece) * 2 * parts + (at // 2) * parts
            weight_ref[pl.ds(first, parts), :] = term[piece * parts : (piece + 1) * parts]
    for offset in range(OFFS):
        total_ref[...] = jnp.zeros_like(total_ref)

        def product(tile):
            return jnp.dot(
                scaled_ref[dest_ref[tile]], tiles_ref[tile], preferred_element_type=F32
            )

        live_tiles(offset, count_ref, product, lambda tile: source_ref[tile] % blocks, total_ref)
        for block in range(blocks):
            outs[offset][:, pl.ds(block * BLOCK, BLOCK)] = total_ref[block].astype(
                outs[offset].dtype
            )


def back_kernel(own_ref, *refs):
    received, refs = refs[: OFFS - 1], refs[OFFS - 1 :]
    grad_ref, self_ref, neighbour_ref, keep_ref, send_ref = refs
    spread = own_ref[...]
    for part in received:
        spread = spread + part[...].astype(F32)
    spread = spread.astype(BF16)
    half = keep_ref.shape[0]
    for at, out in enumerate((keep_ref, send_ref)):
        rows = pl.ds(at * half, half)
        value = jnp.dot(self_ref[rows, :], grad_ref[...], preferred_element_type=F32)
        value = value + jnp.dot(neighbour_ref[rows, :], spread, preferred_element_type=F32)
        out[...] = value.astype(out.dtype)


def call(kernel, in_specs, out_shape, scratch, flops, moved):
    return pl.pallas_call(
        kernel,
        in_specs=in_specs,
        out_shape=out_shape,
        out_specs=jax.tree.map(lambda _: VMEM, out_shape),
        scratch_shapes=scratch,
        compiler_params=pltpu.CompilerParams(vmem_limit_bytes=VMEM_BYTES),
        cost_estimate=pl.CostEstimate(flops=flops, bytes_accessed=moved, transcendentals=0),
    )


def shifted(value, steps):
    count = lax.axis_size("rows")
    pairs = [(source, (source + steps) % count) for source in range(count)]
    return lax.ppermute(value, "rows", pairs)


def on_device(
    features,
    tile_values,
    dest_block,
    source_block,
    tile_count,
    degree,
    self_weight,
    neighbour_weight,
    hidden_bias,
    cotangent,
):
    node_dev, width = features.shape
    blocks = node_dev // BLOCK
    groups = lax.axis_size("rows")
    feats = lax.axis_size("feat")
    stacks = feats // CORES
    hidden_dev = hidden_bias.shape[0]
    core = lax.axis_index("feat") % CORES
    same_core = [[z * CORES + c for z in range(stacks)] for c in range(CORES)]
    other_core = [(f, f ^ 1) for f in range(feats)]

    def over_stacks(value):
        return lax.all_to_all(value, "feat", 0, 0, axis_index_groups=same_core)

    def whole(value):
        copies = jnp.broadcast_to(value[None], (stacks,) + value.shape)
        own = over_stacks(copies).reshape(stacks * value.shape[0], value.shape[1])
        return own, lax.ppermute(own, "feat", other_core)

    turned = features.T
    incoming = [
        turned if offset == REACH else shifted(turned, REACH - offset) for offset in range(OFFS)
    ]

    both = jnp.stack([self_weight, neighbour_weight])
    both = both.reshape(2, width, feats, hidden_dev).transpose(2, 0, 1, 3)
    both = lax.all_to_all(both, "feat", 0, 0).reshape(stacks, CORES, 2, width, hidden_dev)
    own_core = lax.dynamic_index_in_dim(both, core, 1, False)
    far_core = lax.dynamic_index_in_dim(both, 1 - core, 1, False)
    both = jnp.stack([own_core, far_core]).transpose(2, 0, 1, 3, 4)
    both = both.reshape(2, CORES * stacks * width, hidden_dev)
    weight_self, weight_neighbour = both[0], both[1]

    features_own, features_far = whole(turned)

    degrees = degree.reshape(1, node_dev)
    scalars = (tile_count, dest_block, source_block)
    tile_flops = 2 * OFFS * SLOTS * BLOCK * BLOCK * BLOCK
    aggregate = call(
        gather_kernel,
        [SMEM] * 3 + [VMEM] * (2 + OFFS),
        jax.ShapeDtypeStruct((width, node_dev), BF16),
        [pltpu.VMEM((blocks + 1, width, BLOCK), F32)],
        tile_flops,
        tile_values.size * 2,
    )(*scalars, tile_values, degrees, *incoming)
    aggregate_own, aggregate_far = whole(aggregate)

    half = stacks * width
    outs = [
        jax.ShapeDtypeStruct((hidden_dev, node_dev), F32 if offset == REACH else BF16)
        for offset in range(OFFS)
    ]
    middle = call(
        middle_kernel,
        [SMEM] * 3 + [VMEM] * 10,
        [
            jax.ShapeDtypeStruct((node_dev, hidden_dev), BF16),
            jax.ShapeDtypeStruct((hidden_dev, node_dev), BF16),
            jax.ShapeDtypeStruct((4 * half, hidden_dev), BF16),
            jax.ShapeDtypeStruct((8, hidden_dev), F32),
        ]
        + outs,
        [
            pltpu.VMEM((blocks, hidden_dev, BLOCK), BF16),
            pltpu.VMEM((blocks + 1, hidden_dev, BLOCK), F32),
        ],
        tile_flops * 2,
        tile_values.size * 2,
    )(
        *scalars,
        tile_values,
        degrees,
        features_own,
        features_far,
        aggregate_own,
        aggregate_far,
        weight_self,
        weight_neighbour,
        hidden_bias.reshape(1, hidden_dev),
        cotangent,
    )
    activations, grad_turned, weight_part, bias_part = middle[:4]
    outgoing = middle[4:]
    received = [
        shifted(outgoing[offset], offset - REACH) for offset in range(OFFS) if offset != REACH
    ]

    rows_each = 4 * half // groups
    weight_part = weight_part.reshape(groups, rows_each, hidden_dev)
    bias_rows = jnp.broadcast_to(bias_part.astype(BF16)[None], (groups, 8, hidden_dev))
    sent = jnp.concatenate([weight_part, bias_rows], axis=1)
    summed = jnp.sum(lax.all_to_all(sent, "rows", 0, 0).astype(F32), axis=0)
    grad_bias = summed[rows_each]
    piece = summed[:rows_each].astype(BF16)
    per_stack = groups // feats
    pairs = []
    for row in range(groups):
        far, stack, part = row // (groups // 2), row // per_stack % stacks, row % per_stack
        for feat in range(feats):
            column = stack * CORES + (feat % CORES + far) % CORES
            pairs.append((row * feats + feat, (part * feats + feat) * feats + column))
    piece = lax.ppermute(piece, ("rows", "feat"), pairs)
    pieces = lax.all_to_all(
        jnp.broadcast_to(piece[None], (groups,) + piece.shape), "rows", 0, 0
    )
    pieces = pieces.reshape(per_stack, feats, rows_each, hidden_dev).transpose(0, 2, 1, 3)
    pieces = pieces.reshape(2, width, feats * hidden_dev).astype(F32)

    keep, send = call(
        back_kernel,
        [VMEM] * (OFFS + 3),
        [
            jax.ShapeDtypeStruct((half, node_dev), F32),
            jax.ShapeDtypeStruct((half, node_dev), BF16),
        ],
        [],
        8 * half * node_dev * hidden_dev,
        4 * half * node_dev,
    )(outgoing[REACH], *received, grad_turned, weight_self, weight_neighbour)
    got = lax.ppermute(send, "feat", other_core)
    chip_sum = (keep + got.astype(F32)).astype(BF16).reshape(stacks, width, node_dev)
    grad_features = jnp.sum(over_stacks(chip_sum).astype(F32), axis=0).astype(BF16).T
    return (activations, grad_features, pieces[0], pieces[1], grad_bias)


def solution(mesh):
    in_specs = (
        P("rows", "feat"),
        P("rows", None, None),
        P("rows"),
        P("rows"),
        P("rows"),
        P("rows"),
        P("feat", None),
        P("feat", None),
        P("feat"),
        P("rows", "feat"),
    )
    out_specs = (P("rows", "feat"), P("rows", "feat"), P("feat", None), P("feat", None), P("feat"))
    return jax.shard_map(
        on_device, mesh=mesh, in_specs=in_specs, out_specs=out_specs, check_vma=False
    )
```

time: 1580 us -> 215 us (0.14)
  the two profiles are of different devices: /device:TPU:192 before, /device:TPU:1 now
where the time goes in v2:
time: 215 us; the launch traced here: 211 us
  starting transfers between devices  121 us (56%)
  waiting for transfers between devices  64 us (30%)
  local copies, waits for them, and re-layouts  11.6 us (5%)
  Pallas kernels  11.3 us (5%)
  other arithmetic  2.75 us (1%)
    ppermute x12, starting transfers between devices, shifted(): return lax.ppermute(value, 'rows', pairs)  44.2 us
    all_to_all x3, starting transfers between devices, over_stacks(): return lax.all_to_all(value, 'feat', 0, 0, axis_index_groups=same_core)  31.8 us
    all_to_all x3, waiting for transfers between devices, over_stacks(): return lax.all_to_all(value, 'feat', 0, 0, axis_index_groups=same_core)  24.8 us
    ppermute x12, waiting for transfers between devices, shifted(): return lax.ppermute(value, 'rows', pairs)  16.4 us
    all_to_all x1, starting transfers between devices, on_device(): lax.all_to_all(jnp.broadcast_to(piece[None], (groups,) + piece.shape), 'r...  14.1 us
    all_to_all x1, waiting for transfers between devices, on_device(): lax.all_to_all(jnp.broadcast_to(piece[None], (groups,) + piece.shape), 'r...  11.4 us
    all_to_all x1, starting transfers between devices, on_device(): summed = jnp.sum(lax.all_to_all(sent, 'rows', 0, 0).astype(F32), axis=0)  10.9 us
    all_to_all x1, waiting for transfers between devices, on_device(): lax.all_to_all(both, 'feat', 0, 0)  10.1 us
  transfers between devices with their start and end apart: 22, of which 11 were waited for; matrix products, arithmetic and copies ran while one was open for 2% of the time, Pallas kernels for 2%

profile of v2, /device:TPU:1, one launch (start us, length us, event | category | flops | bytes accessed | tf_op | source)
XLA Modules:
  0.0 211.4 jit_solution(15947779974129308942)
XLA Ops:
  2.4 15.0 %all-to-all-start = ((bf16[4,96,512]{2,1,0:T(8,128)(2,1)}), bf16[4,96,512]{2,1,0:T(8,128)(2,1)S(1)}, u32[]{:S(2)}, u32[]{:S(2)}) async-start(bf16[4,96,512]{2,1,0:T(8,128)(2,1)} %broadcast_in_dim.8), calls=%async_computation | async-start | bytes 786432 | tf_op jit(solution)/shard_map/all_to_all | solution.py:171
  17.5 7.3 %collective-permute-start.6 = (bf16[96,512]{1,0:T(8,128)(2,1)S(1)}, bf16[96,512]{1,0:T(8,128)(2,1)S(1)}, u32[]{:S(2)}, u32[]{:S(2)}) collective-permute-start(bf16[96,512]{1,0:T(8,128)(2,1)S(1)} %bitcast.51), channel_id=1, source_target_pairs={{0,744},{8,752},{16,760},{24,0},{32,8},{40,16},{48,24},{56,32},{64... | collective-permute-start | bytes 294920 | tf_op jit(solution)/shard_map/ppermute | solution.py:145
  24.8 3.9 %collective-permute-start.5 = (bf16[96,512]{1,0:T(8,128)(2,1)S(1)}, bf16[96,512]{1,0:T(8,128)(2,1)S(1)}, u32[]{:S(2)}, u32[]{:S(2)}) collective-permute-start(bf16[96,512]{1,0:T(8,128)(2,1)S(1)} %bitcast.52), channel_id=1, source_target_pairs={{0,752},{8,760},{16,0},{24,8},{32,16},{40,24},{48,32},{56,40},{64,... | collective-permute-start | bytes 294920 | tf_op jit(solution)/shard_map/ppermute | solution.py:145
  28.6 3.1 %collective-permute-start.4 = (bf16[96,512]{1,0:T(8,128)(2,1)S(1)}, bf16[96,512]{1,0:T(8,128)(2,1)S(1)}, u32[]{:S(2)}, u32[]{:S(2)}) collective-permute-start(bf16[96,512]{1,0:T(8,128)(2,1)S(1)} %bitcast.53), channel_id=1, source_target_pairs={{0,760},{8,0},{16,8},{24,16},{32,24},{40,32},{48,40},{56,48},{64,5... | collective-permute-start | bytes 294920 | tf_op jit(solution)/shard_map/ppermute | solution.py:145
  33.9 4.1 %collective-permute-start.2 = (bf16[96,512]{1,0:T(8,128)(2,1)S(1)}, bf16[96,512]{1,0:T(8,128)(2,1)S(1)}, u32[]{:S(2)}, u32[]{:S(2)}) collective-permute-start(bf16[96,512]{1,0:T(8,128)(2,1)S(1)} %bitcast.55), channel_id=1, source_target_pairs={{0,16},{8,24},{16,32},{24,40},{32,48},{40,56},{48,64},{56,72},{64,... | collective-permute-start | bytes 294920 | tf_op jit(solution)/shard_map/ppermute | solution.py:145
  40.0 2.7 %collective-permute-done.3.refs_2_ = bf16[96,512]{1,0:T(8,128)(2,1)S(1)} collective-permute-done((bf16[96,512]{1,0:T(8,128)(2,1)S(1)}, bf16[96,512]{1,0:T(8,128)(2,1)S(1)}, u32[]{:S(2)}, u32[]{:S(2)}) %collective-permute-start.3) | collective-permute-done | bytes 98336 | tf_op jit(solution)/shard_map/ppermute | solution.py:145
  44.6 2.9 %collective-permute-done.1.refs_0_ = bf16[96,512]{1,0:T(8,128)(2,1)S(1)} collective-permute-done((bf16[96,512]{1,0:T(8,128)(2,1)S(1)}, bf16[96,512]{1,0:T(8,128)(2,1)S(1)}, u32[]{:S(2)}, u32[]{:S(2)}) %collective-permute-start.1) | collective-permute-done | bytes 98336 | tf_op jit(solution)/shard_map/ppermute | solution.py:145
  49.6 4.6 %shard_map.137 = bf16[96,512]{1,0:T(8,128)(2,1)S(1)} custom-call(s32[7]{0:T(128)S(1)} %copy-done.5, s32[112]{0:T(128)S(1)} %copy-done.6, s32[112]{0:T(128)S(1)} %copy-done.7, bf16[112,128,128]{2,1,0:T(8,128)(2,1)S(1)} %copy-done, s32[1,512]{1,0:T(1,128)S(1)} %bitcast.58, bf16[96,512]{1,0:T(8,128)(2,1)S(1)} %collective-permute-done.1.refs_0_, ...), custom_call_target="tpu_custom_call" | custom-call | flops 469762048 | bytes 3670016 | tf_op jit(solution)/shard_map/pallas_call | solution.py:197
  55.1 10.6 %all-to-all-start.1 = ((bf16[4,96,512]{2,1,0:T(8,128)(2,1)}), bf16[4,96,512]{2,1,0:T(8,128)(2,1)S(1)}, u32[]{:S(2)}, u32[]{:S(2)}) async-start(bf16[4,96,512]{2,1,0:T(8,128)(2,1)} %broadcast_in_dim.9), calls=%async_computation.1 | async-start | bytes 786432 | tf_op jit(solution)/shard_map/all_to_all | solution.py:171
  66.6 13.0 %all-to-all-done.1 = bf16[4,96,512]{2,1,0:T(8,128)(2,1)S(1)} async-done(((bf16[4,96,512]{2,1,0:T(8,128)(2,1)}), bf16[4,96,512]{2,1,0:T(8,128)(2,1)S(1)}, u32[]{:S(2)}, u32[]{:S(2)}) %all-to-all-start.1) | async-done | bytes 393248 | tf_op jit(solution)/shard_map/all_to_all | solution.py:171
  79.7 9.5 %all-to-all-start.2 = ((bf16[8,2,96,128]{3,2,1,0:T(8,128)(2,1)}), bf16[8,2,96,128]{3,2,1,0:T(8,128)(2,1)S(1)}, u32[]{:S(2)}, u32[]{:S(2)}) async-start(bf16[8,2,96,128]{3,2,1,0:T(8,128)(2,1)} %copy.27), calls=%async_computation.2 | async-start | bytes 786432 | tf_op jit(solution)/shard_map/all_to_all | solution.py:185
  93.4 10.1 %all-to-all-done.2 = bf16[8,2,96,128]{3,2,1,0:T(8,128)(2,1)S(1)} async-done(((bf16[8,2,96,128]{3,2,1,0:T(8,128)(2,1)}), bf16[8,2,96,128]{3,2,1,0:T(8,128)(2,1)S(1)}, u32[]{:S(2)}, u32[]{:S(2)}) %all-to-all-start.2) | async-done | bytes 393248 | tf_op jit(solution)/shard_map/all_to_all | solution.py:185
  106.5 6.1 %shard_map.138 = (bf16[512,128]{1,0:T(8,128)(2,1)}, bf16[128,512]{1,0:T(8,128)(2,1)S(1)}, bf16[1536,128]{1,0:T(8,128)(2,1)S(1)}, f32[8,128]{1,0:T(8,128)S(1)}, b...) custom-call(s32[7]{0:T(128)S(1)} %copy-done.5, ...), custom_call_target="tpu_custom_call" | custom-call | flops 939524096 | bytes 3670016 | tf_op jit(solution)/shard_map/pallas_call | solution.py:212
  113.5 10.9 %all-to-all-start.4 = ((bf16[96,24,128]{2,1,0:T(8,128)(2,1)}), bf16[96,24,128]{2,1,0:T(8,128)(2,1)S(1)}, u32[]{:S(2)}, u32[]{:S(2)}) async-start(bf16[96,24,128]{2,1,0:T(8,128)(2,1)} %pad_maximum_fusion), calls=%async_computation.4 | async-start | bytes 1179648 | tf_op jit(solution)/shard_map/all_to_all | solution.py:251
  124.4 6.5 %collective-permute-start.8 = (bf16[128,512]{1,0:T(8,128)(2,1)S(1)}, bf16[128,512]{1,0:T(8,128)(2,1)S(1)}, u32[]{:S(2)}, u32[]{:S(2)}) collective-permute-start(bf16[128,512]{1,0:T(8,128)(2,1)S(1)} %get-tuple-element.20), channel_id=1, source_target_pairs={{0,744},{8,752},{16,760},{24,0},{32,8},{40,16},{48,24},{56,32},{64... | collective-permute-start | bytes 393224 | tf_op jit(solution)/shard_map/ppermute | solution.py:145
  131.0 4.0 %collective-permute-start.9 = (bf16[128,512]{1,0:T(8,128)(2,1)S(1)}, bf16[128,512]{1,0:T(8,128)(2,1)S(1)}, u32[]{:S(2)}, u32[]{:S(2)}) collective-permute-start(bf16[128,512]{1,0:T(8,128)(2,1)S(1)} %get-tuple-element.21), channel_id=1, source_target_pairs={{0,752},{8,760},{16,0},{24,8},{32,16},{40,24},{48,32},{56,40},{64,... | collective-permute-start | bytes 393224 | tf_op jit(solution)/shard_map/ppermute | solution.py:145
  135.0 3.1 %collective-permute-start.10 = (bf16[128,512]{1,0:T(8,128)(2,1)S(1)}, bf16[128,512]{1,0:T(8,128)(2,1)S(1)}, u32[]{:S(2)}, u32[]{:S(2)}) collective-permute-start(bf16[128,512]{1,0:T(8,128)(2,1)S(1)} %get-tuple-element.22), channel_id=1, source_target_pairs={{0,760},{8,0},{16,8},{24,16},{32,24},{40,32},{48,40},{56,48},{64,5... | collective-permute-start | bytes 393224 | tf_op jit(solution)/shard_map/ppermute | solution.py:145
  140.3 4.0 %collective-permute-start.12 = (bf16[128,512]{1,0:T(8,128)(2,1)S(1)}, bf16[128,512]{1,0:T(8,128)(2,1)S(1)}, u32[]{:S(2)}, u32[]{:S(2)}) collective-permute-start(bf16[128,512]{1,0:T(8,128)(2,1)S(1)} %get-tuple-element.24), channel_id=1, source_target_pairs={{0,16},{8,24},{16,32},{24,40},{32,48},{40,56},{48,64},{56,72},{64,... | collective-permute-start | bytes 393224 | tf_op jit(solution)/shard_map/ppermute | solution.py:145
  150.9 4.1 %collective-permute-done.13.refs_5_ = bf16[128,512]{1,0:T(8,128)(2,1)S(1)} collective-permute-done((bf16[128,512]{1,0:T(8,128)(2,1)S(1)}, bf16[128,512]{1,0:T(8,128)(2,1)S(1)}, u32[]{:S(2)}, u32[]{:S(2)}) %collective-permute-start.13) | collective-permute-done | bytes 131104 | tf_op jit(solution)/shard_map/ppermute | solution.py:145
  155.7 4.0 %collective-permute-start.14 = (bf16[384,512]{1,0:T(8,128)(2,1)S(1)}, bf16[384,512]{1,0:T(8,128)(2,1)S(1)}, u32[]{:S(2)}, u32[]{:S(2)}) collective-permute-start(bf16[384,512]{1,0:T(8,128)(2,1)S(1)} %get-tuple-element.28), channel_id=1, source_target_pairs={{0,1},{1,0},{2,3},{3,2},{4,5},{5,4},{6,7},{7,6},{8,9},{9,8},{10,11... | collective-permute-start | bytes 1179656 | tf_op jit(solution)/shard_map/ppermute | solution.py:279
  161.9 6.1 %all-to-all-start.3 = ((bf16[4,96,512]{2,1,0:T(8,128)(2,1)}), bf16[4,96,512]{2,1,0:T(8,128)(2,1)S(1)}, u32[]{:S(2)}, u32[]{:S(2)}) async-start(bf16[4,96,512]{2,1,0:T(8,128)(2,1)} %bitcast.12), calls=%async_computation.3 | async-start | bytes 786432 | tf_op jit(solution)/shard_map/all_to_all | solution.py:171
  170.1 11.7 %all-to-all-done.3 = bf16[4,96,512]{2,1,0:T(8,128)(2,1)S(1)} async-done(((bf16[4,96,512]{2,1,0:T(8,128)(2,1)}), bf16[4,96,512]{2,1,0:T(8,128)(2,1)S(1)}, u32[]{:S(2)}, u32[]{:S(2)}) %all-to-all-start.3) | async-done | bytes 393248 | tf_op jit(solution)/shard_map/all_to_all | solution.py:171
  182.6 14.1 %all-to-all-start.5 = ((bf16[96,16,128]{2,1,0:T(8,128)(2,1)}), bf16[96,16,128]{2,1,0:T(8,128)(2,1)S(1)}, u32[]{:S(2)}, u32[]{:S(2)}) async-start(bf16[96,16,128]{2,1,0:T(8,128)(2,1)} %broadcast_in_dim.11), calls=%async_computation.5 | async-start | bytes 786432 | tf_op jit(solution)/shard_map/all_to_all | solution.py:262
  198.0 11.4 %all-to-all-done.5 = bf16[96,16,128]{2,1,0:T(8,128)(2,1)S(1)} async-done(((bf16[96,16,128]{2,1,0:T(8,128)(2,1)}), bf16[96,16,128]{2,1,0:T(8,128)(2,1)S(1)}, u32[]{:S(2)}, u32[]{:S(2)}) %all-to-all-start.5) | async-done | bytes 393248 | tf_op jit(solution)/shard_map/all_to_all | solution.py:262
  (70 shorter events, 37.5 us)
Async XLA Ops:
  0.6 46.9 %copy-start.5 = (s32[7]{0:T(128)S(1)}, s32[7]{0:T(128)}, u32[]{:S(2)}) copy-start(s32[7]{0:T(128)} %count_ref.3) | copy-start | bytes 88
  0.7 46.9 %copy-start.7 = (s32[112]{0:T(128)S(1)}, s32[112]{0:T(128)}, u32[]{:S(2)}) copy-start(s32[112]{0:T(128)} %source_ref.3) | copy-start | bytes 1348
  2.4 51.9 %all-to-all-start = ((bf16[4,96,512]{2,1,0:T(8,128)(2,1)}), bf16[4,96,512]{2,1,0:T(8,128)(2,1)S(1)}, u32[]{:S(2)}, u32[]{:S(2)}) async-start(bf16[4,96,512]{2,1,0:T(8,128)(2,1)} %broadcast_in_dim.8), calls=%async_computation | async-start | bytes 786432 | tf_op jit(solution)/shard_map/all_to_all | solution.py:171
  17.5 20.6 %collective-permute-start.6 = (bf16[96,512]{1,0:T(8,128)(2,1)S(1)}, bf16[96,512]{1,0:T(8,128)(2,1)S(1)}, u32[]{:S(2)}, u32[]{:S(2)}) collective-permute-start(bf16[96,512]{1,0:T(8,128)(2,1)S(1)} %bitcast.51), channel_id=1, source_target_pairs={{0,744},{8,752},{16,760},{24,0},{32,8},{40,16},{48,24},{56,32},{64... | collective-permute-start | bytes 294920 | tf_op jit(solution)/shard_map/ppermute | solution.py:145
  24.8 15.2 %collective-permute-start.5 = (bf16[96,512]{1,0:T(8,128)(2,1)S(1)}, bf16[96,512]{1,0:T(8,128)(2,1)S(1)}, u32[]{:S(2)}, u32[]{:S(2)}) collective-permute-start(bf16[96,512]{1,0:T(8,128)(2,1)S(1)} %bitcast.52), channel_id=1, source_target_pairs={{0,752},{8,760},{16,0},{24,8},{32,16},{40,24},{48,32},{56,40},{64,... | collective-permute-start | bytes 294920 | tf_op jit(solution)/shard_map/ppermute | solution.py:145
  28.6 11.4 %collective-permute-start.4 = (bf16[96,512]{1,0:T(8,128)(2,1)S(1)}, bf16[96,512]{1,0:T(8,128)(2,1)S(1)}, u32[]{:S(2)}, u32[]{:S(2)}) collective-permute-start(bf16[96,512]{1,0:T(8,128)(2,1)S(1)} %bitcast.53), channel_id=1, source_target_pairs={{0,760},{8,0},{16,8},{24,16},{32,24},{40,32},{48,40},{56,48},{64,5... | collective-permute-start | bytes 294920 | tf_op jit(solution)/shard_map/ppermute | solution.py:145
  31.7 11.0 %collective-permute-start.3 = (bf16[96,512]{1,0:T(8,128)(2,1)S(1)}, bf16[96,512]{1,0:T(8,128)(2,1)S(1)}, u32[]{:S(2)}, u32[]{:S(2)}) collective-permute-start(bf16[96,512]{1,0:T(8,128)(2,1)S(1)} %bitcast.54), channel_id=1, source_target_pairs={{0,8},{8,16},{16,24},{24,32},{32,40},{40,48},{48,56},{56,64},{64,7... | collective-permute-start | bytes 294920 | tf_op jit(solution)/shard_map/ppermute | solution.py:145
  33.9 10.7 %collective-permute-start.2 = (bf16[96,512]{1,0:T(8,128)(2,1)S(1)}, bf16[96,512]{1,0:T(8,128)(2,1)S(1)}, u32[]{:S(2)}, u32[]{:S(2)}) collective-permute-start(bf16[96,512]{1,0:T(8,128)(2,1)S(1)} %bitcast.55), channel_id=1, source_target_pairs={{0,16},{8,24},{16,32},{24,40},{32,48},{40,56},{48,64},{56,72},{64,... | collective-permute-start | bytes 294920 | tf_op jit(solution)/shard_map/ppermute | solution.py:145
  38.1 9.5 %collective-permute-start.1 = (bf16[96,512]{1,0:T(8,128)(2,1)S(1)}, bf16[96,512]{1,0:T(8,128)(2,1)S(1)}, u32[]{:S(2)}, u32[]{:S(2)}) collective-permute-start(bf16[96,512]{1,0:T(8,128)(2,1)S(1)} %bitcast.56), channel_id=1, source_target_pairs={{0,24},{8,32},{16,40},{24,48},{32,56},{40,64},{48,72},{56,80},{64,... | collective-permute-start | bytes 294920 | tf_op jit(solution)/shard_map/ppermute | solution.py:145
  55.1 24.6 %all-to-all-start.1 = ((bf16[4,96,512]{2,1,0:T(8,128)(2,1)}), bf16[4,96,512]{2,1,0:T(8,128)(2,1)S(1)}, u32[]{:S(2)}, u32[]{:S(2)}) async-start(bf16[4,96,512]{2,1,0:T(8,128)(2,1)} %broadcast_in_dim.9), calls=%async_computation.1 | async-start | bytes 786432 | tf_op jit(solution)/shard_map/all_to_all | solution.py:171
  79.7 23.9 %all-to-all-start.2 = ((bf16[8,2,96,128]{3,2,1,0:T(8,128)(2,1)}), bf16[8,2,96,128]{3,2,1,0:T(8,128)(2,1)S(1)}, u32[]{:S(2)}, u32[]{:S(2)}) async-start(bf16[8,2,96,128]{3,2,1,0:T(8,128)(2,1)} %copy.27), calls=%async_computation.2 | async-start | bytes 786432 | tf_op jit(solution)/shard_map/all_to_all | solution.py:185
  89.1 14.6 %collective-permute-start = (bf16[384,512]{1,0:T(8,128)(2,1)S(1)}, bf16[384,512]{1,0:T(8,128)(2,1)S(1)}, u32[]{:S(2)}, u32[]{:S(2)}) collective-permute-start(bf16[384,512]{1,0:T(8,128)(2,1)S(1)} %bitcast.45), channel_id=1, source_target_pairs={{0,1},{1,0},{2,3},{3,2},{4,5},{5,4},{6,7},{7,6},{8,9},{9,8},{10,11... | collective-permute-start | bytes 1179656 | tf_op jit(solution)/shard_map/ppermute | solution.py:176
  91.0 12.7 %collective-permute-start.7 = (bf16[384,512]{1,0:T(8,128)(2,1)S(1)}, bf16[384,512]{1,0:T(8,128)(2,1)S(1)}, u32[]{:S(2)}, u32[]{:S(2)}) collective-permute-start(bf16[384,512]{1,0:T(8,128)(2,1)S(1)} %bitcast.47), channel_id=1, source_target_pairs={{0,1},{1,0},{2,3},{3,2},{4,5},{5,4},{6,7},{7,6},{8,9},{9,8},{10,11... | collective-permute-start | bytes 1179656 | tf_op jit(solution)/shard_map/ppermute | solution.py:176
  113.5 48.4 %all-to-all-start.4 = ((bf16[96,24,128]{2,1,0:T(8,128)(2,1)}), bf16[96,24,128]{2,1,0:T(8,128)(2,1)S(1)}, u32[]{:S(2)}, u32[]{:S(2)}) async-start(bf16[96,24,128]{2,1,0:T(8,128)(2,1)} %pad_maximum_fusion), calls=%async_computation.4 | async-start | bytes 1179648 | tf_op jit(solution)/shard_map/all_to_all | solution.py:251
  124.4 19.8 %collective-permute-start.8 = (bf16[128,512]{1,0:T(8,128)(2,1)S(1)}, bf16[128,512]{1,0:T(8,128)(2,1)S(1)}, u32[]{:S(2)}, u32[]{:S(2)}) collective-permute-start(bf16[128,512]{1,0:T(8,128)(2,1)S(1)} %get-tuple-element.20), channel_id=1, source_target_pairs={{0,744},{8,752},{16,760},{24,0},{32,8},{40,16},{48,24},{56,32},{64... | collective-permute-start | bytes 393224 | tf_op jit(solution)/shard_map/ppermute | solution.py:145
  131.0 15.2 %collective-permute-start.9 = (bf16[128,512]{1,0:T(8,128)(2,1)S(1)}, bf16[128,512]{1,0:T(8,128)(2,1)S(1)}, u32[]{:S(2)}, u32[]{:S(2)}) collective-permute-start(bf16[128,512]{1,0:T(8,128)(2,1)S(1)} %get-tuple-element.21), channel_id=1, source_target_pairs={{0,752},{8,760},{16,0},{24,8},{32,16},{40,24},{48,32},{56,40},{64,... | collective-permute-start | bytes 393224 | tf_op jit(solution)/shard_map/ppermute | solution.py:145
  135.0 11.3 %collective-permute-start.10 = (bf16[128,512]{1,0:T(8,128)(2,1)S(1)}, bf16[128,512]{1,0:T(8,128)(2,1)S(1)}, u32[]{:S(2)}, u32[]{:S(2)}) collective-permute-start(bf16[128,512]{1,0:T(8,128)(2,1)S(1)} %get-tuple-element.22), channel_id=1, source_target_pairs={{0,760},{8,0},{16,8},{24,16},{32,24},{40,32},{48,40},{56,48},{64,5... | collective-permute-start | bytes 393224 | tf_op jit(solution)/shard_map/ppermute | solution.py:145
  138.1 10.8 %collective-permute-start.11 = (bf16[128,512]{1,0:T(8,128)(2,1)S(1)}, bf16[128,512]{1,0:T(8,128)(2,1)S(1)}, u32[]{:S(2)}, u32[]{:S(2)}) collective-permute-start(bf16[128,512]{1,0:T(8,128)(2,1)S(1)} %get-tuple-element.23), channel_id=1, source_target_pairs={{0,8},{8,16},{16,24},{24,32},{32,40},{40,48},{48,56},{56,64},{64,7... | collective-permute-start | bytes 393224 | tf_op jit(solution)/shard_map/ppermute | solution.py:145
  140.3 10.7 %collective-permute-start.12 = (bf16[128,512]{1,0:T(8,128)(2,1)S(1)}, bf16[128,512]{1,0:T(8,128)(2,1)S(1)}, u32[]{:S(2)}, u32[]{:S(2)}) collective-permute-start(bf16[128,512]{1,0:T(8,128)(2,1)S(1)} %get-tuple-element.24), channel_id=1, source_target_pairs={{0,16},{8,24},{16,32},{24,40},{32,48},{40,56},{48,64},{56,72},{64,... | collective-permute-start | bytes 393224 | tf_op jit(solution)/shard_map/ppermute | solution.py:145
  144.3 10.7 %collective-permute-start.13 = (bf16[128,512]{1,0:T(8,128)(2,1)S(1)}, bf16[128,512]{1,0:T(8,128)(2,1)S(1)}, u32[]{:S(2)}, u32[]{:S(2)}) collective-permute-start(bf16[128,512]{1,0:T(8,128)(2,1)S(1)} %get-tuple-element.25), channel_id=1, source_target_pairs={{0,24},{8,32},{16,40},{24,48},{32,56},{40,64},{48,72},{56,80},{64,... | collective-permute-start | bytes 393224 | tf_op jit(solution)/shard_map/ppermute | solution.py:145
  155.7 5.4 %collective-permute-start.14 = (bf16[384,512]{1,0:T(8,128)(2,1)S(1)}, bf16[384,512]{1,0:T(8,128)(2,1)S(1)}, u32[]{:S(2)}, u32[]{:S(2)}) collective-permute-start(bf16[384,512]{1,0:T(8,128)(2,1)S(1)} %get-tuple-element.28), channel_id=1, source_target_pairs={{0,1},{1,0},{2,3},{3,2},{4,5},{5,4},{6,7},{7,6},{8,9},{9,8},{10,11... | collective-permute-start | bytes 1179656 | tf_op jit(solution)/shard_map/ppermute | solution.py:279
  161.9 19.9 %all-to-all-start.3 = ((bf16[4,96,512]{2,1,0:T(8,128)(2,1)}), bf16[4,96,512]{2,1,0:T(8,128)(2,1)S(1)}, u32[]{:S(2)}, u32[]{:S(2)}) async-start(bf16[4,96,512]{2,1,0:T(8,128)(2,1)} %bitcast.12), calls=%async_computation.3 | async-start | bytes 786432 | tf_op jit(solution)/shard_map/all_to_all | solution.py:171
  168.1 13.7 %collective-permute-start.15 = (bf16[16,128]{1,0:T(8,128)(2,1)S(1)}, bf16[16,128]{1,0:T(8,128)(2,1)S(1)}, u32[]{:S(2)}, u32[]{:S(2)}) collective-permute-start(bf16[16,128]{1,0:T(8,128)(2,1)S(1)} %slice.37), channel_id=1, source_target_pairs={{0,0},{1,9},{2,16},{3,25},{4,32},{5,41},{6,48},{7,57},{8,64},{9,73... | collective-permute-start | bytes 12296 | tf_op jit(solution)/shard_map/ppermute | solution.py:261
  182.6 26.7 %all-to-all-start.5 = ((bf16[96,16,128]{2,1,0:T(8,128)(2,1)}), bf16[96,16,128]{2,1,0:T(8,128)(2,1)S(1)}, u32[]{:S(2)}, u32[]{:S(2)}) async-start(bf16[96,16,128]{2,1,0:T(8,128)(2,1)} %broadcast_in_dim.11), calls=%async_computation.5 | async-start | bytes 786432 | tf_op jit(solution)/shard_map/all_to_all | solution.py:262
  (9 other events, 139.5 us)

commit v3 on v2

v3 whole, which is shorter than its diff:
```python
import functools

import jax
import jax.numpy as jnp
from jax import lax
from jax.experimental import pallas as pl
from jax.experimental.pallas import tpu as pltpu
from jax.sharding import PartitionSpec as P

REACH = 3
SLOTS = 16
OFFS = 2 * REACH + 1
BLOCK = 128
GROUP = 4
CORES = 2
TRIO = 3
F32 = jnp.float32
BF16 = jnp.bfloat16
VMEM_BYTES = 40 * 1024 * 1024
VMEM = pl.BlockSpec(memory_space=pltpu.VMEM)
SMEM = pl.BlockSpec(memory_space=pltpu.SMEM)


def lanes(block):
    return pl.ds(pl.multiple_of(block * BLOCK, BLOCK), BLOCK)


def live_tiles(offset, count_ref, product, place_of, total_ref):
    count = count_ref[offset]
    spare = total_ref.shape[0] - 1

    def step(at, carry):
        products = []
        places = []
        for inner in range(GROUP):
            slot = at * GROUP + inner
            tile = offset * SLOTS + slot
            products.append(product(tile))
            places.append(jnp.where(slot < count, place_of(tile), spare))
        for place, value in zip(places, products):
            total_ref[place] += value
        return carry

    lax.fori_loop(0, (count + GROUP - 1) // GROUP, step, 0)


def band_slot(place_ref, offset):
    return (place_ref[0] + offset) // TRIO * TRIO + offset % TRIO


def pack_kernel(features_ref, self_ref, neighbour_ref, out_ref):
    width = features_ref.shape[0]
    for stack in range(out_ref.shape[0]):
        out_ref[stack, pl.ds(0, width), :] = features_ref[...]
        for core in range(CORES):
            for kind, ref in enumerate((self_ref, neighbour_ref)):
                out_ref[stack, pl.ds(width, width), pl.ds((core * 2 + kind) * BLOCK, BLOCK)] = ref[
                    :, pl.ds((stack * CORES + core) * BLOCK, BLOCK)
                ]


def gather_kernel(
    place_ref,
    count_ref,
    dest_ref,
    source_ref,
    tiles_ref,
    degree_ref,
    below_ref,
    level_ref,
    above_ref,
    out_ref,
    total_ref,
    band_ref,
):
    blocks = total_ref.shape[0] - 1
    total_ref[...] = jnp.zeros_like(total_ref)
    for trio, ref in enumerate((below_ref, level_ref, above_ref)):
        band_ref[pl.ds(trio * TRIO, TRIO)] = ref[...]
    for offset in range(OFFS):
        slot = band_slot(place_ref, offset)

        def product(tile, slot=slot):
            picked = band_ref[slot, :, lanes(source_ref[tile] % blocks)]
            return lax.dot_general(
                picked, tiles_ref[tile], (((1,), (1,)), ((), ())), preferred_element_type=F32
            )

        live_tiles(offset, count_ref, product, lambda tile: dest_ref[tile], total_ref)
    for block in range(blocks):
        part = pl.ds(block * BLOCK, BLOCK)
        value = (total_ref[block] / degree_ref[:, part].astype(F32)).astype(BF16)
        for copy in range(out_ref.shape[0]):
            out_ref[copy, :, part] = value


def middle_kernel(place_ref, core_ref, count_ref, dest_ref, source_ref, tiles_ref, degree_ref, *refs):
    packed, aggregates, refs = refs[:2], refs[2:4], refs[4:]
    bias_ref, cotangent_ref, refs = *refs[:2], refs[2:]
    act_ref, grad_ref, weight_ref, bias_out_ref, self_ref, neighbour_ref, refs = (
        *refs[:6],
        refs[6:],
    )
    below_ref, level_ref, above_ref, features_ref, scaled_ref, total_ref = refs
    blocks = scaled_ref.shape[0]
    stacks, width, _ = aggregates[0].shape
    half = stacks * width
    contract_first = (((0,), (0,)), ((), ()))
    for far, ref in enumerate(packed):
        for stack in range(stacks):
            rows = pl.ds(far * half + stack * width, width)
            features_ref[rows, :] = ref[stack, pl.ds(0, width), :]
            for kind, out in enumerate((self_ref, neighbour_ref)):
                out[rows, :] = ref[stack, pl.ds(width, width), lanes(core_ref[0] * 2 + kind)]
    pre = lax.dot_general(
        self_ref[...], features_ref[...], contract_first, preferred_element_type=F32
    )
    for far, ref in enumerate(aggregates):
        pre = pre + lax.dot_general(
            neighbour_ref[pl.ds(far * half, half), :],
            ref[...].reshape(half, -1),
            contract_first,
            preferred_element_type=F32,
        )
    preact = pre.T + bias_ref[...].astype(F32)
    gate_value = jax.nn.sigmoid(preact)
    act_ref[...] = (preact * gate_value).astype(BF16)
    grad = cotangent_ref[...].astype(F32) * gate_value * (1.0 + preact * (1.0 - gate_value))
    grad_pre = grad.astype(BF16)
    grad = grad_pre.astype(F32)
    bias_out_ref[...] = jnp.broadcast_to(
        jnp.sum(grad, axis=0, keepdims=True), bias_out_ref.shape
    ).astype(bias_out_ref.dtype)
    turned = grad.T
    grad_ref[...] = turned.astype(BF16)
    scaled = (turned / degree_ref[...].astype(F32)).astype(BF16)
    for block in range(blocks):
        scaled_ref[block] = scaled[:, block * BLOCK : (block + 1) * BLOCK]
    for far in range(CORES):
        operands = (features_ref[pl.ds(far * half, half), :], aggregates[far][...].reshape(half, -1))
        for kind, operand in enumerate(operands):
            term = jnp.dot(operand, grad_pre, preferred_element_type=F32).astype(BF16)
            for stack in range(stacks):
                first = ((far * stacks + stack) * 2 + kind) * width
                weight_ref[pl.ds(first, width), :] = term[stack * width : (stack + 1) * width]
    total_ref[...] = jnp.zeros_like(total_ref)
    for offset in range(OFFS):
        slot = band_slot(place_ref, offset)

        def product(tile):
            return jnp.dot(
                scaled_ref[dest_ref[tile]], tiles_ref[tile], preferred_element_type=F32
            )

        def place(tile, slot=slot):
            return slot * blocks + source_ref[tile] % blocks

        live_tiles(offset, count_ref, product, place, total_ref)
    for trio, out in enumerate((below_ref, level_ref, above_ref)):
        for slot in range(TRIO):
            for block in range(blocks):
                out[slot, :, pl.ds(block * BLOCK, BLOCK)] = total_ref[
                    (trio * TRIO + slot) * blocks + block
                ].astype(out.dtype)


def trio_kernel(level_ref, below_ref, above_ref, *outs):
    for slot, out in enumerate(outs):
        value = level_ref[slot] + below_ref[slot].astype(F32) + above_ref[slot].astype(F32)
        out[...] = value.astype(out.dtype)


def back_kernel(own_ref, first_ref, second_ref, grad_ref, self_ref, neighbour_ref, keep_ref, send_ref):
    spread = own_ref[...] + first_ref[...].astype(F32) + second_ref[...].astype(F32)
    spread = spread.astype(BF16)
    half = keep_ref.shape[0]
    for at, out in enumerate((keep_ref, send_ref)):
        rows = pl.ds(at * half, half)
        value = jnp.dot(self_ref[rows, :], grad_ref[...], preferred_element_type=F32)
        value = value + jnp.dot(neighbour_ref[rows, :], spread, preferred_element_type=F32)
        out[...] = value.astype(out.dtype)


def chip_kernel(stack_ref, keep_ref, got_ref, *outs):
    for at, out in enumerate(outs):
        piece = (stack_ref[0] + at) % len(outs)
        out[...] = (keep_ref[piece] + got_ref[piece].astype(F32)).astype(out.dtype)


def lay_kernel(pieces_ref, self_ref, neighbour_ref):
    groups, rows, lane = pieces_ref.shape
    feats = self_ref.shape[1] // lane
    for piece in range(groups):
        part, feat = piece // feats, piece % feats
        for first in range(0, rows, 16):
            kind, row = divmod(part * rows + first, self_ref.shape[0])
            out = (self_ref, neighbour_ref)[kind]
            out[pl.ds(row, 16), pl.ds(feat * lane, lane)] = pieces_ref[
                piece, pl.ds(first, 16), :
            ].astype(F32)


def call(kernel, in_specs, out_shape, scratch, flops, moved):
    return pl.pallas_call(
        kernel,
        in_specs=in_specs,
        out_shape=out_shape,
        out_specs=jax.tree.map(lambda _: VMEM, out_shape),
        scratch_shapes=scratch,
        compiler_params=pltpu.CompilerParams(vmem_limit_bytes=VMEM_BYTES),
        cost_estimate=pl.CostEstimate(flops=flops, bytes_accessed=moved, transcendentals=0),
    )


def shifted(value, steps):
    count = lax.axis_size("rows")
    pairs = [(source, (source + steps) % count) for source in range(count)]
    return lax.ppermute(value, "rows", pairs)


def turned_in_trio(value, steps):
    count = lax.axis_size("rows")
    pairs = [
        (source, source // TRIO * TRIO + (source + steps) % TRIO) for source in range(count)
    ]
    return lax.ppermute(value, "rows", pairs)


def on_device(
    features,
    tile_values,
    dest_block,
    source_block,
    tile_count,
    degree,
    self_weight,
    neighbour_weight,
    hidden_bias,
    cotangent,
):
    node_dev, width = features.shape
    blocks = node_dev // BLOCK
    groups = lax.axis_size("rows")
    feats = lax.axis_size("feat")
    stacks = feats // CORES
    half = stacks * width
    hidden_dev = hidden_bias.shape[0]
    core = (lax.axis_index("feat") % CORES).reshape(1)
    stack = (lax.axis_index("feat") // CORES).reshape(1)
    place = (lax.axis_index("rows") % TRIO).reshape(1)
    same_core = [[z * CORES + c for z in range(stacks)] for c in range(CORES)]
    other_core = [(f, f ^ 1) for f in range(feats)]

    def over_stacks(value):
        return lax.all_to_all(value, "feat", 0, 0, axis_index_groups=same_core)

    def to_stack(value, steps):
        pairs = [(f, (f + steps * CORES) % feats) for f in range(feats)]
        return lax.ppermute(value, "feat", pairs)

    turned = features.T
    level = jnp.stack([turned, turned_in_trio(turned, -1), turned_in_trio(turned, -2)])
    below = shifted(level, TRIO)
    above = shifted(level, -TRIO)

    packed = call(
        pack_kernel,
        [VMEM] * 3,
        jax.ShapeDtypeStruct((stacks, 2 * width, node_dev), BF16),
        [],
        0,
        6 * stacks * width * node_dev,
    )(turned, self_weight, neighbour_weight)
    packed_own = over_stacks(packed)
    packed_far = lax.ppermute(packed_own, "feat", other_core)

    degrees = degree.reshape(1, node_dev)
    scalars = (tile_count, dest_block, source_block)
    tile_flops = 2 * OFFS * SLOTS * BLOCK * BLOCK * BLOCK
    aggregate = call(
        gather_kernel,
        [SMEM] * 4 + [VMEM] * 5,
        jax.ShapeDtypeStruct((stacks, width, node_dev), BF16),
        [
            pltpu.VMEM((blocks + 1, width, BLOCK), F32),
            pltpu.VMEM((TRIO * TRIO, width, node_dev), BF16),
        ],
        tile_flops,
        tile_values.size * 2,
    )(place, *scalars, tile_values, degrees, below, level, above)
    aggregate_own = over_stacks(aggregate)
    aggregate_far = lax.ppermute(aggregate_own, "feat", other_core)

    def trio(dtype):
        return jax.ShapeDtypeStruct((TRIO, hidden_dev, node_dev), dtype)

    middle = call(
        middle_kernel,
        [SMEM] * 5 + [VMEM] * 8,
        [
            jax.ShapeDtypeStruct((node_dev, hidden_dev), BF16),
            jax.ShapeDtypeStruct((hidden_dev, node_dev), BF16),
            jax.ShapeDtypeStruct((4 * half, hidden_dev), BF16),
            jax.ShapeDtypeStruct((8, hidden_dev), F32),
            jax.ShapeDtypeStruct((2 * half, hidden_dev), BF16),
            jax.ShapeDtypeStruct((2 * half, hidden_dev), BF16),
            trio(BF16),
            trio(F32),
            trio(BF16),
        ],
        [
            pltpu.VMEM((2 * half, node_dev), BF16),
            pltpu.VMEM((blocks, hidden_dev, BLOCK), BF16),
            pltpu.VMEM((TRIO * TRIO * blocks + 1, hidden_dev, BLOCK), F32),
        ],
        tile_flops * 2,
        tile_values.size * 2,
    )(
        place,
        core,
        *scalars,
        tile_values,
        degrees,
        packed_own,
        packed_far,
        aggregate_own,
        aggregate_far,
        hidden_bias.reshape(1, hidden_dev),
        cotangent,
    )
    activations, grad_turned, weight_part, bias_part, weight_self, weight_neighbour = middle[:6]
    to_below, to_level, to_above = middle[6:]
    from_above = shifted(to_below, -TRIO)
    from_below = shifted(to_above, TRIO)

    rows_each = 4 * half // groups
    weight_part = weight_part.reshape(groups, rows_each, hidden_dev)
    bias_rows = jnp.broadcast_to(bias_part.astype(BF16)[None], (groups, 8, hidden_dev))
    sent = jnp.concatenate([weight_part, bias_rows], axis=1)
    summed = jnp.sum(lax.all_to_all(sent, "rows", 0, 0).astype(F32), axis=0)
    grad_bias = summed[rows_each]
    piece = summed[:rows_each].astype(BF16)
    per_stack = groups // feats
    pairs = []
    for row in range(groups):
        far, at, part = row // (groups // 2), row // per_stack % stacks, row % per_stack
        for feat in range(feats):
            column = at * CORES + (feat % CORES + far) % CORES
            pairs.append((row * feats + feat, (part * feats + feat) * feats + column))
    piece = lax.ppermute(piece, ("rows", "feat"), pairs)
    pieces = lax.all_to_all(
        jnp.broadcast_to(piece[None], (groups,) + piece.shape), "rows", 0, 0
    )
    grad_weight = jax.ShapeDtypeStruct((width, feats * hidden_dev), F32)
    grad_self, grad_neighbour = call(
        lay_kernel, [VMEM], [grad_weight, grad_weight], [], 0, pieces.size * 6
    )(pieces)

    spread = jax.ShapeDtypeStruct((hidden_dev, node_dev), BF16)
    own, first, second = call(
        trio_kernel,
        [VMEM] * 3,
        [jax.ShapeDtypeStruct(spread.shape, F32), spread, spread],
        [],
        9 * spread.size,
        20 * spread.size,
    )(to_level, from_below, from_above)
    first = turned_in_trio(first, 1)
    second = turned_in_trio(second, 2)
    keep, send = call(
        back_kernel,
        [VMEM] * 6,
        [
            jax.ShapeDtypeStruct((half, node_dev), F32),
            jax.ShapeDtypeStruct((half, node_dev), BF16),
        ],
        [],
        8 * half * node_dev * hidden_dev,
        4 * half * node_dev,
    )(own, first, second, grad_turned, weight_self, weight_neighbour)
    got = lax.ppermute(send, "feat", other_core)
    part = jax.ShapeDtypeStruct((width, node_dev), BF16)
    parts = call(
        chip_kernel,
        [SMEM] + [VMEM] * 2,
        [jax.ShapeDtypeStruct(part.shape, F32)] + [part] * (stacks - 1),
        [],
        4 * half * node_dev,
        8 * half * node_dev,
    )(
        stack,
        keep.reshape(stacks, width, node_dev),
        got.reshape(stacks, width, node_dev),
    )
    grad_turned = parts[0]
    for steps in range(1, stacks):
        grad_turned = grad_turned + to_stack(parts[steps], steps).astype(F32)
    return (activations, grad_turned.astype(BF16).T, grad_self, grad_neighbour, grad_bias)


def solution(mesh):
    in_specs = (
        P("rows", "feat"),
        P("rows", None, None),
        P("rows"),
        P("rows"),
        P("rows"),
        P("rows"),
        P("feat", None),
        P("feat", None),
        P("feat"),
        P("rows", "feat"),
    )
    out_specs = (P("rows", "feat"), P("rows", "feat"), P("feat", None), P("feat", None), P("feat"))
    return jax.shard_map(
        on_device, mesh=mesh, in_specs=in_specs, out_specs=out_specs, check_vma=False
    )
```

time: 215 us -> 218 us (1.014)
  waiting for transfers between devices: 64 us -> 74.6 us
  starting transfers between devices: 121 us -> 111 us
  Pallas kernels: 11.3 us -> 13.8 us
    ppermute x2 -> x9, waiting for transfers between devices: 0.01 us -> 41.7 us  [the longest x4 30.8 us: turned_in_trio(): return lax.ppermute(value, 'rows', pairs)]
    ppermute x2 -> x9, starting transfers between devices: 4.31 us -> 37.8 us  [the longest x3 13.1 us: to_stack(): return lax.ppermute(value, 'feat', pairs)]
    ppermute x12 -> x4, starting transfers between devices: 44.2 us -> 17.8 us  [shifted(): return lax.ppermute(value, 'rows', pairs)]
    all_to_all x3 -> x2, waiting for transfers between devices: 24.8 us -> 8.17 us  [over_stacks(): return lax.all_to_all(value, 'feat', 0, 0, axis_index_groups=same_core)]
    all_to_all x1, waiting for transfers between devices: 11.4 us -> 0.01 us  [on_device(): lax.all_to_all(jnp.broadcast_to(piece[None], (groups,) + piece.shape), 'r...]
    all_to_all x1, waiting for transfers between devices: 0.01 us -> 10.2 us  [on_device(): summed = jnp.sum(lax.all_to_all(sent, 'rows', 0, 0).astype(F32), axis=0)]
    all_to_all x1 -> x0, waiting for transfers between devices: 10.1 us -> none  [on_device(): lax.all_to_all(both, 'feat', 0, 0)]
    all_to_all x1 -> x0, starting transfers between devices: 9.46 us -> none  [on_device(): lax.all_to_all(both, 'feat', 0, 0)]
  transfers between devices with their start and end apart: 22 -> 19, of which waited for: 11 -> 11; matrix products, arithmetic and copies ran while one was open for 2% -> 1% of each run, Pallas kernels for 2% -> 3%
where the time goes in v3:
time: 218 us; the launch traced here: 215 us
  starting transfers between devices  111 us (51%)
  waiting for transfers between devices  74.6 us (34%)
  Pallas kernels  13.8 us (6%)
  local copies, waits for them, and re-layouts  11.9 us (5%)
  other arithmetic  2.83 us (1%)
    ppermute x4, waiting for transfers between devices, turned_in_trio(): return lax.ppermute(value, 'rows', pairs)  30.8 us
    all_to_all x2, starting transfers between devices, over_stacks(): return lax.all_to_all(value, 'feat', 0, 0, axis_index_groups=same_core)  22.4 us
    ppermute x4, starting transfers between devices, shifted(): return lax.ppermute(value, 'rows', pairs)  17.8 us
    all_to_all x1, starting transfers between devices, on_device(): lax.all_to_all(jnp.broadcast_to(piece[None], (groups,) + piece.shape), 'r...  16.3 us
    ppermute x3, starting transfers between devices, to_stack(): return lax.ppermute(value, 'feat', pairs)  13.1 us
    ppermute x4, starting transfers between devices, turned_in_trio(): return lax.ppermute(value, 'rows', pairs)  11.5 us
    unnamed x36, local copies, waits for them, and re-layouts  10.5 us
    ppermute x4, waiting for transfers between devices, shifted(): return lax.ppermute(value, 'rows', pairs)  10.5 us
  transfers between devices with their start and end apart: 19, of which 11 were waited for; matrix products, arithmetic and copies ran while one was open for 1% of the time, Pallas kernels for 3%

profile of v3, /device:TPU:1, one launch (start us, length us, event | category | flops | bytes accessed | tf_op | source)
XLA Modules:
  0.0 215.0 jit_solution(5345098885524480556)
XLA Ops:
  4.4 15.2 %all-to-all-start = ((bf16[4,192,512]{2,1,0:T(8,128)(2,1)}), bf16[4,192,512]{2,1,0:T(8,128)(2,1)S(1)}, u32[]{:S(2)}, u32[]{:S(2)}) async-start(bf16[4,192,512]{2,1,0:T(8,128)(2,1)} %shard_map.137), calls=%async_computation | async-start | bytes 1572864 | tf_op jit(solution)/shard_map/all_to_all | solution.py:255
  19.6 3.4 %collective-permute-start.1 = (bf16[96,512]{1,0:T(8,128)(2,1)S(1)}, bf16[96,512]{1,0:T(8,128)(2,1)S(1)}, u32[]{:S(2)}, u32[]{:S(2)}) collective-permute-start(bf16[96,512]{1,0:T(8,128)(2,1)S(1)} %bitcast.19), channel_id=1, source_target_pairs={{0,16},{8,0},{16,8},{24,40},{32,24},{40,32},{48,64},{56,48},{64,56... | collective-permute-start | bytes 294920 | tf_op jit(solution)/shard_map/ppermute | solution.py:226
  24.9 25.9 %collective-permute-done.1 = bf16[96,512]{1,0:T(8,128)(2,1)S(1)} collective-permute-done((bf16[96,512]{1,0:T(8,128)(2,1)S(1)}, bf16[96,512]{1,0:T(8,128)(2,1)S(1)}, u32[]{:S(2)}, u32[]{:S(2)}) %collective-permute-start.1) | collective-permute-done | bytes 98336 | tf_op jit(solution)/shard_map/ppermute | solution.py:226
  50.9 7.3 %collective-permute-start.4 = (bf16[3,96,512]{2,1,0:T(8,128)(2,1)S(1)}, bf16[3,96,512]{2,1,0:T(8,128)(2,1)S(1)}, u32[]{:S(2)}, u32[]{:S(2)}) collective-permute-start(bf16[3,96,512]{2,1,0:T(8,128)(2,1)S(1)} %pad_maximum_fusion.1.level_ref), channel_id=1, source_target_pairs={{0,744},{8,752},{16,760},{24,0},{32,8},{40,16},{48,24},{56,32},{64... | collective-permute-start | bytes 884744 | tf_op jit(solution)/shard_map/ppermute | solution.py:218
  60.2 3.3 %collective-permute-done.4.above_ref = bf16[3,96,512]{2,1,0:T(8,128)(2,1)S(1)} collective-permute-done((bf16[3,96,512]{2,1,0:T(8,128)(2,1)S(1)}, bf16[3,96,512]{2,1,0:T(8,128)(2,1)S(1)}, u32[]{:S(2)}, u32[]{:S(2)}) %collective-permute-start.4) | collective-permute-done | bytes 294944 | tf_op jit(solution)/shard_map/ppermute | solution.py:218
  63.5 7.2 %collective-permute-done.3.below_ref = bf16[3,96,512]{2,1,0:T(8,128)(2,1)S(1)} collective-permute-done((bf16[3,96,512]{2,1,0:T(8,128)(2,1)S(1)}, bf16[3,96,512]{2,1,0:T(8,128)(2,1)S(1)}, u32[]{:S(2)}, u32[]{:S(2)}) %collective-permute-start.3) | collective-permute-done | bytes 294944 | tf_op jit(solution)/shard_map/ppermute | solution.py:218
  72.7 5.3 %shard_map.138 = bf16[4,96,512]{2,1,0:T(8,128)(2,1)} custom-call(s32[1]{0:T(128)} %bitcast.place_ref, s32[7]{0:T(128)S(1)} %copy-done.10, s32[112]{0:T(128)S(1)} %copy-done.11, s32[112]{0:T(128)S(1)} %copy-done.12, bf16[112,128,128]{2,1,0:T(8,128)(2,1)S(1)} %copy-done, s32[1,512]{1,0:T(1,128)S(1)} %bitcast.24, ...), custom_call_target="tpu_custom_call" | custom-call | flops 469762048 | bytes 3670016 | tf_op jit(solution)/shard_map/pallas_call | solution.py:280
  78.0 7.2 %all-to-all-start.1 = ((bf16[4,96,512]{2,1,0:T(8,128)(2,1)}), bf16[4,96,512]{2,1,0:T(8,128)(2,1)S(1)}, u32[]{:S(2)}, u32[]{:S(2)}) async-start(bf16[4,96,512]{2,1,0:T(8,128)(2,1)} %shard_map.138), calls=%async_computation.1 | async-start | bytes 786432 | tf_op jit(solution)/shard_map/all_to_all | solution.py:255
  85.2 5.5 %collective-permute-start = (bf16[4,192,512]{2,1,0:T(8,128)(2,1)S(1)}, bf16[4,192,512]{2,1,0:T(8,128)(2,1)S(1)}, u32[]{:S(2)}, u32[]{:S(2)}) collective-permute-start(bf16[4,192,512]{2,1,0:T(8,128)(2,1)S(1)} %all-to-all-done.refs_0_), channel_id=1, source_target_pairs={{0,1},{1,0},{2,3},{3,2},{4,5},{5,4},{6,7},{7,6},{8,9},{9,8},{10,11... | collective-permute-start | bytes 2359304 | tf_op jit(solution)/shard_map/ppermute | solution.py:275
  90.7 8.2 %all-to-all-done.1.refs_2_ = bf16[4,96,512]{2,1,0:T(8,128)(2,1)S(1)} async-done(((bf16[4,96,512]{2,1,0:T(8,128)(2,1)}), bf16[4,96,512]{2,1,0:T(8,128)(2,1)S(1)}, u32[]{:S(2)}, u32[]{:S(2)}) %all-to-all-start.1) | async-done | bytes 393248 | tf_op jit(solution)/shard_map/all_to_all | solution.py:255
  98.9 7.7 %collective-permute-start.5 = (bf16[4,96,512]{2,1,0:T(8,128)(2,1)S(1)}, bf16[4,96,512]{2,1,0:T(8,128)(2,1)S(1)}, u32[]{:S(2)}, u32[]{:S(2)}) collective-permute-start(bf16[4,96,512]{2,1,0:T(8,128)(2,1)S(1)} %all-to-all-done.1.refs_2_), channel_id=1, source_target_pairs={{0,1},{1,0},{2,3},{3,2},{4,5},{5,4},{6,7},{7,6},{8,9},{9,8},{10,11... | collective-permute-start | bytes 1179656 | tf_op jit(solution)/shard_map/ppermute | solution.py:292
  111.5 5.9 %shard_map.139 = (bf16[512,128]{1,0:T(8,128)(2,1)}, bf16[128,512]{1,0:T(8,128)(2,1)S(1)}, bf16[1536,128]{1,0:T(8,128)(2,1)S(1)}, f32[8,128]{1,0:T(8,128)S(1)}, b...) custom-call(s32[1]{0:T(128)} %bitcast.place_ref, ...), custom_call_target="tpu_custom_call" | custom-call | flops 939524096 | bytes 3670016 | tf_op jit(solution)/shard_map/pallas_call | solution.py:297
  120.5 7.6 %all-to-all-start.2 = ((bf16[96,24,128]{2,1,0:T(8,128)(2,1)}), bf16[96,24,128]{2,1,0:T(8,128)(2,1)}, u32[]{:S(2)}, u32[]{:S(2)}) async-start(bf16[96,24,128]{2,1,0:T(8,128)(2,1)} %pad_maximum_fusion), calls=%async_computation.2 | async-start | bytes 1179648 | tf_op jit(solution)/shard_map/all_to_all | solution.py:340
  130.9 6.0 %collective-permute-start.7 = (bf16[3,128,512]{2,1,0:T(8,128)(2,1)S(1)}, bf16[3,128,512]{2,1,0:T(8,128)(2,1)S(1)}, u32[]{:S(2)}, u32[]{:S(2)}) collective-permute-start(bf16[3,128,512]{2,1,0:T(8,128)(2,1)S(1)} %copy-done.15), channel_id=1, source_target_pairs={{0,744},{8,752},{16,760},{24,0},{32,8},{40,16},{48,24},{56,32},{64... | collective-permute-start | bytes 1179656 | tf_op jit(solution)/shard_map/ppermute | solution.py:218
  136.8 10.2 %all-to-all-done.2 = bf16[96,24,128]{2,1,0:T(8,128)(2,1)} async-done(((bf16[96,24,128]{2,1,0:T(8,128)(2,1)}), bf16[96,24,128]{2,1,0:T(8,128)(2,1)}, u32[]{:S(2)}, u32[]{:S(2)}) %all-to-all-start.2) | async-done | bytes 589856 | tf_op jit(solution)/shard_map/all_to_all | solution.py:340
  148.3 3.7 %collective-permute-start.14 = (bf16[16,128]{1,0:T(8,128)(2,1)S(1)}, bf16[16,128]{1,0:T(8,128)(2,1)S(1)}, u32[]{:S(2)}, u32[]{:S(2)}) collective-permute-start(bf16[16,128]{1,0:T(8,128)(2,1)S(1)} %slice.13), channel_id=1, source_target_pairs={{0,0},{1,9},{2,16},{3,25},{4,32},{5,41},{6,48},{7,57},{8,64},{9,73... | collective-permute-start | bytes 12296 | tf_op jit(solution)/shard_map/ppermute | solution.py:350
  151.9 2.7 %collective-permute-done.14 = bf16[16,128]{1,0:T(8,128)(2,1)S(1)} collective-permute-done((bf16[16,128]{1,0:T(8,128)(2,1)S(1)}, bf16[16,128]{1,0:T(8,128)(2,1)S(1)}, u32[]{:S(2)}, u32[]{:S(2)}) %collective-permute-start.14) | collective-permute-done | bytes 4128 | tf_op jit(solution)/shard_map/ppermute | solution.py:350
  155.5 16.3 %all-to-all-start.3 = ((bf16[96,16,128]{2,1,0:T(8,128)(2,1)}), bf16[96,16,128]{2,1,0:T(8,128)(2,1)S(1)}, u32[]{:S(2)}, u32[]{:S(2)}) async-start(bf16[96,16,128]{2,1,0:T(8,128)(2,1)} %broadcast_in_dim.5), calls=%async_computation.3 | async-start | bytes 786432 | tf_op jit(solution)/shard_map/all_to_all | solution.py:351
  174.7 3.5 %collective-permute-start.9 = (bf16[128,512]{1,0:T(8,128)(2,1)S(1)}, bf16[128,512]{1,0:T(8,128)(2,1)S(1)}, u32[]{:S(2)}, u32[]{:S(2)}) collective-permute-start(bf16[128,512]{1,0:T(8,128)(2,1)S(1)} %get-tuple-element.31), channel_id=1, source_target_pairs={{0,16},{8,0},{16,8},{24,40},{32,24},{40,32},{48,64},{56,48},{64,56... | collective-permute-start | bytes 393224 | tf_op jit(solution)/shard_map/ppermute | solution.py:226
  178.6 4.5 %collective-permute-done.9.second_ref = bf16[128,512]{1,0:T(8,128)(2,1)S(1)} collective-permute-done((bf16[128,512]{1,0:T(8,128)(2,1)S(1)}, bf16[128,512]{1,0:T(8,128)(2,1)S(1)}, u32[]{:S(2)}, u32[]{:S(2)}) %collective-permute-start.9) | collective-permute-done | bytes 131104 | tf_op jit(solution)/shard_map/ppermute | solution.py:226
  183.6 5.2 %collective-permute-start.10 = (bf16[384,512]{1,0:T(8,128)(2,1)S(1)}, bf16[384,512]{1,0:T(8,128)(2,1)S(1)}, u32[]{:S(2)}, u32[]{:S(2)}) collective-permute-start(bf16[384,512]{1,0:T(8,128)(2,1)S(1)} %get-tuple-element.36), channel_id=1, source_target_pairs={{0,1},{1,0},{2,3},{3,2},{4,5},{5,4},{6,7},{7,6},{8,9},{9,8},{10,11... | collective-permute-start | bytes 1179656 | tf_op jit(solution)/shard_map/ppermute | solution.py:381
  190.2 4.1 %collective-permute-start.11 = (bf16[96,512]{1,0:T(8,128)(2,1)S(1)}, bf16[96,512]{1,0:T(8,128)(2,1)S(1)}, u32[]{:S(2)}, u32[]{:S(2)}) collective-permute-start(bf16[96,512]{1,0:T(8,128)(2,1)S(1)} %get-tuple-element.38), channel_id=1, source_target_pairs={{0,2},{1,3},{2,4},{3,5},{4,6},{5,7},{6,0},{7,1},{8,10},{9,11},{10,... | collective-permute-start | bytes 294920 | tf_op jit(solution)/shard_map/ppermute | solution.py:259
  194.3 7.1 %collective-permute-start.12 = (bf16[96,512]{1,0:T(8,128)(2,1)S(1)}, bf16[96,512]{1,0:T(8,128)(2,1)S(1)}, u32[]{:S(2)}, u32[]{:S(2)}) collective-permute-start(bf16[96,512]{1,0:T(8,128)(2,1)S(1)} %get-tuple-element.39), channel_id=1, source_target_pairs={{0,4},{1,5},{2,6},{3,7},{4,0},{5,1},{6,2},{7,3},{8,12},{9,13},{10,... | collective-permute-start | bytes 294920 | tf_op jit(solution)/shard_map/ppermute | solution.py:259
  203.3 9.5 %collective-permute-done.12 = bf16[96,512]{1,0:T(8,128)(2,1)S(1)} collective-permute-done((bf16[96,512]{1,0:T(8,128)(2,1)S(1)}, bf16[96,512]{1,0:T(8,128)(2,1)S(1)}, u32[]{:S(2)}, u32[]{:S(2)}) %collective-permute-start.12) | collective-permute-done | bytes 98336 | tf_op jit(solution)/shard_map/ppermute | solution.py:259
  (66 shorter events, 31.5 us)
Async XLA Ops:
  4.4 66.3 %copy-start.9 = (s32[512]{0:T(512)S(1)}, s32[512]{0:T(512)}, u32[]{:S(2)}) copy-start(s32[512]{0:T(512)} %param.15) | copy-start | bytes 6148
  4.4 66.3 %copy-start.10 = (s32[7]{0:T(128)S(1)}, s32[7]{0:T(128)}, u32[]{:S(2)}) copy-start(s32[7]{0:T(128)} %count_ref.3) | copy-start | bytes 88
  4.4 66.3 %copy-start.11 = (s32[112]{0:T(128)S(1)}, s32[112]{0:T(128)}, u32[]{:S(2)}) copy-start(s32[112]{0:T(128)} %dest_ref.3) | copy-start | bytes 1348
  4.4 66.3 %copy-start.12 = (s32[112]{0:T(128)S(1)}, s32[112]{0:T(128)}, u32[]{:S(2)}) copy-start(s32[112]{0:T(128)} %source_ref.3) | copy-start | bytes 1348
  4.4 73.6 %all-to-all-start = ((bf16[4,192,512]{2,1,0:T(8,128)(2,1)}), bf16[4,192,512]{2,1,0:T(8,128)(2,1)S(1)}, u32[]{:S(2)}, u32[]{:S(2)}) async-start(bf16[4,192,512]{2,1,0:T(8,128)(2,1)} %shard_map.137), calls=%async_computation | async-start | bytes 1572864 | tf_op jit(solution)/shard_map/all_to_all | solution.py:255
  19.6 31.3 %collective-permute-start.1 = (bf16[96,512]{1,0:T(8,128)(2,1)S(1)}, bf16[96,512]{1,0:T(8,128)(2,1)S(1)}, u32[]{:S(2)}, u32[]{:S(2)}) collective-permute-start(bf16[96,512]{1,0:T(8,128)(2,1)S(1)} %bitcast.19), channel_id=1, source_target_pairs={{0,16},{8,0},{16,8},{24,40},{32,24},{40,32},{48,64},{56,48},{64,56... | collective-permute-start | bytes 294920 | tf_op jit(solution)/shard_map/ppermute | solution.py:226
  23.0 27.9 %collective-permute-start.2 = (bf16[96,512]{1,0:T(8,128)(2,1)S(1)}, bf16[96,512]{1,0:T(8,128)(2,1)S(1)}, u32[]{:S(2)}, u32[]{:S(2)}) collective-permute-start(bf16[96,512]{1,0:T(8,128)(2,1)S(1)} %bitcast.20), channel_id=1, source_target_pairs={{0,8},{8,16},{16,0},{24,32},{32,40},{40,24},{48,56},{56,64},{64,48... | collective-permute-start | bytes 294920 | tf_op jit(solution)/shard_map/ppermute | solution.py:226
  50.9 12.6 %collective-permute-start.4 = (bf16[3,96,512]{2,1,0:T(8,128)(2,1)S(1)}, bf16[3,96,512]{2,1,0:T(8,128)(2,1)S(1)}, u32[]{:S(2)}, u32[]{:S(2)}) collective-permute-start(bf16[3,96,512]{2,1,0:T(8,128)(2,1)S(1)} %pad_maximum_fusion.1.level_ref), channel_id=1, source_target_pairs={{0,744},{8,752},{16,760},{24,0},{32,8},{40,16},{48,24},{56,32},{64... | collective-permute-start | bytes 884744 | tf_op jit(solution)/shard_map/ppermute | solution.py:218
  58.2 12.4 %collective-permute-start.3 = (bf16[3,96,512]{2,1,0:T(8,128)(2,1)S(1)}, bf16[3,96,512]{2,1,0:T(8,128)(2,1)S(1)}, u32[]{:S(2)}, u32[]{:S(2)}) collective-permute-start(bf16[3,96,512]{2,1,0:T(8,128)(2,1)S(1)} %pad_maximum_fusion.1.level_ref), channel_id=1, source_target_pairs={{0,24},{8,32},{16,40},{24,48},{32,56},{40,64},{48,72},{56,80},{64,... | collective-permute-start | bytes 884744 | tf_op jit(solution)/shard_map/ppermute | solution.py:218
  78.0 20.9 %all-to-all-start.1 = ((bf16[4,96,512]{2,1,0:T(8,128)(2,1)}), bf16[4,96,512]{2,1,0:T(8,128)(2,1)S(1)}, u32[]{:S(2)}, u32[]{:S(2)}) async-start(bf16[4,96,512]{2,1,0:T(8,128)(2,1)} %shard_map.138), calls=%async_computation.1 | async-start | bytes 786432 | tf_op jit(solution)/shard_map/all_to_all | solution.py:255
  85.2 22.7 %collective-permute-start = (bf16[4,192,512]{2,1,0:T(8,128)(2,1)S(1)}, bf16[4,192,512]{2,1,0:T(8,128)(2,1)S(1)}, u32[]{:S(2)}, u32[]{:S(2)}) collective-permute-start(bf16[4,192,512]{2,1,0:T(8,128)(2,1)S(1)} %all-to-all-done.refs_0_), channel_id=1, source_target_pairs={{0,1},{1,0},{2,3},{3,2},{4,5},{5,4},{6,7},{7,6},{8,9},{9,8},{10,11... | collective-permute-start | bytes 2359304 | tf_op jit(solution)/shard_map/ppermute | solution.py:275
  98.9 9.1 %collective-permute-start.5 = (bf16[4,96,512]{2,1,0:T(8,128)(2,1)S(1)}, bf16[4,96,512]{2,1,0:T(8,128)(2,1)S(1)}, u32[]{:S(2)}, u32[]{:S(2)}) collective-permute-start(bf16[4,96,512]{2,1,0:T(8,128)(2,1)S(1)} %all-to-all-done.1.refs_2_), channel_id=1, source_target_pairs={{0,1},{1,0},{2,3},{3,2},{4,5},{5,4},{6,7},{7,6},{8,9},{9,8},{10,11... | collective-permute-start | bytes 1179656 | tf_op jit(solution)/shard_map/ppermute | solution.py:292
  120.5 26.5 %all-to-all-start.2 = ((bf16[96,24,128]{2,1,0:T(8,128)(2,1)}), bf16[96,24,128]{2,1,0:T(8,128)(2,1)}, u32[]{:S(2)}, u32[]{:S(2)}) async-start(bf16[96,24,128]{2,1,0:T(8,128)(2,1)} %pad_maximum_fusion), calls=%async_computation.2 | async-start | bytes 1179648 | tf_op jit(solution)/shard_map/all_to_all | solution.py:340
  128.2 43.6 %collective-permute-start.6 = (bf16[3,128,512]{2,1,0:T(8,128)(2,1)S(1)}, bf16[3,128,512]{2,1,0:T(8,128)(2,1)S(1)}, u32[]{:S(2)}, u32[]{:S(2)}) collective-permute-start(bf16[3,128,512]{2,1,0:T(8,128)(2,1)S(1)} %copy-done.17), channel_id=1, source_target_pairs={{0,24},{8,32},{16,40},{24,48},{32,56},{40,64},{48,72},{56,80},{64,... | collective-permute-start | bytes 1179656 | tf_op jit(solution)/shard_map/ppermute | solution.py:218
  130.9 41.0 %collective-permute-start.7 = (bf16[3,128,512]{2,1,0:T(8,128)(2,1)S(1)}, bf16[3,128,512]{2,1,0:T(8,128)(2,1)S(1)}, u32[]{:S(2)}, u32[]{:S(2)}) collective-permute-start(bf16[3,128,512]{2,1,0:T(8,128)(2,1)S(1)} %copy-done.15), channel_id=1, source_target_pairs={{0,744},{8,752},{16,760},{24,0},{32,8},{40,16},{48,24},{56,32},{64... | collective-permute-start | bytes 1179656 | tf_op jit(solution)/shard_map/ppermute | solution.py:218
  148.3 6.4 %collective-permute-start.14 = (bf16[16,128]{1,0:T(8,128)(2,1)S(1)}, bf16[16,128]{1,0:T(8,128)(2,1)S(1)}, u32[]{:S(2)}, u32[]{:S(2)}) collective-permute-start(bf16[16,128]{1,0:T(8,128)(2,1)S(1)} %slice.13), channel_id=1, source_target_pairs={{0,0},{1,9},{2,16},{3,25},{4,32},{5,41},{6,48},{7,57},{8,64},{9,73... | collective-permute-start | bytes 12296 | tf_op jit(solution)/shard_map/ppermute | solution.py:350
  155.5 27.6 %copy-start.8 = (bf16[128,512]{1,0:T(8,128)(2,1)S(1)}, bf16[128,512]{1,0:T(8,128)(2,1)}, u32[]{:S(2)}) copy-start(bf16[128,512]{1,0:T(8,128)(2,1)} %copy-done.7) | copy-start | bytes 393220
  155.5 58.6 %all-to-all-start.3 = ((bf16[96,16,128]{2,1,0:T(8,128)(2,1)}), bf16[96,16,128]{2,1,0:T(8,128)(2,1)S(1)}, u32[]{:S(2)}, u32[]{:S(2)}) async-start(bf16[96,16,128]{2,1,0:T(8,128)(2,1)} %broadcast_in_dim.5), calls=%async_computation.3 | async-start | bytes 786432 | tf_op jit(solution)/shard_map/all_to_all | solution.py:351
  172.0 6.6 %collective-permute-start.8 = (bf16[128,512]{1,0:T(8,128)(2,1)S(1)}, bf16[128,512]{1,0:T(8,128)(2,1)S(1)}, u32[]{:S(2)}, u32[]{:S(2)}) collective-permute-start(bf16[128,512]{1,0:T(8,128)(2,1)S(1)} %get-tuple-element.30), channel_id=1, source_target_pairs={{0,8},{8,16},{16,0},{24,32},{32,40},{40,24},{48,56},{56,64},{64,48... | collective-permute-start | bytes 393224 | tf_op jit(solution)/shard_map/ppermute | solution.py:226
  174.7 8.4 %collective-permute-start.9 = (bf16[128,512]{1,0:T(8,128)(2,1)S(1)}, bf16[128,512]{1,0:T(8,128)(2,1)S(1)}, u32[]{:S(2)}, u32[]{:S(2)}) collective-permute-start(bf16[128,512]{1,0:T(8,128)(2,1)S(1)} %get-tuple-element.31), channel_id=1, source_target_pairs={{0,16},{8,0},{16,8},{24,40},{32,24},{40,32},{48,64},{56,48},{64,56... | collective-permute-start | bytes 393224 | tf_op jit(solution)/shard_map/ppermute | solution.py:226
  183.6 6.5 %collective-permute-start.10 = (bf16[384,512]{1,0:T(8,128)(2,1)S(1)}, bf16[384,512]{1,0:T(8,128)(2,1)S(1)}, u32[]{:S(2)}, u32[]{:S(2)}) collective-permute-start(bf16[384,512]{1,0:T(8,128)(2,1)S(1)} %get-tuple-element.36), channel_id=1, source_target_pairs={{0,1},{1,0},{2,3},{3,2},{4,5},{5,4},{6,7},{7,6},{8,9},{9,8},{10,11... | collective-permute-start | bytes 1179656 | tf_op jit(solution)/shard_map/ppermute | solution.py:381
  190.2 13.1 %collective-permute-start.11 = (bf16[96,512]{1,0:T(8,128)(2,1)S(1)}, bf16[96,512]{1,0:T(8,128)(2,1)S(1)}, u32[]{:S(2)}, u32[]{:S(2)}) collective-permute-start(bf16[96,512]{1,0:T(8,128)(2,1)S(1)} %get-tuple-element.38), channel_id=1, source_target_pairs={{0,2},{1,3},{2,4},{3,5},{4,6},{5,7},{6,0},{7,1},{8,10},{9,11},{10,... | collective-permute-start | bytes 294920 | tf_op jit(solution)/shard_map/ppermute | solution.py:259
  194.3 18.6 %collective-permute-start.12 = (bf16[96,512]{1,0:T(8,128)(2,1)S(1)}, bf16[96,512]{1,0:T(8,128)(2,1)S(1)}, u32[]{:S(2)}, u32[]{:S(2)}) collective-permute-start(bf16[96,512]{1,0:T(8,128)(2,1)S(1)} %get-tuple-element.39), channel_id=1, source_target_pairs={{0,4},{1,5},{2,6},{3,7},{4,0},{5,1},{6,2},{7,3},{8,12},{9,13},{10,... | collective-permute-start | bytes 294920 | tf_op jit(solution)/shard_map/ppermute | solution.py:259
  201.4 11.5 %collective-permute-start.13 = (bf16[96,512]{1,0:T(8,128)(2,1)S(1)}, bf16[96,512]{1,0:T(8,128)(2,1)S(1)}, u32[]{:S(2)}, u32[]{:S(2)}) collective-permute-start(bf16[96,512]{1,0:T(8,128)(2,1)S(1)} %get-tuple-element.40), channel_id=1, source_target_pairs={{0,6},{1,7},{2,0},{3,1},{4,2},{5,3},{6,4},{7,5},{8,14},{9,15},{10,... | collective-permute-start | bytes 294920 | tf_op jit(solution)/shard_map/ppermute | solution.py:259
  (13 other events, 46.5 us)

commit v4 on v3

--- a/solution.py
+++ b/solution.py
@@ -16,9 +16,13 @@
 TRIO = 3
 F32 = jnp.float32
 BF16 = jnp.bfloat16
-VMEM_BYTES = 40 * 1024 * 1024
+VMEM_BYTES = 16 * 1024 * 1024
+TILES_VMEM_BYTES = 60_500_000
 VMEM = pl.BlockSpec(memory_space=pltpu.VMEM)
 SMEM = pl.BlockSpec(memory_space=pltpu.SMEM)
+ANY = pl.BlockSpec(memory_space=pl.ANY)
+HBM = pl.BlockSpec(memory_space=pltpu.HBM)
+WHOLE = pl.BlockSpec()
 
 
 def lanes(block):
@@ -48,8 +52,10 @@
     return (place_ref[0] + offset) // TRIO * TRIO + offset % TRIO
 
 
-def pack_kernel(features_ref, self_ref, neighbour_ref, out_ref):
+def pack_kernel(features_ref, first_ref, second_ref, self_ref, neighbour_ref, level_ref, out_ref):
     width = features_ref.shape[0]
+    for slot, ref in enumerate((features_ref, first_ref, second_ref)):
+        level_ref[slot] = ref[...]
     for stack in range(out_ref.shape[0]):
         out_ref[stack, pl.ds(0, width), :] = features_ref[...]
         for core in range(CORES):
@@ -59,12 +65,29 @@
                 ]
 
 
+def repeat_kernel(piece_ref, after_ref, out_ref):
+    for copy in range(out_ref.shape[0]):
+        out_ref[copy] = piece_ref[...]
+
+
+def tile_copies(tiles_hbm, tiles_ref, copied):
+    copies = []
+    for offset in range(OFFS):
+        part = pl.ds(offset * SLOTS, SLOTS)
+        copies.append(
+            pltpu.make_async_copy(tiles_hbm.at[part], tiles_ref.at[part], copied.at[offset])
+        )
+    for copy in copies:
+        copy.start()
+    return copies
+
+
 def gather_kernel(
     place_ref,
     count_ref,
     dest_ref,
     source_ref,
-    tiles_ref,
+    tiles_hbm,
     degree_ref,
     below_ref,
     level_ref,
@@ -72,7 +95,10 @@
     out_ref,
     total_ref,
     band_ref,
+    tiles_ref,
+    copied,
 ):
+    copies = tile_copies(tiles_hbm, tiles_ref, copied)
     blocks = total_ref.shape[0] - 1
     total_ref[...] = jnp.zeros_like(total_ref)
     for trio, ref in enumerate((below_ref, level_ref, above_ref)):
@@ -86,6 +112,7 @@
                 picked, tiles_ref[tile], (((1,), (1,)), ((), ())), preferred_element_type=F32
             )
 
+        copies[offset].wait()
         live_tiles(offset, count_ref, product, lambda tile: dest_ref[tile], total_ref)
     for block in range(blocks):
         part = pl.ds(block * BLOCK, BLOCK)
@@ -94,14 +121,25 @@
             out_ref[copy, :, part] = value
 
 
-def middle_kernel(place_ref, core_ref, count_ref, dest_ref, source_ref, tiles_ref, degree_ref, *refs):
+def middle_kernel(
+    place_ref, core_ref, count_ref, dest_ref, source_ref, tiles_hbm, degree_ref, *refs
+):
     packed, aggregates, refs = refs[:2], refs[2:4], refs[4:]
     bias_ref, cotangent_ref, refs = *refs[:2], refs[2:]
     act_ref, grad_ref, weight_ref, bias_out_ref, self_ref, neighbour_ref, refs = (
         *refs[:6],
         refs[6:],
     )
-    below_ref, level_ref, above_ref, features_ref, scaled_ref, total_ref = refs
+    level_ref, below_ref, above_ref, *refs = refs
+    features_ref, scaled_ref, total_ref, tiles_ref, copied, *refs = refs
+    turned_ref, to_below_ref, to_above_ref, stored = refs
+    copies = tile_copies(tiles_hbm, tiles_ref, copied)
+    stores = [
+        pltpu.make_async_copy(source, target, stored.at[at])
+        for at, (source, target) in enumerate(
+            ((turned_ref, grad_ref), (to_below_ref, below_ref), (to_above_ref, above_ref))
+        )
+    ]
     blocks = scaled_ref.shape[0]
     stacks, width, _ = aggregates[0].shape
     half = stacks * width
@@ -132,7 +170,8 @@
         jnp.sum(grad, axis=0, keepdims=True), bias_out_ref.shape
     ).astype(bias_out_ref.dtype)
     turned = grad.T
-    grad_ref[...] = turned.astype(BF16)
+    turned_ref[...] = turned.astype(BF16)
+    stores[0].start()
     scaled = (turned / degree_ref[...].astype(F32)).astype(BF16)
     for block in range(blocks):
         scaled_ref[block] = scaled[:, block * BLOCK : (block + 1) * BLOCK]
@@ -155,13 +194,22 @@
         def place(tile, slot=slot):
             return slot * blocks + source_ref[tile] % blocks
 
+        copies[offset].wait()
         live_tiles(offset, count_ref, product, place, total_ref)
-    for trio, out in enumerate((below_ref, level_ref, above_ref)):
+    for trio, out, store in (
+        (0, to_below_ref, stores[1]),
+        (2, to_above_ref, stores[2]),
+        (1, level_ref, None),
+    ):
         for slot in range(TRIO):
             for block in range(blocks):
                 out[slot, :, pl.ds(block * BLOCK, BLOCK)] = total_ref[
                     (trio * TRIO + slot) * blocks + block
                 ].astype(out.dtype)
+        if store is not None:
+            store.start()
+    for store in stores:
+        store.wait()
 
 
 def trio_kernel(level_ref, below_ref, above_ref, *outs):
@@ -200,14 +248,14 @@
             ].astype(F32)
 
 
-def call(kernel, in_specs, out_shape, scratch, flops, moved):
+def call(kernel, in_specs, out_shape, scratch, flops, moved, out_specs=None, limit=VMEM_BYTES):
     return pl.pallas_call(
         kernel,
         in_specs=in_specs,
         out_shape=out_shape,
-        out_specs=jax.tree.map(lambda _: VMEM, out_shape),
+        out_specs=out_specs or jax.tree.map(lambda _: VMEM, out_shape),
         scratch_shapes=scratch,
-        compiler_params=pltpu.CompilerParams(vmem_limit_bytes=VMEM_BYTES),
+        compiler_params=pltpu.CompilerParams(vmem_limit_bytes=limit),
         cost_estimate=pl.CostEstimate(flops=flops, bytes_accessed=moved, transcendentals=0),
     )
 
@@ -259,18 +307,25 @@
         return lax.ppermute(value, "feat", pairs)
 
     turned = features.T
-    level = jnp.stack([turned, turned_in_trio(turned, -1), turned_in_trio(turned, -2)])
-    below = shifted(level, TRIO)
-    above = shifted(level, -TRIO)
-
-    packed = call(
+    level, packed = call(
         pack_kernel,
-        [VMEM] * 3,
-        jax.ShapeDtypeStruct((stacks, 2 * width, node_dev), BF16),
+        [WHOLE] * 5,
+        [
+            jax.ShapeDtypeStruct((TRIO, width, node_dev), BF16),
+            jax.ShapeDtypeStruct((stacks, 2 * width, node_dev), BF16),
+        ],
         [],
         0,
         6 * stacks * width * node_dev,
-    )(turned, self_weight, neighbour_weight)
+    )(
+        turned,
+        turned_in_trio(turned, -1),
+        turned_in_trio(turned, -2),
+        self_weight,
+        neighbour_weight,
+    )
+    below = shifted(level, TRIO)
+    above = shifted(level, -TRIO)
     packed_own = over_stacks(packed)
     packed_far = lax.ppermute(packed_own, "feat", other_core)
 
@@ -279,14 +334,17 @@
     tile_flops = 2 * OFFS * SLOTS * BLOCK * BLOCK * BLOCK
     aggregate = call(
         gather_kernel,
-        [SMEM] * 4 + [VMEM] * 5,
+        [SMEM] * 4 + [HBM] + [VMEM] * 4,
         jax.ShapeDtypeStruct((stacks, width, node_dev), BF16),
         [
             pltpu.VMEM((blocks + 1, width, BLOCK), F32),
             pltpu.VMEM((TRIO * TRIO, width, node_dev), BF16),
+            pltpu.VMEM(tile_values.shape, BF16),
+            pltpu.SemaphoreType.DMA((OFFS,)),
         ],
         tile_flops,
         tile_values.size * 2,
+        limit=TILES_VMEM_BYTES,
     )(place, *scalars, tile_values, degrees, below, level, above)
     aggregate_own = over_stacks(aggregate)
     aggregate_far = lax.ppermute(aggregate_own, "feat", other_core)
@@ -296,7 +354,7 @@
 
     middle = call(
         middle_kernel,
-        [SMEM] * 5 + [VMEM] * 8,
+        [SMEM] * 5 + [HBM] + [VMEM] * 5 + [WHOLE] * 2,
         [
             jax.ShapeDtypeStruct((node_dev, hidden_dev), BF16),
             jax.ShapeDtypeStruct((hidden_dev, node_dev), BF16),
@@ -304,17 +362,25 @@
             jax.ShapeDtypeStruct((8, hidden_dev), F32),
             jax.ShapeDtypeStruct((2 * half, hidden_dev), BF16),
             jax.ShapeDtypeStruct((2 * half, hidden_dev), BF16),
+            trio(F32),
             trio(BF16),
-            trio(F32),
             trio(BF16),
         ],
         [
             pltpu.VMEM((2 * half, node_dev), BF16),
             pltpu.VMEM((blocks, hidden_dev, BLOCK), BF16),
             pltpu.VMEM((TRIO * TRIO * blocks + 1, hidden_dev, BLOCK), F32),
+            pltpu.VMEM(tile_values.shape, BF16),
+            pltpu.SemaphoreType.DMA((OFFS,)),
+            pltpu.VMEM((hidden_dev, node_dev), BF16),
+            pltpu.VMEM((TRIO, hidden_dev, node_dev), BF16),
+            pltpu.VMEM((TRIO, hidden_dev, node_dev), BF16),
+            pltpu.SemaphoreType.DMA((3,)),
         ],
         tile_flops * 2,
         tile_values.size * 2,
+        [WHOLE, HBM, VMEM, VMEM, VMEM, VMEM, VMEM, HBM, HBM],
+        TILES_VMEM_BYTES,
     )(
         place,
         core,
@@ -329,7 +395,7 @@
         cotangent,
     )
     activations, grad_turned, weight_part, bias_part, weight_self, weight_neighbour = middle[:6]
-    to_below, to_level, to_above = middle[6:]
+    to_level, to_below, to_above = middle[6:]
     from_above = shifted(to_below, -TRIO)
     from_below = shifted(to_above, TRIO)
 
@@ -348,14 +414,6 @@
             column = at * CORES + (feat % CORES + far) % CORES
             pairs.append((row * feats + feat, (part * feats + feat) * feats + column))
     piece = lax.ppermute(piece, ("rows", "feat"), pairs)
-    pieces = lax.all_to_all(
-        jnp.broadcast_to(piece[None], (groups,) + piece.shape), "rows", 0, 0
-    )
-    grad_weight = jax.ShapeDtypeStruct((width, feats * hidden_dev), F32)
-    grad_self, grad_neighbour = call(
-        lay_kernel, [VMEM], [grad_weight, grad_weight], [], 0, pieces.size * 6
-    )(pieces)
-
     spread = jax.ShapeDtypeStruct((hidden_dev, node_dev), BF16)
     own, first, second = call(
         trio_kernel,
@@ -392,6 +450,24 @@
         keep.reshape(stacks, width, node_dev),
         got.reshape(stacks, width, node_dev),
     )
+    pieces = lax.all_to_all(
+        call(
+            repeat_kernel,
+            [VMEM, ANY],
+            jax.ShapeDtypeStruct((groups,) + piece.shape, BF16),
+            [],
+            0,
+            groups * piece.size * 2,
+        )(piece, parts[0]),
+        "rows",
+        0,
+        0,
+    )
+    grad_weight = jax.ShapeDtypeStruct((width, feats * hidden_dev), F32)
+    grad_self, grad_neighbour = call(
+        lay_kernel, [VMEM], [grad_weight, grad_weight], [], 0, pieces.size * 6
+    )(pieces)
+
     grad_turned = parts[0]
     for steps in range(1, stacks):
         grad_turned = grad_turned + to_stack(parts[steps], steps).astype(F32)

time: 218 us -> 204 us (0.936)
  the two profiles are of different devices: /device:TPU:1 before, /device:TPU:64 now
where the time goes in v4:
time: 204 us; the launch traced here: 203 us
  starting transfers between devices  104 us (51%)
  waiting for transfers between devices  71.2 us (35%)
  Pallas kernels  18.6 us (9%)
  local copies, waits for them, and re-layouts  5.03 us (2%)
  other arithmetic  3.54 us (2%)
    ppermute x4, waiting for transfers between devices, shifted(): return lax.ppermute(value, 'rows', pairs)  27.3 us
    all_to_all x1, starting transfers between devices, on_device(): lax.all_to_all(call(repeat_kernel, [VMEM, ANY], jax.ShapeDtypeStruct((gro...  18.7 us
    ppermute x4, starting transfers between devices, shifted(): return lax.ppermute(value, 'rows', pairs)  18.6 us
    ppermute x4, starting transfers between devices, turned_in_trio(): return lax.ppermute(value, 'rows', pairs)  18.3 us
    all_to_all x2, waiting for transfers between devices, over_stacks(): return lax.all_to_all(value, 'feat', 0, 0, axis_index_groups=same_core)  17.4 us
    all_to_all x2, starting transfers between devices, over_stacks(): return lax.all_to_all(value, 'feat', 0, 0, axis_index_groups=same_core)  16.3 us
    ppermute x3, starting transfers between devices, to_stack(): return lax.ppermute(value, 'feat', pairs)  14.1 us
    ppermute x3, waiting for transfers between devices, to_stack(): return lax.ppermute(value, 'feat', pairs)  11 us
  transfers between devices with their start and end apart: 19, of which 14 were waited for; matrix products, arithmetic and copies ran while one was open for 1% of the time, Pallas kernels for 4%

profile of v4, /device:TPU:64, one launch (start us, length us, event | category | flops | bytes accessed | tf_op | source)
XLA Modules:
  0.0 203.3 jit_solution(3326464203017039837)
XLA Ops:
  0.6 4.3 %collective-permute-start.1 = (bf16[96,512]{1,0:T(8,128)(2,1)}, bf16[96,512]{1,0:T(8,128)(2,1)S(1)}, u32[]{:S(2)}, u32[]{:S(2)}) collective-permute-start(bf16[96,512]{1,0:T(8,128)(2,1)} %bitcast.15), channel_id=1, source_target_pairs={{0,8},{8,16},{16,0},{24,32},{32,40},{40,24},{48,56},{56,64},{64,48... | collective-permute-start | bytes 294920 | tf_op jit(solution)/shard_map/ppermute | solution.py:274
  4.9 8.2 %collective-permute-start = (bf16[96,512]{1,0:T(8,128)(2,1)}, bf16[96,512]{1,0:T(8,128)(2,1)S(1)}, u32[]{:S(2)}, u32[]{:S(2)}) collective-permute-start(bf16[96,512]{1,0:T(8,128)(2,1)} %bitcast.16), channel_id=1, source_target_pairs={{0,16},{8,0},{16,8},{24,40},{32,24},{40,32},{48,64},{56,48},{64,56... | collective-permute-start | bytes 294920 | tf_op jit(solution)/shard_map/ppermute | solution.py:274
  14.0 3.4 %collective-permute-done.first_ref = bf16[96,512]{1,0:T(8,128)(2,1)S(1)} collective-permute-done((bf16[96,512]{1,0:T(8,128)(2,1)}, bf16[96,512]{1,0:T(8,128)(2,1)S(1)}, u32[]{:S(2)}, u32[]{:S(2)}) %collective-permute-start) | collective-permute-done | bytes 98336 | tf_op jit(solution)/shard_map/ppermute | solution.py:274
  21.1 8.2 %all-to-all-start = ((bf16[4,192,512]{2,1,0:T(8,128)(2,1)}), bf16[4,192,512]{2,1,0:T(8,128)(2,1)S(1)}, u32[]{:S(2)}, u32[]{:S(2)}) async-start(bf16[4,192,512]{2,1,0:T(8,128)(2,1)} %get-tuple-element.27), calls=%async_computation | async-start | bytes 1572864 | tf_op jit(solution)/shard_map/all_to_all | solution.py:303
  29.3 7.6 %collective-permute-start.4 = (bf16[3,96,512]{2,1,0:T(8,128)(2,1)S(1)}, bf16[3,96,512]{2,1,0:T(8,128)(2,1)S(1)}, u32[]{:S(2)}, u32[]{:S(2)}) collective-permute-start(bf16[3,96,512]{2,1,0:T(8,128)(2,1)S(1)} %get-tuple-element.28.level_ref), channel_id=1, source_target_pairs={{0,744},{8,752},{16,760},{24,0},{32,8},{40,16},{48,24},{56,32},{64... | collective-permute-start | bytes 884744 | tf_op jit(solution)/shard_map/ppermute | solution.py:266
  38.8 2.6 %collective-permute-done.4.above_ref = bf16[3,96,512]{2,1,0:T(8,128)(2,1)S(1)} collective-permute-done((bf16[3,96,512]{2,1,0:T(8,128)(2,1)S(1)}, bf16[3,96,512]{2,1,0:T(8,128)(2,1)S(1)}, u32[]{:S(2)}, u32[]{:S(2)}) %collective-permute-start.4) | collective-permute-done | bytes 294944 | tf_op jit(solution)/shard_map/ppermute | solution.py:266
  41.4 7.4 %collective-permute-done.3.below_ref = bf16[3,96,512]{2,1,0:T(8,128)(2,1)S(1)} collective-permute-done((bf16[3,96,512]{2,1,0:T(8,128)(2,1)S(1)}, bf16[3,96,512]{2,1,0:T(8,128)(2,1)S(1)}, u32[]{:S(2)}, u32[]{:S(2)}) %collective-permute-start.3) | collective-permute-done | bytes 294944 | tf_op jit(solution)/shard_map/ppermute | solution.py:266
  49.6 6.8 %shard_map.138 = bf16[4,96,512]{2,1,0:T(8,128)(2,1)} custom-call(s32[1]{0:T(128)} %bitcast.place_ref, s32[7]{0:T(128)} %count_ref.3, s32[112]{0:T(128)} %dest_ref.3, s32[112]{0:T(128)} %source_ref.3, bf16[112,128,128]{2,1,0:T(8,128)(2,1)} %tiles_hbm.3, s32[1,512]{1,0:T(1,128)} %bitcast.19, bf16[3,96,512]{2,1,0:T(8,128)(2,1)} %copy-done.13, ...), custom_call_target="tpu_custom_call" | custom-call | flops 469762048 | bytes 3670016 | tf_op jit(solution)/shard_map/pallas_call | solution.py:335
  57.8 8.2 %all-to-all-start.1 = ((bf16[4,96,512]{2,1,0:T(8,128)(2,1)}), bf16[4,96,512]{2,1,0:T(8,128)(2,1)S(1)}, u32[]{:S(2)}, u32[]{:S(2)}) async-start(bf16[4,96,512]{2,1,0:T(8,128)(2,1)} %shard_map.138), calls=%async_computation.1 | async-start | bytes 786432 | tf_op jit(solution)/shard_map/all_to_all | solution.py:303
  67.9 16.0 %all-to-all-done.1.refs_2_ = bf16[4,96,512]{2,1,0:T(8,128)(2,1)S(1)} async-done(((bf16[4,96,512]{2,1,0:T(8,128)(2,1)}), bf16[4,96,512]{2,1,0:T(8,128)(2,1)S(1)}, u32[]{:S(2)}, u32[]{:S(2)}) %all-to-all-start.1) | async-done | bytes 393248 | tf_op jit(solution)/shard_map/all_to_all | solution.py:303
  88.4 8.4 %shard_map.139 = (bf16[512,128]{1,0:T(8,128)(2,1)}, bf16[128,512]{1,0:T(8,128)(2,1)}, bf16[1536,128]{1,0:T(8,128)(2,1)}, f32[8,128]{1,0:T(8,128)}, bf16[768,128]...) custom-call(s32[1]{0:T(128)} %bitcast.place_ref, ...), custom_call_target="tpu_custom_call" | custom-call | flops 939524096 | bytes 3670016 | tf_op jit(solution)/shard_map/pallas_call | solution.py:355
  99.6 10.0 %all-to-all-start.2 = ((bf16[96,24,128]{2,1,0:T(8,128)(2,1)}), bf16[96,24,128]{2,1,0:T(8,128)(2,1)S(1)}, u32[]{:S(2)}, u32[]{:S(2)}) async-start(bf16[96,24,128]{2,1,0:T(8,128)(2,1)} %pad_maximum_fusion), calls=%async_computation.2 | async-start | bytes 1179648 | tf_op jit(solution)/shard_map/all_to_all | solution.py:406
  109.7 3.4 %collective-permute-start.6 = (bf16[3,128,512]{2,1,0:T(8,128)(2,1)S(1)}, bf16[3,128,512]{2,1,0:T(8,128)(2,1)S(1)}, u32[]{:S(2)}, u32[]{:S(2)}) collective-permute-start(bf16[3,128,512]{2,1,0:T(8,128)(2,1)S(1)} %copy-done.15), channel_id=1, source_target_pairs={{0,24},{8,32},{16,40},{24,48},{32,56},{40,64},{48,72},{56,80},{64,... | collective-permute-start | bytes 1179656 | tf_op jit(solution)/shard_map/ppermute | solution.py:266
  113.0 5.8 %collective-permute-start.7 = (bf16[3,128,512]{2,1,0:T(8,128)(2,1)S(1)}, bf16[3,128,512]{2,1,0:T(8,128)(2,1)S(1)}, u32[]{:S(2)}, u32[]{:S(2)}) collective-permute-start(bf16[3,128,512]{2,1,0:T(8,128)(2,1)S(1)} %copy-done.14), channel_id=1, source_target_pairs={{0,744},{8,752},{16,760},{24,0},{32,8},{40,16},{48,24},{56,32},{64... | collective-permute-start | bytes 1179656 | tf_op jit(solution)/shard_map/ppermute | solution.py:266
  118.8 17.2 %collective-permute-done.6.below_ref = bf16[3,128,512]{2,1,0:T(8,128)(2,1)S(1)} collective-permute-done((bf16[3,128,512]{2,1,0:T(8,128)(2,1)S(1)}, bf16[3,128,512]{2,1,0:T(8,128)(2,1)S(1)}, u32[]{:S(2)}, u32[]{:S(2)}) %collective-permute-start.6) | collective-permute-done | bytes 393248 | tf_op jit(solution)/shard_map/ppermute | solution.py:266
  136.2 3.4 %collective-permute-start.8 = (bf16[128,512]{1,0:T(8,128)(2,1)S(1)}, bf16[128,512]{1,0:T(8,128)(2,1)S(1)}, u32[]{:S(2)}, u32[]{:S(2)}) collective-permute-start(bf16[128,512]{1,0:T(8,128)(2,1)S(1)} %get-tuple-element.34), channel_id=1, source_target_pairs={{0,8},{8,16},{16,0},{24,32},{32,40},{40,24},{48,56},{56,64},{64,48... | collective-permute-start | bytes 393224 | tf_op jit(solution)/shard_map/ppermute | solution.py:274
  143.1 3.4 %collective-permute-done.9.second_ref = bf16[128,512]{1,0:T(8,128)(2,1)S(1)} collective-permute-done((bf16[128,512]{1,0:T(8,128)(2,1)S(1)}, bf16[128,512]{1,0:T(8,128)(2,1)S(1)}, u32[]{:S(2)}, u32[]{:S(2)}) %collective-permute-start.9) | collective-permute-done | bytes 131104 | tf_op jit(solution)/shard_map/ppermute | solution.py:274
  151.1 5.3 %collective-permute-done.14.piece_ref = bf16[16,128]{1,0:T(8,128)(2,1)S(1)} collective-permute-done((bf16[16,128]{1,0:T(8,128)(2,1)S(1)}, bf16[16,128]{1,0:T(8,128)(2,1)S(1)}, u32[]{:S(2)}, u32[]{:S(2)}) %collective-permute-start.14) | collective-permute-done | bytes 4128 | tf_op jit(solution)/shard_map/ppermute | solution.py:416
  157.2 18.7 %all-to-all-start.3 = ((bf16[96,16,128]{2,1,0:T(8,128)(2,1)}), bf16[96,16,128]{2,1,0:T(8,128)(2,1)S(1)}, u32[]{:S(2)}, u32[]{:S(2)}) async-start(bf16[96,16,128]{2,1,0:T(8,128)(2,1)} %shard_map.143), calls=%async_computation.3 | async-start | bytes 786432 | tf_op jit(solution)/shard_map/all_to_all | solution.py:453
  176.0 6.4 %collective-permute-start.11 = (bf16[96,512]{1,0:T(8,128)(2,1)S(1)}, bf16[96,512]{1,0:T(8,128)(2,1)S(1)}, u32[]{:S(2)}, u32[]{:S(2)}) collective-permute-start(bf16[96,512]{1,0:T(8,128)(2,1)S(1)} %get-tuple-element.42), channel_id=1, source_target_pairs={{0,2},{1,3},{2,4},{3,5},{4,6},{5,7},{6,0},{7,1},{8,10},{9,11},{10,... | collective-permute-start | bytes 294920 | tf_op jit(solution)/shard_map/ppermute | solution.py:307
  182.4 3.4 %collective-permute-start.12 = (bf16[96,512]{1,0:T(8,128)(2,1)S(1)}, bf16[96,512]{1,0:T(8,128)(2,1)S(1)}, u32[]{:S(2)}, u32[]{:S(2)}) collective-permute-start(bf16[96,512]{1,0:T(8,128)(2,1)S(1)} %get-tuple-element.43), channel_id=1, source_target_pairs={{0,4},{1,5},{2,6},{3,7},{4,0},{5,1},{6,2},{7,3},{8,12},{9,13},{10,... | collective-permute-start | bytes 294920 | tf_op jit(solution)/shard_map/ppermute | solution.py:307
  185.9 4.3 %collective-permute-start.13 = (bf16[96,512]{1,0:T(8,128)(2,1)S(1)}, bf16[96,512]{1,0:T(8,128)(2,1)S(1)}, u32[]{:S(2)}, u32[]{:S(2)}) collective-permute-start(bf16[96,512]{1,0:T(8,128)(2,1)S(1)} %get-tuple-element.44), channel_id=1, source_target_pairs={{0,6},{1,7},{2,0},{3,1},{4,2},{5,3},{6,4},{7,5},{8,14},{9,15},{10,... | collective-permute-start | bytes 294920 | tf_op jit(solution)/shard_map/ppermute | solution.py:307
  190.7 7.7 %collective-permute-done.12 = bf16[96,512]{1,0:T(8,128)(2,1)S(1)} collective-permute-done((bf16[96,512]{1,0:T(8,128)(2,1)S(1)}, bf16[96,512]{1,0:T(8,128)(2,1)S(1)}, u32[]{:S(2)}, u32[]{:S(2)}) %collective-permute-start.12) | collective-permute-done | bytes 98336 | tf_op jit(solution)/shard_map/ppermute | solution.py:307
  198.3 2.8 %collective-permute-done.13 = bf16[96,512]{1,0:T(8,128)(2,1)S(1)} collective-permute-done((bf16[96,512]{1,0:T(8,128)(2,1)S(1)}, bf16[96,512]{1,0:T(8,128)(2,1)S(1)}, u32[]{:S(2)}, u32[]{:S(2)}) %collective-permute-start.13) | collective-permute-done | bytes 98336 | tf_op jit(solution)/shard_map/ppermute | solution.py:307
  (61 shorter events, 29.6 us)
Async XLA Ops:
  0.6 13.4 %collective-permute-start.1 = (bf16[96,512]{1,0:T(8,128)(2,1)}, bf16[96,512]{1,0:T(8,128)(2,1)S(1)}, u32[]{:S(2)}, u32[]{:S(2)}) collective-permute-start(bf16[96,512]{1,0:T(8,128)(2,1)} %bitcast.15), channel_id=1, source_target_pairs={{0,8},{8,16},{16,0},{24,32},{32,40},{40,24},{48,56},{56,64},{64,48... | collective-permute-start | bytes 294920 | tf_op jit(solution)/shard_map/ppermute | solution.py:274
  4.9 12.5 %collective-permute-start = (bf16[96,512]{1,0:T(8,128)(2,1)}, bf16[96,512]{1,0:T(8,128)(2,1)S(1)}, u32[]{:S(2)}, u32[]{:S(2)}) collective-permute-start(bf16[96,512]{1,0:T(8,128)(2,1)} %bitcast.16), channel_id=1, source_target_pairs={{0,16},{8,0},{16,8},{24,40},{32,24},{40,32},{48,64},{56,48},{64,56... | collective-permute-start | bytes 294920 | tf_op jit(solution)/shard_map/ppermute | solution.py:274
  21.1 36.6 %all-to-all-start = ((bf16[4,192,512]{2,1,0:T(8,128)(2,1)}), bf16[4,192,512]{2,1,0:T(8,128)(2,1)S(1)}, u32[]{:S(2)}, u32[]{:S(2)}) async-start(bf16[4,192,512]{2,1,0:T(8,128)(2,1)} %get-tuple-element.27), calls=%async_computation | async-start | bytes 1572864 | tf_op jit(solution)/shard_map/all_to_all | solution.py:303
  29.3 12.1 %collective-permute-start.4 = (bf16[3,96,512]{2,1,0:T(8,128)(2,1)S(1)}, bf16[3,96,512]{2,1,0:T(8,128)(2,1)S(1)}, u32[]{:S(2)}, u32[]{:S(2)}) collective-permute-start(bf16[3,96,512]{2,1,0:T(8,128)(2,1)S(1)} %get-tuple-element.28.level_ref), channel_id=1, source_target_pairs={{0,744},{8,752},{16,760},{24,0},{32,8},{40,16},{48,24},{56,32},{64... | collective-permute-start | bytes 884744 | tf_op jit(solution)/shard_map/ppermute | solution.py:266
  36.9 12.0 %collective-permute-start.3 = (bf16[3,96,512]{2,1,0:T(8,128)(2,1)S(1)}, bf16[3,96,512]{2,1,0:T(8,128)(2,1)S(1)}, u32[]{:S(2)}, u32[]{:S(2)}) collective-permute-start(bf16[3,96,512]{2,1,0:T(8,128)(2,1)S(1)} %get-tuple-element.28.level_ref), channel_id=1, source_target_pairs={{0,24},{8,32},{16,40},{24,48},{32,56},{40,64},{48,72},{56,80},{64,... | collective-permute-start | bytes 884744 | tf_op jit(solution)/shard_map/ppermute | solution.py:266
  57.8 29.7 %copy-start.8 = (bf16[4,192,512]{2,1,0:T(8,128)(2,1)}, bf16[4,192,512]{2,1,0:T(8,128)(2,1)S(1)}, u32[]{:S(2)}) copy-start(bf16[4,192,512]{2,1,0:T(8,128)(2,1)S(1)} %all-to-all-done.refs_0_) | copy-start | bytes 2359300
  57.8 26.0 %all-to-all-start.1 = ((bf16[4,96,512]{2,1,0:T(8,128)(2,1)}), bf16[4,96,512]{2,1,0:T(8,128)(2,1)S(1)}, u32[]{:S(2)}, u32[]{:S(2)}) async-start(bf16[4,96,512]{2,1,0:T(8,128)(2,1)} %shard_map.138), calls=%async_computation.1 | async-start | bytes 786432 | tf_op jit(solution)/shard_map/all_to_all | solution.py:303
  65.9 21.5 %collective-permute-start.2 = (bf16[4,192,512]{2,1,0:T(8,128)(2,1)S(1)}, bf16[4,192,512]{2,1,0:T(8,128)(2,1)S(1)}, u32[]{:S(2)}, u32[]{:S(2)}) collective-permute-start(bf16[4,192,512]{2,1,0:T(8,128)(2,1)S(1)} %all-to-all-done.refs_0_), channel_id=1, source_target_pairs={{0,1},{1,0},{2,3},{3,2},{4,5},{5,4},{6,7},{7,6},{8,9},{9,8},{10,11... | collective-permute-start | bytes 2359304 | tf_op jit(solution)/shard_map/ppermute | solution.py:330
  83.8 3.6 %collective-permute-start.5 = (bf16[4,96,512]{2,1,0:T(8,128)(2,1)S(1)}, bf16[4,96,512]{2,1,0:T(8,128)(2,1)S(1)}, u32[]{:S(2)}, u32[]{:S(2)}) collective-permute-start(bf16[4,96,512]{2,1,0:T(8,128)(2,1)S(1)} %all-to-all-done.1.refs_2_), channel_id=1, source_target_pairs={{0,1},{1,0},{2,3},{3,2},{4,5},{5,4},{6,7},{7,6},{8,9},{9,8},{10,11... | collective-permute-start | bytes 1179656 | tf_op jit(solution)/shard_map/ppermute | solution.py:350
  97.6 38.5 %copy-start = (f32[3,128,512]{2,1,0:T(8,128)S(1)}, f32[3,128,512]{2,1,0:T(8,128)}, u32[]{:S(2)}) copy-start(f32[3,128,512]{2,1,0:T(8,128)} %get-tuple-element.30.level_ref) | copy-start | bytes 2359300
  99.6 46.8 %copy-start.2 = (bf16[768,128]{1,0:T(8,128)(2,1)S(1)}, bf16[768,128]{1,0:T(8,128)(2,1)}, u32[]{:S(2)}) copy-start(bf16[768,128]{1,0:T(8,128)(2,1)} %get-tuple-element.37.self_ref) | copy-start | bytes 589828
  99.6 46.8 %copy-start.3 = (bf16[768,128]{1,0:T(8,128)(2,1)S(1)}, bf16[768,128]{1,0:T(8,128)(2,1)}, u32[]{:S(2)}) copy-start(bf16[768,128]{1,0:T(8,128)(2,1)} %get-tuple-element.38.neighbour_ref) | copy-start | bytes 589828
  99.6 46.8 %copy-start.6 = (bf16[128,512]{1,0:T(8,128)(2,1)S(1)}, bf16[128,512]{1,0:T(8,128)(2,1)}, u32[]{:S(2)}) copy-start(bf16[128,512]{1,0:T(8,128)(2,1)} %get-tuple-element.36.grad_ref) | copy-start | bytes 393220
  99.6 49.3 %all-to-all-start.2 = ((bf16[96,24,128]{2,1,0:T(8,128)(2,1)}), bf16[96,24,128]{2,1,0:T(8,128)(2,1)S(1)}, u32[]{:S(2)}, u32[]{:S(2)}) async-start(bf16[96,24,128]{2,1,0:T(8,128)(2,1)} %pad_maximum_fusion), calls=%async_computation.2 | async-start | bytes 1179648 | tf_op jit(solution)/shard_map/all_to_all | solution.py:406
  109.7 26.4 %collective-permute-start.6 = (bf16[3,128,512]{2,1,0:T(8,128)(2,1)S(1)}, bf16[3,128,512]{2,1,0:T(8,128)(2,1)S(1)}, u32[]{:S(2)}, u32[]{:S(2)}) collective-permute-start(bf16[3,128,512]{2,1,0:T(8,128)(2,1)S(1)} %copy-done.15), channel_id=1, source_target_pairs={{0,24},{8,32},{16,40},{24,48},{32,56},{40,64},{48,72},{56,80},{64,... | collective-permute-start | bytes 1179656 | tf_op jit(solution)/shard_map/ppermute | solution.py:266
  113.0 23.0 %collective-permute-start.7 = (bf16[3,128,512]{2,1,0:T(8,128)(2,1)S(1)}, bf16[3,128,512]{2,1,0:T(8,128)(2,1)S(1)}, u32[]{:S(2)}, u32[]{:S(2)}) collective-permute-start(bf16[3,128,512]{2,1,0:T(8,128)(2,1)S(1)} %copy-done.14), channel_id=1, source_target_pairs={{0,744},{8,752},{16,760},{24,0},{32,8},{40,16},{48,24},{56,32},{64... | collective-permute-start | bytes 1179656 | tf_op jit(solution)/shard_map/ppermute | solution.py:266
  136.2 6.9 %collective-permute-start.8 = (bf16[128,512]{1,0:T(8,128)(2,1)S(1)}, bf16[128,512]{1,0:T(8,128)(2,1)S(1)}, u32[]{:S(2)}, u32[]{:S(2)}) collective-permute-start(bf16[128,512]{1,0:T(8,128)(2,1)S(1)} %get-tuple-element.34), channel_id=1, source_target_pairs={{0,8},{8,16},{16,0},{24,32},{32,40},{40,24},{48,56},{56,64},{64,48... | collective-permute-start | bytes 393224 | tf_op jit(solution)/shard_map/ppermute | solution.py:274
  139.6 6.9 %collective-permute-start.9 = (bf16[128,512]{1,0:T(8,128)(2,1)S(1)}, bf16[128,512]{1,0:T(8,128)(2,1)S(1)}, u32[]{:S(2)}, u32[]{:S(2)}) collective-permute-start(bf16[128,512]{1,0:T(8,128)(2,1)S(1)} %get-tuple-element.35), channel_id=1, source_target_pairs={{0,16},{8,0},{16,8},{24,40},{32,24},{40,32},{48,64},{56,48},{64,56... | collective-permute-start | bytes 393224 | tf_op jit(solution)/shard_map/ppermute | solution.py:274
  147.0 4.0 %collective-permute-start.10 = (bf16[384,512]{1,0:T(8,128)(2,1)S(1)}, bf16[384,512]{1,0:T(8,128)(2,1)S(1)}, u32[]{:S(2)}, u32[]{:S(2)}) collective-permute-start(bf16[384,512]{1,0:T(8,128)(2,1)S(1)} %get-tuple-element.40), channel_id=1, source_target_pairs={{0,1},{1,0},{2,3},{3,2},{4,5},{5,4},{6,7},{7,6},{8,9},{9,8},{10,11... | collective-permute-start | bytes 1179656 | tf_op jit(solution)/shard_map/ppermute | solution.py:439
  149.1 7.3 %collective-permute-start.14 = (bf16[16,128]{1,0:T(8,128)(2,1)S(1)}, bf16[16,128]{1,0:T(8,128)(2,1)S(1)}, u32[]{:S(2)}, u32[]{:S(2)}) collective-permute-start(bf16[16,128]{1,0:T(8,128)(2,1)S(1)} %slice.13), channel_id=1, source_target_pairs={{0,0},{1,9},{2,16},{3,25},{4,32},{5,41},{6,48},{7,57},{8,64},{9,73... | collective-permute-start | bytes 12296 | tf_op jit(solution)/shard_map/ppermute | solution.py:416
  157.2 45.1 %all-to-all-start.3 = ((bf16[96,16,128]{2,1,0:T(8,128)(2,1)}), bf16[96,16,128]{2,1,0:T(8,128)(2,1)S(1)}, u32[]{:S(2)}, u32[]{:S(2)}) async-start(bf16[96,16,128]{2,1,0:T(8,128)(2,1)} %shard_map.143), calls=%async_computation.3 | async-start | bytes 786432 | tf_op jit(solution)/shard_map/all_to_all | solution.py:453
  176.0 14.7 %collective-permute-start.11 = (bf16[96,512]{1,0:T(8,128)(2,1)S(1)}, bf16[96,512]{1,0:T(8,128)(2,1)S(1)}, u32[]{:S(2)}, u32[]{:S(2)}) collective-permute-start(bf16[96,512]{1,0:T(8,128)(2,1)S(1)} %get-tuple-element.42), channel_id=1, source_target_pairs={{0,2},{1,3},{2,4},{3,5},{4,6},{5,7},{6,0},{7,1},{8,10},{9,11},{10,... | collective-permute-start | bytes 294920 | tf_op jit(solution)/shard_map/ppermute | solution.py:307
  182.4 15.9 %collective-permute-start.12 = (bf16[96,512]{1,0:T(8,128)(2,1)S(1)}, bf16[96,512]{1,0:T(8,128)(2,1)S(1)}, u32[]{:S(2)}, u32[]{:S(2)}) collective-permute-start(bf16[96,512]{1,0:T(8,128)(2,1)S(1)} %get-tuple-element.43), channel_id=1, source_target_pairs={{0,4},{1,5},{2,6},{3,7},{4,0},{5,1},{6,2},{7,3},{8,12},{9,13},{10,... | collective-permute-start | bytes 294920 | tf_op jit(solution)/shard_map/ppermute | solution.py:307
  185.9 15.3 %collective-permute-start.13 = (bf16[96,512]{1,0:T(8,128)(2,1)S(1)}, bf16[96,512]{1,0:T(8,128)(2,1)S(1)}, u32[]{:S(2)}, u32[]{:S(2)}) collective-permute-start(bf16[96,512]{1,0:T(8,128)(2,1)S(1)} %get-tuple-element.44), channel_id=1, source_target_pairs={{0,6},{1,7},{2,0},{3,1},{4,2},{5,3},{6,4},{7,5},{8,14},{9,15},{10,... | collective-permute-start | bytes 294920 | tf_op jit(solution)/shard_map/ppermute | solution.py:307
  (11 other events, 71.6 us)

commit v5 on v4

--- a/solution.py
+++ b/solution.py
@@ -14,6 +14,8 @@
 GROUP = 4
 CORES = 2
 TRIO = 3
+COLUMN = 8
+PIECE = 16
 F32 = jnp.float32
 BF16 = jnp.bfloat16
 VMEM_BYTES = 16 * 1024 * 1024
@@ -63,11 +65,6 @@
                 out_ref[stack, pl.ds(width, width), pl.ds((core * 2 + kind) * BLOCK, BLOCK)] = ref[
                     :, pl.ds((stack * CORES + core) * BLOCK, BLOCK)
                 ]
-
-
-def repeat_kernel(piece_ref, after_ref, out_ref):
-    for copy in range(out_ref.shape[0]):
-        out_ref[copy] = piece_ref[...]
 
 
 def tile_copies(tiles_hbm, tiles_ref, copied):
@@ -122,14 +119,11 @@
 
 
 def middle_kernel(
-    place_ref, core_ref, count_ref, dest_ref, source_ref, tiles_hbm, degree_ref, *refs
+    place_ref, core_ref, stack_ref, count_ref, dest_ref, source_ref, tiles_hbm, degree_ref, *refs
 ):
     packed, aggregates, refs = refs[:2], refs[2:4], refs[4:]
     bias_ref, cotangent_ref, refs = *refs[:2], refs[2:]
-    act_ref, grad_ref, weight_ref, bias_out_ref, self_ref, neighbour_ref, refs = (
-        *refs[:6],
-        refs[6:],
-    )
+    act_ref, grad_ref, weight_ref, self_ref, neighbour_ref, refs = *refs[:5], refs[5:]
     level_ref, below_ref, above_ref, *refs = refs
     features_ref, scaled_ref, total_ref, tiles_ref, copied, *refs = refs
     turned_ref, to_below_ref, to_above_ref, stored = refs
@@ -166,9 +160,10 @@
     grad = cotangent_ref[...].astype(F32) * gate_value * (1.0 + preact * (1.0 - gate_value))
     grad_pre = grad.astype(BF16)
     grad = grad_pre.astype(F32)
-    bias_out_ref[...] = jnp.broadcast_to(
-        jnp.sum(grad, axis=0, keepdims=True), bias_out_ref.shape
-    ).astype(bias_out_ref.dtype)
+    planes, _, rows, lane = weight_ref.shape
+    bias_rows = jnp.broadcast_to(jnp.sum(grad, axis=0, keepdims=True), (rows, lane)).astype(BF16)
+    for plane in range(planes):
+        weight_ref[plane, COLUMN] = bias_rows
     turned = grad.T
     turned_ref[...] = turned.astype(BF16)
     stores[0].start()
@@ -180,8 +175,11 @@
         for kind, operand in enumerate(operands):
             term = jnp.dot(operand, grad_pre, preferred_element_type=F32).astype(BF16)
             for stack in range(stacks):
-                first = ((far * stacks + stack) * 2 + kind) * width
-                weight_ref[pl.ds(first, width), :] = term[stack * width : (stack + 1) * width]
+                column = (stack ^ stack_ref[0]) * CORES + far
+                for first in range(0, width, PIECE):
+                    plane, row = divmod(kind * width + first, rows)
+                    begin = stack * width + first
+                    weight_ref[plane, column, pl.ds(row, PIECE), :] = term[begin : begin + PIECE]
     total_ref[...] = jnp.zeros_like(total_ref)
     for offset in range(OFFS):
         slot = band_slot(place_ref, offset)
@@ -235,17 +233,37 @@
         out[...] = (keep_ref[piece] + got_ref[piece].astype(F32)).astype(out.dtype)
 
 
-def lay_kernel(pieces_ref, self_ref, neighbour_ref):
-    groups, rows, lane = pieces_ref.shape
-    feats = self_ref.shape[1] // lane
-    for piece in range(groups):
-        part, feat = piece // feats, piece % feats
-        for first in range(0, rows, 16):
-            kind, row = divmod(part * rows + first, self_ref.shape[0])
+def planes_kernel(got_ref, out_ref):
+    for column in range(COLUMN + 1):
+        value = got_ref[0, column].astype(F32)
+        for plane in range(1, got_ref.shape[0]):
+            value = value + got_ref[plane, column].astype(F32)
+        value = value.astype(BF16)
+        if column < COLUMN:
+            out_ref[column, 0] = value
+        else:
+            for copy in range(COLUMN):
+                out_ref[copy, 1] = value
+
+
+def column_kernel(got_ref, piece_ref, bias_ref):
+    for at, out in enumerate((piece_ref, bias_ref)):
+        value = got_ref[0, at].astype(F32)
+        for column in range(1, COLUMN):
+            value = value + got_ref[column, at].astype(F32)
+        out[...] = value.astype(out.dtype)
+
+
+def lay_kernel(feat_ref, pieces_ref, self_ref, neighbour_ref):
+    planes, _, rows, _ = pieces_ref.shape
+    for plane in range(planes):
+        for first in range(0, rows, PIECE):
+            kind, row = divmod(plane * rows + first, self_ref.shape[0])
             out = (self_ref, neighbour_ref)[kind]
-            out[pl.ds(row, 16), pl.ds(feat * lane, lane)] = pieces_ref[
-                piece, pl.ds(first, 16), :
-            ].astype(F32)
+            for column in range(COLUMN):
+                out[pl.ds(row, PIECE), lanes(column ^ feat_ref[0])] = pieces_ref[
+                    plane, column, pl.ds(first, PIECE), :
+                ].astype(F32)
 
 
 def call(kernel, in_specs, out_shape, scratch, flops, moved, out_specs=None, limit=VMEM_BYTES):
@@ -298,6 +316,11 @@
     place = (lax.axis_index("rows") % TRIO).reshape(1)
     same_core = [[z * CORES + c for z in range(stacks)] for c in range(CORES)]
     other_core = [(f, f ^ 1) for f in range(feats)]
+    same_plane = [
+        [(p // TRIO * COLUMN + c) * TRIO + p % TRIO for c in range(COLUMN)]
+        for p in range(groups // COLUMN)
+    ]
+    same_column = [list(members) for members in zip(*same_plane)]
 
     def over_stacks(value):
         return lax.all_to_all(value, "feat", 0, 0, axis_index_groups=same_core)
@@ -349,17 +372,19 @@
     aggregate_own = over_stacks(aggregate)
     aggregate_far = lax.ppermute(aggregate_own, "feat", other_core)
 
+    planes = groups // COLUMN
+    rows_each = 4 * half // groups
+
     def trio(dtype):
         return jax.ShapeDtypeStruct((TRIO, hidden_dev, node_dev), dtype)
 
     middle = call(
         middle_kernel,
-        [SMEM] * 5 + [HBM] + [VMEM] * 5 + [WHOLE] * 2,
+        [SMEM] * 6 + [HBM] + [VMEM] * 5 + [WHOLE] * 2,
         [
             jax.ShapeDtypeStruct((node_dev, hidden_dev), BF16),
             jax.ShapeDtypeStruct((hidden_dev, node_dev), BF16),
-            jax.ShapeDtypeStruct((4 * half, hidden_dev), BF16),
-            jax.ShapeDtypeStruct((8, hidden_dev), F32),
+            jax.ShapeDtypeStruct((planes, COLUMN + 1, rows_each, hidden_dev), BF16),
             jax.ShapeDtypeStruct((2 * half, hidden_dev), BF16),
             jax.ShapeDtypeStruct((2 * half, hidden_dev), BF16),
             trio(F32),
@@ -379,11 +404,12 @@
         ],
         tile_flops * 2,
         tile_values.size * 2,
-        [WHOLE, HBM, VMEM, VMEM, VMEM, VMEM, VMEM, HBM, HBM],
+        [WHOLE, HBM, VMEM, VMEM, VMEM, VMEM, HBM, HBM],
         TILES_VMEM_BYTES,
     )(
         place,
         core,
+        stack,
         *scalars,
         tile_values,
         degrees,
@@ -394,26 +420,49 @@
         hidden_bias.reshape(1, hidden_dev),
         cotangent,
     )
-    activations, grad_turned, weight_part, bias_part, weight_self, weight_neighbour = middle[:6]
-    to_level, to_below, to_above = middle[6:]
+    activations, grad_turned, weight_part, weight_self, weight_neighbour = middle[:5]
+    to_level, to_below, to_above = middle[5:]
     from_above = shifted(to_below, -TRIO)
     from_below = shifted(to_above, TRIO)
 
-    rows_each = 4 * half // groups
-    weight_part = weight_part.reshape(groups, rows_each, hidden_dev)
-    bias_rows = jnp.broadcast_to(bias_part.astype(BF16)[None], (groups, 8, hidden_dev))
-    sent = jnp.concatenate([weight_part, bias_rows], axis=1)
-    summed = jnp.sum(lax.all_to_all(sent, "rows", 0, 0).astype(F32), axis=0)
-    grad_bias = summed[rows_each]
-    piece = summed[:rows_each].astype(BF16)
-    per_stack = groups // feats
-    pairs = []
-    for row in range(groups):
-        far, at, part = row // (groups // 2), row // per_stack % stacks, row % per_stack
-        for feat in range(feats):
-            column = at * CORES + (feat % CORES + far) % CORES
-            pairs.append((row * feats + feat, (part * feats + feat) * feats + column))
+    got = jax.ShapeDtypeStruct((COLUMN, 2, rows_each, hidden_dev), BF16)
+    got = call(planes_kernel, [VMEM], got, [], weight_part.size, weight_part.size * 2)(
+        lax.all_to_all(weight_part, "rows", 0, 0, axis_index_groups=same_column)
+    )
+    piece = jax.ShapeDtypeStruct((rows_each, hidden_dev), BF16)
+    piece, bias_sum = call(
+        column_kernel,
+        [VMEM],
+        [piece, jax.ShapeDtypeStruct(piece.shape, F32)],
+        [],
+        got.size,
+        got.size * 2,
+    )(lax.all_to_all(got, "rows", 0, 0, axis_index_groups=same_plane))
+    pairs = [
+        (row * feats + feat, row * feats + (feat ^ (row // TRIO % COLUMN)))
+        for row in range(groups)
+        for feat in range(feats)
+    ]
     piece = lax.ppermute(piece, ("rows", "feat"), pairs)
+    pieces = lax.all_to_all(
+        jnp.broadcast_to(piece[None], (COLUMN,) + piece.shape),
+        "rows",
+        0,
+        0,
+        axis_index_groups=same_plane,
+    )
+    pieces = lax.all_to_all(
+        jnp.broadcast_to(pieces[None], (planes,) + pieces.shape),
+        "rows",
+        0,
+        0,
+        axis_index_groups=same_column,
+    )
+    grad_weight = jax.ShapeDtypeStruct((width, feats * hidden_dev), F32)
+    grad_self, grad_neighbour = call(
+        lay_kernel, [SMEM, VMEM], [grad_weight, grad_weight], [], 0, pieces.size * 6
+    )(lax.axis_index("feat").reshape(1), pieces)
+
     spread = jax.ShapeDtypeStruct((hidden_dev, node_dev), BF16)
     own, first, second = call(
         trio_kernel,
@@ -450,28 +499,10 @@
         keep.reshape(stacks, width, node_dev),
         got.reshape(stacks, width, node_dev),
     )
-    pieces = lax.all_to_all(
-        call(
-            repeat_kernel,
-            [VMEM, ANY],
-            jax.ShapeDtypeStruct((groups,) + piece.shape, BF16),
-            [],
-            0,
-            groups * piece.size * 2,
-        )(piece, parts[0]),
-        "rows",
-        0,
-        0,
-    )
-    grad_weight = jax.ShapeDtypeStruct((width, feats * hidden_dev), F32)
-    grad_self, grad_neighbour = call(
-        lay_kernel, [VMEM], [grad_weight, grad_weight], [], 0, pieces.size * 6
-    )(pieces)
-
     grad_turned = parts[0]
     for steps in range(1, stacks):
         grad_turned = grad_turned + to_stack(parts[steps], steps).astype(F32)
-    return (activations, grad_turned.astype(BF16).T, grad_self, grad_neighbour, grad_bias)
+    return (activations, grad_turned.astype(BF16).T, grad_self, grad_neighbour, bias_sum[0])
 
 
 def solution(mesh):

time: 204 us -> 191 us (0.936)
  the two profiles are of different devices: /device:TPU:64 before, /device:TPU:72 now
where the time goes in v5:
time: 191 us; the launch traced here: 190 us
  starting transfers between devices  92 us (48%)
  waiting for transfers between devices  55.3 us (29%)
  Pallas kernels  19.6 us (10%)
  blocking collectives  14.1 us (7%)
  local copies, waits for them, and re-layouts  7.54 us (4%)
    all_to_all x2, waiting for transfers between devices, over_stacks(): return lax.all_to_all(value, 'feat', 0, 0, axis_index_groups=same_core)  20.7 us
    all_to_all x2, starting transfers between devices, over_stacks(): return lax.all_to_all(value, 'feat', 0, 0, axis_index_groups=same_core)  20.3 us
    ppermute x3, starting transfers between devices, to_stack(): return lax.ppermute(value, 'feat', pairs)  17.3 us
    all_to_all x1, blocking collectives, on_device(): lax.all_to_all(got, 'rows', 0, 0, axis_index_groups=same_plane)  14.1 us
    ppermute x4, starting transfers between devices, turned_in_trio(): return lax.ppermute(value, 'rows', pairs)  12 us
    all_to_all x1, starting transfers between devices, on_device(): lax.all_to_all(jnp.broadcast_to(piece[None], (COLUMN,) + piece.shape), 'r...  12 us
    ppermute x4, starting transfers between devices, shifted(): return lax.ppermute(value, 'rows', pairs)  11.7 us
    ppermute x3, waiting for transfers between devices, to_stack(): return lax.ppermute(value, 'feat', pairs)  11.2 us
  transfers between devices with their start and end apart: 20, of which 12 were waited for; matrix products, arithmetic and copies ran while one was open for 1% of the time, Pallas kernels for 4%

profile of v5, /device:TPU:72, one launch (start us, length us, event | category | flops | bytes accessed | tf_op | source)
XLA Modules:
  0.0 190.1 jit_solution(11437537922507908607)
XLA Ops:
  0.6 4.3 %collective-permute-start.1 = (bf16[96,512]{1,0:T(8,128)(2,1)}, bf16[96,512]{1,0:T(8,128)(2,1)S(1)}, u32[]{:S(2)}, u32[]{:S(2)}) collective-permute-start(bf16[96,512]{1,0:T(8,128)(2,1)} %bitcast.15), channel_id=1, source_target_pairs={{0,8},{8,16},{16,0},{24,32},{32,40},{40,24},{48,56},{56,64},{64,48... | collective-permute-start | bytes 294920 | tf_op jit(solution)/shard_map/ppermute | solution.py:292
  7.4 4.2 %collective-permute-done.first_ref = bf16[96,512]{1,0:T(8,128)(2,1)S(1)} collective-permute-done((bf16[96,512]{1,0:T(8,128)(2,1)}, bf16[96,512]{1,0:T(8,128)(2,1)S(1)}, u32[]{:S(2)}, u32[]{:S(2)}) %collective-permute-start) | collective-permute-done | bytes 98336 | tf_op jit(solution)/shard_map/ppermute | solution.py:292
  15.4 13.9 %all-to-all-start = ((bf16[4,192,512]{2,1,0:T(8,128)(2,1)}), bf16[4,192,512]{2,1,0:T(8,128)(2,1)S(1)}, u32[]{:S(2)}, u32[]{:S(2)}) async-start(bf16[4,192,512]{2,1,0:T(8,128)(2,1)} %get-tuple-element.28), calls=%async_computation | async-start | bytes 1572864 | tf_op jit(solution)/shard_map/all_to_all | solution.py:326
  29.3 2.3 %collective-permute-start.4 = (bf16[3,96,512]{2,1,0:T(8,128)(2,1)S(1)}, bf16[3,96,512]{2,1,0:T(8,128)(2,1)S(1)}, u32[]{:S(2)}, u32[]{:S(2)}) collective-permute-start(bf16[3,96,512]{2,1,0:T(8,128)(2,1)S(1)} %get-tuple-element.29.level_ref), channel_id=1, source_target_pairs={{0,744},{8,752},{16,760},{24,0},{32,8},{40,16},{48,24},{56,32},{64... | collective-permute-start | bytes 884744 | tf_op jit(solution)/shard_map/ppermute | solution.py:284
  31.7 3.5 %collective-permute-start.3 = (bf16[3,96,512]{2,1,0:T(8,128)(2,1)S(1)}, bf16[3,96,512]{2,1,0:T(8,128)(2,1)S(1)}, u32[]{:S(2)}, u32[]{:S(2)}) collective-permute-start(bf16[3,96,512]{2,1,0:T(8,128)(2,1)S(1)} %get-tuple-element.29.level_ref), channel_id=1, source_target_pairs={{0,24},{8,32},{16,40},{24,48},{32,56},{40,64},{48,72},{56,80},{64,... | collective-permute-start | bytes 884744 | tf_op jit(solution)/shard_map/ppermute | solution.py:284
  35.2 3.0 %collective-permute-done.4.above_ref = bf16[3,96,512]{2,1,0:T(8,128)(2,1)S(1)} collective-permute-done((bf16[3,96,512]{2,1,0:T(8,128)(2,1)S(1)}, bf16[3,96,512]{2,1,0:T(8,128)(2,1)S(1)}, u32[]{:S(2)}, u32[]{:S(2)}) %collective-permute-start.4) | collective-permute-done | bytes 294944 | tf_op jit(solution)/shard_map/ppermute | solution.py:284
  38.2 6.0 %collective-permute-done.3.below_ref = bf16[3,96,512]{2,1,0:T(8,128)(2,1)S(1)} collective-permute-done((bf16[3,96,512]{2,1,0:T(8,128)(2,1)S(1)}, bf16[3,96,512]{2,1,0:T(8,128)(2,1)S(1)}, u32[]{:S(2)}, u32[]{:S(2)}) %collective-permute-start.3) | collective-permute-done | bytes 294944 | tf_op jit(solution)/shard_map/ppermute | solution.py:284
  45.0 7.6 %shard_map.138 = bf16[4,96,512]{2,1,0:T(8,128)(2,1)} custom-call(s32[1]{0:T(128)} %bitcast.place_ref, s32[7]{0:T(128)} %count_ref.3, s32[112]{0:T(128)} %dest_ref.3, s32[112]{0:T(128)} %source_ref.3, bf16[112,128,128]{2,1,0:T(8,128)(2,1)} %tiles_hbm.3, s32[1,512]{1,0:T(1,128)} %bitcast.18, bf16[3,96,512]{2,1,0:T(8,128)(2,1)} %copy-done.13, ...), custom_call_target="tpu_custom_call" | custom-call | flops 469762048 | bytes 3670016 | tf_op jit(solution)/shard_map/pallas_call | solution.py:358
  52.6 5.2 %all-to-all-done.refs_0_ = bf16[4,192,512]{2,1,0:T(8,128)(2,1)S(1)} async-done(((bf16[4,192,512]{2,1,0:T(8,128)(2,1)}), bf16[4,192,512]{2,1,0:T(8,128)(2,1)S(1)}, u32[]{:S(2)}, u32[]{:S(2)}) %all-to-all-start) | async-done | bytes 786464 | tf_op jit(solution)/shard_map/all_to_all | solution.py:326
  57.8 6.4 %all-to-all-start.1 = ((bf16[4,96,512]{2,1,0:T(8,128)(2,1)}), bf16[4,96,512]{2,1,0:T(8,128)(2,1)S(1)}, u32[]{:S(2)}, u32[]{:S(2)}) async-start(bf16[4,96,512]{2,1,0:T(8,128)(2,1)} %shard_map.138), calls=%async_computation.1 | async-start | bytes 786432 | tf_op jit(solution)/shard_map/all_to_all | solution.py:326
  66.1 15.5 %all-to-all-done.1.refs_2_ = bf16[4,96,512]{2,1,0:T(8,128)(2,1)S(1)} async-done(((bf16[4,96,512]{2,1,0:T(8,128)(2,1)}), bf16[4,96,512]{2,1,0:T(8,128)(2,1)S(1)}, u32[]{:S(2)}, u32[]{:S(2)}) %all-to-all-start.1) | async-done | bytes 393248 | tf_op jit(solution)/shard_map/all_to_all | solution.py:326
  86.2 9.2 %shard_map.139 = (bf16[512,128]{1,0:T(8,128)(2,1)}, bf16[128,512]{1,0:T(8,128)(2,1)}, bf16[12,9,16,128]{3,2,1,0:T(8,128)(2,1)}, bf16[768,128]{1,0:T(8,128)(2,1)}...) custom-call(s32[1]{0:T(128)} %bitcast.place_ref, ...), custom_call_target="tpu_custom_call" | custom-call | flops 939524096 | bytes 3670016 | tf_op jit(solution)/shard_map/pallas_call | solution.py:381
  95.4 5.7 %all-to-all-start.2 = ((bf16[12,9,16,128]{3,2,1,0:T(8,128)(2,1)}), bf16[12,9,16,128]{3,2,1,0:T(8,128)(2,1)S(1)}, u32[]{:S(2)}, u32[]{:S(2)}) async-start(bf16[12,9,16,128]{3,2,1,0:T(8,128)(2,1)} %get-tuple-element.46), calls=%async_computation.2 | async-start | bytes 884736 | tf_op jit(solution)/shard_map/all_to_all | solution.py:430
  101.1 3.7 %collective-permute-start.6 = (bf16[3,128,512]{2,1,0:T(8,128)(2,1)}, bf16[3,128,512]{2,1,0:T(8,128)(2,1)S(1)}, u32[]{:S(2)}, u32[]{:S(2)}) collective-permute-start(bf16[3,128,512]{2,1,0:T(8,128)(2,1)} %get-tuple-element.32), channel_id=1, source_target_pairs={{0,24},{8,32},{16,40},{24,48},{32,56},{40,64},{48,72},{56,80},{64,... | collective-permute-start | bytes 1179656 | tf_op jit(solution)/shard_map/ppermute | solution.py:284
  104.8 2.2 %collective-permute-start.7 = (bf16[3,128,512]{2,1,0:T(8,128)(2,1)}, bf16[3,128,512]{2,1,0:T(8,128)(2,1)S(1)}, u32[]{:S(2)}, u32[]{:S(2)}) collective-permute-start(bf16[3,128,512]{2,1,0:T(8,128)(2,1)} %get-tuple-element.33), channel_id=1, source_target_pairs={{0,744},{8,752},{16,760},{24,0},{32,8},{40,16},{48,24},{56,32},{64... | collective-permute-start | bytes 1179656 | tf_op jit(solution)/shard_map/ppermute | solution.py:284
  107.0 5.0 %all-to-all-done.2.got_ref = bf16[12,9,16,128]{3,2,1,0:T(8,128)(2,1)S(1)} async-done(((bf16[12,9,16,128]{3,2,1,0:T(8,128)(2,1)}), bf16[12,9,16,128]{3,2,1,0:T(8,128)(2,1)S(1)}, u32[]{:S(2)}, u32[]{:S(2)}) %all-to-all-start.2) | async-done | bytes 442400 | tf_op jit(solution)/shard_map/all_to_all | solution.py:430
  112.0 14.1 %all_to_all.30.got_ref = bf16[8,2,16,128]{3,2,1,0:T(8,128)(2,1)S(1)} all-to-all(bf16[8,2,16,128]{3,2,1,0:T(8,128)(2,1)S(1)} %shard_map.143), channel_id=1, replica_groups={{0,24,48,72,96,120,144,168},{8,32,56,80,104,128,152,176},{16,40,64,88,1..., dimensions={0} | all-to-all | bytes 131072 | tf_op jit(solution)/shard_map/all_to_all | solution.py:440
  129.8 12.0 %all-to-all-start.4 = ((bf16[8,16,128]{2,1,0:T(8,128)(2,1)}), bf16[8,16,128]{2,1,0:T(8,128)(2,1)S(1)}, u32[]{:S(2)}, u32[]{:S(2)}) async-start(bf16[8,16,128]{2,1,0:T(8,128)(2,1)} %broadcast_in_dim.4), calls=%async_computation.4 | async-start | bytes 65536 | tf_op jit(solution)/shard_map/all_to_all | solution.py:447
  143.1 2.2 %collective-permute-start.8 = (bf16[128,512]{1,0:T(8,128)(2,1)S(1)}, bf16[128,512]{1,0:T(8,128)(2,1)S(1)}, u32[]{:S(2)}, u32[]{:S(2)}) collective-permute-start(bf16[128,512]{1,0:T(8,128)(2,1)S(1)} %get-tuple-element.35), channel_id=1, source_target_pairs={{0,8},{8,16},{16,0},{24,32},{32,40},{40,24},{48,56},{56,64},{64,48... | collective-permute-start | bytes 393224 | tf_op jit(solution)/shard_map/ppermute | solution.py:292
  145.3 3.7 %collective-permute-start.9 = (bf16[128,512]{1,0:T(8,128)(2,1)S(1)}, bf16[128,512]{1,0:T(8,128)(2,1)S(1)}, u32[]{:S(2)}, u32[]{:S(2)}) collective-permute-start(bf16[128,512]{1,0:T(8,128)(2,1)S(1)} %get-tuple-element.36), channel_id=1, source_target_pairs={{0,16},{8,0},{16,8},{24,40},{32,24},{40,32},{48,64},{56,48},{64,56... | collective-permute-start | bytes 393224 | tf_op jit(solution)/shard_map/ppermute | solution.py:292
  149.8 5.4 %all-to-all-start.5 = ((bf16[12,8,16,128]{3,2,1,0:T(8,128)(2,1)}), bf16[12,8,16,128]{3,2,1,0:T(8,128)(2,1)S(1)}, u32[]{:S(2)}, u32[]{:S(2)}) async-start(bf16[12,8,16,128]{3,2,1,0:T(8,128)(2,1)} %broadcast_in_dim.5), calls=%async_computation.5 | async-start | bytes 786432 | tf_op jit(solution)/shard_map/all_to_all | solution.py:454
  159.5 9.6 %collective-permute-start.11 = (bf16[96,512]{1,0:T(8,128)(2,1)S(1)}, bf16[96,512]{1,0:T(8,128)(2,1)S(1)}, u32[]{:S(2)}, u32[]{:S(2)}) collective-permute-start(bf16[96,512]{1,0:T(8,128)(2,1)S(1)} %get-tuple-element.43), channel_id=1, source_target_pairs={{0,2},{1,3},{2,4},{3,5},{4,6},{5,7},{6,0},{7,1},{8,10},{9,11},{10,... | collective-permute-start | bytes 294920 | tf_op jit(solution)/shard_map/ppermute | solution.py:330
  171.0 5.8 %collective-permute-start.13 = (bf16[96,512]{1,0:T(8,128)(2,1)S(1)}, bf16[96,512]{1,0:T(8,128)(2,1)S(1)}, u32[]{:S(2)}, u32[]{:S(2)}) collective-permute-start(bf16[96,512]{1,0:T(8,128)(2,1)S(1)} %get-tuple-element.45), channel_id=1, source_target_pairs={{0,6},{1,7},{2,0},{3,1},{4,2},{5,3},{6,4},{7,5},{8,14},{9,15},{10,... | collective-permute-start | bytes 294920 | tf_op jit(solution)/shard_map/ppermute | solution.py:330
  178.8 9.2 %collective-permute-done.12 = bf16[96,512]{1,0:T(8,128)(2,1)S(1)} collective-permute-done((bf16[96,512]{1,0:T(8,128)(2,1)S(1)}, bf16[96,512]{1,0:T(8,128)(2,1)S(1)}, u32[]{:S(2)}, u32[]{:S(2)}) %collective-permute-start.12) | collective-permute-done | bytes 98336 | tf_op jit(solution)/shard_map/ppermute | solution.py:330
  (58 shorter events, 29.6 us)
Async XLA Ops:
  0.6 6.8 %collective-permute-start.1 = (bf16[96,512]{1,0:T(8,128)(2,1)}, bf16[96,512]{1,0:T(8,128)(2,1)S(1)}, u32[]{:S(2)}, u32[]{:S(2)}) collective-permute-start(bf16[96,512]{1,0:T(8,128)(2,1)} %bitcast.15), channel_id=1, source_target_pairs={{0,8},{8,16},{16,0},{24,32},{32,40},{40,24},{48,56},{56,64},{64,48... | collective-permute-start | bytes 294920 | tf_op jit(solution)/shard_map/ppermute | solution.py:292
  4.9 6.7 %collective-permute-start = (bf16[96,512]{1,0:T(8,128)(2,1)}, bf16[96,512]{1,0:T(8,128)(2,1)S(1)}, u32[]{:S(2)}, u32[]{:S(2)}) collective-permute-start(bf16[96,512]{1,0:T(8,128)(2,1)} %bitcast.16), channel_id=1, source_target_pairs={{0,16},{8,0},{16,8},{24,40},{32,24},{40,32},{48,64},{56,48},{64,56... | collective-permute-start | bytes 294920 | tf_op jit(solution)/shard_map/ppermute | solution.py:292
  15.4 28.9 %copy-start.1 = (bf16[3,96,512]{2,1,0:T(8,128)(2,1)}, bf16[3,96,512]{2,1,0:T(8,128)(2,1)S(1)}, u32[]{:S(2)}) copy-start(bf16[3,96,512]{2,1,0:T(8,128)(2,1)S(1)} %get-tuple-element.29.level_ref) | copy-start | bytes 884740
  15.4 42.4 %all-to-all-start = ((bf16[4,192,512]{2,1,0:T(8,128)(2,1)}), bf16[4,192,512]{2,1,0:T(8,128)(2,1)S(1)}, u32[]{:S(2)}, u32[]{:S(2)}) async-start(bf16[4,192,512]{2,1,0:T(8,128)(2,1)} %get-tuple-element.28), calls=%async_computation | async-start | bytes 1572864 | tf_op jit(solution)/shard_map/all_to_all | solution.py:326
  29.3 8.9 %collective-permute-start.4 = (bf16[3,96,512]{2,1,0:T(8,128)(2,1)S(1)}, bf16[3,96,512]{2,1,0:T(8,128)(2,1)S(1)}, u32[]{:S(2)}, u32[]{:S(2)}) collective-permute-start(bf16[3,96,512]{2,1,0:T(8,128)(2,1)S(1)} %get-tuple-element.29.level_ref), channel_id=1, source_target_pairs={{0,744},{8,752},{16,760},{24,0},{32,8},{40,16},{48,24},{56,32},{64... | collective-permute-start | bytes 884744 | tf_op jit(solution)/shard_map/ppermute | solution.py:284
  31.7 12.6 %collective-permute-start.3 = (bf16[3,96,512]{2,1,0:T(8,128)(2,1)S(1)}, bf16[3,96,512]{2,1,0:T(8,128)(2,1)S(1)}, u32[]{:S(2)}, u32[]{:S(2)}) collective-permute-start(bf16[3,96,512]{2,1,0:T(8,128)(2,1)S(1)} %get-tuple-element.29.level_ref), channel_id=1, source_target_pairs={{0,24},{8,32},{16,40},{24,48},{32,56},{40,64},{48,72},{56,80},{64,... | collective-permute-start | bytes 884744 | tf_op jit(solution)/shard_map/ppermute | solution.py:284
  57.8 23.9 %all-to-all-start.1 = ((bf16[4,96,512]{2,1,0:T(8,128)(2,1)}), bf16[4,96,512]{2,1,0:T(8,128)(2,1)S(1)}, u32[]{:S(2)}, u32[]{:S(2)}) async-start(bf16[4,96,512]{2,1,0:T(8,128)(2,1)} %shard_map.138), calls=%async_computation.1 | async-start | bytes 786432 | tf_op jit(solution)/shard_map/all_to_all | solution.py:326
  64.2 21.1 %collective-permute-start.2 = (bf16[4,192,512]{2,1,0:T(8,128)(2,1)S(1)}, bf16[4,192,512]{2,1,0:T(8,128)(2,1)S(1)}, u32[]{:S(2)}, u32[]{:S(2)}) collective-permute-start(bf16[4,192,512]{2,1,0:T(8,128)(2,1)S(1)} %all-to-all-done.refs_0_), channel_id=1, source_target_pairs={{0,1},{1,0},{2,3},{3,2},{4,5},{5,4},{6,7},{7,6},{8,9},{9,8},{10,11... | collective-permute-start | bytes 2359304 | tf_op jit(solution)/shard_map/ppermute | solution.py:353
  81.6 3.6 %collective-permute-start.5 = (bf16[4,96,512]{2,1,0:T(8,128)(2,1)S(1)}, bf16[4,96,512]{2,1,0:T(8,128)(2,1)S(1)}, u32[]{:S(2)}, u32[]{:S(2)}) collective-permute-start(bf16[4,96,512]{2,1,0:T(8,128)(2,1)S(1)} %all-to-all-done.1.refs_2_), channel_id=1, source_target_pairs={{0,1},{1,0},{2,3},{3,2},{4,5},{5,4},{6,7},{7,6},{8,9},{9,8},{10,11... | collective-permute-start | bytes 1179656 | tf_op jit(solution)/shard_map/ppermute | solution.py:373
  95.4 59.8 %copy-start.2 = (bf16[768,128]{1,0:T(8,128)(2,1)S(1)}, bf16[768,128]{1,0:T(8,128)(2,1)}, u32[]{:S(2)}) copy-start(bf16[768,128]{1,0:T(8,128)(2,1)} %get-tuple-element.38.self_ref) | copy-start | bytes 589828
  95.4 59.8 %copy-start.3 = (bf16[768,128]{1,0:T(8,128)(2,1)S(1)}, bf16[768,128]{1,0:T(8,128)(2,1)}, u32[]{:S(2)}) copy-start(bf16[768,128]{1,0:T(8,128)(2,1)} %get-tuple-element.39.neighbour_ref) | copy-start | bytes 589828
  95.4 59.8 %copy-start.6 = (bf16[128,512]{1,0:T(8,128)(2,1)S(1)}, bf16[128,512]{1,0:T(8,128)(2,1)}, u32[]{:S(2)}) copy-start(bf16[128,512]{1,0:T(8,128)(2,1)} %get-tuple-element.37.grad_ref) | copy-start | bytes 393220
  95.4 16.5 %all-to-all-start.2 = ((bf16[12,9,16,128]{3,2,1,0:T(8,128)(2,1)}), bf16[12,9,16,128]{3,2,1,0:T(8,128)(2,1)S(1)}, u32[]{:S(2)}, u32[]{:S(2)}) async-start(bf16[12,9,16,128]{3,2,1,0:T(8,128)(2,1)} %get-tuple-element.46), calls=%async_computation.2 | async-start | bytes 884736 | tf_op jit(solution)/shard_map/all_to_all | solution.py:430
  101.1 40.6 %collective-permute-start.6 = (bf16[3,128,512]{2,1,0:T(8,128)(2,1)}, bf16[3,128,512]{2,1,0:T(8,128)(2,1)S(1)}, u32[]{:S(2)}, u32[]{:S(2)}) collective-permute-start(bf16[3,128,512]{2,1,0:T(8,128)(2,1)} %get-tuple-element.32), channel_id=1, source_target_pairs={{0,24},{8,32},{16,40},{24,48},{32,56},{40,64},{48,72},{56,80},{64,... | collective-permute-start | bytes 1179656 | tf_op jit(solution)/shard_map/ppermute | solution.py:284
  104.8 37.0 %collective-permute-start.7 = (bf16[3,128,512]{2,1,0:T(8,128)(2,1)}, bf16[3,128,512]{2,1,0:T(8,128)(2,1)S(1)}, u32[]{:S(2)}, u32[]{:S(2)}) collective-permute-start(bf16[3,128,512]{2,1,0:T(8,128)(2,1)} %get-tuple-element.33), channel_id=1, source_target_pairs={{0,744},{8,752},{16,760},{24,0},{32,8},{40,16},{48,24},{56,32},{64... | collective-permute-start | bytes 1179656 | tf_op jit(solution)/shard_map/ppermute | solution.py:284
  126.1 3.1 %collective-permute-start.14 = (bf16[16,128]{1,0:T(8,128)(2,1)S(1)}, bf16[16,128]{1,0:T(8,128)(2,1)S(1)}, u32[]{:S(2)}, u32[]{:S(2)}) collective-permute-start(bf16[16,128]{1,0:T(8,128)(2,1)S(1)} %get-tuple-element.47), channel_id=1, source_target_pairs={{0,0},{1,1},{2,2},{3,3},{4,4},{5,5},{6,6},{7,7},{8,8},{9,9},{10,10... | collective-permute-start | bytes 12296 | tf_op jit(solution)/shard_map/ppermute | solution.py:446
  129.8 19.1 %all-to-all-start.4 = ((bf16[8,16,128]{2,1,0:T(8,128)(2,1)}), bf16[8,16,128]{2,1,0:T(8,128)(2,1)S(1)}, u32[]{:S(2)}, u32[]{:S(2)}) async-start(bf16[8,16,128]{2,1,0:T(8,128)(2,1)} %broadcast_in_dim.4), calls=%async_computation.4 | async-start | bytes 65536 | tf_op jit(solution)/shard_map/all_to_all | solution.py:447
  143.1 12.1 %collective-permute-start.8 = (bf16[128,512]{1,0:T(8,128)(2,1)S(1)}, bf16[128,512]{1,0:T(8,128)(2,1)S(1)}, u32[]{:S(2)}, u32[]{:S(2)}) collective-permute-start(bf16[128,512]{1,0:T(8,128)(2,1)S(1)} %get-tuple-element.35), channel_id=1, source_target_pairs={{0,8},{8,16},{16,0},{24,32},{32,40},{40,24},{48,56},{56,64},{64,48... | collective-permute-start | bytes 393224 | tf_op jit(solution)/shard_map/ppermute | solution.py:292
  145.3 9.9 %collective-permute-start.9 = (bf16[128,512]{1,0:T(8,128)(2,1)S(1)}, bf16[128,512]{1,0:T(8,128)(2,1)S(1)}, u32[]{:S(2)}, u32[]{:S(2)}) collective-permute-start(bf16[128,512]{1,0:T(8,128)(2,1)S(1)} %get-tuple-element.36), channel_id=1, source_target_pairs={{0,16},{8,0},{16,8},{24,40},{32,24},{40,32},{48,64},{56,48},{64,56... | collective-permute-start | bytes 393224 | tf_op jit(solution)/shard_map/ppermute | solution.py:292
  149.8 39.4 %all-to-all-start.5 = ((bf16[12,8,16,128]{3,2,1,0:T(8,128)(2,1)}), bf16[12,8,16,128]{3,2,1,0:T(8,128)(2,1)S(1)}, u32[]{:S(2)}, u32[]{:S(2)}) async-start(bf16[12,8,16,128]{3,2,1,0:T(8,128)(2,1)} %broadcast_in_dim.5), calls=%async_computation.5 | async-start | bytes 786432 | tf_op jit(solution)/shard_map/all_to_all | solution.py:454
  155.8 3.6 %collective-permute-start.10 = (bf16[384,512]{1,0:T(8,128)(2,1)S(1)}, bf16[384,512]{1,0:T(8,128)(2,1)S(1)}, u32[]{:S(2)}, u32[]{:S(2)}) collective-permute-start(bf16[384,512]{1,0:T(8,128)(2,1)S(1)} %get-tuple-element.41), channel_id=1, source_target_pairs={{0,1},{1,0},{2,3},{3,2},{4,5},{5,4},{6,7},{7,6},{8,9},{9,8},{10,11... | collective-permute-start | bytes 1179656 | tf_op jit(solution)/shard_map/ppermute | solution.py:488
  159.5 19.3 %collective-permute-start.11 = (bf16[96,512]{1,0:T(8,128)(2,1)S(1)}, bf16[96,512]{1,0:T(8,128)(2,1)S(1)}, u32[]{:S(2)}, u32[]{:S(2)}) collective-permute-start(bf16[96,512]{1,0:T(8,128)(2,1)S(1)} %get-tuple-element.43), channel_id=1, source_target_pairs={{0,2},{1,3},{2,4},{3,5},{4,6},{5,7},{6,0},{7,1},{8,10},{9,11},{10,... | collective-permute-start | bytes 294920 | tf_op jit(solution)/shard_map/ppermute | solution.py:330
  169.0 18.9 %collective-permute-start.12 = (bf16[96,512]{1,0:T(8,128)(2,1)S(1)}, bf16[96,512]{1,0:T(8,128)(2,1)S(1)}, u32[]{:S(2)}, u32[]{:S(2)}) collective-permute-start(bf16[96,512]{1,0:T(8,128)(2,1)S(1)} %get-tuple-element.44), channel_id=1, source_target_pairs={{0,4},{1,5},{2,6},{3,7},{4,0},{5,1},{6,2},{7,3},{8,12},{9,13},{10,... | collective-permute-start | bytes 294920 | tf_op jit(solution)/shard_map/ppermute | solution.py:330
  171.0 17.0 %collective-permute-start.13 = (bf16[96,512]{1,0:T(8,128)(2,1)S(1)}, bf16[96,512]{1,0:T(8,128)(2,1)S(1)}, u32[]{:S(2)}, u32[]{:S(2)}) collective-permute-start(bf16[96,512]{1,0:T(8,128)(2,1)S(1)} %get-tuple-element.45), channel_id=1, source_target_pairs={{0,6},{1,7},{2,0},{3,1},{4,2},{5,3},{6,4},{7,5},{8,14},{9,15},{10,... | collective-permute-start | bytes 294920 | tf_op jit(solution)/shard_map/ppermute | solution.py:330
  (10 other events, 43.5 us)

commit v6 on v5

--- a/solution.py
+++ b/solution.py
@@ -50,14 +50,22 @@
     lax.fori_loop(0, (count + GROUP - 1) // GROUP, step, 0)
 
 
-def band_slot(place_ref, offset):
-    return (place_ref[0] + offset) // TRIO * TRIO + offset % TRIO
-
-
-def pack_kernel(features_ref, first_ref, second_ref, self_ref, neighbour_ref, level_ref, out_ref):
+def relay_kernel(place_ref, below_ref, level_ref, above_ref, *outs):
+    for steps, out in enumerate(outs, 1):
+
+        @pl.when(place_ref[0] < steps)
+        def _(out=out):
+            out[0] = level_ref[...]
+            out[1] = above_ref[...]
+
+        @pl.when(place_ref[0] >= steps)
+        def _(out=out):
+            out[0] = below_ref[...]
+            out[1] = level_ref[...]
+
+
+def pack_kernel(features_ref, self_ref, neighbour_ref, first_ref, second_ref, out_ref):
     width = features_ref.shape[0]
-    for slot, ref in enumerate((features_ref, first_ref, second_ref)):
-        level_ref[slot] = ref[...]
     for stack in range(out_ref.shape[0]):
         out_ref[stack, pl.ds(0, width), :] = features_ref[...]
         for core in range(CORES):
@@ -80,7 +88,6 @@
 
 
 def gather_kernel(
-    place_ref,
     count_ref,
     dest_ref,
     source_ref,
@@ -89,22 +96,23 @@
     below_ref,
     level_ref,
     above_ref,
+    first_ref,
+    second_ref,
     out_ref,
     total_ref,
-    band_ref,
     tiles_ref,
     copied,
 ):
     copies = tile_copies(tiles_hbm, tiles_ref, copied)
     blocks = total_ref.shape[0] - 1
     total_ref[...] = jnp.zeros_like(total_ref)
-    for trio, ref in enumerate((below_ref, level_ref, above_ref)):
-        band_ref[pl.ds(trio * TRIO, TRIO)] = ref[...]
+    straight = (below_ref, level_ref, above_ref)
     for offset in range(OFFS):
-        slot = band_slot(place_ref, offset)
-
-        def product(tile, slot=slot):
-            picked = band_ref[slot, :, lanes(source_ref[tile] % blocks)]
+        turns, part = offset % TRIO, offset // TRIO
+        operand = straight[part] if turns == 0 else (first_ref, second_ref)[turns - 1].at[part]
+
+        def product(tile, operand=operand):
+            picked = operand[:, lanes(source_ref[tile] % blocks)]
             return lax.dot_general(
                 picked, tiles_ref[tile], (((1,), (1,)), ((), ())), preferred_element_type=F32
             )
@@ -119,19 +127,19 @@
 
 
 def middle_kernel(
-    place_ref, core_ref, stack_ref, count_ref, dest_ref, source_ref, tiles_hbm, degree_ref, *refs
+    core_ref, stack_ref, count_ref, dest_ref, source_ref, tiles_hbm, degree_ref, *refs
 ):
     packed, aggregates, refs = refs[:2], refs[2:4], refs[4:]
     bias_ref, cotangent_ref, refs = *refs[:2], refs[2:]
     act_ref, grad_ref, weight_ref, self_ref, neighbour_ref, refs = *refs[:5], refs[5:]
-    level_ref, below_ref, above_ref, *refs = refs
+    level_ref, first_ref, second_ref, *refs = refs
     features_ref, scaled_ref, total_ref, tiles_ref, copied, *refs = refs
-    turned_ref, to_below_ref, to_above_ref, stored = refs
+    turned_ref, to_first_ref, to_second_ref, stored = refs
     copies = tile_copies(tiles_hbm, tiles_ref, copied)
     stores = [
         pltpu.make_async_copy(source, target, stored.at[at])
         for at, (source, target) in enumerate(
-            ((turned_ref, grad_ref), (to_below_ref, below_ref), (to_above_ref, above_ref))
+            ((turned_ref, grad_ref), (to_first_ref, first_ref), (to_second_ref, second_ref))
         )
     ]
     blocks = scaled_ref.shape[0]
@@ -182,27 +190,27 @@
                     weight_ref[plane, column, pl.ds(row, PIECE), :] = term[begin : begin + PIECE]
     total_ref[...] = jnp.zeros_like(total_ref)
     for offset in range(OFFS):
-        slot = band_slot(place_ref, offset)
+
 
         def product(tile):
             return jnp.dot(
                 scaled_ref[dest_ref[tile]], tiles_ref[tile], preferred_element_type=F32
             )
 
-        def place(tile, slot=slot):
-            return slot * blocks + source_ref[tile] % blocks
+        def place(tile, offset=offset):
+            return offset * blocks + source_ref[tile] % blocks
 
         copies[offset].wait()
         live_tiles(offset, count_ref, product, place, total_ref)
-    for trio, out, store in (
-        (0, to_below_ref, stores[1]),
-        (2, to_above_ref, stores[2]),
-        (1, level_ref, None),
+    for turns, out, store in (
+        (1, to_first_ref, stores[1]),
+        (2, to_second_ref, stores[2]),
+        (0, level_ref, None),
     ):
-        for slot in range(TRIO):
+        for part, offset in enumerate(range(turns, OFFS, TRIO)):
             for block in range(blocks):
-                out[slot, :, pl.ds(block * BLOCK, BLOCK)] = total_ref[
-                    (trio * TRIO + slot) * blocks + block
+                out[part, :, pl.ds(block * BLOCK, BLOCK)] = total_ref[
+                    offset * blocks + block
                 ].astype(out.dtype)
         if store is not None:
             store.start()
@@ -210,14 +218,20 @@
         store.wait()
 
 
-def trio_kernel(level_ref, below_ref, above_ref, *outs):
-    for slot, out in enumerate(outs):
-        value = level_ref[slot] + below_ref[slot].astype(F32) + above_ref[slot].astype(F32)
+def trio_kernel(place_ref, level_ref, first_ref, second_ref, keep_ref, below_ref, above_ref):
+    sums = [level_ref[part] for part in range(TRIO)]
+    for steps, ref in enumerate((first_ref, second_ref), 1):
+        past = (place_ref[0] < steps).astype(F32)
+        lower, upper = ref[0].astype(F32), ref[1].astype(F32)
+        sums[0] += lower * (1.0 - past)
+        sums[1] += lower * past + upper * (1.0 - past)
+        sums[2] += upper * past
+    for value, out in zip(sums, (below_ref, keep_ref, above_ref)):
         out[...] = value.astype(out.dtype)
 
 
-def back_kernel(own_ref, first_ref, second_ref, grad_ref, self_ref, neighbour_ref, keep_ref, send_ref):
-    spread = own_ref[...] + first_ref[...].astype(F32) + second_ref[...].astype(F32)
+def back_kernel(own_ref, below_ref, above_ref, grad_ref, self_ref, neighbour_ref, keep_ref, send_ref):
+    spread = own_ref[...] + below_ref[...].astype(F32) + above_ref[...].astype(F32)
     spread = spread.astype(BF16)
     half = keep_ref.shape[0]
     for at, out in enumerate((keep_ref, send_ref)):
@@ -330,25 +344,22 @@
         return lax.ppermute(value, "feat", pairs)
 
     turned = features.T
-    level, packed = call(
+    below = shifted(turned, TRIO)
+    above = shifted(turned, -TRIO)
+    pair = jax.ShapeDtypeStruct((2, width, node_dev), BF16)
+    first, second = call(
+        relay_kernel, [SMEM] + [VMEM] * 3, [pair, pair], [], 0, 8 * turned.size
+    )(place, below, turned, above)
+    first = turned_in_trio(first, -1)
+    second = turned_in_trio(second, -2)
+    packed = call(
         pack_kernel,
-        [WHOLE] * 5,
-        [
-            jax.ShapeDtypeStruct((TRIO, width, node_dev), BF16),
-            jax.ShapeDtypeStruct((stacks, 2 * width, node_dev), BF16),
-        ],
+        [WHOLE] * 3 + [ANY] * 2,
+        jax.ShapeDtypeStruct((stacks, 2 * width, node_dev), BF16),
         [],
         0,
         6 * stacks * width * node_dev,
-    )(
-        turned,
-        turned_in_trio(turned, -1),
-        turned_in_trio(turned, -2),
-        self_weight,
-        neighbour_weight,
-    )
-    below = shifted(level, TRIO)
-    above = shifted(level, -TRIO)
+    )(turned, self_weight, neighbour_weight, first, second)
     packed_own = over_stacks(packed)
     packed_far = lax.ppermute(packed_own, "feat", other_core)
 
@@ -357,49 +368,47 @@
     tile_flops = 2 * OFFS * SLOTS * BLOCK * BLOCK * BLOCK
     aggregate = call(
         gather_kernel,
-        [SMEM] * 4 + [HBM] + [VMEM] * 4,
+        [SMEM] * 3 + [HBM] + [VMEM] * 6,
         jax.ShapeDtypeStruct((stacks, width, node_dev), BF16),
         [
             pltpu.VMEM((blocks + 1, width, BLOCK), F32),
-            pltpu.VMEM((TRIO * TRIO, width, node_dev), BF16),
             pltpu.VMEM(tile_values.shape, BF16),
             pltpu.SemaphoreType.DMA((OFFS,)),
         ],
         tile_flops,
         tile_values.size * 2,
         limit=TILES_VMEM_BYTES,
-    )(place, *scalars, tile_values, degrees, below, level, above)
+    )(*scalars, tile_values, degrees, below, turned, above, first, second)
     aggregate_own = over_stacks(aggregate)
     aggregate_far = lax.ppermute(aggregate_own, "feat", other_core)
 
     planes = groups // COLUMN
     rows_each = 4 * half // groups
 
-    def trio(dtype):
-        return jax.ShapeDtypeStruct((TRIO, hidden_dev, node_dev), dtype)
+    pair = jax.ShapeDtypeStruct((2, hidden_dev, node_dev), BF16)
 
     middle = call(
         middle_kernel,
-        [SMEM] * 6 + [HBM] + [VMEM] * 5 + [WHOLE] * 2,
+        [SMEM] * 5 + [HBM] + [VMEM] * 5 + [WHOLE] * 2,
         [
             jax.ShapeDtypeStruct((node_dev, hidden_dev), BF16),
             jax.ShapeDtypeStruct((hidden_dev, node_dev), BF16),
             jax.ShapeDtypeStruct((planes, COLUMN + 1, rows_each, hidden_dev), BF16),
             jax.ShapeDtypeStruct((2 * half, hidden_dev), BF16),
             jax.ShapeDtypeStruct((2 * half, hidden_dev), BF16),
-            trio(F32),
-            trio(BF16),
-            trio(BF16),
+            jax.ShapeDtypeStruct((TRIO, hidden_dev, node_dev), F32),
+            pair,
+            pair,
         ],
         [
             pltpu.VMEM((2 * half, node_dev), BF16),
             pltpu.VMEM((blocks, hidden_dev, BLOCK), BF16),
-            pltpu.VMEM((TRIO * TRIO * blocks + 1, hidden_dev, BLOCK), F32),
+            pltpu.VMEM((OFFS * blocks + 1, hidden_dev, BLOCK), F32),
             pltpu.VMEM(tile_values.shape, BF16),
             pltpu.SemaphoreType.DMA((OFFS,)),
             pltpu.VMEM((hidden_dev, node_dev), BF16),
-            pltpu.VMEM((TRIO, hidden_dev, node_dev), BF16),
-            pltpu.VMEM((TRIO, hidden_dev, node_dev), BF16),
+            pltpu.VMEM(pair.shape, BF16),
+            pltpu.VMEM(pair.shape, BF16),
             pltpu.SemaphoreType.DMA((3,)),
         ],
         tile_flops * 2,
@@ -407,7 +416,6 @@
         [WHOLE, HBM, VMEM, VMEM, VMEM, VMEM, HBM, HBM],
         TILES_VMEM_BYTES,
     )(
-        place,
         core,
         stack,
         *scalars,
@@ -421,9 +429,9 @@
         cotangent,
     )
     activations, grad_turned, weight_part, weight_self, weight_neighbour = middle[:5]
-    to_level, to_below, to_above = middle[5:]
-    from_above = shifted(to_below, -TRIO)
-    from_below = shifted(to_above, TRIO)
+    to_level, first, second = middle[5:]
+    first = turned_in_trio(first, 1)
+    second = turned_in_trio(second, 2)
 
     got = jax.ShapeDtypeStruct((COLUMN, 2, rows_each, hidden_dev), BF16)
     got = call(planes_kernel, [VMEM], got, [], weight_part.size, weight_part.size * 2)(
@@ -464,16 +472,16 @@
     )(lax.axis_index("feat").reshape(1), pieces)
 
     spread = jax.ShapeDtypeStruct((hidden_dev, node_dev), BF16)
-    own, first, second = call(
+    own, to_below, to_above = call(
         trio_kernel,
-        [VMEM] * 3,
+        [SMEM] + [VMEM] * 3,
         [jax.ShapeDtypeStruct(spread.shape, F32), spread, spread],
         [],
         9 * spread.size,
         20 * spread.size,
-    )(to_level, from_below, from_above)
-    first = turned_in_trio(first, 1)
-    second = turned_in_trio(second, 2)
+    )(place, to_level, first, second)
+    from_above = shifted(to_below, -TRIO)
+    from_below = shifted(to_above, TRIO)
     keep, send = call(
         back_kernel,
         [VMEM] * 6,
@@ -484,7 +492,7 @@
         [],
         8 * half * node_dev * hidden_dev,
         4 * half * node_dev,
-    )(own, first, second, grad_turned, weight_self, weight_neighbour)
+    )(own, from_below, from_above, grad_turned, weight_self, weight_neighbour)
     got = lax.ppermute(send, "feat", other_core)
     part = jax.ShapeDtypeStruct((width, node_dev), BF16)
     parts = call(

time: 191 us -> 209 us (1.094)
  the two profiles are of different devices: /device:TPU:72 before, /device:TPU:2 now
where the time goes in v6:
time: 209 us; the launch traced here: 208 us
  starting transfers between devices  94.2 us (45%)
  waiting for transfers between devices  74.8 us (36%)
  Pallas kernels  18.3 us (9%)
  blocking collectives  10.8 us (5%)
  local copies, waits for them, and re-layouts  7.78 us (4%)
    all_to_all x2, waiting for transfers between devices, over_stacks(): return lax.all_to_all(value, 'feat', 0, 0, axis_index_groups=same_core)  39.3 us
    all_to_all x2, starting transfers between devices, over_stacks(): return lax.all_to_all(value, 'feat', 0, 0, axis_index_groups=same_core)  18 us
    ppermute x4, starting transfers between devices, shifted(): return lax.ppermute(value, 'rows', pairs)  15.2 us
    ppermute x4, starting transfers between devices, turned_in_trio(): return lax.ppermute(value, 'rows', pairs)  14.7 us
    ppermute x3, waiting for transfers between devices, to_stack(): return lax.ppermute(value, 'feat', pairs)  14.2 us
    ppermute x3, starting transfers between devices, to_stack(): return lax.ppermute(value, 'feat', pairs)  13.4 us
    all_to_all x1, starting transfers between devices, on_device(): lax.all_to_all(jnp.broadcast_to(piece[None], (COLUMN,) + piece.shape), 'r...  12.9 us
    all_to_all x1, blocking collectives, on_device(): lax.all_to_all(got, 'rows', 0, 0, axis_index_groups=same_plane)  10.8 us
  transfers between devices with their start and end apart: 20, of which 11 were waited for; matrix products, arithmetic and copies ran while one was open for 1% of the time, Pallas kernels for 4%

profile of v6, /device:TPU:2, one launch (start us, length us, event | category | flops | bytes accessed | tf_op | source)
XLA Modules:
  0.0 207.5 jit_solution(1122993490556981838)
XLA Ops:
  0.6 5.4 %collective-permute-start.1 = (bf16[96,512]{1,0:T(8,128)(2,1)}, bf16[96,512]{1,0:T(8,128)(2,1)S(1)}, u32[]{:S(2)}, u32[]{:S(2)}) collective-permute-start(bf16[96,512]{1,0:T(8,128)(2,1)} %bitcast.13), channel_id=1, source_target_pairs={{0,744},{8,752},{16,760},{24,0},{32,8},{40,16},{48,24},{56,32},{64... | collective-permute-start | bytes 294920 | tf_op jit(solution)/shard_map/ppermute | solution.py:298
  8.5 6.3 %collective-permute-done.below_ref = bf16[96,512]{1,0:T(8,128)(2,1)S(1)} collective-permute-done((bf16[96,512]{1,0:T(8,128)(2,1)}, bf16[96,512]{1,0:T(8,128)(2,1)S(1)}, u32[]{:S(2)}, u32[]{:S(2)}) %collective-permute-start) | collective-permute-done | bytes 98336 | tf_op jit(solution)/shard_map/ppermute | solution.py:298
  15.8 6.1 %collective-permute-start.2 = (bf16[2,96,512]{2,1,0:T(8,128)(2,1)S(1)}, bf16[2,96,512]{2,1,0:T(8,128)(2,1)S(1)}, u32[]{:S(2)}, u32[]{:S(2)}) collective-permute-start(bf16[2,96,512]{2,1,0:T(8,128)(2,1)S(1)} %get-tuple-element.28), channel_id=1, source_target_pairs={{0,16},{8,0},{16,8},{24,40},{32,24},{40,32},{48,64},{56,48},{64,56... | collective-permute-start | bytes 589832 | tf_op jit(solution)/shard_map/ppermute | solution.py:306
  23.8 2.9 %collective-permute-done.2.first_ref = bf16[2,96,512]{2,1,0:T(8,128)(2,1)S(1)} collective-permute-done((bf16[2,96,512]{2,1,0:T(8,128)(2,1)S(1)}, bf16[2,96,512]{2,1,0:T(8,128)(2,1)S(1)}, u32[]{:S(2)}, u32[]{:S(2)}) %collective-permute-start.2) | collective-permute-done | bytes 196640 | tf_op jit(solution)/shard_map/ppermute | solution.py:306
  26.7 3.6 %collective-permute-done.3.second_ref = bf16[2,96,512]{2,1,0:T(8,128)(2,1)S(1)} collective-permute-done((bf16[2,96,512]{2,1,0:T(8,128)(2,1)S(1)}, bf16[2,96,512]{2,1,0:T(8,128)(2,1)S(1)}, u32[]{:S(2)}, u32[]{:S(2)}) %collective-permute-start.3) | collective-permute-done | bytes 196640 | tf_op jit(solution)/shard_map/ppermute | solution.py:306
  34.1 14.5 %all-to-all-start = ((bf16[4,192,512]{2,1,0:T(8,128)(2,1)}), bf16[4,192,512]{2,1,0:T(8,128)(2,1)S(1)}, u32[]{:S(2)}, u32[]{:S(2)}) async-start(bf16[4,192,512]{2,1,0:T(8,128)(2,1)} %shard_map.138), calls=%async_computation | async-start | bytes 1572864 | tf_op jit(solution)/shard_map/all_to_all | solution.py:340
  48.6 6.9 %shard_map.139 = bf16[4,96,512]{2,1,0:T(8,128)(2,1)} custom-call(s32[7]{0:T(128)} %count_ref.3, s32[112]{0:T(128)} %dest_ref.3, s32[112]{0:T(128)} %source_ref.3, bf16[112,128,128]{2,1,0:T(8,128)(2,1)} %tiles_hbm.3, s32[1,512]{1,0:T(1,128)} %bitcast.20, bf16[96,512]{1,0:T(8,128)(2,1)} %copy-done.6, bf16[96,512]{1,0:T(8,128)(2,1)} %bitcast.15, ...), custom_call_target="tpu_custom_call" | custom-call | flops 469762048 | bytes 3670016 | tf_op jit(solution)/shard_map/pallas_call | solution.py:369
  55.6 23.6 %all-to-all-done.refs_0_ = bf16[4,192,512]{2,1,0:T(8,128)(2,1)S(1)} async-done(((bf16[4,192,512]{2,1,0:T(8,128)(2,1)}), bf16[4,192,512]{2,1,0:T(8,128)(2,1)S(1)}, u32[]{:S(2)}, u32[]{:S(2)}) %all-to-all-start) | async-done | bytes 786464 | tf_op jit(solution)/shard_map/all_to_all | solution.py:340
  79.2 3.5 %all-to-all-start.1 = ((bf16[4,96,512]{2,1,0:T(8,128)(2,1)}), bf16[4,96,512]{2,1,0:T(8,128)(2,1)S(1)}, u32[]{:S(2)}, u32[]{:S(2)}) async-start(bf16[4,96,512]{2,1,0:T(8,128)(2,1)} %shard_map.139), calls=%async_computation.1 | async-start | bytes 786432 | tf_op jit(solution)/shard_map/all_to_all | solution.py:340
  84.6 15.7 %all-to-all-done.1.refs_2_ = bf16[4,96,512]{2,1,0:T(8,128)(2,1)S(1)} async-done(((bf16[4,96,512]{2,1,0:T(8,128)(2,1)}), bf16[4,96,512]{2,1,0:T(8,128)(2,1)S(1)}, u32[]{:S(2)}, u32[]{:S(2)}) %all-to-all-start.1) | async-done | bytes 393248 | tf_op jit(solution)/shard_map/all_to_all | solution.py:340
  104.9 8.4 %shard_map.140 = (bf16[512,128]{1,0:T(8,128)(2,1)}, bf16[128,512]{1,0:T(8,128)(2,1)}, bf16[12,9,16,128]{3,2,1,0:T(8,128)(2,1)}, bf16[768,128]{1,0:T(8,128)(2,1)}...) custom-call(s32[1]{0:T(128)} %bitcast.core_ref, ...), custom_call_target="tpu_custom_call" | custom-call | flops 939524096 | bytes 3670016 | tf_op jit(solution)/shard_map/pallas_call | solution.py:390
  113.4 7.5 %all-to-all-start.2 = ((bf16[12,9,16,128]{3,2,1,0:T(8,128)(2,1)}), bf16[12,9,16,128]{3,2,1,0:T(8,128)(2,1)S(1)}, u32[]{:S(2)}, u32[]{:S(2)}) async-start(bf16[12,9,16,128]{3,2,1,0:T(8,128)(2,1)} %get-tuple-element.46), calls=%async_computation.2 | async-start | bytes 884736 | tf_op jit(solution)/shard_map/all_to_all | solution.py:438
  120.9 3.4 %collective-permute-start.6 = (bf16[2,128,512]{2,1,0:T(8,128)(2,1)}, bf16[2,128,512]{2,1,0:T(8,128)(2,1)S(1)}, u32[]{:S(2)}, u32[]{:S(2)}) collective-permute-start(bf16[2,128,512]{2,1,0:T(8,128)(2,1)} %get-tuple-element.32), channel_id=1, source_target_pairs={{0,8},{8,16},{16,0},{24,32},{32,40},{40,24},{48,56},{56,64},{64,48... | collective-permute-start | bytes 786440 | tf_op jit(solution)/shard_map/ppermute | solution.py:306
  124.3 3.4 %collective-permute-start.7 = (bf16[2,128,512]{2,1,0:T(8,128)(2,1)}, bf16[2,128,512]{2,1,0:T(8,128)(2,1)S(1)}, u32[]{:S(2)}, u32[]{:S(2)}) collective-permute-start(bf16[2,128,512]{2,1,0:T(8,128)(2,1)} %get-tuple-element.33), channel_id=1, source_target_pairs={{0,16},{8,0},{16,8},{24,40},{32,24},{40,32},{48,64},{56,48},{64,56... | collective-permute-start | bytes 786440 | tf_op jit(solution)/shard_map/ppermute | solution.py:306
  127.7 4.5 %all-to-all-done.2.got_ref = bf16[12,9,16,128]{3,2,1,0:T(8,128)(2,1)S(1)} async-done(((bf16[12,9,16,128]{3,2,1,0:T(8,128)(2,1)}), bf16[12,9,16,128]{3,2,1,0:T(8,128)(2,1)S(1)}, u32[]{:S(2)}, u32[]{:S(2)}) %all-to-all-start.2) | async-done | bytes 442400 | tf_op jit(solution)/shard_map/all_to_all | solution.py:438
  132.2 10.8 %all_to_all.30.got_ref = bf16[8,2,16,128]{3,2,1,0:T(8,128)(2,1)S(1)} all-to-all(bf16[8,2,16,128]{3,2,1,0:T(8,128)(2,1)S(1)} %shard_map.144), channel_id=1, replica_groups={{0,24,48,72,96,120,144,168},{8,32,56,80,104,128,152,176},{16,40,64,88,1..., dimensions={0} | all-to-all | bytes 131072 | tf_op jit(solution)/shard_map/all_to_all | solution.py:448
  144.3 12.9 %all-to-all-start.4 = ((bf16[8,16,128]{2,1,0:T(8,128)(2,1)}), bf16[8,16,128]{2,1,0:T(8,128)(2,1)S(1)}, u32[]{:S(2)}, u32[]{:S(2)}) async-start(bf16[8,16,128]{2,1,0:T(8,128)(2,1)} %broadcast_in_dim.4), calls=%async_computation.4 | async-start | bytes 65536 | tf_op jit(solution)/shard_map/all_to_all | solution.py:455
  158.5 3.9 %collective-permute-start.8 = (bf16[128,512]{1,0:T(8,128)(2,1)S(1)}, bf16[128,512]{1,0:T(8,128)(2,1)S(1)}, u32[]{:S(2)}, u32[]{:S(2)}) collective-permute-start(bf16[128,512]{1,0:T(8,128)(2,1)S(1)} %get-tuple-element.35), channel_id=1, source_target_pairs={{0,24},{8,32},{16,40},{24,48},{32,56},{40,64},{48,72},{56,80},{64,... | collective-permute-start | bytes 393224 | tf_op jit(solution)/shard_map/ppermute | solution.py:298
  162.5 4.0 %collective-permute-start.9 = (bf16[128,512]{1,0:T(8,128)(2,1)S(1)}, bf16[128,512]{1,0:T(8,128)(2,1)S(1)}, u32[]{:S(2)}, u32[]{:S(2)}) collective-permute-start(bf16[128,512]{1,0:T(8,128)(2,1)S(1)} %get-tuple-element.36), channel_id=1, source_target_pairs={{0,744},{8,752},{16,760},{24,0},{32,8},{40,16},{48,24},{56,32},{64... | collective-permute-start | bytes 393224 | tf_op jit(solution)/shard_map/ppermute | solution.py:298
  167.3 6.1 %all-to-all-start.5 = ((bf16[12,8,16,128]{3,2,1,0:T(8,128)(2,1)}), bf16[12,8,16,128]{3,2,1,0:T(8,128)(2,1)S(1)}, u32[]{:S(2)}, u32[]{:S(2)}) async-start(bf16[12,8,16,128]{3,2,1,0:T(8,128)(2,1)} %broadcast_in_dim.5), calls=%async_computation.5 | async-start | bytes 786432 | tf_op jit(solution)/shard_map/all_to_all | solution.py:462
  177.7 3.1 %collective-permute-start.11 = (bf16[96,512]{1,0:T(8,128)(2,1)S(1)}, bf16[96,512]{1,0:T(8,128)(2,1)S(1)}, u32[]{:S(2)}, u32[]{:S(2)}) collective-permute-start(bf16[96,512]{1,0:T(8,128)(2,1)S(1)} %get-tuple-element.43), channel_id=1, source_target_pairs={{0,2},{1,3},{2,4},{3,5},{4,6},{5,7},{6,0},{7,1},{8,10},{9,11},{10,... | collective-permute-start | bytes 294920 | tf_op jit(solution)/shard_map/ppermute | solution.py:344
  180.8 8.4 %collective-permute-start.12 = (bf16[96,512]{1,0:T(8,128)(2,1)S(1)}, bf16[96,512]{1,0:T(8,128)(2,1)S(1)}, u32[]{:S(2)}, u32[]{:S(2)}) collective-permute-start(bf16[96,512]{1,0:T(8,128)(2,1)S(1)} %get-tuple-element.44), channel_id=1, source_target_pairs={{0,4},{1,5},{2,6},{3,7},{4,0},{5,1},{6,2},{7,3},{8,12},{9,13},{10,... | collective-permute-start | bytes 294920 | tf_op jit(solution)/shard_map/ppermute | solution.py:344
  191.2 4.1 %collective-permute-done.12 = bf16[96,512]{1,0:T(8,128)(2,1)S(1)} collective-permute-done((bf16[96,512]{1,0:T(8,128)(2,1)S(1)}, bf16[96,512]{1,0:T(8,128)(2,1)S(1)}, u32[]{:S(2)}, u32[]{:S(2)}) %collective-permute-start.12) | collective-permute-done | bytes 98336 | tf_op jit(solution)/shard_map/ppermute | solution.py:344
  195.3 10.1 %collective-permute-done.13 = bf16[96,512]{1,0:T(8,128)(2,1)S(1)} collective-permute-done((bf16[96,512]{1,0:T(8,128)(2,1)S(1)}, bf16[96,512]{1,0:T(8,128)(2,1)S(1)}, u32[]{:S(2)}, u32[]{:S(2)}) %collective-permute-start.13) | collective-permute-done | bytes 98336 | tf_op jit(solution)/shard_map/ppermute | solution.py:344
  (63 shorter events, 27.5 us)
Async XLA Ops:
  0.6 7.9 %collective-permute-start.1 = (bf16[96,512]{1,0:T(8,128)(2,1)}, bf16[96,512]{1,0:T(8,128)(2,1)S(1)}, u32[]{:S(2)}, u32[]{:S(2)}) collective-permute-start(bf16[96,512]{1,0:T(8,128)(2,1)} %bitcast.13), channel_id=1, source_target_pairs={{0,744},{8,752},{16,760},{24,0},{32,8},{40,16},{48,24},{56,32},{64... | collective-permute-start | bytes 294920 | tf_op jit(solution)/shard_map/ppermute | solution.py:298
  6.0 8.8 %collective-permute-start = (bf16[96,512]{1,0:T(8,128)(2,1)}, bf16[96,512]{1,0:T(8,128)(2,1)S(1)}, u32[]{:S(2)}, u32[]{:S(2)}) collective-permute-start(bf16[96,512]{1,0:T(8,128)(2,1)} %bitcast.14), channel_id=1, source_target_pairs={{0,24},{8,32},{16,40},{24,48},{32,56},{40,64},{48,72},{56,80},{64,... | collective-permute-start | bytes 294920 | tf_op jit(solution)/shard_map/ppermute | solution.py:298
  8.5 40.1 %copy-start.5 = (bf16[96,512]{1,0:T(8,128)(2,1)}, bf16[96,512]{1,0:T(8,128)(2,1)S(1)}, u32[]{:S(2)}) copy-start(bf16[96,512]{1,0:T(8,128)(2,1)S(1)} %collective-permute-done.1.above_ref) | copy-start | bytes 294916
  15.8 10.9 %collective-permute-start.2 = (bf16[2,96,512]{2,1,0:T(8,128)(2,1)S(1)}, bf16[2,96,512]{2,1,0:T(8,128)(2,1)S(1)}, u32[]{:S(2)}, u32[]{:S(2)}) collective-permute-start(bf16[2,96,512]{2,1,0:T(8,128)(2,1)S(1)} %get-tuple-element.28), channel_id=1, source_target_pairs={{0,16},{8,0},{16,8},{24,40},{32,24},{40,32},{48,64},{56,48},{64,56... | collective-permute-start | bytes 589832 | tf_op jit(solution)/shard_map/ppermute | solution.py:306
  21.9 8.5 %collective-permute-start.3 = (bf16[2,96,512]{2,1,0:T(8,128)(2,1)S(1)}, bf16[2,96,512]{2,1,0:T(8,128)(2,1)S(1)}, u32[]{:S(2)}, u32[]{:S(2)}) collective-permute-start(bf16[2,96,512]{2,1,0:T(8,128)(2,1)S(1)} %get-tuple-element.29), channel_id=1, source_target_pairs={{0,8},{8,16},{16,0},{24,32},{32,40},{40,24},{48,56},{56,64},{64,48... | collective-permute-start | bytes 589832 | tf_op jit(solution)/shard_map/ppermute | solution.py:306
  34.1 45.1 %all-to-all-start = ((bf16[4,192,512]{2,1,0:T(8,128)(2,1)}), bf16[4,192,512]{2,1,0:T(8,128)(2,1)S(1)}, u32[]{:S(2)}, u32[]{:S(2)}) async-start(bf16[4,192,512]{2,1,0:T(8,128)(2,1)} %shard_map.138), calls=%async_computation | async-start | bytes 1572864 | tf_op jit(solution)/shard_map/all_to_all | solution.py:340
  79.2 21.1 %all-to-all-start.1 = ((bf16[4,96,512]{2,1,0:T(8,128)(2,1)}), bf16[4,96,512]{2,1,0:T(8,128)(2,1)S(1)}, u32[]{:S(2)}, u32[]{:S(2)}) async-start(bf16[4,96,512]{2,1,0:T(8,128)(2,1)} %shard_map.139), calls=%async_computation.1 | async-start | bytes 786432 | tf_op jit(solution)/shard_map/all_to_all | solution.py:340
  82.7 21.2 %collective-permute-start.4 = (bf16[4,192,512]{2,1,0:T(8,128)(2,1)S(1)}, bf16[4,192,512]{2,1,0:T(8,128)(2,1)S(1)}, u32[]{:S(2)}, u32[]{:S(2)}) collective-permute-start(bf16[4,192,512]{2,1,0:T(8,128)(2,1)S(1)} %all-to-all-done.refs_0_), channel_id=1, source_target_pairs={{0,1},{1,0},{2,3},{3,2},{4,5},{5,4},{6,7},{7,6},{8,9},{9,8},{10,11... | collective-permute-start | bytes 2359304 | tf_op jit(solution)/shard_map/ppermute | solution.py:364
  100.3 3.6 %collective-permute-start.5 = (bf16[4,96,512]{2,1,0:T(8,128)(2,1)S(1)}, bf16[4,96,512]{2,1,0:T(8,128)(2,1)S(1)}, u32[]{:S(2)}, u32[]{:S(2)}) collective-permute-start(bf16[4,96,512]{2,1,0:T(8,128)(2,1)S(1)} %all-to-all-done.1.refs_2_), channel_id=1, source_target_pairs={{0,1},{1,0},{2,3},{3,2},{4,5},{5,4},{6,7},{7,6},{8,9},{9,8},{10,11... | collective-permute-start | bytes 1179656 | tf_op jit(solution)/shard_map/ppermute | solution.py:383
  113.4 60.1 %copy-start.9 = (bf16[768,128]{1,0:T(8,128)(2,1)S(1)}, bf16[768,128]{1,0:T(8,128)(2,1)}, u32[]{:S(2)}) copy-start(bf16[768,128]{1,0:T(8,128)(2,1)} %get-tuple-element.38.self_ref) | copy-start | bytes 589828
  113.4 60.1 %copy-start.10 = (bf16[768,128]{1,0:T(8,128)(2,1)S(1)}, bf16[768,128]{1,0:T(8,128)(2,1)}, u32[]{:S(2)}) copy-start(bf16[768,128]{1,0:T(8,128)(2,1)} %get-tuple-element.39.neighbour_ref) | copy-start | bytes 589828
  113.4 60.1 %copy-start.11 = (bf16[128,512]{1,0:T(8,128)(2,1)S(1)}, bf16[128,512]{1,0:T(8,128)(2,1)}, u32[]{:S(2)}) copy-start(bf16[128,512]{1,0:T(8,128)(2,1)} %get-tuple-element.37.grad_ref) | copy-start | bytes 393220
  113.4 18.7 %all-to-all-start.2 = ((bf16[12,9,16,128]{3,2,1,0:T(8,128)(2,1)}), bf16[12,9,16,128]{3,2,1,0:T(8,128)(2,1)S(1)}, u32[]{:S(2)}, u32[]{:S(2)}) async-start(bf16[12,9,16,128]{3,2,1,0:T(8,128)(2,1)} %get-tuple-element.46), calls=%async_computation.2 | async-start | bytes 884736 | tf_op jit(solution)/shard_map/all_to_all | solution.py:438
  120.9 36.2 %collective-permute-start.6 = (bf16[2,128,512]{2,1,0:T(8,128)(2,1)}, bf16[2,128,512]{2,1,0:T(8,128)(2,1)S(1)}, u32[]{:S(2)}, u32[]{:S(2)}) collective-permute-start(bf16[2,128,512]{2,1,0:T(8,128)(2,1)} %get-tuple-element.32), channel_id=1, source_target_pairs={{0,8},{8,16},{16,0},{24,32},{32,40},{40,24},{48,56},{56,64},{64,48... | collective-permute-start | bytes 786440 | tf_op jit(solution)/shard_map/ppermute | solution.py:306
  124.3 32.9 %collective-permute-start.7 = (bf16[2,128,512]{2,1,0:T(8,128)(2,1)}, bf16[2,128,512]{2,1,0:T(8,128)(2,1)S(1)}, u32[]{:S(2)}, u32[]{:S(2)}) collective-permute-start(bf16[2,128,512]{2,1,0:T(8,128)(2,1)} %get-tuple-element.33), channel_id=1, source_target_pairs={{0,16},{8,0},{16,8},{24,40},{32,24},{40,32},{48,64},{56,48},{64,56... | collective-permute-start | bytes 786440 | tf_op jit(solution)/shard_map/ppermute | solution.py:306
  143.0 0.7 collective-permute-start.14
  144.3 22.2 %all-to-all-start.4 = ((bf16[8,16,128]{2,1,0:T(8,128)(2,1)}), bf16[8,16,128]{2,1,0:T(8,128)(2,1)S(1)}, u32[]{:S(2)}, u32[]{:S(2)}) async-start(bf16[8,16,128]{2,1,0:T(8,128)(2,1)} %broadcast_in_dim.4), calls=%async_computation.4 | async-start | bytes 65536 | tf_op jit(solution)/shard_map/all_to_all | solution.py:455
  158.5 14.9 %collective-permute-start.8 = (bf16[128,512]{1,0:T(8,128)(2,1)S(1)}, bf16[128,512]{1,0:T(8,128)(2,1)S(1)}, u32[]{:S(2)}, u32[]{:S(2)}) collective-permute-start(bf16[128,512]{1,0:T(8,128)(2,1)S(1)} %get-tuple-element.35), channel_id=1, source_target_pairs={{0,24},{8,32},{16,40},{24,48},{32,56},{40,64},{48,72},{56,80},{64,... | collective-permute-start | bytes 393224 | tf_op jit(solution)/shard_map/ppermute | solution.py:298
  162.5 11.0 %collective-permute-start.9 = (bf16[128,512]{1,0:T(8,128)(2,1)S(1)}, bf16[128,512]{1,0:T(8,128)(2,1)S(1)}, u32[]{:S(2)}, u32[]{:S(2)}) collective-permute-start(bf16[128,512]{1,0:T(8,128)(2,1)S(1)} %get-tuple-element.36), channel_id=1, source_target_pairs={{0,744},{8,752},{16,760},{24,0},{32,8},{40,16},{48,24},{56,32},{64... | collective-permute-start | bytes 393224 | tf_op jit(solution)/shard_map/ppermute | solution.py:298
  167.3 39.3 %all-to-all-start.5 = ((bf16[12,8,16,128]{3,2,1,0:T(8,128)(2,1)}), bf16[12,8,16,128]{3,2,1,0:T(8,128)(2,1)S(1)}, u32[]{:S(2)}, u32[]{:S(2)}) async-start(bf16[12,8,16,128]{3,2,1,0:T(8,128)(2,1)} %broadcast_in_dim.5), calls=%async_computation.5 | async-start | bytes 786432 | tf_op jit(solution)/shard_map/all_to_all | solution.py:462
  174.1 3.6 %collective-permute-start.10 = (bf16[384,512]{1,0:T(8,128)(2,1)S(1)}, bf16[384,512]{1,0:T(8,128)(2,1)S(1)}, u32[]{:S(2)}, u32[]{:S(2)}) collective-permute-start(bf16[384,512]{1,0:T(8,128)(2,1)S(1)} %get-tuple-element.41), channel_id=1, source_target_pairs={{0,1},{1,0},{2,3},{3,2},{4,5},{5,4},{6,7},{7,6},{8,9},{9,8},{10,11... | collective-permute-start | bytes 1179656 | tf_op jit(solution)/shard_map/ppermute | solution.py:496
  177.7 13.4 %collective-permute-start.11 = (bf16[96,512]{1,0:T(8,128)(2,1)S(1)}, bf16[96,512]{1,0:T(8,128)(2,1)S(1)}, u32[]{:S(2)}, u32[]{:S(2)}) collective-permute-start(bf16[96,512]{1,0:T(8,128)(2,1)S(1)} %get-tuple-element.43), channel_id=1, source_target_pairs={{0,2},{1,3},{2,4},{3,5},{4,6},{5,7},{6,0},{7,1},{8,10},{9,11},{10,... | collective-permute-start | bytes 294920 | tf_op jit(solution)/shard_map/ppermute | solution.py:344
  180.8 14.4 %collective-permute-start.12 = (bf16[96,512]{1,0:T(8,128)(2,1)S(1)}, bf16[96,512]{1,0:T(8,128)(2,1)S(1)}, u32[]{:S(2)}, u32[]{:S(2)}) collective-permute-start(bf16[96,512]{1,0:T(8,128)(2,1)S(1)} %get-tuple-element.44), channel_id=1, source_target_pairs={{0,4},{1,5},{2,6},{3,7},{4,0},{5,1},{6,2},{7,3},{8,12},{9,13},{10,... | collective-permute-start | bytes 294920 | tf_op jit(solution)/shard_map/ppermute | solution.py:344
  189.2 16.2 %collective-permute-start.13 = (bf16[96,512]{1,0:T(8,128)(2,1)S(1)}, bf16[96,512]{1,0:T(8,128)(2,1)S(1)}, u32[]{:S(2)}, u32[]{:S(2)}) collective-permute-start(bf16[96,512]{1,0:T(8,128)(2,1)S(1)} %get-tuple-element.45), channel_id=1, source_target_pairs={{0,6},{1,7},{2,0},{3,1},{4,2},{5,3},{6,4},{7,5},{8,14},{9,15},{10,... | collective-permute-start | bytes 294920 | tf_op jit(solution)/shard_map/ppermute | solution.py:344
  (12 other events, 106.1 us)

commit v7 on v6

--- a/solution.py
+++ b/solution.py
@@ -64,15 +64,18 @@
             out[1] = level_ref[...]
 
 
-def pack_kernel(features_ref, self_ref, neighbour_ref, first_ref, second_ref, out_ref):
-    width = features_ref.shape[0]
+def pack_kernel(self_ref, neighbour_ref, first_ref, second_ref, third_ref, out_ref):
     for stack in range(out_ref.shape[0]):
-        out_ref[stack, pl.ds(0, width), :] = features_ref[...]
         for core in range(CORES):
             for kind, ref in enumerate((self_ref, neighbour_ref)):
-                out_ref[stack, pl.ds(width, width), pl.ds((core * 2 + kind) * BLOCK, BLOCK)] = ref[
+                out_ref[stack, :, pl.ds((core * 2 + kind) * BLOCK, BLOCK)] = ref[
                     :, pl.ds((stack * CORES + core) * BLOCK, BLOCK)
                 ]
+
+
+def repeat_kernel(value_ref, after_ref, out_ref):
+    for copy in range(out_ref.shape[0]):
+        out_ref[copy] = value_ref[...]
 
 
 def tile_copies(tiles_hbm, tiles_ref, copied):
@@ -122,18 +125,17 @@
     for block in range(blocks):
         part = pl.ds(block * BLOCK, BLOCK)
         value = (total_ref[block] / degree_ref[:, part].astype(F32)).astype(BF16)
-        for copy in range(out_ref.shape[0]):
-            out_ref[copy, :, part] = value
+        out_ref[:, part] = value
 
 
 def middle_kernel(
     core_ref, stack_ref, count_ref, dest_ref, source_ref, tiles_hbm, degree_ref, *refs
 ):
-    packed, aggregates, refs = refs[:2], refs[2:4], refs[4:]
+    packed, inputs, refs = refs[:2], refs[2:6], refs[6:]
     bias_ref, cotangent_ref, refs = *refs[:2], refs[2:]
     act_ref, grad_ref, weight_ref, self_ref, neighbour_ref, refs = *refs[:5], refs[5:]
     level_ref, first_ref, second_ref, *refs = refs
-    features_ref, scaled_ref, total_ref, tiles_ref, copied, *refs = refs
+    scaled_ref, total_ref, tiles_ref, copied, *refs = refs
     turned_ref, to_first_ref, to_second_ref, stored = refs
     copies = tile_copies(tiles_hbm, tiles_ref, copied)
     stores = [
@@ -143,25 +145,23 @@
         )
     ]
     blocks = scaled_ref.shape[0]
-    stacks, width, _ = aggregates[0].shape
+    stacks, width, _ = inputs[0].shape
     half = stacks * width
     contract_first = (((0,), (0,)), ((), ()))
     for far, ref in enumerate(packed):
         for stack in range(stacks):
             rows = pl.ds(far * half + stack * width, width)
-            features_ref[rows, :] = ref[stack, pl.ds(0, width), :]
             for kind, out in enumerate((self_ref, neighbour_ref)):
-                out[rows, :] = ref[stack, pl.ds(width, width), lanes(core_ref[0] * 2 + kind)]
-    pre = lax.dot_general(
-        self_ref[...], features_ref[...], contract_first, preferred_element_type=F32
-    )
-    for far, ref in enumerate(aggregates):
-        pre = pre + lax.dot_general(
-            neighbour_ref[pl.ds(far * half, half), :],
+                out[rows, :] = ref[stack, :, lanes(core_ref[0] * 2 + kind)]
+    pre = None
+    for at, ref in enumerate(inputs):
+        term = lax.dot_general(
+            (self_ref, neighbour_ref)[at // CORES][pl.ds(at % CORES * half, half), :],
             ref[...].reshape(half, -1),
             contract_first,
             preferred_element_type=F32,
         )
+        pre = term if pre is None else pre + term
     preact = pre.T + bias_ref[...].astype(F32)
     gate_value = jax.nn.sigmoid(preact)
     act_ref[...] = (preact * gate_value).astype(BF16)
@@ -179,8 +179,8 @@
     for block in range(blocks):
         scaled_ref[block] = scaled[:, block * BLOCK : (block + 1) * BLOCK]
     for far in range(CORES):
-        operands = (features_ref[pl.ds(far * half, half), :], aggregates[far][...].reshape(half, -1))
-        for kind, operand in enumerate(operands):
+        for kind, ref in enumerate((inputs[far], inputs[CORES + far])):
+            operand = ref[...].reshape(half, -1)
             term = jnp.dot(operand, grad_pre, preferred_element_type=F32).astype(BF16)
             for stack in range(stacks):
                 column = (stack ^ stack_ref[0]) * CORES + far
@@ -247,7 +247,7 @@
         out[...] = (keep_ref[piece] + got_ref[piece].astype(F32)).astype(out.dtype)
 
 
-def planes_kernel(got_ref, out_ref):
+def planes_kernel(got_ref, after_ref, out_ref):
     for column in range(COLUMN + 1):
         value = got_ref[0, column].astype(F32)
         for plane in range(1, got_ref.shape[0]):
@@ -343,7 +343,22 @@
         pairs = [(f, (f + steps * CORES) % feats) for f in range(feats)]
         return lax.ppermute(value, "feat", pairs)
 
+    def repeated(value, copies, after):
+        return call(
+            repeat_kernel,
+            [VMEM, ANY],
+            jax.ShapeDtypeStruct((copies,) + value.shape, value.dtype),
+            [],
+            0,
+            copies * value.size * 2,
+        )(value, after)
+
     turned = features.T
+    def whole(value):
+        own = over_stacks(value)
+        return own, lax.ppermute(own, "feat", other_core)
+
+    features_both = whole(jnp.broadcast_to(turned[None], (stacks,) + turned.shape))
     below = shifted(turned, TRIO)
     above = shifted(turned, -TRIO)
     pair = jax.ShapeDtypeStruct((2, width, node_dev), BF16)
@@ -352,16 +367,16 @@
     )(place, below, turned, above)
     first = turned_in_trio(first, -1)
     second = turned_in_trio(second, -2)
-    packed = call(
-        pack_kernel,
-        [WHOLE] * 3 + [ANY] * 2,
-        jax.ShapeDtypeStruct((stacks, 2 * width, node_dev), BF16),
-        [],
-        0,
-        6 * stacks * width * node_dev,
-    )(turned, self_weight, neighbour_weight, first, second)
-    packed_own = over_stacks(packed)
-    packed_far = lax.ppermute(packed_own, "feat", other_core)
+    weights_both = whole(
+        call(
+            pack_kernel,
+            [WHOLE] * 2 + [ANY] * 3,
+            jax.ShapeDtypeStruct((stacks, width, 2 * CORES * hidden_dev), BF16),
+            [],
+            0,
+            4 * self_weight.size * 2,
+        )(self_weight, neighbour_weight, first, second, features_both[0])
+    )
 
     degrees = degree.reshape(1, node_dev)
     scalars = (tile_count, dest_block, source_block)
@@ -369,7 +384,7 @@
     aggregate = call(
         gather_kernel,
         [SMEM] * 3 + [HBM] + [VMEM] * 6,
-        jax.ShapeDtypeStruct((stacks, width, node_dev), BF16),
+        jax.ShapeDtypeStruct((width, node_dev), BF16),
         [
             pltpu.VMEM((blocks + 1, width, BLOCK), F32),
             pltpu.VMEM(tile_values.shape, BF16),
@@ -379,8 +394,7 @@
         tile_values.size * 2,
         limit=TILES_VMEM_BYTES,
     )(*scalars, tile_values, degrees, below, turned, above, first, second)
-    aggregate_own = over_stacks(aggregate)
-    aggregate_far = lax.ppermute(aggregate_own, "feat", other_core)
+    aggregate_both = whole(repeated(aggregate, stacks, weights_both[0]))
 
     planes = groups // COLUMN
     rows_each = 4 * half // groups
@@ -389,7 +403,7 @@
 
     middle = call(
         middle_kernel,
-        [SMEM] * 5 + [HBM] + [VMEM] * 5 + [WHOLE] * 2,
+        [SMEM] * 5 + [HBM] + [VMEM] * 7 + [WHOLE] * 2,
         [
             jax.ShapeDtypeStruct((node_dev, hidden_dev), BF16),
             jax.ShapeDtypeStruct((hidden_dev, node_dev), BF16),
@@ -401,7 +415,6 @@
             pair,
         ],
         [
-            pltpu.VMEM((2 * half, node_dev), BF16),
             pltpu.VMEM((blocks, hidden_dev, BLOCK), BF16),
             pltpu.VMEM((OFFS * blocks + 1, hidden_dev, BLOCK), F32),
             pltpu.VMEM(tile_values.shape, BF16),
@@ -421,10 +434,9 @@
         *scalars,
         tile_values,
         degrees,
-        packed_own,
-        packed_far,
-        aggregate_own,
-        aggregate_far,
+        *weights_both,
+        *features_both,
+        *aggregate_both,
         hidden_bias.reshape(1, hidden_dev),
         cotangent,
     )
@@ -432,44 +444,6 @@
     to_level, first, second = middle[5:]
     first = turned_in_trio(first, 1)
     second = turned_in_trio(second, 2)
-
-    got = jax.ShapeDtypeStruct((COLUMN, 2, rows_each, hidden_dev), BF16)
-    got = call(planes_kernel, [VMEM], got, [], weight_part.size, weight_part.size * 2)(
-        lax.all_to_all(weight_part, "rows", 0, 0, axis_index_groups=same_column)
-    )
-    piece = jax.ShapeDtypeStruct((rows_each, hidden_dev), BF16)
-    piece, bias_sum = call(
-        column_kernel,
-        [VMEM],
-        [piece, jax.ShapeDtypeStruct(piece.shape, F32)],
-        [],
-        got.size,
-        got.size * 2,
-    )(lax.all_to_all(got, "rows", 0, 0, axis_index_groups=same_plane))
-    pairs = [
-        (row * feats + feat, row * feats + (feat ^ (row // TRIO % COLUMN)))
-        for row in range(groups)
-        for feat in range(feats)
-    ]
-    piece = lax.ppermute(piece, ("rows", "feat"), pairs)
-    pieces = lax.all_to_all(
-        jnp.broadcast_to(piece[None], (COLUMN,) + piece.shape),
-        "rows",
-        0,
-        0,
-        axis_index_groups=same_plane,
-    )
-    pieces = lax.all_to_all(
-        jnp.broadcast_to(pieces[None], (planes,) + pieces.shape),
-        "rows",
-        0,
-        0,
-        axis_index_groups=same_column,
-    )
-    grad_weight = jax.ShapeDtypeStruct((width, feats * hidden_dev), F32)
-    grad_self, grad_neighbour = call(
-        lay_kernel, [SMEM, VMEM], [grad_weight, grad_weight], [], 0, pieces.size * 6
-    )(lax.axis_index("feat").reshape(1), pieces)
 
     spread = jax.ShapeDtypeStruct((hidden_dev, node_dev), BF16)
     own, to_below, to_above = call(
@@ -493,6 +467,26 @@
         8 * half * node_dev * hidden_dev,
         4 * half * node_dev,
     )(own, from_below, from_above, grad_turned, weight_self, weight_neighbour)
+    mid = jax.ShapeDtypeStruct((COLUMN, 2, rows_each, hidden_dev), BF16)
+    mid = call(planes_kernel, [VMEM, ANY], mid, [], weight_part.size, weight_part.size * 2)(
+        lax.all_to_all(weight_part, "rows", 0, 0, axis_index_groups=same_column),
+        keep,
+    )
+    piece = jax.ShapeDtypeStruct((rows_each, hidden_dev), BF16)
+    piece, bias_sum = call(
+        column_kernel,
+        [VMEM],
+        [piece, jax.ShapeDtypeStruct(piece.shape, F32)],
+        [],
+        mid.size,
+        mid.size * 2,
+    )(lax.all_to_all(mid, "rows", 0, 0, axis_index_groups=same_plane))
+    pairs = [
+        (row * feats + feat, row * feats + (feat ^ (row // TRIO % COLUMN)))
+        for row in range(groups)
+        for feat in range(feats)
+    ]
+    piece = lax.ppermute(piece, ("rows", "feat"), pairs)
     got = lax.ppermute(send, "feat", other_core)
     part = jax.ShapeDtypeStruct((width, node_dev), BF16)
     parts = call(
@@ -507,6 +501,25 @@
         keep.reshape(stacks, width, node_dev),
         got.reshape(stacks, width, node_dev),
     )
+    pieces = lax.all_to_all(
+        repeated(piece, COLUMN, parts[0]),
+        "rows",
+        0,
+        0,
+        axis_index_groups=same_plane,
+    )
+    pieces = lax.all_to_all(
+        jnp.broadcast_to(pieces[None], (planes,) + pieces.shape),
+        "rows",
+        0,
+        0,
+        axis_index_groups=same_column,
+    )
+    grad_weight = jax.ShapeDtypeStruct((width, feats * hidden_dev), F32)
+    grad_self, grad_neighbour = call(
+        lay_kernel, [SMEM, VMEM], [grad_weight, grad_weight], [], 0, pieces.size * 6
+    )(lax.axis_index("feat").reshape(1), pieces)
+
     grad_turned = parts[0]
     for steps in range(1, stacks):
         grad_turned = grad_turned + to_stack(parts[steps], steps).astype(F32)

time: 209 us -> 224 us (1.072)
  blocking collectives: 10.8 us -> 34.6 us
  waiting for transfers between devices: 74.8 us -> 62.9 us
  local copies, waits for them, and re-layouts: 7.78 us -> 11.4 us
    all_to_all x1 -> x2, blocking collectives: 10.8 us -> 34.6 us  [the longest x1 20.6 us: on_device(): lax.all_to_all(repeated(piece, COLUMN, parts[0]), 'rows', 0, 0, axis_inde...]
    all_to_all x2 -> x3, waiting for transfers between devices: 39.3 us -> 21.3 us  [over_stacks(): return lax.all_to_all(value, 'feat', 0, 0, axis_index_groups=same_core)]
    ppermute x4, waiting for transfers between devices: 6.54 us -> 20.3 us  [turned_in_trio(): return lax.ppermute(value, 'rows', pairs)]
    all_to_all x1 -> x0, starting transfers between devices: 12.9 us -> none  [on_device(): lax.all_to_all(jnp.broadcast_to(piece[None], (COLUMN,) + piece.shape), 'r...]
    all_to_all x2 -> x3, starting transfers between devices: 18 us -> 29.2 us  [over_stacks(): return lax.all_to_all(value, 'feat', 0, 0, axis_index_groups=same_core)]
    all_to_all x1, waiting for transfers between devices: 4.46 us -> 0.01 us  [on_device(): lax.all_to_all(weight_part, 'rows', 0, 0, axis_index_groups=same_column)]
    ppermute x3, waiting for transfers between devices: 14.2 us -> 10.2 us  [to_stack(): return lax.ppermute(value, 'feat', pairs)]
    unnamed x32 -> x36, local copies, waits for them, and re-layouts: 5.83 us -> 8.39 us
  transfers between devices with their start and end apart: 20 -> 21, of which waited for: 11 -> 14; matrix products, arithmetic and copies ran while one was open for 1% -> 1% of each run, Pallas kernels for 4% -> 4%
where the time goes in v7:
time: 224 us; the launch traced here: 223 us
  starting transfers between devices  92.9 us (41%)
  waiting for transfers between devices  62.9 us (28%)
  blocking collectives  34.6 us (15%)
  Pallas kernels  19.2 us (9%)
  local copies, waits for them, and re-layouts  11.4 us (5%)
    all_to_all x3, starting transfers between devices, over_stacks(): return lax.all_to_all(value, 'feat', 0, 0, axis_index_groups=same_core)  29.2 us
    all_to_all x3, waiting for transfers between devices, over_stacks(): return lax.all_to_all(value, 'feat', 0, 0, axis_index_groups=same_core)  21.3 us
    all_to_all x1, blocking collectives, on_device(): lax.all_to_all(repeated(piece, COLUMN, parts[0]), 'rows', 0, 0, axis_inde...  20.6 us
    ppermute x4, waiting for transfers between devices, turned_in_trio(): return lax.ppermute(value, 'rows', pairs)  20.3 us
    ppermute x4, starting transfers between devices, shifted(): return lax.ppermute(value, 'rows', pairs)  15.2 us
    all_to_all x1, blocking collectives, on_device(): lax.all_to_all(mid, 'rows', 0, 0, axis_index_groups=same_plane)  14 us
    ppermute x3, starting transfers between devices, to_stack(): return lax.ppermute(value, 'feat', pairs)  13 us
    ppermute x4, starting transfers between devices, turned_in_trio(): return lax.ppermute(value, 'rows', pairs)  12.6 us
  transfers between devices with their start and end apart: 21, of which 14 were waited for; matrix products, arithmetic and copies ran while one was open for 1% of the time, Pallas kernels for 4%

profile of v7, /device:TPU:2, one launch (start us, length us, event | category | flops | bytes accessed | tf_op | source)
XLA Modules:
  0.0 222.7 jit_solution(4855865133360792600)
XLA Ops:
  2.3 14.5 %all-to-all-start = ((bf16[4,96,512]{2,1,0:T(8,128)(2,1)}), bf16[4,96,512]{2,1,0:T(8,128)(2,1)S(1)}, u32[]{:S(2)}, u32[]{:S(2)}) async-start(bf16[4,96,512]{2,1,0:T(8,128)(2,1)} %broadcast_in_dim.4), calls=%async_computation | async-start | bytes 786432 | tf_op jit(solution)/shard_map/all_to_all | solution.py:340
  16.8 5.3 %collective-permute-start.1 = (bf16[96,512]{1,0:T(8,128)(2,1)}, bf16[96,512]{1,0:T(8,128)(2,1)S(1)}, u32[]{:S(2)}, u32[]{:S(2)}) collective-permute-start(bf16[96,512]{1,0:T(8,128)(2,1)} %bitcast.15), channel_id=1, source_target_pairs={{0,744},{8,752},{16,760},{24,0},{32,8},{40,16},{48,24},{56,32},{64... | collective-permute-start | bytes 294920 | tf_op jit(solution)/shard_map/ppermute | solution.py:298
  24.7 6.3 %collective-permute-done.below_ref = bf16[96,512]{1,0:T(8,128)(2,1)S(1)} collective-permute-done((bf16[96,512]{1,0:T(8,128)(2,1)}, bf16[96,512]{1,0:T(8,128)(2,1)S(1)}, u32[]{:S(2)}, u32[]{:S(2)}) %collective-permute-start) | collective-permute-done | bytes 98336 | tf_op jit(solution)/shard_map/ppermute | solution.py:298
  32.0 3.7 %collective-permute-start.2 = (bf16[2,96,512]{2,1,0:T(8,128)(2,1)S(1)}, bf16[2,96,512]{2,1,0:T(8,128)(2,1)S(1)}, u32[]{:S(2)}, u32[]{:S(2)}) collective-permute-start(bf16[2,96,512]{2,1,0:T(8,128)(2,1)S(1)} %get-tuple-element.28), channel_id=1, source_target_pairs={{0,16},{8,0},{16,8},{24,40},{32,24},{40,32},{48,64},{56,48},{64,56... | collective-permute-start | bytes 589832 | tf_op jit(solution)/shard_map/ppermute | solution.py:306
  40.8 4.2 %collective-permute-done.3.second_ref = bf16[2,96,512]{2,1,0:T(8,128)(2,1)S(1)} collective-permute-done((bf16[2,96,512]{2,1,0:T(8,128)(2,1)S(1)}, bf16[2,96,512]{2,1,0:T(8,128)(2,1)S(1)}, u32[]{:S(2)}, u32[]{:S(2)}) %collective-permute-start.3) | collective-permute-done | bytes 196640 | tf_op jit(solution)/shard_map/ppermute | solution.py:306
  47.7 11.2 %all-to-all-start.1 = ((bf16[4,96,512]{2,1,0:T(8,128)(2,1)}), bf16[4,96,512]{2,1,0:T(8,128)(2,1)S(1)}, u32[]{:S(2)}, u32[]{:S(2)}) async-start(bf16[4,96,512]{2,1,0:T(8,128)(2,1)} %shard_map.138), calls=%async_computation.1 | async-start | bytes 786432 | tf_op jit(solution)/shard_map/all_to_all | solution.py:340
  59.0 7.0 %shard_map.139.value_ref = bf16[96,512]{1,0:T(8,128)(2,1)} custom-call(s32[7]{0:T(128)} %count_ref.3, s32[112]{0:T(128)} %dest_ref.3, s32[112]{0:T(128)} %source_ref.3, bf16[112,128,128]{2,1,0:T(8,128)(2,1)} %tiles_hbm.3, s32[1,512]{1,0:T(1,128)} %bitcast.20, bf16[96,512]{1,0:T(8,128)(2,1)} %copy-done.8, bf16[96,512]{1,0:T(8,128)(2,1)} %bitcast.17, ...), custom_call_target="tpu_custom_call" | custom-call | flops 469762048 | bytes 3670016 | tf_op jit(solution)/shard_map/pallas_call | solution.py:384
  66.0 9.0 %all-to-all-done.1.after_ref.refs_0_ = bf16[4,96,512]{2,1,0:T(8,128)(2,1)S(1)} async-done(((bf16[4,96,512]{2,1,0:T(8,128)(2,1)}), bf16[4,96,512]{2,1,0:T(8,128)(2,1)S(1)}, u32[]{:S(2)}, u32[]{:S(2)}) %all-to-all-start.1) | async-done | bytes 393248 | tf_op jit(solution)/shard_map/all_to_all | solution.py:340
  76.7 3.5 %all-to-all-start.2 = ((bf16[4,96,512]{2,1,0:T(8,128)(2,1)}), bf16[4,96,512]{2,1,0:T(8,128)(2,1)S(1)}, u32[]{:S(2)}, u32[]{:S(2)}) async-start(bf16[4,96,512]{2,1,0:T(8,128)(2,1)} %shard_map.140), calls=%async_computation.2 | async-start | bytes 786432 | tf_op jit(solution)/shard_map/all_to_all | solution.py:340
  84.5 12.3 %all-to-all-done.2.refs_4_ = bf16[4,96,512]{2,1,0:T(8,128)(2,1)S(1)} async-done(((bf16[4,96,512]{2,1,0:T(8,128)(2,1)}), bf16[4,96,512]{2,1,0:T(8,128)(2,1)S(1)}, u32[]{:S(2)}, u32[]{:S(2)}) %all-to-all-start.2) | async-done | bytes 393248 | tf_op jit(solution)/shard_map/all_to_all | solution.py:340
  101.2 8.6 %shard_map.141 = (bf16[512,128]{1,0:T(8,128)(2,1)}, bf16[128,512]{1,0:T(8,128)(2,1)}, bf16[12,9,16,128]{3,2,1,0:T(8,128)(2,1)}, bf16[768,128]{1,0:T(8,128)(2,1)}...) custom-call(s32[1]{0:T(128)} %bitcast.core_ref, ...), custom_call_target="tpu_custom_call" | custom-call | flops 939524096 | bytes 3670016 | tf_op jit(solution)/shard_map/pallas_call | solution.py:404
  109.8 8.4 %all-to-all-start.3 = ((bf16[12,9,16,128]{3,2,1,0:T(8,128)(2,1)}), bf16[12,9,16,128]{3,2,1,0:T(8,128)(2,1)S(1)}, u32[]{:S(2)}, u32[]{:S(2)}) async-start(bf16[12,9,16,128]{3,2,1,0:T(8,128)(2,1)} %get-tuple-element.46), calls=%async_computation.3 | async-start | bytes 884736 | tf_op jit(solution)/shard_map/all_to_all | solution.py:472
  118.2 3.4 %collective-permute-start.7 = (bf16[2,128,512]{2,1,0:T(8,128)(2,1)}, bf16[2,128,512]{2,1,0:T(8,128)(2,1)S(1)}, u32[]{:S(2)}, u32[]{:S(2)}) collective-permute-start(bf16[2,128,512]{2,1,0:T(8,128)(2,1)} %get-tuple-element.32), channel_id=1, source_target_pairs={{0,8},{8,16},{16,0},{24,32},{32,40},{40,24},{48,56},{56,64},{64,48... | collective-permute-start | bytes 786440 | tf_op jit(solution)/shard_map/ppermute | solution.py:306
  121.6 3.4 %collective-permute-start.8 = (bf16[2,128,512]{2,1,0:T(8,128)(2,1)}, bf16[2,128,512]{2,1,0:T(8,128)(2,1)S(1)}, u32[]{:S(2)}, u32[]{:S(2)}) collective-permute-start(bf16[2,128,512]{2,1,0:T(8,128)(2,1)} %get-tuple-element.33), channel_id=1, source_target_pairs={{0,16},{8,0},{16,8},{24,40},{32,24},{40,32},{48,64},{56,48},{64,56... | collective-permute-start | bytes 786440 | tf_op jit(solution)/shard_map/ppermute | solution.py:306
  124.9 9.3 %collective-permute-done.7.first_ref = bf16[2,128,512]{2,1,0:T(8,128)(2,1)S(1)} collective-permute-done((bf16[2,128,512]{2,1,0:T(8,128)(2,1)}, bf16[2,128,512]{2,1,0:T(8,128)(2,1)S(1)}, u32[]{:S(2)}, u32[]{:S(2)}) %collective-permute-start.7) | collective-permute-done | bytes 262176 | tf_op jit(solution)/shard_map/ppermute | solution.py:306
  134.2 3.9 %collective-permute-done.8.second_ref = bf16[2,128,512]{2,1,0:T(8,128)(2,1)S(1)} collective-permute-done((bf16[2,128,512]{2,1,0:T(8,128)(2,1)}, bf16[2,128,512]{2,1,0:T(8,128)(2,1)S(1)}, u32[]{:S(2)}, u32[]{:S(2)}) %collective-permute-start.8) | collective-permute-done | bytes 262176 | tf_op jit(solution)/shard_map/ppermute | solution.py:306
  141.4 6.0 %collective-permute-start.10 = (bf16[128,512]{1,0:T(8,128)(2,1)S(1)}, bf16[128,512]{1,0:T(8,128)(2,1)S(1)}, u32[]{:S(2)}, u32[]{:S(2)}) collective-permute-start(bf16[128,512]{1,0:T(8,128)(2,1)S(1)} %get-tuple-element.36), channel_id=1, source_target_pairs={{0,744},{8,752},{16,760},{24,0},{32,8},{40,16},{48,24},{56,32},{64... | collective-permute-start | bytes 393224 | tf_op jit(solution)/shard_map/ppermute | solution.py:298
  155.3 14.0 %all_to_all.35.got_ref = bf16[8,2,16,128]{3,2,1,0:T(8,128)(2,1)S(1)} all-to-all(bf16[8,2,16,128]{3,2,1,0:T(8,128)(2,1)S(1)} %shard_map.145), channel_id=1, replica_groups={{0,24,48,72,96,120,144,168},{8,32,56,80,104,128,152,176},{16,40,64,88,1..., dimensions={0} | all-to-all | bytes 131072 | tf_op jit(solution)/shard_map/all_to_all | solution.py:483
  170.2 20.6 %all_to_all.36 = bf16[8,16,128]{2,1,0:T(8,128)(2,1)S(1)} all-to-all(bf16[8,16,128]{2,1,0:T(8,128)(2,1)S(1)} %shard_map.147), channel_id=1, replica_groups={{0,24,48,72,96,120,144,168},{8,32,56,80,104,128,152,176},{16,40,64,88,1..., dimensions={0} | all-to-all | bytes 65536 | tf_op jit(solution)/shard_map/all_to_all | solution.py:504
  191.6 5.7 %all-to-all-start.6 = ((bf16[12,8,16,128]{3,2,1,0:T(8,128)(2,1)}), bf16[12,8,16,128]{3,2,1,0:T(8,128)(2,1)S(1)}, u32[]{:S(2)}, u32[]{:S(2)}) async-start(bf16[12,8,16,128]{3,2,1,0:T(8,128)(2,1)} %broadcast_in_dim.5), calls=%async_computation.6 | async-start | bytes 786432 | tf_op jit(solution)/shard_map/all_to_all | solution.py:511
  199.7 6.8 %collective-permute-start.13 = (bf16[96,512]{1,0:T(8,128)(2,1)S(1)}, bf16[96,512]{1,0:T(8,128)(2,1)S(1)}, u32[]{:S(2)}, u32[]{:S(2)}) collective-permute-start(bf16[96,512]{1,0:T(8,128)(2,1)S(1)} %get-tuple-element.44), channel_id=1, source_target_pairs={{0,4},{1,5},{2,6},{3,7},{4,0},{5,1},{6,2},{7,3},{8,12},{9,13},{10,... | collective-permute-start | bytes 294920 | tf_op jit(solution)/shard_map/ppermute | solution.py:344
  206.5 3.8 %collective-permute-start.14 = (bf16[96,512]{1,0:T(8,128)(2,1)S(1)}, bf16[96,512]{1,0:T(8,128)(2,1)S(1)}, u32[]{:S(2)}, u32[]{:S(2)}) collective-permute-start(bf16[96,512]{1,0:T(8,128)(2,1)S(1)} %get-tuple-element.45), channel_id=1, source_target_pairs={{0,6},{1,7},{2,0},{3,1},{4,2},{5,3},{6,4},{7,5},{8,14},{9,15},{10,... | collective-permute-start | bytes 294920 | tf_op jit(solution)/shard_map/ppermute | solution.py:344
  210.6 4.2 %collective-permute-done.13 = bf16[96,512]{1,0:T(8,128)(2,1)S(1)} collective-permute-done((bf16[96,512]{1,0:T(8,128)(2,1)S(1)}, bf16[96,512]{1,0:T(8,128)(2,1)S(1)}, u32[]{:S(2)}, u32[]{:S(2)}) %collective-permute-start.13) | collective-permute-done | bytes 98336 | tf_op jit(solution)/shard_map/ppermute | solution.py:344
  214.8 5.8 %collective-permute-done.14 = bf16[96,512]{1,0:T(8,128)(2,1)S(1)} collective-permute-done((bf16[96,512]{1,0:T(8,128)(2,1)S(1)}, bf16[96,512]{1,0:T(8,128)(2,1)S(1)}, u32[]{:S(2)}, u32[]{:S(2)}) %collective-permute-start.14) | collective-permute-done | bytes 98336 | tf_op jit(solution)/shard_map/ppermute | solution.py:344
  (72 shorter events, 40.8 us)
Async XLA Ops:
  2.3 42.6 %all-to-all-start = ((bf16[4,96,512]{2,1,0:T(8,128)(2,1)}), bf16[4,96,512]{2,1,0:T(8,128)(2,1)S(1)}, u32[]{:S(2)}, u32[]{:S(2)}) async-start(bf16[4,96,512]{2,1,0:T(8,128)(2,1)} %broadcast_in_dim.4), calls=%async_computation | async-start | bytes 786432 | tf_op jit(solution)/shard_map/all_to_all | solution.py:340
  16.8 7.9 %collective-permute-start.1 = (bf16[96,512]{1,0:T(8,128)(2,1)}, bf16[96,512]{1,0:T(8,128)(2,1)S(1)}, u32[]{:S(2)}, u32[]{:S(2)}) collective-permute-start(bf16[96,512]{1,0:T(8,128)(2,1)} %bitcast.15), channel_id=1, source_target_pairs={{0,744},{8,752},{16,760},{24,0},{32,8},{40,16},{48,24},{56,32},{64... | collective-permute-start | bytes 294920 | tf_op jit(solution)/shard_map/ppermute | solution.py:298
  22.1 8.8 %collective-permute-start = (bf16[96,512]{1,0:T(8,128)(2,1)}, bf16[96,512]{1,0:T(8,128)(2,1)S(1)}, u32[]{:S(2)}, u32[]{:S(2)}) collective-permute-start(bf16[96,512]{1,0:T(8,128)(2,1)} %bitcast.16), channel_id=1, source_target_pairs={{0,24},{8,32},{16,40},{24,48},{32,56},{40,64},{48,72},{56,80},{64,... | collective-permute-start | bytes 294920 | tf_op jit(solution)/shard_map/ppermute | solution.py:298
  24.7 34.3 %copy-start.7 = (bf16[96,512]{1,0:T(8,128)(2,1)}, bf16[96,512]{1,0:T(8,128)(2,1)S(1)}, u32[]{:S(2)}) copy-start(bf16[96,512]{1,0:T(8,128)(2,1)S(1)} %collective-permute-done.1.above_ref) | copy-start | bytes 294916
  31.0 28.0 %copy-start.8 = (bf16[96,512]{1,0:T(8,128)(2,1)}, bf16[96,512]{1,0:T(8,128)(2,1)S(1)}, u32[]{:S(2)}) copy-start(bf16[96,512]{1,0:T(8,128)(2,1)S(1)} %collective-permute-done.below_ref) | copy-start | bytes 294916
  32.0 8.8 %collective-permute-start.2 = (bf16[2,96,512]{2,1,0:T(8,128)(2,1)S(1)}, bf16[2,96,512]{2,1,0:T(8,128)(2,1)S(1)}, u32[]{:S(2)}, u32[]{:S(2)}) collective-permute-start(bf16[2,96,512]{2,1,0:T(8,128)(2,1)S(1)} %get-tuple-element.28), channel_id=1, source_target_pairs={{0,16},{8,0},{16,8},{24,40},{32,24},{40,32},{48,64},{56,48},{64,56... | collective-permute-start | bytes 589832 | tf_op jit(solution)/shard_map/ppermute | solution.py:306
  35.7 9.3 %collective-permute-start.3 = (bf16[2,96,512]{2,1,0:T(8,128)(2,1)S(1)}, bf16[2,96,512]{2,1,0:T(8,128)(2,1)S(1)}, u32[]{:S(2)}, u32[]{:S(2)}) collective-permute-start(bf16[2,96,512]{2,1,0:T(8,128)(2,1)S(1)} %get-tuple-element.29), channel_id=1, source_target_pairs={{0,8},{8,16},{16,0},{24,32},{32,40},{40,24},{48,56},{56,64},{64,48... | collective-permute-start | bytes 589832 | tf_op jit(solution)/shard_map/ppermute | solution.py:306
  46.9 33.3 %copy-start.1 = (bf16[4,96,512]{2,1,0:T(8,128)(2,1)}, bf16[4,96,512]{2,1,0:T(8,128)(2,1)S(1)}, u32[]{:S(2)}) copy-start(bf16[4,96,512]{2,1,0:T(8,128)(2,1)S(1)} %all-to-all-done.third_ref.refs_2_) | copy-start | bytes 1179652
  47.7 27.3 %all-to-all-start.1 = ((bf16[4,96,512]{2,1,0:T(8,128)(2,1)}), bf16[4,96,512]{2,1,0:T(8,128)(2,1)S(1)}, u32[]{:S(2)}, u32[]{:S(2)}) async-start(bf16[4,96,512]{2,1,0:T(8,128)(2,1)} %shard_map.138), calls=%async_computation.1 | async-start | bytes 786432 | tf_op jit(solution)/shard_map/all_to_all | solution.py:340
  76.7 20.1 %all-to-all-start.2 = ((bf16[4,96,512]{2,1,0:T(8,128)(2,1)}), bf16[4,96,512]{2,1,0:T(8,128)(2,1)S(1)}, u32[]{:S(2)}, u32[]{:S(2)}) async-start(bf16[4,96,512]{2,1,0:T(8,128)(2,1)} %shard_map.140), calls=%async_computation.2 | async-start | bytes 786432 | tf_op jit(solution)/shard_map/all_to_all | solution.py:340
  80.2 18.6 %collective-permute-start.5 = (bf16[4,96,512]{2,1,0:T(8,128)(2,1)S(1)}, bf16[4,96,512]{2,1,0:T(8,128)(2,1)S(1)}, u32[]{:S(2)}, u32[]{:S(2)}) collective-permute-start(bf16[4,96,512]{2,1,0:T(8,128)(2,1)S(1)} %all-to-all-done.third_ref.refs_2_), channel_id=1, source_target_pairs={{0,1},{1,0},{2,3},{3,2},{4,5},{5,4},{6,7},{7,6},{8,9},{9,8},{10,11... | collective-permute-start | bytes 1179656 | tf_op jit(solution)/shard_map/ppermute | solution.py:359
  82.1 16.7 %collective-permute-start.4 = (bf16[4,96,512]{2,1,0:T(8,128)(2,1)S(1)}, bf16[4,96,512]{2,1,0:T(8,128)(2,1)S(1)}, u32[]{:S(2)}, u32[]{:S(2)}) collective-permute-start(bf16[4,96,512]{2,1,0:T(8,128)(2,1)S(1)} %all-to-all-done.1.after_ref.refs_0_), channel_id=1, source_target_pairs={{0,1},{1,0},{2,3},{3,2},{4,5},{5,4},{6,7},{7,6},{8,9},{9,8},{10,11... | collective-permute-start | bytes 1179656 | tf_op jit(solution)/shard_map/ppermute | solution.py:359
  96.8 3.6 %collective-permute-start.6 = (bf16[4,96,512]{2,1,0:T(8,128)(2,1)S(1)}, bf16[4,96,512]{2,1,0:T(8,128)(2,1)S(1)}, u32[]{:S(2)}, u32[]{:S(2)}) collective-permute-start(bf16[4,96,512]{2,1,0:T(8,128)(2,1)S(1)} %all-to-all-done.2.refs_4_), channel_id=1, source_target_pairs={{0,1},{1,0},{2,3},{3,2},{4,5},{5,4},{6,7},{7,6},{8,9},{9,8},{10,11... | collective-permute-start | bytes 1179656 | tf_op jit(solution)/shard_map/ppermute | solution.py:359
  109.8 45.4 %all-to-all-start.3 = ((bf16[12,9,16,128]{3,2,1,0:T(8,128)(2,1)}), bf16[12,9,16,128]{3,2,1,0:T(8,128)(2,1)S(1)}, u32[]{:S(2)}, u32[]{:S(2)}) async-start(bf16[12,9,16,128]{3,2,1,0:T(8,128)(2,1)} %get-tuple-element.46), calls=%async_computation.3 | async-start | bytes 884736 | tf_op jit(solution)/shard_map/all_to_all | solution.py:472
  118.2 16.0 %collective-permute-start.7 = (bf16[2,128,512]{2,1,0:T(8,128)(2,1)}, bf16[2,128,512]{2,1,0:T(8,128)(2,1)S(1)}, u32[]{:S(2)}, u32[]{:S(2)}) collective-permute-start(bf16[2,128,512]{2,1,0:T(8,128)(2,1)} %get-tuple-element.32), channel_id=1, source_target_pairs={{0,8},{8,16},{16,0},{24,32},{32,40},{40,24},{48,56},{56,64},{64,48... | collective-permute-start | bytes 786440 | tf_op jit(solution)/shard_map/ppermute | solution.py:306
  121.6 16.6 %collective-permute-start.8 = (bf16[2,128,512]{2,1,0:T(8,128)(2,1)}, bf16[2,128,512]{2,1,0:T(8,128)(2,1)S(1)}, u32[]{:S(2)}, u32[]{:S(2)}) collective-permute-start(bf16[2,128,512]{2,1,0:T(8,128)(2,1)} %get-tuple-element.33), channel_id=1, source_target_pairs={{0,16},{8,0},{16,8},{24,40},{32,24},{40,32},{48,64},{56,48},{64,56... | collective-permute-start | bytes 786440 | tf_op jit(solution)/shard_map/ppermute | solution.py:306
  139.5 9.0 %collective-permute-start.9 = (bf16[128,512]{1,0:T(8,128)(2,1)S(1)}, bf16[128,512]{1,0:T(8,128)(2,1)S(1)}, u32[]{:S(2)}, u32[]{:S(2)}) collective-permute-start(bf16[128,512]{1,0:T(8,128)(2,1)S(1)} %get-tuple-element.35), channel_id=1, source_target_pairs={{0,24},{8,32},{16,40},{24,48},{32,56},{40,64},{48,72},{56,80},{64,... | collective-permute-start | bytes 393224 | tf_op jit(solution)/shard_map/ppermute | solution.py:298
  141.4 8.5 %collective-permute-start.10 = (bf16[128,512]{1,0:T(8,128)(2,1)S(1)}, bf16[128,512]{1,0:T(8,128)(2,1)S(1)}, u32[]{:S(2)}, u32[]{:S(2)}) collective-permute-start(bf16[128,512]{1,0:T(8,128)(2,1)S(1)} %get-tuple-element.36), channel_id=1, source_target_pairs={{0,744},{8,752},{16,760},{24,0},{32,8},{40,16},{48,24},{56,32},{64... | collective-permute-start | bytes 393224 | tf_op jit(solution)/shard_map/ppermute | solution.py:298
  153.3 16.7 %collective-permute-start.11 = (bf16[384,512]{1,0:T(8,128)(2,1)S(1)}, bf16[384,512]{1,0:T(8,128)(2,1)S(1)}, u32[]{:S(2)}, u32[]{:S(2)}) collective-permute-start(bf16[384,512]{1,0:T(8,128)(2,1)S(1)} %get-tuple-element.41), channel_id=1, source_target_pairs={{0,1},{1,0},{2,3},{3,2},{4,5},{5,4},{6,7},{7,6},{8,9},{9,8},{10,11... | collective-permute-start | bytes 1179656 | tf_op jit(solution)/shard_map/ppermute | solution.py:490
  169.4 0.8 collective-permute-start.15
  191.6 30.2 %all-to-all-start.6 = ((bf16[12,8,16,128]{3,2,1,0:T(8,128)(2,1)}), bf16[12,8,16,128]{3,2,1,0:T(8,128)(2,1)S(1)}, u32[]{:S(2)}, u32[]{:S(2)}) async-start(bf16[12,8,16,128]{3,2,1,0:T(8,128)(2,1)} %broadcast_in_dim.5), calls=%async_computation.6 | async-start | bytes 786432 | tf_op jit(solution)/shard_map/all_to_all | solution.py:511
  197.3 13.3 %collective-permute-start.12 = (bf16[96,512]{1,0:T(8,128)(2,1)S(1)}, bf16[96,512]{1,0:T(8,128)(2,1)S(1)}, u32[]{:S(2)}, u32[]{:S(2)}) collective-permute-start(bf16[96,512]{1,0:T(8,128)(2,1)S(1)} %get-tuple-element.43), channel_id=1, source_target_pairs={{0,2},{1,3},{2,4},{3,5},{4,6},{5,7},{6,0},{7,1},{8,10},{9,11},{10,... | collective-permute-start | bytes 294920 | tf_op jit(solution)/shard_map/ppermute | solution.py:344
  199.7 15.0 %collective-permute-start.13 = (bf16[96,512]{1,0:T(8,128)(2,1)S(1)}, bf16[96,512]{1,0:T(8,128)(2,1)S(1)}, u32[]{:S(2)}, u32[]{:S(2)}) collective-permute-start(bf16[96,512]{1,0:T(8,128)(2,1)S(1)} %get-tuple-element.44), channel_id=1, source_target_pairs={{0,4},{1,5},{2,6},{3,7},{4,0},{5,1},{6,2},{7,3},{8,12},{9,13},{10,... | collective-permute-start | bytes 294920 | tf_op jit(solution)/shard_map/ppermute | solution.py:344
  206.5 14.0 %collective-permute-start.14 = (bf16[96,512]{1,0:T(8,128)(2,1)S(1)}, bf16[96,512]{1,0:T(8,128)(2,1)S(1)}, u32[]{:S(2)}, u32[]{:S(2)}) collective-permute-start(bf16[96,512]{1,0:T(8,128)(2,1)S(1)} %get-tuple-element.45), channel_id=1, source_target_pairs={{0,6},{1,7},{2,0},{3,1},{4,2},{5,3},{6,4},{7,5},{8,14},{9,15},{10,... | collective-permute-start | bytes 294920 | tf_op jit(solution)/shard_map/ppermute | solution.py:344
  (15 other events, 72.1 us)

commit v8 on v6

--- a/solution.py
+++ b/solution.py
@@ -64,7 +64,16 @@
             out[1] = level_ref[...]
 
 
-def pack_kernel(features_ref, self_ref, neighbour_ref, first_ref, second_ref, out_ref):
+def row_group(plane, column):
+    return (plane // TRIO * COLUMN + column) * TRIO + plane % TRIO
+
+
+def repeat_kernel(value_ref, after_ref, out_ref):
+    for copy in range(out_ref.shape[0]):
+        out_ref[copy] = value_ref[...]
+
+
+def pack_kernel(features_ref, self_ref, neighbour_ref, out_ref):
     width = features_ref.shape[0]
     for stack in range(out_ref.shape[0]):
         out_ref[stack, pl.ds(0, width), :] = features_ref[...]
@@ -131,7 +140,10 @@
 ):
     packed, aggregates, refs = refs[:2], refs[2:4], refs[4:]
     bias_ref, cotangent_ref, refs = *refs[:2], refs[2:]
-    act_ref, grad_ref, weight_ref, self_ref, neighbour_ref, refs = *refs[:5], refs[5:]
+    act_ref, grad_ref, weight_ref, bias_out_ref, self_ref, neighbour_ref, refs = (
+        *refs[:6],
+        refs[6:],
+    )
     level_ref, first_ref, second_ref, *refs = refs
     features_ref, scaled_ref, total_ref, tiles_ref, copied, *refs = refs
     turned_ref, to_first_ref, to_second_ref, stored = refs
@@ -168,10 +180,10 @@
     grad = cotangent_ref[...].astype(F32) * gate_value * (1.0 + preact * (1.0 - gate_value))
     grad_pre = grad.astype(BF16)
     grad = grad_pre.astype(F32)
-    planes, _, rows, lane = weight_ref.shape
-    bias_rows = jnp.broadcast_to(jnp.sum(grad, axis=0, keepdims=True), (rows, lane)).astype(BF16)
-    for plane in range(planes):
-        weight_ref[plane, COLUMN] = bias_rows
+    bias_out_ref[...] = jnp.broadcast_to(
+        jnp.sum(grad, axis=0, keepdims=True), bias_out_ref.shape
+    ).astype(bias_out_ref.dtype)
+    rows = weight_ref.shape[1]
     turned = grad.T
     turned_ref[...] = turned.astype(BF16)
     stores[0].start()
@@ -187,7 +199,9 @@
                 for first in range(0, width, PIECE):
                     plane, row = divmod(kind * width + first, rows)
                     begin = stack * width + first
-                    weight_ref[plane, column, pl.ds(row, PIECE), :] = term[begin : begin + PIECE]
+                    weight_ref[row_group(plane, column), pl.ds(row, PIECE), :] = term[
+                        begin : begin + PIECE
+                    ]
     total_ref[...] = jnp.zeros_like(total_ref)
     for offset in range(OFFS):
 
@@ -247,36 +261,15 @@
         out[...] = (keep_ref[piece] + got_ref[piece].astype(F32)).astype(out.dtype)
 
 
-def planes_kernel(got_ref, out_ref):
-    for column in range(COLUMN + 1):
-        value = got_ref[0, column].astype(F32)
-        for plane in range(1, got_ref.shape[0]):
-            value = value + got_ref[plane, column].astype(F32)
-        value = value.astype(BF16)
-        if column < COLUMN:
-            out_ref[column, 0] = value
-        else:
-            for copy in range(COLUMN):
-                out_ref[copy, 1] = value
-
-
-def column_kernel(got_ref, piece_ref, bias_ref):
-    for at, out in enumerate((piece_ref, bias_ref)):
-        value = got_ref[0, at].astype(F32)
-        for column in range(1, COLUMN):
-            value = value + got_ref[column, at].astype(F32)
-        out[...] = value.astype(out.dtype)
-
-
 def lay_kernel(feat_ref, pieces_ref, self_ref, neighbour_ref):
-    planes, _, rows, _ = pieces_ref.shape
-    for plane in range(planes):
+    groups, rows, _ = pieces_ref.shape
+    for plane in range(groups // COLUMN):
         for first in range(0, rows, PIECE):
             kind, row = divmod(plane * rows + first, self_ref.shape[0])
             out = (self_ref, neighbour_ref)[kind]
             for column in range(COLUMN):
                 out[pl.ds(row, PIECE), lanes(column ^ feat_ref[0])] = pieces_ref[
-                    plane, column, pl.ds(first, PIECE), :
+                    row_group(plane, column), pl.ds(first, PIECE), :
                 ].astype(F32)
 
 
@@ -330,11 +323,6 @@
     place = (lax.axis_index("rows") % TRIO).reshape(1)
     same_core = [[z * CORES + c for z in range(stacks)] for c in range(CORES)]
     other_core = [(f, f ^ 1) for f in range(feats)]
-    same_plane = [
-        [(p // TRIO * COLUMN + c) * TRIO + p % TRIO for c in range(COLUMN)]
-        for p in range(groups // COLUMN)
-    ]
-    same_column = [list(members) for members in zip(*same_plane)]
 
     def over_stacks(value):
         return lax.all_to_all(value, "feat", 0, 0, axis_index_groups=same_core)
@@ -354,12 +342,12 @@
     second = turned_in_trio(second, -2)
     packed = call(
         pack_kernel,
-        [WHOLE] * 3 + [ANY] * 2,
+        [WHOLE] * 3,
         jax.ShapeDtypeStruct((stacks, 2 * width, node_dev), BF16),
         [],
         0,
         6 * stacks * width * node_dev,
-    )(turned, self_weight, neighbour_weight, first, second)
+    )(turned, self_weight, neighbour_weight)
     packed_own = over_stacks(packed)
     packed_far = lax.ppermute(packed_own, "feat", other_core)
 
@@ -382,7 +370,6 @@
     aggregate_own = over_stacks(aggregate)
     aggregate_far = lax.ppermute(aggregate_own, "feat", other_core)
 
-    planes = groups // COLUMN
     rows_each = 4 * half // groups
 
     pair = jax.ShapeDtypeStruct((2, hidden_dev, node_dev), BF16)
@@ -393,7 +380,8 @@
         [
             jax.ShapeDtypeStruct((node_dev, hidden_dev), BF16),
             jax.ShapeDtypeStruct((hidden_dev, node_dev), BF16),
-            jax.ShapeDtypeStruct((planes, COLUMN + 1, rows_each, hidden_dev), BF16),
+            jax.ShapeDtypeStruct((groups, rows_each, hidden_dev), BF16),
+            jax.ShapeDtypeStruct((8, hidden_dev), F32),
             jax.ShapeDtypeStruct((2 * half, hidden_dev), BF16),
             jax.ShapeDtypeStruct((2 * half, hidden_dev), BF16),
             jax.ShapeDtypeStruct((TRIO, hidden_dev, node_dev), F32),
@@ -413,7 +401,7 @@
         ],
         tile_flops * 2,
         tile_values.size * 2,
-        [WHOLE, HBM, VMEM, VMEM, VMEM, VMEM, HBM, HBM],
+        [WHOLE, HBM, VMEM, VMEM, VMEM, VMEM, VMEM, HBM, HBM],
         TILES_VMEM_BYTES,
     )(
         core,
@@ -428,48 +416,20 @@
         hidden_bias.reshape(1, hidden_dev),
         cotangent,
     )
-    activations, grad_turned, weight_part, weight_self, weight_neighbour = middle[:5]
-    to_level, first, second = middle[5:]
+    activations, grad_turned, weight_part, bias_part, weight_self, weight_neighbour = middle[:6]
+    to_level, first, second = middle[6:]
     first = turned_in_trio(first, 1)
     second = turned_in_trio(second, 2)
 
-    got = jax.ShapeDtypeStruct((COLUMN, 2, rows_each, hidden_dev), BF16)
-    got = call(planes_kernel, [VMEM], got, [], weight_part.size, weight_part.size * 2)(
-        lax.all_to_all(weight_part, "rows", 0, 0, axis_index_groups=same_column)
-    )
-    piece = jax.ShapeDtypeStruct((rows_each, hidden_dev), BF16)
-    piece, bias_sum = call(
-        column_kernel,
-        [VMEM],
-        [piece, jax.ShapeDtypeStruct(piece.shape, F32)],
-        [],
-        got.size,
-        got.size * 2,
-    )(lax.all_to_all(got, "rows", 0, 0, axis_index_groups=same_plane))
+    bias_rows = jnp.broadcast_to(bias_part.astype(BF16)[None], (groups,) + bias_part.shape)
+    sent = jnp.concatenate([weight_part, bias_rows], axis=1)
+    summed = jnp.sum(lax.all_to_all(sent, "rows", 0, 0).astype(F32), axis=0)
     pairs = [
         (row * feats + feat, row * feats + (feat ^ (row // TRIO % COLUMN)))
         for row in range(groups)
         for feat in range(feats)
     ]
-    piece = lax.ppermute(piece, ("rows", "feat"), pairs)
-    pieces = lax.all_to_all(
-        jnp.broadcast_to(piece[None], (COLUMN,) + piece.shape),
-        "rows",
-        0,
-        0,
-        axis_index_groups=same_plane,
-    )
-    pieces = lax.all_to_all(
-        jnp.broadcast_to(pieces[None], (planes,) + pieces.shape),
-        "rows",
-        0,
-        0,
-        axis_index_groups=same_column,
-    )
-    grad_weight = jax.ShapeDtypeStruct((width, feats * hidden_dev), F32)
-    grad_self, grad_neighbour = call(
-        lay_kernel, [SMEM, VMEM], [grad_weight, grad_weight], [], 0, pieces.size * 6
-    )(lax.axis_index("feat").reshape(1), pieces)
+    piece = lax.ppermute(summed[:rows_each].astype(BF16), ("rows", "feat"), pairs)
 
     spread = jax.ShapeDtypeStruct((hidden_dev, node_dev), BF16)
     own, to_below, to_above = call(
@@ -507,10 +467,23 @@
         keep.reshape(stacks, width, node_dev),
         got.reshape(stacks, width, node_dev),
     )
+    pieces = call(
+        repeat_kernel,
+        [VMEM, ANY],
+        jax.ShapeDtypeStruct((groups,) + piece.shape, BF16),
+        [],
+        0,
+        groups * piece.size * 2,
+    )(piece, parts[0])
+    pieces = lax.all_to_all(pieces, "rows", 0, 0)
+    grad_weight = jax.ShapeDtypeStruct((width, feats * hidden_dev), F32)
+    grad_self, grad_neighbour = call(
+        lay_kernel, [SMEM, VMEM], [grad_weight, grad_weight], [], 0, pieces.size * 6
+    )(lax.axis_index("feat").reshape(1), pieces)
     grad_turned = parts[0]
     for steps in range(1, stacks):
         grad_turned = grad_turned + to_stack(parts[steps], steps).astype(F32)
-    return (activations, grad_turned.astype(BF16).T, grad_self, grad_neighbour, bias_sum[0])
+    return (activations, grad_turned.astype(BF16).T, grad_self, grad_neighbour, summed[rows_each])
 
 
 def solution(mesh):

time: 209 us -> 204 us (0.976)
  the two profiles are of different devices: /device:TPU:2 before, /device:TPU:1 now
where the time goes in v8:
time: 204 us; the launch traced here: 201 us
  starting transfers between devices  107 us (52%)
  waiting for transfers between devices  65.4 us (32%)
  Pallas kernels  19.3 us (9%)
  local copies, waits for them, and re-layouts  4.98 us (2%)
  other arithmetic  3.5 us (2%)
    ppermute x4, waiting for transfers between devices, turned_in_trio(): return lax.ppermute(value, 'rows', pairs)  31.1 us
    all_to_all x2, starting transfers between devices, over_stacks(): return lax.all_to_all(value, 'feat', 0, 0, axis_index_groups=same_core)  21.9 us
    all_to_all x1, starting transfers between devices, on_device(): pieces = lax.all_to_all(pieces, 'rows', 0, 0)  18.9 us
    ppermute x4, starting transfers between devices, shifted(): return lax.ppermute(value, 'rows', pairs)  18.1 us
    all_to_all x2, waiting for transfers between devices, over_stacks(): return lax.all_to_all(value, 'feat', 0, 0, axis_index_groups=same_core)  14.6 us
    all_to_all x1, starting transfers between devices, on_device(): summed = jnp.sum(lax.all_to_all(sent, 'rows', 0, 0).astype(F32), axis=0)  12.9 us
    ppermute x3, starting transfers between devices, to_stack(): return lax.ppermute(value, 'feat', pairs)  12.5 us
    ppermute x4, starting transfers between devices, turned_in_trio(): return lax.ppermute(value, 'rows', pairs)  11.5 us
  transfers between devices with their start and end apart: 19, of which 13 were waited for; matrix products, arithmetic and copies ran while one was open for 1% of the time, Pallas kernels for 4%

profile of v8, /device:TPU:1, one launch (start us, length us, event | category | flops | bytes accessed | tf_op | source)
XLA Modules:
  0.0 200.9 jit_solution(7544013610157022453)
XLA Ops:
  4.4 15.0 %all-to-all-start = ((bf16[4,192,512]{2,1,0:T(8,128)(2,1)}), bf16[4,192,512]{2,1,0:T(8,128)(2,1)S(1)}, u32[]{:S(2)}, u32[]{:S(2)}) async-start(bf16[4,192,512]{2,1,0:T(8,128)(2,1)} %shard_map.137), calls=%async_computation | async-start | bytes 1572864 | tf_op jit(solution)/shard_map/all_to_all | solution.py:328
  19.4 7.3 %collective-permute-start.2 = (bf16[96,512]{1,0:T(8,128)(2,1)S(1)}, bf16[96,512]{1,0:T(8,128)(2,1)S(1)}, u32[]{:S(2)}, u32[]{:S(2)}) collective-permute-start(bf16[96,512]{1,0:T(8,128)(2,1)S(1)} %bitcast.15), channel_id=1, source_target_pairs={{0,744},{8,752},{16,760},{24,0},{32,8},{40,16},{48,24},{56,32},{64... | collective-permute-start | bytes 294920 | tf_op jit(solution)/shard_map/ppermute | solution.py:291
  28.7 7.0 %collective-permute-done.1.below_ref = bf16[96,512]{1,0:T(8,128)(2,1)S(1)} collective-permute-done((bf16[96,512]{1,0:T(8,128)(2,1)S(1)}, bf16[96,512]{1,0:T(8,128)(2,1)S(1)}, u32[]{:S(2)}, u32[]{:S(2)}) %collective-permute-start.1) | collective-permute-done | bytes 98336 | tf_op jit(solution)/shard_map/ppermute | solution.py:291
  35.7 3.3 %collective-permute-start.3 = (bf16[2,96,512]{2,1,0:T(8,128)(2,1)S(1)}, bf16[2,96,512]{2,1,0:T(8,128)(2,1)S(1)}, u32[]{:S(2)}, u32[]{:S(2)}) collective-permute-start(bf16[2,96,512]{2,1,0:T(8,128)(2,1)S(1)} %get-tuple-element.27), channel_id=1, source_target_pairs={{0,16},{8,0},{16,8},{24,40},{32,24},{40,32},{48,64},{56,48},{64,56... | collective-permute-start | bytes 589832 | tf_op jit(solution)/shard_map/ppermute | solution.py:299
  41.0 11.5 %collective-permute-done.3.first_ref = bf16[2,96,512]{2,1,0:T(8,128)(2,1)S(1)} collective-permute-done((bf16[2,96,512]{2,1,0:T(8,128)(2,1)S(1)}, bf16[2,96,512]{2,1,0:T(8,128)(2,1)S(1)}, u32[]{:S(2)}, u32[]{:S(2)}) %collective-permute-start.3) | collective-permute-done | bytes 196640 | tf_op jit(solution)/shard_map/ppermute | solution.py:299
  52.6 5.3 %collective-permute-done.4.second_ref = bf16[2,96,512]{2,1,0:T(8,128)(2,1)S(1)} collective-permute-done((bf16[2,96,512]{2,1,0:T(8,128)(2,1)S(1)}, bf16[2,96,512]{2,1,0:T(8,128)(2,1)S(1)}, u32[]{:S(2)}, u32[]{:S(2)}) %collective-permute-start.4) | collective-permute-done | bytes 196640 | tf_op jit(solution)/shard_map/ppermute | solution.py:299
  58.6 7.1 %shard_map.139 = bf16[4,96,512]{2,1,0:T(8,128)(2,1)} custom-call(s32[7]{0:T(128)} %count_ref.3, s32[112]{0:T(128)} %dest_ref.3, s32[112]{0:T(128)} %source_ref.3, bf16[112,128,128]{2,1,0:T(8,128)(2,1)} %tiles_hbm.3, s32[1,512]{1,0:T(1,128)} %bitcast.20, bf16[96,512]{1,0:T(8,128)(2,1)} %copy-done.4, bf16[96,512]{1,0:T(8,128)(2,1)} %bitcast.13, ...), custom_call_target="tpu_custom_call" | custom-call | flops 469762048 | bytes 3670016 | tf_op jit(solution)/shard_map/pallas_call | solution.py:357
  65.7 6.8 %all-to-all-start.1 = ((bf16[4,96,512]{2,1,0:T(8,128)(2,1)}), bf16[4,96,512]{2,1,0:T(8,128)(2,1)S(1)}, u32[]{:S(2)}, u32[]{:S(2)}) async-start(bf16[4,96,512]{2,1,0:T(8,128)(2,1)} %shard_map.139), calls=%async_computation.1 | async-start | bytes 786432 | tf_op jit(solution)/shard_map/all_to_all | solution.py:328
  72.5 2.8 %collective-permute-start = (bf16[4,192,512]{2,1,0:T(8,128)(2,1)S(1)}, bf16[4,192,512]{2,1,0:T(8,128)(2,1)S(1)}, u32[]{:S(2)}, u32[]{:S(2)}) collective-permute-start(bf16[4,192,512]{2,1,0:T(8,128)(2,1)S(1)} %all-to-all-done.refs_0_), channel_id=1, source_target_pairs={{0,1},{1,0},{2,3},{3,2},{4,5},{5,4},{6,7},{7,6},{8,9},{9,8},{10,11... | collective-permute-start | bytes 2359304 | tf_op jit(solution)/shard_map/ppermute | solution.py:352
  75.4 14.6 %all-to-all-done.1.refs_2_ = bf16[4,96,512]{2,1,0:T(8,128)(2,1)S(1)} async-done(((bf16[4,96,512]{2,1,0:T(8,128)(2,1)}), bf16[4,96,512]{2,1,0:T(8,128)(2,1)S(1)}, u32[]{:S(2)}, u32[]{:S(2)}) %all-to-all-start.1) | async-done | bytes 393248 | tf_op jit(solution)/shard_map/all_to_all | solution.py:328
  89.9 3.7 %collective-permute-start.5 = (bf16[4,96,512]{2,1,0:T(8,128)(2,1)S(1)}, bf16[4,96,512]{2,1,0:T(8,128)(2,1)S(1)}, u32[]{:S(2)}, u32[]{:S(2)}) collective-permute-start(bf16[4,96,512]{2,1,0:T(8,128)(2,1)S(1)} %all-to-all-done.1.refs_2_), channel_id=1, source_target_pairs={{0,1},{1,0},{2,3},{3,2},{4,5},{5,4},{6,7},{7,6},{8,9},{9,8},{10,11... | collective-permute-start | bytes 1179656 | tf_op jit(solution)/shard_map/ppermute | solution.py:371
  96.0 8.5 %shard_map.140 = (bf16[512,128]{1,0:T(8,128)(2,1)}, bf16[128,512]{1,0:T(8,128)(2,1)}, bf16[96,16,128]{2,1,0:T(8,128)(2,1)}, f32[8,128]{1,0:T(8,128)}, bf16[768,1...) custom-call(s32[1]{0:T(128)} %bitcast.core_ref, ...), custom_call_target="tpu_custom_call" | custom-call | flops 939524096 | bytes 3670016 | tf_op jit(solution)/shard_map/pallas_call | solution.py:377
  107.2 12.9 %all-to-all-start.2 = ((bf16[96,24,128]{2,1,0:T(8,128)(2,1)}), bf16[96,24,128]{2,1,0:T(8,128)(2,1)S(1)}, u32[]{:S(2)}, u32[]{:S(2)}) async-start(bf16[96,24,128]{2,1,0:T(8,128)(2,1)} %pad_maximum_fusion), calls=%async_computation.2 | async-start | bytes 1179648 | tf_op jit(solution)/shard_map/all_to_all | solution.py:426
  120.2 2.7 %collective-permute-start.6 = (bf16[2,128,512]{2,1,0:T(8,128)(2,1)S(1)}, bf16[2,128,512]{2,1,0:T(8,128)(2,1)S(1)}, u32[]{:S(2)}, u32[]{:S(2)}) collective-permute-start(bf16[2,128,512]{2,1,0:T(8,128)(2,1)S(1)} %copy-done.17), channel_id=1, source_target_pairs={{0,8},{8,16},{16,0},{24,32},{32,40},{40,24},{48,56},{56,64},{64,48... | collective-permute-start | bytes 786440 | tf_op jit(solution)/shard_map/ppermute | solution.py:299
  122.9 3.5 %collective-permute-start.7 = (bf16[2,128,512]{2,1,0:T(8,128)(2,1)S(1)}, bf16[2,128,512]{2,1,0:T(8,128)(2,1)S(1)}, u32[]{:S(2)}, u32[]{:S(2)}) collective-permute-start(bf16[2,128,512]{2,1,0:T(8,128)(2,1)S(1)} %copy-done.16), channel_id=1, source_target_pairs={{0,16},{8,0},{16,8},{24,40},{32,24},{40,32},{48,64},{56,48},{64,56... | collective-permute-start | bytes 786440 | tf_op jit(solution)/shard_map/ppermute | solution.py:299
  126.4 9.2 %collective-permute-done.6.first_ref = bf16[2,128,512]{2,1,0:T(8,128)(2,1)S(1)} collective-permute-done((bf16[2,128,512]{2,1,0:T(8,128)(2,1)S(1)}, bf16[2,128,512]{2,1,0:T(8,128)(2,1)S(1)}, u32[]{:S(2)}, u32[]{:S(2)}) %collective-permute-start.6) | collective-permute-done | bytes 262176 | tf_op jit(solution)/shard_map/ppermute | solution.py:299
  135.6 5.0 %collective-permute-done.7.second_ref = bf16[2,128,512]{2,1,0:T(8,128)(2,1)S(1)} collective-permute-done((bf16[2,128,512]{2,1,0:T(8,128)(2,1)S(1)}, bf16[2,128,512]{2,1,0:T(8,128)(2,1)S(1)}, u32[]{:S(2)}, u32[]{:S(2)}) %collective-permute-start.7) | collective-permute-done | bytes 262176 | tf_op jit(solution)/shard_map/ppermute | solution.py:299
  140.8 3.1 %collective-permute-start.8 = (bf16[128,512]{1,0:T(8,128)(2,1)S(1)}, bf16[128,512]{1,0:T(8,128)(2,1)S(1)}, u32[]{:S(2)}, u32[]{:S(2)}) collective-permute-start(bf16[128,512]{1,0:T(8,128)(2,1)S(1)} %get-tuple-element.34), channel_id=1, source_target_pairs={{0,24},{8,32},{16,40},{24,48},{32,56},{40,64},{48,72},{56,80},{64,... | collective-permute-start | bytes 393224 | tf_op jit(solution)/shard_map/ppermute | solution.py:291
  143.9 5.8 %collective-permute-start.9 = (bf16[128,512]{1,0:T(8,128)(2,1)S(1)}, bf16[128,512]{1,0:T(8,128)(2,1)S(1)}, u32[]{:S(2)}, u32[]{:S(2)}) collective-permute-start(bf16[128,512]{1,0:T(8,128)(2,1)S(1)} %get-tuple-element.35), channel_id=1, source_target_pairs={{0,744},{8,752},{16,760},{24,0},{32,8},{40,16},{48,24},{56,32},{64... | collective-permute-start | bytes 393224 | tf_op jit(solution)/shard_map/ppermute | solution.py:291
  152.2 4.0 %collective-permute-start.10 = (bf16[384,512]{1,0:T(8,128)(2,1)S(1)}, bf16[384,512]{1,0:T(8,128)(2,1)S(1)}, u32[]{:S(2)}, u32[]{:S(2)}) collective-permute-start(bf16[384,512]{1,0:T(8,128)(2,1)S(1)} %get-tuple-element.40), channel_id=1, source_target_pairs={{0,1},{1,0},{2,3},{3,2},{4,5},{5,4},{6,7},{7,6},{8,9},{9,8},{10,11... | collective-permute-start | bytes 1179656 | tf_op jit(solution)/shard_map/ppermute | solution.py:456
  158.5 18.9 %all-to-all-start.3 = ((bf16[96,16,128]{2,1,0:T(8,128)(2,1)}), bf16[96,16,128]{2,1,0:T(8,128)(2,1)S(1)}, u32[]{:S(2)}, u32[]{:S(2)}) async-start(bf16[96,16,128]{2,1,0:T(8,128)(2,1)} %shard_map.144), calls=%async_computation.3 | async-start | bytes 786432 | tf_op jit(solution)/shard_map/all_to_all | solution.py:478
  177.3 3.4 %collective-permute-start.11 = (bf16[96,512]{1,0:T(8,128)(2,1)S(1)}, bf16[96,512]{1,0:T(8,128)(2,1)S(1)}, u32[]{:S(2)}, u32[]{:S(2)}) collective-permute-start(bf16[96,512]{1,0:T(8,128)(2,1)S(1)} %get-tuple-element.42), channel_id=1, source_target_pairs={{0,2},{1,3},{2,4},{3,5},{4,6},{5,7},{6,0},{7,1},{8,10},{9,11},{10,... | collective-permute-start | bytes 294920 | tf_op jit(solution)/shard_map/ppermute | solution.py:332
  180.7 6.5 %collective-permute-start.12 = (bf16[96,512]{1,0:T(8,128)(2,1)S(1)}, bf16[96,512]{1,0:T(8,128)(2,1)S(1)}, u32[]{:S(2)}, u32[]{:S(2)}) collective-permute-start(bf16[96,512]{1,0:T(8,128)(2,1)S(1)} %get-tuple-element.43), channel_id=1, source_target_pairs={{0,4},{1,5},{2,6},{3,7},{4,0},{5,1},{6,2},{7,3},{8,12},{9,13},{10,... | collective-permute-start | bytes 294920 | tf_op jit(solution)/shard_map/ppermute | solution.py:332
  192.7 6.1 %collective-permute-done.13 = bf16[96,512]{1,0:T(8,128)(2,1)S(1)} collective-permute-done((bf16[96,512]{1,0:T(8,128)(2,1)S(1)}, bf16[96,512]{1,0:T(8,128)(2,1)S(1)}, u32[]{:S(2)}, u32[]{:S(2)}) %collective-permute-start.13) | collective-permute-done | bytes 98336 | tf_op jit(solution)/shard_map/ppermute | solution.py:332
  (66 shorter events, 25.9 us)
Async XLA Ops:
  4.4 61.3 %all-to-all-start = ((bf16[4,192,512]{2,1,0:T(8,128)(2,1)}), bf16[4,192,512]{2,1,0:T(8,128)(2,1)S(1)}, u32[]{:S(2)}, u32[]{:S(2)}) async-start(bf16[4,192,512]{2,1,0:T(8,128)(2,1)} %shard_map.137), calls=%async_computation | async-start | bytes 1572864 | tf_op jit(solution)/shard_map/all_to_all | solution.py:328
  19.4 9.2 %collective-permute-start.2 = (bf16[96,512]{1,0:T(8,128)(2,1)S(1)}, bf16[96,512]{1,0:T(8,128)(2,1)S(1)}, u32[]{:S(2)}, u32[]{:S(2)}) collective-permute-start(bf16[96,512]{1,0:T(8,128)(2,1)S(1)} %bitcast.15), channel_id=1, source_target_pairs={{0,744},{8,752},{16,760},{24,0},{32,8},{40,16},{48,24},{56,32},{64... | collective-permute-start | bytes 294920 | tf_op jit(solution)/shard_map/ppermute | solution.py:291
  26.7 9.0 %collective-permute-start.1 = (bf16[96,512]{1,0:T(8,128)(2,1)S(1)}, bf16[96,512]{1,0:T(8,128)(2,1)S(1)}, u32[]{:S(2)}, u32[]{:S(2)}) collective-permute-start(bf16[96,512]{1,0:T(8,128)(2,1)S(1)} %bitcast.16), channel_id=1, source_target_pairs={{0,24},{8,32},{16,40},{24,48},{32,56},{40,64},{48,72},{56,80},{64,... | collective-permute-start | bytes 294920 | tf_op jit(solution)/shard_map/ppermute | solution.py:291
  28.7 29.2 %copy-start.3 = (bf16[96,512]{1,0:T(8,128)(2,1)}, bf16[96,512]{1,0:T(8,128)(2,1)S(1)}, u32[]{:S(2)}) copy-start(bf16[96,512]{1,0:T(8,128)(2,1)S(1)} %collective-permute-done.2.above_ref) | copy-start | bytes 294916
  35.7 16.8 %collective-permute-start.3 = (bf16[2,96,512]{2,1,0:T(8,128)(2,1)S(1)}, bf16[2,96,512]{2,1,0:T(8,128)(2,1)S(1)}, u32[]{:S(2)}, u32[]{:S(2)}) collective-permute-start(bf16[2,96,512]{2,1,0:T(8,128)(2,1)S(1)} %get-tuple-element.27), channel_id=1, source_target_pairs={{0,16},{8,0},{16,8},{24,40},{32,24},{40,32},{48,64},{56,48},{64,56... | collective-permute-start | bytes 589832 | tf_op jit(solution)/shard_map/ppermute | solution.py:299
  39.0 18.9 %collective-permute-start.4 = (bf16[2,96,512]{2,1,0:T(8,128)(2,1)S(1)}, bf16[2,96,512]{2,1,0:T(8,128)(2,1)S(1)}, u32[]{:S(2)}, u32[]{:S(2)}) collective-permute-start(bf16[2,96,512]{2,1,0:T(8,128)(2,1)S(1)} %get-tuple-element.28), channel_id=1, source_target_pairs={{0,8},{8,16},{16,0},{24,32},{32,40},{40,24},{48,56},{56,64},{64,48... | collective-permute-start | bytes 589832 | tf_op jit(solution)/shard_map/ppermute | solution.py:299
  65.7 24.2 %all-to-all-start.1 = ((bf16[4,96,512]{2,1,0:T(8,128)(2,1)}), bf16[4,96,512]{2,1,0:T(8,128)(2,1)S(1)}, u32[]{:S(2)}, u32[]{:S(2)}) async-start(bf16[4,96,512]{2,1,0:T(8,128)(2,1)} %shard_map.139), calls=%async_computation.1 | async-start | bytes 786432 | tf_op jit(solution)/shard_map/all_to_all | solution.py:328
  72.5 22.4 %collective-permute-start = (bf16[4,192,512]{2,1,0:T(8,128)(2,1)S(1)}, bf16[4,192,512]{2,1,0:T(8,128)(2,1)S(1)}, u32[]{:S(2)}, u32[]{:S(2)}) collective-permute-start(bf16[4,192,512]{2,1,0:T(8,128)(2,1)S(1)} %all-to-all-done.refs_0_), channel_id=1, source_target_pairs={{0,1},{1,0},{2,3},{3,2},{4,5},{5,4},{6,7},{7,6},{8,9},{9,8},{10,11... | collective-permute-start | bytes 2359304 | tf_op jit(solution)/shard_map/ppermute | solution.py:352
  89.9 5.0 %collective-permute-start.5 = (bf16[4,96,512]{2,1,0:T(8,128)(2,1)S(1)}, bf16[4,96,512]{2,1,0:T(8,128)(2,1)S(1)}, u32[]{:S(2)}, u32[]{:S(2)}) collective-permute-start(bf16[4,96,512]{2,1,0:T(8,128)(2,1)S(1)} %all-to-all-done.1.refs_2_), channel_id=1, source_target_pairs={{0,1},{1,0},{2,3},{3,2},{4,5},{5,4},{6,7},{7,6},{8,9},{9,8},{10,11... | collective-permute-start | bytes 1179656 | tf_op jit(solution)/shard_map/ppermute | solution.py:371
  105.2 35.4 %copy-start.2 = (f32[3,128,512]{2,1,0:T(8,128)S(1)}, f32[3,128,512]{2,1,0:T(8,128)}, u32[]{:S(2)}) copy-start(f32[3,128,512]{2,1,0:T(8,128)} %get-tuple-element.30.level_ref) | copy-start | bytes 2359300
  107.2 44.4 %copy-start.7 = (bf16[768,128]{1,0:T(8,128)(2,1)S(1)}, bf16[768,128]{1,0:T(8,128)(2,1)}, u32[]{:S(2)}) copy-start(bf16[768,128]{1,0:T(8,128)(2,1)} %get-tuple-element.37.self_ref) | copy-start | bytes 589828
  107.2 44.4 %copy-start.8 = (bf16[768,128]{1,0:T(8,128)(2,1)S(1)}, bf16[768,128]{1,0:T(8,128)(2,1)}, u32[]{:S(2)}) copy-start(bf16[768,128]{1,0:T(8,128)(2,1)} %get-tuple-element.38.neighbour_ref) | copy-start | bytes 589828
  107.2 44.4 %copy-start.9 = (bf16[128,512]{1,0:T(8,128)(2,1)S(1)}, bf16[128,512]{1,0:T(8,128)(2,1)}, u32[]{:S(2)}) copy-start(bf16[128,512]{1,0:T(8,128)(2,1)} %get-tuple-element.36.grad_ref) | copy-start | bytes 393220
  107.2 49.0 %all-to-all-start.2 = ((bf16[96,24,128]{2,1,0:T(8,128)(2,1)}), bf16[96,24,128]{2,1,0:T(8,128)(2,1)S(1)}, u32[]{:S(2)}, u32[]{:S(2)}) async-start(bf16[96,24,128]{2,1,0:T(8,128)(2,1)} %pad_maximum_fusion), calls=%async_computation.2 | async-start | bytes 1179648 | tf_op jit(solution)/shard_map/all_to_all | solution.py:426
  120.2 15.4 %collective-permute-start.6 = (bf16[2,128,512]{2,1,0:T(8,128)(2,1)S(1)}, bf16[2,128,512]{2,1,0:T(8,128)(2,1)S(1)}, u32[]{:S(2)}, u32[]{:S(2)}) collective-permute-start(bf16[2,128,512]{2,1,0:T(8,128)(2,1)S(1)} %copy-done.17), channel_id=1, source_target_pairs={{0,8},{8,16},{16,0},{24,32},{32,40},{40,24},{48,56},{56,64},{64,48... | collective-permute-start | bytes 786440 | tf_op jit(solution)/shard_map/ppermute | solution.py:299
  122.9 17.7 %collective-permute-start.7 = (bf16[2,128,512]{2,1,0:T(8,128)(2,1)S(1)}, bf16[2,128,512]{2,1,0:T(8,128)(2,1)S(1)}, u32[]{:S(2)}, u32[]{:S(2)}) collective-permute-start(bf16[2,128,512]{2,1,0:T(8,128)(2,1)S(1)} %copy-done.16), channel_id=1, source_target_pairs={{0,16},{8,0},{16,8},{24,40},{32,24},{40,32},{48,64},{56,48},{64,56... | collective-permute-start | bytes 786440 | tf_op jit(solution)/shard_map/ppermute | solution.py:299
  140.8 9.3 %collective-permute-start.8 = (bf16[128,512]{1,0:T(8,128)(2,1)S(1)}, bf16[128,512]{1,0:T(8,128)(2,1)S(1)}, u32[]{:S(2)}, u32[]{:S(2)}) collective-permute-start(bf16[128,512]{1,0:T(8,128)(2,1)S(1)} %get-tuple-element.34), channel_id=1, source_target_pairs={{0,24},{8,32},{16,40},{24,48},{32,56},{40,64},{48,72},{56,80},{64,... | collective-permute-start | bytes 393224 | tf_op jit(solution)/shard_map/ppermute | solution.py:291
  143.9 7.7 %collective-permute-start.9 = (bf16[128,512]{1,0:T(8,128)(2,1)S(1)}, bf16[128,512]{1,0:T(8,128)(2,1)S(1)}, u32[]{:S(2)}, u32[]{:S(2)}) collective-permute-start(bf16[128,512]{1,0:T(8,128)(2,1)S(1)} %get-tuple-element.35), channel_id=1, source_target_pairs={{0,744},{8,752},{16,760},{24,0},{32,8},{40,16},{48,24},{56,32},{64... | collective-permute-start | bytes 393224 | tf_op jit(solution)/shard_map/ppermute | solution.py:291
  152.2 5.3 %collective-permute-start.10 = (bf16[384,512]{1,0:T(8,128)(2,1)S(1)}, bf16[384,512]{1,0:T(8,128)(2,1)S(1)}, u32[]{:S(2)}, u32[]{:S(2)}) collective-permute-start(bf16[384,512]{1,0:T(8,128)(2,1)S(1)} %get-tuple-element.40), channel_id=1, source_target_pairs={{0,1},{1,0},{2,3},{3,2},{4,5},{5,4},{6,7},{7,6},{8,9},{9,8},{10,11... | collective-permute-start | bytes 1179656 | tf_op jit(solution)/shard_map/ppermute | solution.py:456
  156.4 1.3 collective-permute-start.14
  158.5 41.6 %all-to-all-start.3 = ((bf16[96,16,128]{2,1,0:T(8,128)(2,1)}), bf16[96,16,128]{2,1,0:T(8,128)(2,1)S(1)}, u32[]{:S(2)}, u32[]{:S(2)}) async-start(bf16[96,16,128]{2,1,0:T(8,128)(2,1)} %shard_map.144), calls=%async_computation.3 | async-start | bytes 786432 | tf_op jit(solution)/shard_map/all_to_all | solution.py:478
  177.3 12.7 %collective-permute-start.11 = (bf16[96,512]{1,0:T(8,128)(2,1)S(1)}, bf16[96,512]{1,0:T(8,128)(2,1)S(1)}, u32[]{:S(2)}, u32[]{:S(2)}) collective-permute-start(bf16[96,512]{1,0:T(8,128)(2,1)S(1)} %get-tuple-element.42), channel_id=1, source_target_pairs={{0,2},{1,3},{2,4},{3,5},{4,6},{5,7},{6,0},{7,1},{8,10},{9,11},{10,... | collective-permute-start | bytes 294920 | tf_op jit(solution)/shard_map/ppermute | solution.py:332
  180.7 12.0 %collective-permute-start.12 = (bf16[96,512]{1,0:T(8,128)(2,1)S(1)}, bf16[96,512]{1,0:T(8,128)(2,1)S(1)}, u32[]{:S(2)}, u32[]{:S(2)}) collective-permute-start(bf16[96,512]{1,0:T(8,128)(2,1)S(1)} %get-tuple-element.43), channel_id=1, source_target_pairs={{0,4},{1,5},{2,6},{3,7},{4,0},{5,1},{6,2},{7,3},{8,12},{9,13},{10,... | collective-permute-start | bytes 294920 | tf_op jit(solution)/shard_map/ppermute | solution.py:332
  187.2 11.6 %collective-permute-start.13 = (bf16[96,512]{1,0:T(8,128)(2,1)S(1)}, bf16[96,512]{1,0:T(8,128)(2,1)S(1)}, u32[]{:S(2)}, u32[]{:S(2)}) collective-permute-start(bf16[96,512]{1,0:T(8,128)(2,1)S(1)} %get-tuple-element.44), channel_id=1, source_target_pairs={{0,6},{1,7},{2,0},{3,1},{4,2},{5,3},{6,4},{7,5},{8,14},{9,15},{10,... | collective-permute-start | bytes 294920 | tf_op jit(solution)/shard_map/ppermute | solution.py:332
  (13 other events, 115.7 us)

commit v9 on v5

--- a/solution.py
+++ b/solution.py
@@ -227,10 +227,8 @@
         out[...] = value.astype(out.dtype)
 
 
-def chip_kernel(stack_ref, keep_ref, got_ref, *outs):
-    for at, out in enumerate(outs):
-        piece = (stack_ref[0] + at) % len(outs)
-        out[...] = (keep_ref[piece] + got_ref[piece].astype(F32)).astype(out.dtype)
+def chip_kernel(keep_ref, got_ref, out_ref):
+    out_ref[...] = (keep_ref[...] + got_ref[...].astype(F32)).astype(BF16)
 
 
 def planes_kernel(got_ref, out_ref):
@@ -325,10 +323,6 @@
     def over_stacks(value):
         return lax.all_to_all(value, "feat", 0, 0, axis_index_groups=same_core)
 
-    def to_stack(value, steps):
-        pairs = [(f, (f + steps * CORES) % feats) for f in range(feats)]
-        return lax.ppermute(value, "feat", pairs)
-
     turned = features.T
     level, packed = call(
         pack_kernel,
@@ -340,6 +334,7 @@
         [],
         0,
         6 * stacks * width * node_dev,
+        limit=TILES_VMEM_BYTES,
     )(
         turned,
         turned_in_trio(turned, -1),
@@ -486,22 +481,16 @@
         4 * half * node_dev,
     )(own, first, second, grad_turned, weight_self, weight_neighbour)
     got = lax.ppermute(send, "feat", other_core)
-    part = jax.ShapeDtypeStruct((width, node_dev), BF16)
-    parts = call(
+    chip_sum = call(
         chip_kernel,
-        [SMEM] + [VMEM] * 2,
-        [jax.ShapeDtypeStruct(part.shape, F32)] + [part] * (stacks - 1),
+        [VMEM] * 2,
+        jax.ShapeDtypeStruct((half, node_dev), BF16),
         [],
-        4 * half * node_dev,
+        half * node_dev,
         8 * half * node_dev,
-    )(
-        stack,
-        keep.reshape(stacks, width, node_dev),
-        got.reshape(stacks, width, node_dev),
-    )
-    grad_turned = parts[0]
-    for steps in range(1, stacks):
-        grad_turned = grad_turned + to_stack(parts[steps], steps).astype(F32)
+    )(keep, got)
+    shares = over_stacks(chip_sum.reshape(stacks, width, node_dev))
+    grad_turned = jnp.sum(shares.astype(F32), axis=0)
     return (activations, grad_turned.astype(BF16).T, grad_self, grad_neighbour, bias_sum[0])
 
 

time: 191 us -> 214 us (1.12)
  the two profiles are of different devices: /device:TPU:72 before, /device:TPU:1 now
where the time goes in v9:
time: 214 us; the launch traced here: 212 us
  starting transfers between devices  105 us (49%)
  waiting for transfers between devices  47.5 us (22%)
  blocking collectives  30.8 us (14%)
  Pallas kernels  18 us (8%)
  local copies, waits for them, and re-layouts  8.22 us (4%)
    all_to_all x2, starting transfers between devices, over_stacks(): return lax.all_to_all(value, 'feat', 0, 0, axis_index_groups=same_core)  23.1 us
    all_to_all x1, blocking collectives, over_stacks(): return lax.all_to_all(value, 'feat', 0, 0, axis_index_groups=same_core)  20.6 us
    ppermute x4, waiting for transfers between devices, shifted(): return lax.ppermute(value, 'rows', pairs)  19.9 us
    ppermute x4, starting transfers between devices, shifted(): return lax.ppermute(value, 'rows', pairs)  17.8 us
    ppermute x4, starting transfers between devices, turned_in_trio(): return lax.ppermute(value, 'rows', pairs)  14.7 us
    ppermute x1, starting transfers between devices, on_device(): aggregate_far = lax.ppermute(aggregate_own, 'feat', other_core)  12.6 us
    all_to_all x1, starting transfers between devices, on_device(): lax.all_to_all(jnp.broadcast_to(piece[None], (COLUMN,) + piece.shape), 'r...  12.3 us
    all_to_all x1, starting transfers between devices, on_device(): lax.all_to_all(jnp.broadcast_to(pieces[None], (planes,) + pieces.shape),...  11.7 us
  transfers between devices with their start and end apart: 17, of which 11 were waited for; matrix products, arithmetic and copies ran while one was open for 1% of the time, Pallas kernels for 3%

profile of v9, /device:TPU:1, one launch (start us, length us, event | category | flops | bytes accessed | tf_op | source)
XLA Modules:
  0.0 211.5 jit_solution(10987909921382263144)
XLA Ops:
  0.6 4.8 %collective-permute-start.1 = (bf16[96,512]{1,0:T(8,128)(2,1)}, bf16[96,512]{1,0:T(8,128)(2,1)S(1)}, u32[]{:S(2)}, u32[]{:S(2)}) collective-permute-start(bf16[96,512]{1,0:T(8,128)(2,1)} %bitcast.13), channel_id=1, source_target_pairs={{0,8},{8,16},{16,0},{24,32},{32,40},{40,24},{48,56},{56,64},{64,48... | collective-permute-start | bytes 294920 | tf_op jit(solution)/shard_map/ppermute | solution.py:290
  5.5 3.7 %collective-permute-start = (bf16[96,512]{1,0:T(8,128)(2,1)}, bf16[96,512]{1,0:T(8,128)(2,1)S(1)}, u32[]{:S(2)}, u32[]{:S(2)}) collective-permute-start(bf16[96,512]{1,0:T(8,128)(2,1)} %bitcast.14), channel_id=1, source_target_pairs={{0,16},{8,0},{16,8},{24,40},{32,24},{40,32},{48,64},{56,48},{64,56... | collective-permute-start | bytes 294920 | tf_op jit(solution)/shard_map/ppermute | solution.py:290
  14.5 14.3 %all-to-all-start = ((bf16[4,192,512]{2,1,0:T(8,128)(2,1)}), bf16[4,192,512]{2,1,0:T(8,128)(2,1)S(1)}, u32[]{:S(2)}, u32[]{:S(2)}) async-start(bf16[4,192,512]{2,1,0:T(8,128)(2,1)} %get-tuple-element.24), calls=%async_computation | async-start | bytes 1572864 | tf_op jit(solution)/shard_map/all_to_all | solution.py:324
  28.9 7.3 %collective-permute-start.4 = (bf16[3,96,512]{2,1,0:T(8,128)(2,1)}, bf16[3,96,512]{2,1,0:T(8,128)(2,1)S(1)}, u32[]{:S(2)}, u32[]{:S(2)}) collective-permute-start(bf16[3,96,512]{2,1,0:T(8,128)(2,1)} %get-tuple-element.25.level_ref), channel_id=1, source_target_pairs={{0,744},{8,752},{16,760},{24,0},{32,8},{40,16},{48,24},{56,32},{64... | collective-permute-start | bytes 884744 | tf_op jit(solution)/shard_map/ppermute | solution.py:282
  38.1 3.1 %collective-permute-done.4.above_ref = bf16[3,96,512]{2,1,0:T(8,128)(2,1)S(1)} collective-permute-done((bf16[3,96,512]{2,1,0:T(8,128)(2,1)}, bf16[3,96,512]{2,1,0:T(8,128)(2,1)S(1)}, u32[]{:S(2)}, u32[]{:S(2)}) %collective-permute-start.4) | collective-permute-done | bytes 294944 | tf_op jit(solution)/shard_map/ppermute | solution.py:282
  41.2 7.0 %collective-permute-done.3.below_ref = bf16[3,96,512]{2,1,0:T(8,128)(2,1)S(1)} collective-permute-done((bf16[3,96,512]{2,1,0:T(8,128)(2,1)}, bf16[3,96,512]{2,1,0:T(8,128)(2,1)S(1)}, u32[]{:S(2)}, u32[]{:S(2)}) %collective-permute-start.3) | collective-permute-done | bytes 294944 | tf_op jit(solution)/shard_map/ppermute | solution.py:282
  49.0 6.1 %shard_map.138 = bf16[4,96,512]{2,1,0:T(8,128)(2,1)} custom-call(s32[1]{0:T(128)} %bitcast.place_ref, s32[7]{0:T(128)} %count_ref.3, s32[112]{0:T(128)} %dest_ref.3, s32[112]{0:T(128)} %source_ref.3, bf16[112,128,128]{2,1,0:T(8,128)(2,1)} %tiles_hbm.3, s32[1,512]{1,0:T(1,128)} %bitcast.16, bf16[3,96,512]{2,1,0:T(8,128)(2,1)} %copy-done.9, ...), custom_call_target="tpu_custom_call" | custom-call | flops 469762048 | bytes 3670016 | tf_op jit(solution)/shard_map/pallas_call | solution.py:353
  55.1 8.8 %all-to-all-start.1 = ((bf16[4,96,512]{2,1,0:T(8,128)(2,1)}), bf16[4,96,512]{2,1,0:T(8,128)(2,1)S(1)}, u32[]{:S(2)}, u32[]{:S(2)}) async-start(bf16[4,96,512]{2,1,0:T(8,128)(2,1)} %shard_map.138), calls=%async_computation.1 | async-start | bytes 786432 | tf_op jit(solution)/shard_map/all_to_all | solution.py:324
  63.9 5.2 %collective-permute-start.2 = (bf16[4,192,512]{2,1,0:T(8,128)(2,1)S(1)}, bf16[4,192,512]{2,1,0:T(8,128)(2,1)S(1)}, u32[]{:S(2)}, u32[]{:S(2)}) collective-permute-start(bf16[4,192,512]{2,1,0:T(8,128)(2,1)S(1)} %all-to-all-done.refs_0_), channel_id=1, source_target_pairs={{0,1},{1,0},{2,3},{3,2},{4,5},{5,4},{6,7},{7,6},{8,9},{9,8},{10,11... | collective-permute-start | bytes 2359304 | tf_op jit(solution)/shard_map/ppermute | solution.py:348
  69.1 6.1 %all-to-all-done.1.refs_2_ = bf16[4,96,512]{2,1,0:T(8,128)(2,1)S(1)} async-done(((bf16[4,96,512]{2,1,0:T(8,128)(2,1)}), bf16[4,96,512]{2,1,0:T(8,128)(2,1)S(1)}, u32[]{:S(2)}, u32[]{:S(2)}) %all-to-all-start.1) | async-done | bytes 393248 | tf_op jit(solution)/shard_map/all_to_all | solution.py:324
  75.3 12.6 %collective-permute-start.5 = (bf16[4,96,512]{2,1,0:T(8,128)(2,1)S(1)}, bf16[4,96,512]{2,1,0:T(8,128)(2,1)S(1)}, u32[]{:S(2)}, u32[]{:S(2)}) collective-permute-start(bf16[4,96,512]{2,1,0:T(8,128)(2,1)S(1)} %all-to-all-done.1.refs_2_), channel_id=1, source_target_pairs={{0,1},{1,0},{2,3},{3,2},{4,5},{5,4},{6,7},{7,6},{8,9},{9,8},{10,11... | collective-permute-start | bytes 1179656 | tf_op jit(solution)/shard_map/ppermute | solution.py:368
  90.3 7.9 %shard_map.139 = (bf16[512,128]{1,0:T(8,128)(2,1)}, bf16[128,512]{1,0:T(8,128)(2,1)}, bf16[12,9,16,128]{3,2,1,0:T(8,128)(2,1)}, bf16[768,128]{1,0:T(8,128)(2,1)}...) custom-call(s32[1]{0:T(128)} %bitcast.place_ref, ...), custom_call_target="tpu_custom_call" | custom-call | flops 939524096 | bytes 3670016 | tf_op jit(solution)/shard_map/pallas_call | solution.py:376
  98.2 3.6 %all-to-all-start.3 = ((bf16[12,9,16,128]{3,2,1,0:T(8,128)(2,1)}), bf16[12,9,16,128]{3,2,1,0:T(8,128)(2,1)S(1)}, u32[]{:S(2)}, u32[]{:S(2)}) async-start(bf16[12,9,16,128]{3,2,1,0:T(8,128)(2,1)} %get-tuple-element.38), calls=%async_computation.3 | async-start | bytes 884736 | tf_op jit(solution)/shard_map/all_to_all | solution.py:425
  104.8 5.6 %collective-permute-start.7 = (bf16[3,128,512]{2,1,0:T(8,128)(2,1)}, bf16[3,128,512]{2,1,0:T(8,128)(2,1)S(1)}, u32[]{:S(2)}, u32[]{:S(2)}) collective-permute-start(bf16[3,128,512]{2,1,0:T(8,128)(2,1)} %get-tuple-element.29), channel_id=1, source_target_pairs={{0,744},{8,752},{16,760},{24,0},{32,8},{40,16},{48,24},{56,32},{64... | collective-permute-start | bytes 1179656 | tf_op jit(solution)/shard_map/ppermute | solution.py:282
  110.4 9.7 %collective-permute-done.6.below_ref = bf16[3,128,512]{2,1,0:T(8,128)(2,1)S(1)} collective-permute-done((bf16[3,128,512]{2,1,0:T(8,128)(2,1)}, bf16[3,128,512]{2,1,0:T(8,128)(2,1)S(1)}, u32[]{:S(2)}, u32[]{:S(2)}) %collective-permute-start.6) | collective-permute-done | bytes 393248 | tf_op jit(solution)/shard_map/ppermute | solution.py:282
  123.8 3.8 %collective-permute-start.9 = (bf16[128,512]{1,0:T(8,128)(2,1)S(1)}, bf16[128,512]{1,0:T(8,128)(2,1)S(1)}, u32[]{:S(2)}, u32[]{:S(2)}) collective-permute-start(bf16[128,512]{1,0:T(8,128)(2,1)S(1)} %get-tuple-element.32), channel_id=1, source_target_pairs={{0,16},{8,0},{16,8},{24,40},{32,24},{40,32},{48,64},{56,48},{64,56... | collective-permute-start | bytes 393224 | tf_op jit(solution)/shard_map/ppermute | solution.py:290
  128.0 3.3 %collective-permute-done.9.second_ref = bf16[128,512]{1,0:T(8,128)(2,1)S(1)} collective-permute-done((bf16[128,512]{1,0:T(8,128)(2,1)S(1)}, bf16[128,512]{1,0:T(8,128)(2,1)S(1)}, u32[]{:S(2)}, u32[]{:S(2)}) %collective-permute-start.9) | collective-permute-done | bytes 131104 | tf_op jit(solution)/shard_map/ppermute | solution.py:290
  134.7 3.6 %collective-permute-start.10 = (bf16[384,512]{1,0:T(8,128)(2,1)S(1)}, bf16[384,512]{1,0:T(8,128)(2,1)S(1)}, u32[]{:S(2)}, u32[]{:S(2)}) collective-permute-start(bf16[384,512]{1,0:T(8,128)(2,1)S(1)} %get-tuple-element.37), channel_id=1, source_target_pairs={{0,1},{1,0},{2,3},{3,2},{4,5},{5,4},{6,7},{7,6},{8,9},{9,8},{10,11... | collective-permute-start | bytes 1179656 | tf_op jit(solution)/shard_map/ppermute | solution.py:483
  138.3 10.3 %all_to_all.35.got_ref = bf16[8,2,16,128]{3,2,1,0:T(8,128)(2,1)S(1)} all-to-all(bf16[8,2,16,128]{3,2,1,0:T(8,128)(2,1)S(1)} %shard_map.143), channel_id=1, replica_groups={{0,24,48,72,96,120,144,168},{8,32,56,80,104,128,152,176},{16,40,64,88,1..., dimensions={0} | all-to-all | bytes 131072 | tf_op jit(solution)/shard_map/all_to_all | solution.py:435
  149.9 12.3 %all-to-all-start.5 = ((bf16[8,16,128]{2,1,0:T(8,128)(2,1)}), bf16[8,16,128]{2,1,0:T(8,128)(2,1)S(1)}, u32[]{:S(2)}, u32[]{:S(2)}) async-start(bf16[8,16,128]{2,1,0:T(8,128)(2,1)} %broadcast_in_dim.4), calls=%async_computation.5 | async-start | bytes 65536 | tf_op jit(solution)/shard_map/all_to_all | solution.py:442
  162.3 6.8 %all-to-all-done.5 = bf16[8,16,128]{2,1,0:T(8,128)(2,1)S(1)} async-done(((bf16[8,16,128]{2,1,0:T(8,128)(2,1)}), bf16[8,16,128]{2,1,0:T(8,128)(2,1)S(1)}, u32[]{:S(2)}, u32[]{:S(2)}) %all-to-all-start.5) | async-done | bytes 32800 | tf_op jit(solution)/shard_map/all_to_all | solution.py:442
  169.1 20.6 %all_to_all.36 = bf16[4,96,512]{2,1,0:T(8,128)(2,1)S(1)} all-to-all(bf16[4,96,512]{2,1,0:T(8,128)(2,1)S(1)} %bitcast.11), channel_id=1, replica_groups={{0,2,4,6},{1,3,5,7},{8,10,12,14},{9,11,13,15},{16,18,20,22},{17,19,21,2..., dimensions={0} | all-to-all | bytes 786432 | tf_op jit(solution)/shard_map/all_to_all | solution.py:324
  190.5 11.7 %all-to-all-start.6 = ((bf16[12,8,16,128]{3,2,1,0:T(8,128)(2,1)}), bf16[12,8,16,128]{3,2,1,0:T(8,128)(2,1)S(1)}, u32[]{:S(2)}, u32[]{:S(2)}) async-start(bf16[12,8,16,128]{3,2,1,0:T(8,128)(2,1)} %broadcast_in_dim.5), calls=%async_computation.6 | async-start | bytes 786432 | tf_op jit(solution)/shard_map/all_to_all | solution.py:449
  203.5 7.1 %all-to-all-done.6.pieces_ref = bf16[12,8,16,128]{3,2,1,0:T(8,128)(2,1)S(1)} async-done(((bf16[12,8,16,128]{3,2,1,0:T(8,128)(2,1)}), bf16[12,8,16,128]{3,2,1,0:T(8,128)(2,1)S(1)}, u32[]{:S(2)}, u32[]{:S(2)}) %all-to-all-start.6) | async-done | bytes 393248 | tf_op jit(solution)/shard_map/all_to_all | solution.py:449
  (49 shorter events, 25.0 us)
Async XLA Ops:
  0.6 8.8 %collective-permute-start.1 = (bf16[96,512]{1,0:T(8,128)(2,1)}, bf16[96,512]{1,0:T(8,128)(2,1)S(1)}, u32[]{:S(2)}, u32[]{:S(2)}) collective-permute-start(bf16[96,512]{1,0:T(8,128)(2,1)} %bitcast.13), channel_id=1, source_target_pairs={{0,8},{8,16},{16,0},{24,32},{32,40},{40,24},{48,56},{56,64},{64,48... | collective-permute-start | bytes 294920 | tf_op jit(solution)/shard_map/ppermute | solution.py:290
  5.5 6.2 %collective-permute-start = (bf16[96,512]{1,0:T(8,128)(2,1)}, bf16[96,512]{1,0:T(8,128)(2,1)S(1)}, u32[]{:S(2)}, u32[]{:S(2)}) collective-permute-start(bf16[96,512]{1,0:T(8,128)(2,1)} %bitcast.14), channel_id=1, source_target_pairs={{0,16},{8,0},{16,8},{24,40},{32,24},{40,32},{48,64},{56,48},{64,56... | collective-permute-start | bytes 294920 | tf_op jit(solution)/shard_map/ppermute | solution.py:290
  9.5 2.2 %copy-start.10 = (bf16[96,512]{1,0:T(8,128)(2,1)}, bf16[96,512]{1,0:T(8,128)(2,1)S(1)}, u32[]{:S(2)}) copy-start(bf16[96,512]{1,0:T(8,128)(2,1)S(1)} %collective-permute-done.1.second_ref) | copy-start | bytes 294916
  14.5 40.6 %all-to-all-start = ((bf16[4,192,512]{2,1,0:T(8,128)(2,1)}), bf16[4,192,512]{2,1,0:T(8,128)(2,1)S(1)}, u32[]{:S(2)}, u32[]{:S(2)}) async-start(bf16[4,192,512]{2,1,0:T(8,128)(2,1)} %get-tuple-element.24), calls=%async_computation | async-start | bytes 1572864 | tf_op jit(solution)/shard_map/all_to_all | solution.py:324
  28.9 12.3 %collective-permute-start.4 = (bf16[3,96,512]{2,1,0:T(8,128)(2,1)}, bf16[3,96,512]{2,1,0:T(8,128)(2,1)S(1)}, u32[]{:S(2)}, u32[]{:S(2)}) collective-permute-start(bf16[3,96,512]{2,1,0:T(8,128)(2,1)} %get-tuple-element.25.level_ref), channel_id=1, source_target_pairs={{0,744},{8,752},{16,760},{24,0},{32,8},{40,16},{48,24},{56,32},{64... | collective-permute-start | bytes 884744 | tf_op jit(solution)/shard_map/ppermute | solution.py:282
  36.2 12.1 %collective-permute-start.3 = (bf16[3,96,512]{2,1,0:T(8,128)(2,1)}, bf16[3,96,512]{2,1,0:T(8,128)(2,1)S(1)}, u32[]{:S(2)}, u32[]{:S(2)}) collective-permute-start(bf16[3,96,512]{2,1,0:T(8,128)(2,1)} %get-tuple-element.25.level_ref), channel_id=1, source_target_pairs={{0,24},{8,32},{16,40},{24,48},{32,56},{40,64},{48,72},{56,80},{64,... | collective-permute-start | bytes 884744 | tf_op jit(solution)/shard_map/ppermute | solution.py:282
  41.2 7.1 %copy-start.8 = (bf16[3,96,512]{2,1,0:T(8,128)(2,1)}, bf16[3,96,512]{2,1,0:T(8,128)(2,1)S(1)}, u32[]{:S(2)}) copy-start(bf16[3,96,512]{2,1,0:T(8,128)(2,1)S(1)} %collective-permute-done.4.above_ref) | copy-start | bytes 884740
  55.1 34.2 %copy-start.4 = (bf16[4,192,512]{2,1,0:T(8,128)(2,1)}, bf16[4,192,512]{2,1,0:T(8,128)(2,1)S(1)}, u32[]{:S(2)}) copy-start(bf16[4,192,512]{2,1,0:T(8,128)(2,1)S(1)} %all-to-all-done.refs_0_) | copy-start | bytes 2359300
  55.1 20.2 %all-to-all-start.1 = ((bf16[4,96,512]{2,1,0:T(8,128)(2,1)}), bf16[4,96,512]{2,1,0:T(8,128)(2,1)S(1)}, u32[]{:S(2)}, u32[]{:S(2)}) async-start(bf16[4,96,512]{2,1,0:T(8,128)(2,1)} %shard_map.138), calls=%async_computation.1 | async-start | bytes 786432 | tf_op jit(solution)/shard_map/all_to_all | solution.py:324
  63.9 25.4 %collective-permute-start.2 = (bf16[4,192,512]{2,1,0:T(8,128)(2,1)S(1)}, bf16[4,192,512]{2,1,0:T(8,128)(2,1)S(1)}, u32[]{:S(2)}, u32[]{:S(2)}) collective-permute-start(bf16[4,192,512]{2,1,0:T(8,128)(2,1)S(1)} %all-to-all-done.refs_0_), channel_id=1, source_target_pairs={{0,1},{1,0},{2,3},{3,2},{4,5},{5,4},{6,7},{7,6},{8,9},{9,8},{10,11... | collective-permute-start | bytes 2359304 | tf_op jit(solution)/shard_map/ppermute | solution.py:348
  75.3 14.0 %copy-start.5 = (bf16[4,96,512]{2,1,0:T(8,128)(2,1)}, bf16[4,96,512]{2,1,0:T(8,128)(2,1)S(1)}, u32[]{:S(2)}) copy-start(bf16[4,96,512]{2,1,0:T(8,128)(2,1)S(1)} %all-to-all-done.1.refs_2_) | copy-start | bytes 1179652
  75.3 14.0 %collective-permute-start.5 = (bf16[4,96,512]{2,1,0:T(8,128)(2,1)S(1)}, bf16[4,96,512]{2,1,0:T(8,128)(2,1)S(1)}, u32[]{:S(2)}, u32[]{:S(2)}) collective-permute-start(bf16[4,96,512]{2,1,0:T(8,128)(2,1)S(1)} %all-to-all-done.1.refs_2_), channel_id=1, source_target_pairs={{0,1},{1,0},{2,3},{3,2},{4,5},{5,4},{6,7},{7,6},{8,9},{9,8},{10,11... | collective-permute-start | bytes 1179656 | tf_op jit(solution)/shard_map/ppermute | solution.py:368
  89.3 1.0 copy-start.6
  98.2 40.1 %all-to-all-start.3 = ((bf16[12,9,16,128]{3,2,1,0:T(8,128)(2,1)}), bf16[12,9,16,128]{3,2,1,0:T(8,128)(2,1)S(1)}, u32[]{:S(2)}, u32[]{:S(2)}) async-start(bf16[12,9,16,128]{3,2,1,0:T(8,128)(2,1)} %get-tuple-element.38), calls=%async_computation.3 | async-start | bytes 884736 | tf_op jit(solution)/shard_map/all_to_all | solution.py:425
  101.8 18.4 %collective-permute-start.6 = (bf16[3,128,512]{2,1,0:T(8,128)(2,1)}, bf16[3,128,512]{2,1,0:T(8,128)(2,1)S(1)}, u32[]{:S(2)}, u32[]{:S(2)}) collective-permute-start(bf16[3,128,512]{2,1,0:T(8,128)(2,1)} %get-tuple-element.28), channel_id=1, source_target_pairs={{0,24},{8,32},{16,40},{24,48},{32,56},{40,64},{48,72},{56,80},{64,... | collective-permute-start | bytes 1179656 | tf_op jit(solution)/shard_map/ppermute | solution.py:282
  104.8 15.4 %collective-permute-start.7 = (bf16[3,128,512]{2,1,0:T(8,128)(2,1)}, bf16[3,128,512]{2,1,0:T(8,128)(2,1)S(1)}, u32[]{:S(2)}, u32[]{:S(2)}) collective-permute-start(bf16[3,128,512]{2,1,0:T(8,128)(2,1)} %get-tuple-element.29), channel_id=1, source_target_pairs={{0,744},{8,752},{16,760},{24,0},{32,8},{40,16},{48,24},{56,32},{64... | collective-permute-start | bytes 1179656 | tf_op jit(solution)/shard_map/ppermute | solution.py:282
  120.2 1.1 copy-start
  121.4 6.6 %collective-permute-start.8 = (bf16[128,512]{1,0:T(8,128)(2,1)S(1)}, bf16[128,512]{1,0:T(8,128)(2,1)S(1)}, u32[]{:S(2)}, u32[]{:S(2)}) collective-permute-start(bf16[128,512]{1,0:T(8,128)(2,1)S(1)} %get-tuple-element.31), channel_id=1, source_target_pairs={{0,8},{8,16},{16,0},{24,32},{32,40},{40,24},{48,56},{56,64},{64,48... | collective-permute-start | bytes 393224 | tf_op jit(solution)/shard_map/ppermute | solution.py:290
  123.8 7.6 %collective-permute-start.9 = (bf16[128,512]{1,0:T(8,128)(2,1)S(1)}, bf16[128,512]{1,0:T(8,128)(2,1)S(1)}, u32[]{:S(2)}, u32[]{:S(2)}) collective-permute-start(bf16[128,512]{1,0:T(8,128)(2,1)S(1)} %get-tuple-element.32), channel_id=1, source_target_pairs={{0,16},{8,0},{16,8},{24,40},{32,24},{40,32},{48,64},{56,48},{64,56... | collective-permute-start | bytes 393224 | tf_op jit(solution)/shard_map/ppermute | solution.py:290
  131.4 0.9 copy-start.1
  134.7 27.6 %collective-permute-start.10 = (bf16[384,512]{1,0:T(8,128)(2,1)S(1)}, bf16[384,512]{1,0:T(8,128)(2,1)S(1)}, u32[]{:S(2)}, u32[]{:S(2)}) collective-permute-start(bf16[384,512]{1,0:T(8,128)(2,1)S(1)} %get-tuple-element.37), channel_id=1, source_target_pairs={{0,1},{1,0},{2,3},{3,2},{4,5},{5,4},{6,7},{7,6},{8,9},{9,8},{10,11... | collective-permute-start | bytes 1179656 | tf_op jit(solution)/shard_map/ppermute | solution.py:483
  148.6 0.7 collective-permute-start.11
  149.9 19.2 %all-to-all-start.5 = ((bf16[8,16,128]{2,1,0:T(8,128)(2,1)}), bf16[8,16,128]{2,1,0:T(8,128)(2,1)S(1)}, u32[]{:S(2)}, u32[]{:S(2)}) async-start(bf16[8,16,128]{2,1,0:T(8,128)(2,1)} %broadcast_in_dim.4), calls=%async_computation.5 | async-start | bytes 65536 | tf_op jit(solution)/shard_map/all_to_all | solution.py:442
  190.5 20.1 %all-to-all-start.6 = ((bf16[12,8,16,128]{3,2,1,0:T(8,128)(2,1)}), bf16[12,8,16,128]{3,2,1,0:T(8,128)(2,1)S(1)}, u32[]{:S(2)}, u32[]{:S(2)}) async-start(bf16[12,8,16,128]{3,2,1,0:T(8,128)(2,1)} %broadcast_in_dim.5), calls=%async_computation.6 | async-start | bytes 786432 | tf_op jit(solution)/shard_map/all_to_all | solution.py:449
  (5 other events, 3.9 us)

commit v10 on v5

--- a/solution.py
+++ b/solution.py
@@ -239,29 +239,29 @@
         for plane in range(1, got_ref.shape[0]):
             value = value + got_ref[plane, column].astype(F32)
         value = value.astype(BF16)
-        if column < COLUMN:
-            out_ref[column, 0] = value
-        else:
-            for copy in range(COLUMN):
-                out_ref[copy, 1] = value
-
-
-def column_kernel(got_ref, piece_ref, bias_ref):
-    for at, out in enumerate((piece_ref, bias_ref)):
+        for copy in range(COLUMN):
+            out_ref[copy, column] = value
+
+
+def column_kernel(feat_ref, got_ref, pieces_ref, bias_ref):
+    for at in range(COLUMN + 1):
         value = got_ref[0, at].astype(F32)
         for column in range(1, COLUMN):
             value = value + got_ref[column, at].astype(F32)
-        out[...] = value.astype(out.dtype)
-
-
-def lay_kernel(feat_ref, pieces_ref, self_ref, neighbour_ref):
+        if at < COLUMN:
+            pieces_ref[at ^ feat_ref[0]] = value.astype(BF16)
+        else:
+            bias_ref[...] = value
+
+
+def lay_kernel(pieces_ref, self_ref, neighbour_ref):
     planes, _, rows, _ = pieces_ref.shape
     for plane in range(planes):
         for first in range(0, rows, PIECE):
             kind, row = divmod(plane * rows + first, self_ref.shape[0])
             out = (self_ref, neighbour_ref)[kind]
             for column in range(COLUMN):
-                out[pl.ds(row, PIECE), lanes(column ^ feat_ref[0])] = pieces_ref[
+                out[pl.ds(row, PIECE), pl.ds(column * BLOCK, BLOCK)] = pieces_ref[
                     plane, column, pl.ds(first, PIECE), :
                 ].astype(F32)
 
@@ -425,32 +425,25 @@
     from_above = shifted(to_below, -TRIO)
     from_below = shifted(to_above, TRIO)
 
-    got = jax.ShapeDtypeStruct((COLUMN, 2, rows_each, hidden_dev), BF16)
+    got = jax.ShapeDtypeStruct((COLUMN, COLUMN + 1, rows_each, hidden_dev), BF16)
     got = call(planes_kernel, [VMEM], got, [], weight_part.size, weight_part.size * 2)(
         lax.all_to_all(weight_part, "rows", 0, 0, axis_index_groups=same_column)
     )
-    piece = jax.ShapeDtypeStruct((rows_each, hidden_dev), BF16)
-    piece, bias_sum = call(
+    pieces, bias_sum = call(
         column_kernel,
-        [VMEM],
-        [piece, jax.ShapeDtypeStruct(piece.shape, F32)],
+        [SMEM, VMEM],
+        [
+            jax.ShapeDtypeStruct((COLUMN, rows_each, hidden_dev), BF16),
+            jax.ShapeDtypeStruct((rows_each, hidden_dev), F32),
+        ],
         [],
         got.size,
         got.size * 2,
-    )(lax.all_to_all(got, "rows", 0, 0, axis_index_groups=same_plane))
-    pairs = [
-        (row * feats + feat, row * feats + (feat ^ (row // TRIO % COLUMN)))
-        for row in range(groups)
-        for feat in range(feats)
-    ]
-    piece = lax.ppermute(piece, ("rows", "feat"), pairs)
-    pieces = lax.all_to_all(
-        jnp.broadcast_to(piece[None], (COLUMN,) + piece.shape),
-        "rows",
-        0,
-        0,
-        axis_index_groups=same_plane,
-    )
+    )(
+        lax.axis_index("feat").reshape(1),
+        lax.all_to_all(got, "rows", 0, 0, axis_index_groups=same_plane),
+    )
+    pieces = lax.all_to_all(pieces, "feat", 0, 0)
     pieces = lax.all_to_all(
         jnp.broadcast_to(pieces[None], (planes,) + pieces.shape),
         "rows",
@@ -460,8 +453,8 @@
     )
     grad_weight = jax.ShapeDtypeStruct((width, feats * hidden_dev), F32)
     grad_self, grad_neighbour = call(
-        lay_kernel, [SMEM, VMEM], [grad_weight, grad_weight], [], 0, pieces.size * 6
-    )(lax.axis_index("feat").reshape(1), pieces)
+        lay_kernel, [VMEM], [grad_weight, grad_weight], [], 0, pieces.size * 6
+    )(pieces)
 
     spread = jax.ShapeDtypeStruct((hidden_dev, node_dev), BF16)
     own, first, second = call(

time: 191 us -> 191 us (level)
  the two profiles are of different devices: /device:TPU:72 before, /device:TPU:65 now
where the time goes in v10:
time: 191 us; the launch traced here: 190 us
  starting transfers between devices  103 us (54%)
  waiting for transfers between devices  44.1 us (23%)
  Pallas kernels  18.9 us (10%)
  blocking collectives  14.8 us (8%)
  local copies, waits for them, and re-layouts  6.93 us (4%)
    all_to_all x2, starting transfers between devices, over_stacks(): return lax.all_to_all(value, 'feat', 0, 0, axis_index_groups=same_core)  24.1 us
    ppermute x4, starting transfers between devices, shifted(): return lax.ppermute(value, 'rows', pairs)  17.8 us
    ppermute x3, starting transfers between devices, to_stack(): return lax.ppermute(value, 'feat', pairs)  16.1 us
    all_to_all x1, blocking collectives, on_device(): lax.all_to_all(weight_part, 'rows', 0, 0, axis_index_groups=same_column)  14.8 us
    all_to_all x2, waiting for transfers between devices, over_stacks(): return lax.all_to_all(value, 'feat', 0, 0, axis_index_groups=same_core)  13 us
    ppermute x4, starting transfers between devices, turned_in_trio(): return lax.ppermute(value, 'rows', pairs)  11.2 us
    all_to_all x1, starting transfers between devices, on_device(): pieces = lax.all_to_all(pieces, 'feat', 0, 0)  11.1 us
    ppermute x3, waiting for transfers between devices, to_stack(): return lax.ppermute(value, 'feat', pairs)  11 us
  transfers between devices with their start and end apart: 19, of which 11 were waited for; matrix products, arithmetic and copies ran while one was open for 1% of the time, Pallas kernels for 4%

profile of v10, /device:TPU:65, one launch (start us, length us, event | category | flops | bytes accessed | tf_op | source)
XLA Modules:
  0.0 189.8 jit_solution(6395861361654038647)
XLA Ops:
  0.6 4.0 %collective-permute-start.1 = (bf16[96,512]{1,0:T(8,128)(2,1)}, bf16[96,512]{1,0:T(8,128)(2,1)S(1)}, u32[]{:S(2)}, u32[]{:S(2)}) collective-permute-start(bf16[96,512]{1,0:T(8,128)(2,1)} %bitcast.15), channel_id=1, source_target_pairs={{0,8},{8,16},{16,0},{24,32},{32,40},{40,24},{48,56},{56,64},{64,48... | collective-permute-start | bytes 294920 | tf_op jit(solution)/shard_map/ppermute | solution.py:292
  6.6 3.6 %collective-permute-done.first_ref = bf16[96,512]{1,0:T(8,128)(2,1)S(1)} collective-permute-done((bf16[96,512]{1,0:T(8,128)(2,1)}, bf16[96,512]{1,0:T(8,128)(2,1)S(1)}, u32[]{:S(2)}, u32[]{:S(2)}) %collective-permute-start) | collective-permute-done | bytes 98336 | tf_op jit(solution)/shard_map/ppermute | solution.py:292
  14.0 13.6 %all-to-all-start = ((bf16[4,192,512]{2,1,0:T(8,128)(2,1)}), bf16[4,192,512]{2,1,0:T(8,128)(2,1)S(1)}, u32[]{:S(2)}, u32[]{:S(2)}) async-start(bf16[4,192,512]{2,1,0:T(8,128)(2,1)} %get-tuple-element.28), calls=%async_computation | async-start | bytes 1572864 | tf_op jit(solution)/shard_map/all_to_all | solution.py:326
  27.6 7.3 %collective-permute-start.4 = (bf16[3,96,512]{2,1,0:T(8,128)(2,1)S(1)}, bf16[3,96,512]{2,1,0:T(8,128)(2,1)S(1)}, u32[]{:S(2)}, u32[]{:S(2)}) collective-permute-start(bf16[3,96,512]{2,1,0:T(8,128)(2,1)S(1)} %get-tuple-element.29.level_ref), channel_id=1, source_target_pairs={{0,744},{8,752},{16,760},{24,0},{32,8},{40,16},{48,24},{56,32},{64... | collective-permute-start | bytes 884744 | tf_op jit(solution)/shard_map/ppermute | solution.py:284
  38.8 7.0 %collective-permute-done.3.below_ref = bf16[3,96,512]{2,1,0:T(8,128)(2,1)S(1)} collective-permute-done((bf16[3,96,512]{2,1,0:T(8,128)(2,1)S(1)}, bf16[3,96,512]{2,1,0:T(8,128)(2,1)S(1)}, u32[]{:S(2)}, u32[]{:S(2)}) %collective-permute-start.3) | collective-permute-done | bytes 294944 | tf_op jit(solution)/shard_map/ppermute | solution.py:284
  46.5 6.6 %shard_map.138 = bf16[4,96,512]{2,1,0:T(8,128)(2,1)} custom-call(s32[1]{0:T(128)} %bitcast.place_ref, s32[7]{0:T(128)} %count_ref.3, s32[112]{0:T(128)} %dest_ref.3, s32[112]{0:T(128)} %source_ref.3, bf16[112,128,128]{2,1,0:T(8,128)(2,1)} %tiles_hbm.3, s32[1,512]{1,0:T(1,128)} %bitcast.18, bf16[3,96,512]{2,1,0:T(8,128)(2,1)} %copy-done.13, ...), custom_call_target="tpu_custom_call" | custom-call | flops 469762048 | bytes 3670016 | tf_op jit(solution)/shard_map/pallas_call | solution.py:358
  53.6 10.4 %all-to-all-start.1 = ((bf16[4,96,512]{2,1,0:T(8,128)(2,1)}), bf16[4,96,512]{2,1,0:T(8,128)(2,1)S(1)}, u32[]{:S(2)}, u32[]{:S(2)}) async-start(bf16[4,96,512]{2,1,0:T(8,128)(2,1)} %shard_map.138), calls=%async_computation.1 | async-start | bytes 786432 | tf_op jit(solution)/shard_map/all_to_all | solution.py:326
  64.0 4.3 %collective-permute-start.2 = (bf16[4,192,512]{2,1,0:T(8,128)(2,1)S(1)}, bf16[4,192,512]{2,1,0:T(8,128)(2,1)S(1)}, u32[]{:S(2)}, u32[]{:S(2)}) collective-permute-start(bf16[4,192,512]{2,1,0:T(8,128)(2,1)S(1)} %all-to-all-done.refs_0_), channel_id=1, source_target_pairs={{0,1},{1,0},{2,3},{3,2},{4,5},{5,4},{6,7},{7,6},{8,9},{9,8},{10,11... | collective-permute-start | bytes 2359304 | tf_op jit(solution)/shard_map/ppermute | solution.py:353
  68.3 12.5 %all-to-all-done.1.refs_2_ = bf16[4,96,512]{2,1,0:T(8,128)(2,1)S(1)} async-done(((bf16[4,96,512]{2,1,0:T(8,128)(2,1)}), bf16[4,96,512]{2,1,0:T(8,128)(2,1)S(1)}, u32[]{:S(2)}, u32[]{:S(2)}) %all-to-all-start.1) | async-done | bytes 393248 | tf_op jit(solution)/shard_map/all_to_all | solution.py:326
  80.8 4.5 %collective-permute-start.5 = (bf16[4,96,512]{2,1,0:T(8,128)(2,1)S(1)}, bf16[4,96,512]{2,1,0:T(8,128)(2,1)S(1)}, u32[]{:S(2)}, u32[]{:S(2)}) collective-permute-start(bf16[4,96,512]{2,1,0:T(8,128)(2,1)S(1)} %all-to-all-done.1.refs_2_), channel_id=1, source_target_pairs={{0,1},{1,0},{2,3},{3,2},{4,5},{5,4},{6,7},{7,6},{8,9},{9,8},{10,11... | collective-permute-start | bytes 1179656 | tf_op jit(solution)/shard_map/ppermute | solution.py:373
  87.6 8.2 %shard_map.139 = (bf16[512,128]{1,0:T(8,128)(2,1)}, bf16[128,512]{1,0:T(8,128)(2,1)}, bf16[12,9,16,128]{3,2,1,0:T(8,128)(2,1)}, bf16[768,128]{1,0:T(8,128)(2,1)}...) custom-call(s32[1]{0:T(128)} %bitcast.place_ref, ...), custom_call_target="tpu_custom_call" | custom-call | flops 939524096 | bytes 3670016 | tf_op jit(solution)/shard_map/pallas_call | solution.py:381
  95.9 14.8 %all_to_all.30.got_ref = bf16[12,9,16,128]{3,2,1,0:T(8,128)(2,1)S(1)} all-to-all(bf16[12,9,16,128]{3,2,1,0:T(8,128)(2,1)} %get-tuple-element.46), channel_id=1, replica_groups={{0,8,16,192,200,208,384,392,400,576,584,592},{24,32,40,216,224,232,408,..., dimensions={0} | all-to-all | bytes 884736 | tf_op jit(solution)/shard_map/all_to_all | solution.py:430
  111.5 7.4 %all-to-all-start.3 = ((bf16[8,9,16,128]{3,2,1,0:T(8,128)(2,1)}), bf16[8,9,16,128]{3,2,1,0:T(8,128)(2,1)S(1)}, u32[]{:S(2)}, u32[]{:S(2)}) async-start(bf16[8,9,16,128]{3,2,1,0:T(8,128)(2,1)} %shard_map.143), calls=%async_computation.3 | async-start | bytes 589824 | tf_op jit(solution)/shard_map/all_to_all | solution.py:444
  118.8 3.4 %collective-permute-start.6 = (bf16[3,128,512]{2,1,0:T(8,128)(2,1)}, bf16[3,128,512]{2,1,0:T(8,128)(2,1)S(1)}, u32[]{:S(2)}, u32[]{:S(2)}) collective-permute-start(bf16[3,128,512]{2,1,0:T(8,128)(2,1)} %get-tuple-element.32), channel_id=1, source_target_pairs={{0,24},{8,32},{16,40},{24,48},{32,56},{40,64},{48,72},{56,80},{64,... | collective-permute-start | bytes 1179656 | tf_op jit(solution)/shard_map/ppermute | solution.py:284
  122.2 5.2 %collective-permute-start.7 = (bf16[3,128,512]{2,1,0:T(8,128)(2,1)}, bf16[3,128,512]{2,1,0:T(8,128)(2,1)S(1)}, u32[]{:S(2)}, u32[]{:S(2)}) collective-permute-start(bf16[3,128,512]{2,1,0:T(8,128)(2,1)} %get-tuple-element.33), channel_id=1, source_target_pairs={{0,744},{8,752},{16,760},{24,0},{32,8},{40,16},{48,24},{56,32},{64... | collective-permute-start | bytes 1179656 | tf_op jit(solution)/shard_map/ppermute | solution.py:284
  129.7 11.1 %all-to-all-start.4 = ((bf16[8,16,128]{2,1,0:T(8,128)(2,1)}), bf16[8,16,128]{2,1,0:T(8,128)(2,1)S(1)}, u32[]{:S(2)}, u32[]{:S(2)}) async-start(bf16[8,16,128]{2,1,0:T(8,128)(2,1)} %get-tuple-element.47), calls=%async_computation.4 | async-start | bytes 65536 | tf_op jit(solution)/shard_map/all_to_all | solution.py:446
  144.0 3.3 %collective-permute-start.9 = (bf16[128,512]{1,0:T(8,128)(2,1)S(1)}, bf16[128,512]{1,0:T(8,128)(2,1)S(1)}, u32[]{:S(2)}, u32[]{:S(2)}) collective-permute-start(bf16[128,512]{1,0:T(8,128)(2,1)S(1)} %get-tuple-element.36), channel_id=1, source_target_pairs={{0,16},{8,0},{16,8},{24,40},{32,24},{40,32},{48,64},{56,48},{64,56... | collective-permute-start | bytes 393224 | tf_op jit(solution)/shard_map/ppermute | solution.py:292
  147.3 3.3 %all-to-all-done.4 = bf16[8,16,128]{2,1,0:T(8,128)(2,1)S(1)} async-done(((bf16[8,16,128]{2,1,0:T(8,128)(2,1)}), bf16[8,16,128]{2,1,0:T(8,128)(2,1)S(1)}, u32[]{:S(2)}, u32[]{:S(2)}) %all-to-all-start.4) | async-done | bytes 32800 | tf_op jit(solution)/shard_map/all_to_all | solution.py:446
  151.5 4.2 %all-to-all-start.5 = ((bf16[12,8,16,128]{3,2,1,0:T(8,128)(2,1)}), bf16[12,8,16,128]{3,2,1,0:T(8,128)(2,1)S(1)}, u32[]{:S(2)}, u32[]{:S(2)}) async-start(bf16[12,8,16,128]{3,2,1,0:T(8,128)(2,1)} %broadcast_in_dim.2), calls=%async_computation.5 | async-start | bytes 786432 | tf_op jit(solution)/shard_map/all_to_all | solution.py:447
  156.3 2.9 %collective-permute-start.10 = (bf16[384,512]{1,0:T(8,128)(2,1)S(1)}, bf16[384,512]{1,0:T(8,128)(2,1)S(1)}, u32[]{:S(2)}, u32[]{:S(2)}) collective-permute-start(bf16[384,512]{1,0:T(8,128)(2,1)S(1)} %get-tuple-element.41), channel_id=1, source_target_pairs={{0,1},{1,0},{2,3},{3,2},{4,5},{5,4},{6,7},{7,6},{8,9},{9,8},{10,11... | collective-permute-start | bytes 1179656 | tf_op jit(solution)/shard_map/ppermute | solution.py:481
  160.6 5.7 %collective-permute-start.11 = (bf16[96,512]{1,0:T(8,128)(2,1)S(1)}, bf16[96,512]{1,0:T(8,128)(2,1)S(1)}, u32[]{:S(2)}, u32[]{:S(2)}) collective-permute-start(bf16[96,512]{1,0:T(8,128)(2,1)S(1)} %get-tuple-element.43), channel_id=1, source_target_pairs={{0,2},{1,3},{2,4},{3,5},{4,6},{5,7},{6,0},{7,1},{8,10},{9,11},{10,... | collective-permute-start | bytes 294920 | tf_op jit(solution)/shard_map/ppermute | solution.py:330
  166.3 4.6 %collective-permute-start.12 = (bf16[96,512]{1,0:T(8,128)(2,1)S(1)}, bf16[96,512]{1,0:T(8,128)(2,1)S(1)}, u32[]{:S(2)}, u32[]{:S(2)}) collective-permute-start(bf16[96,512]{1,0:T(8,128)(2,1)S(1)} %get-tuple-element.44), channel_id=1, source_target_pairs={{0,4},{1,5},{2,6},{3,7},{4,0},{5,1},{6,2},{7,3},{8,12},{9,13},{10,... | collective-permute-start | bytes 294920 | tf_op jit(solution)/shard_map/ppermute | solution.py:330
  170.9 5.8 %collective-permute-start.13 = (bf16[96,512]{1,0:T(8,128)(2,1)S(1)}, bf16[96,512]{1,0:T(8,128)(2,1)S(1)}, u32[]{:S(2)}, u32[]{:S(2)}) collective-permute-start(bf16[96,512]{1,0:T(8,128)(2,1)S(1)} %get-tuple-element.45), channel_id=1, source_target_pairs={{0,6},{1,7},{2,0},{3,1},{4,2},{5,3},{6,4},{7,5},{8,14},{9,15},{10,... | collective-permute-start | bytes 294920 | tf_op jit(solution)/shard_map/ppermute | solution.py:330
  178.0 9.7 %collective-permute-done.13 = bf16[96,512]{1,0:T(8,128)(2,1)S(1)} collective-permute-done((bf16[96,512]{1,0:T(8,128)(2,1)S(1)}, bf16[96,512]{1,0:T(8,128)(2,1)S(1)}, u32[]{:S(2)}, u32[]{:S(2)}) %collective-permute-start.13) | collective-permute-done | bytes 98336 | tf_op jit(solution)/shard_map/ppermute | solution.py:330
  (55 shorter events, 25.6 us)
Async XLA Ops:
  0.6 5.9 %collective-permute-start.1 = (bf16[96,512]{1,0:T(8,128)(2,1)}, bf16[96,512]{1,0:T(8,128)(2,1)S(1)}, u32[]{:S(2)}, u32[]{:S(2)}) collective-permute-start(bf16[96,512]{1,0:T(8,128)(2,1)} %bitcast.15), channel_id=1, source_target_pairs={{0,8},{8,16},{16,0},{24,32},{32,40},{40,24},{48,56},{56,64},{64,48... | collective-permute-start | bytes 294920 | tf_op jit(solution)/shard_map/ppermute | solution.py:292
  4.6 5.6 %collective-permute-start = (bf16[96,512]{1,0:T(8,128)(2,1)}, bf16[96,512]{1,0:T(8,128)(2,1)S(1)}, u32[]{:S(2)}, u32[]{:S(2)}) collective-permute-start(bf16[96,512]{1,0:T(8,128)(2,1)} %bitcast.16), channel_id=1, source_target_pairs={{0,16},{8,0},{16,8},{24,40},{32,24},{40,32},{48,64},{56,48},{64,56... | collective-permute-start | bytes 294920 | tf_op jit(solution)/shard_map/ppermute | solution.py:292
  14.0 31.9 %copy-start.1 = (bf16[3,96,512]{2,1,0:T(8,128)(2,1)}, bf16[3,96,512]{2,1,0:T(8,128)(2,1)S(1)}, u32[]{:S(2)}) copy-start(bf16[3,96,512]{2,1,0:T(8,128)(2,1)S(1)} %get-tuple-element.29.level_ref) | copy-start | bytes 884740
  14.0 39.6 %all-to-all-start = ((bf16[4,192,512]{2,1,0:T(8,128)(2,1)}), bf16[4,192,512]{2,1,0:T(8,128)(2,1)S(1)}, u32[]{:S(2)}, u32[]{:S(2)}) async-start(bf16[4,192,512]{2,1,0:T(8,128)(2,1)} %get-tuple-element.28), calls=%async_computation | async-start | bytes 1572864 | tf_op jit(solution)/shard_map/all_to_all | solution.py:326
  27.6 11.2 %collective-permute-start.4 = (bf16[3,96,512]{2,1,0:T(8,128)(2,1)S(1)}, bf16[3,96,512]{2,1,0:T(8,128)(2,1)S(1)}, u32[]{:S(2)}, u32[]{:S(2)}) collective-permute-start(bf16[3,96,512]{2,1,0:T(8,128)(2,1)S(1)} %get-tuple-element.29.level_ref), channel_id=1, source_target_pairs={{0,744},{8,752},{16,760},{24,0},{32,8},{40,16},{48,24},{56,32},{64... | collective-permute-start | bytes 884744 | tf_op jit(solution)/shard_map/ppermute | solution.py:284
  34.9 10.9 %collective-permute-start.3 = (bf16[3,96,512]{2,1,0:T(8,128)(2,1)S(1)}, bf16[3,96,512]{2,1,0:T(8,128)(2,1)S(1)}, u32[]{:S(2)}, u32[]{:S(2)}) collective-permute-start(bf16[3,96,512]{2,1,0:T(8,128)(2,1)S(1)} %get-tuple-element.29.level_ref), channel_id=1, source_target_pairs={{0,24},{8,32},{16,40},{24,48},{32,56},{40,64},{48,72},{56,80},{64,... | collective-permute-start | bytes 884744 | tf_op jit(solution)/shard_map/ppermute | solution.py:284
  53.6 33.0 %copy-start.8 = (bf16[4,192,512]{2,1,0:T(8,128)(2,1)}, bf16[4,192,512]{2,1,0:T(8,128)(2,1)S(1)}, u32[]{:S(2)}) copy-start(bf16[4,192,512]{2,1,0:T(8,128)(2,1)S(1)} %all-to-all-done.refs_0_) | copy-start | bytes 2359300
  53.6 27.2 %all-to-all-start.1 = ((bf16[4,96,512]{2,1,0:T(8,128)(2,1)}), bf16[4,96,512]{2,1,0:T(8,128)(2,1)S(1)}, u32[]{:S(2)}, u32[]{:S(2)}) async-start(bf16[4,96,512]{2,1,0:T(8,128)(2,1)} %shard_map.138), calls=%async_computation.1 | async-start | bytes 786432 | tf_op jit(solution)/shard_map/all_to_all | solution.py:326
  64.0 22.5 %collective-permute-start.2 = (bf16[4,192,512]{2,1,0:T(8,128)(2,1)S(1)}, bf16[4,192,512]{2,1,0:T(8,128)(2,1)S(1)}, u32[]{:S(2)}, u32[]{:S(2)}) collective-permute-start(bf16[4,192,512]{2,1,0:T(8,128)(2,1)S(1)} %all-to-all-done.refs_0_), channel_id=1, source_target_pairs={{0,1},{1,0},{2,3},{3,2},{4,5},{5,4},{6,7},{7,6},{8,9},{9,8},{10,11... | collective-permute-start | bytes 2359304 | tf_op jit(solution)/shard_map/ppermute | solution.py:353
  80.8 5.8 %collective-permute-start.5 = (bf16[4,96,512]{2,1,0:T(8,128)(2,1)S(1)}, bf16[4,96,512]{2,1,0:T(8,128)(2,1)S(1)}, u32[]{:S(2)}, u32[]{:S(2)}) collective-permute-start(bf16[4,96,512]{2,1,0:T(8,128)(2,1)S(1)} %all-to-all-done.1.refs_2_), channel_id=1, source_target_pairs={{0,1},{1,0},{2,3},{3,2},{4,5},{5,4},{6,7},{7,6},{8,9},{9,8},{10,11... | collective-permute-start | bytes 1179656 | tf_op jit(solution)/shard_map/ppermute | solution.py:373
  95.8 59.8 %copy-start.2 = (bf16[768,128]{1,0:T(8,128)(2,1)S(1)}, bf16[768,128]{1,0:T(8,128)(2,1)}, u32[]{:S(2)}) copy-start(bf16[768,128]{1,0:T(8,128)(2,1)} %get-tuple-element.38.self_ref) | copy-start | bytes 589828
  95.9 59.8 %copy-start.3 = (bf16[768,128]{1,0:T(8,128)(2,1)S(1)}, bf16[768,128]{1,0:T(8,128)(2,1)}, u32[]{:S(2)}) copy-start(bf16[768,128]{1,0:T(8,128)(2,1)} %get-tuple-element.39.neighbour_ref) | copy-start | bytes 589828
  95.9 59.8 %copy-start.6 = (bf16[128,512]{1,0:T(8,128)(2,1)S(1)}, bf16[128,512]{1,0:T(8,128)(2,1)}, u32[]{:S(2)}) copy-start(bf16[128,512]{1,0:T(8,128)(2,1)} %get-tuple-element.37.grad_ref) | copy-start | bytes 393220
  111.5 17.6 %all-to-all-start.3 = ((bf16[8,9,16,128]{3,2,1,0:T(8,128)(2,1)}), bf16[8,9,16,128]{3,2,1,0:T(8,128)(2,1)S(1)}, u32[]{:S(2)}, u32[]{:S(2)}) async-start(bf16[8,9,16,128]{3,2,1,0:T(8,128)(2,1)} %shard_map.143), calls=%async_computation.3 | async-start | bytes 589824 | tf_op jit(solution)/shard_map/all_to_all | solution.py:444
  118.8 21.9 %collective-permute-start.6 = (bf16[3,128,512]{2,1,0:T(8,128)(2,1)}, bf16[3,128,512]{2,1,0:T(8,128)(2,1)S(1)}, u32[]{:S(2)}, u32[]{:S(2)}) collective-permute-start(bf16[3,128,512]{2,1,0:T(8,128)(2,1)} %get-tuple-element.32), channel_id=1, source_target_pairs={{0,24},{8,32},{16,40},{24,48},{32,56},{40,64},{48,72},{56,80},{64,... | collective-permute-start | bytes 1179656 | tf_op jit(solution)/shard_map/ppermute | solution.py:284
  122.2 18.6 %collective-permute-start.7 = (bf16[3,128,512]{2,1,0:T(8,128)(2,1)}, bf16[3,128,512]{2,1,0:T(8,128)(2,1)S(1)}, u32[]{:S(2)}, u32[]{:S(2)}) collective-permute-start(bf16[3,128,512]{2,1,0:T(8,128)(2,1)} %get-tuple-element.33), channel_id=1, source_target_pairs={{0,744},{8,752},{16,760},{24,0},{32,8},{40,16},{48,24},{56,32},{64... | collective-permute-start | bytes 1179656 | tf_op jit(solution)/shard_map/ppermute | solution.py:284
  129.7 20.9 %all-to-all-start.4 = ((bf16[8,16,128]{2,1,0:T(8,128)(2,1)}), bf16[8,16,128]{2,1,0:T(8,128)(2,1)S(1)}, u32[]{:S(2)}, u32[]{:S(2)}) async-start(bf16[8,16,128]{2,1,0:T(8,128)(2,1)} %get-tuple-element.47), calls=%async_computation.4 | async-start | bytes 65536 | tf_op jit(solution)/shard_map/all_to_all | solution.py:446
  142.0 13.6 %collective-permute-start.8 = (bf16[128,512]{1,0:T(8,128)(2,1)S(1)}, bf16[128,512]{1,0:T(8,128)(2,1)S(1)}, u32[]{:S(2)}, u32[]{:S(2)}) collective-permute-start(bf16[128,512]{1,0:T(8,128)(2,1)S(1)} %get-tuple-element.35), channel_id=1, source_target_pairs={{0,8},{8,16},{16,0},{24,32},{32,40},{40,24},{48,56},{56,64},{64,48... | collective-permute-start | bytes 393224 | tf_op jit(solution)/shard_map/ppermute | solution.py:292
  144.0 11.6 %collective-permute-start.9 = (bf16[128,512]{1,0:T(8,128)(2,1)S(1)}, bf16[128,512]{1,0:T(8,128)(2,1)S(1)}, u32[]{:S(2)}, u32[]{:S(2)}) collective-permute-start(bf16[128,512]{1,0:T(8,128)(2,1)S(1)} %get-tuple-element.36), channel_id=1, source_target_pairs={{0,16},{8,0},{16,8},{24,40},{32,24},{40,32},{48,64},{56,48},{64,56... | collective-permute-start | bytes 393224 | tf_op jit(solution)/shard_map/ppermute | solution.py:292
  151.5 37.5 %all-to-all-start.5 = ((bf16[12,8,16,128]{3,2,1,0:T(8,128)(2,1)}), bf16[12,8,16,128]{3,2,1,0:T(8,128)(2,1)S(1)}, u32[]{:S(2)}, u32[]{:S(2)}) async-start(bf16[12,8,16,128]{3,2,1,0:T(8,128)(2,1)} %broadcast_in_dim.2), calls=%async_computation.5 | async-start | bytes 786432 | tf_op jit(solution)/shard_map/all_to_all | solution.py:447
  156.3 4.3 %collective-permute-start.10 = (bf16[384,512]{1,0:T(8,128)(2,1)S(1)}, bf16[384,512]{1,0:T(8,128)(2,1)S(1)}, u32[]{:S(2)}, u32[]{:S(2)}) collective-permute-start(bf16[384,512]{1,0:T(8,128)(2,1)S(1)} %get-tuple-element.41), channel_id=1, source_target_pairs={{0,1},{1,0},{2,3},{3,2},{4,5},{5,4},{6,7},{7,6},{8,9},{9,8},{10,11... | collective-permute-start | bytes 1179656 | tf_op jit(solution)/shard_map/ppermute | solution.py:481
  160.6 16.1 %collective-permute-start.11 = (bf16[96,512]{1,0:T(8,128)(2,1)S(1)}, bf16[96,512]{1,0:T(8,128)(2,1)S(1)}, u32[]{:S(2)}, u32[]{:S(2)}) collective-permute-start(bf16[96,512]{1,0:T(8,128)(2,1)S(1)} %get-tuple-element.43), channel_id=1, source_target_pairs={{0,2},{1,3},{2,4},{3,5},{4,6},{5,7},{6,0},{7,1},{8,10},{9,11},{10,... | collective-permute-start | bytes 294920 | tf_op jit(solution)/shard_map/ppermute | solution.py:330
  166.3 11.7 %collective-permute-start.12 = (bf16[96,512]{1,0:T(8,128)(2,1)S(1)}, bf16[96,512]{1,0:T(8,128)(2,1)S(1)}, u32[]{:S(2)}, u32[]{:S(2)}) collective-permute-start(bf16[96,512]{1,0:T(8,128)(2,1)S(1)} %get-tuple-element.44), channel_id=1, source_target_pairs={{0,4},{1,5},{2,6},{3,7},{4,0},{5,1},{6,2},{7,3},{8,12},{9,13},{10,... | collective-permute-start | bytes 294920 | tf_op jit(solution)/shard_map/ppermute | solution.py:330
  170.9 16.8 %collective-permute-start.13 = (bf16[96,512]{1,0:T(8,128)(2,1)S(1)}, bf16[96,512]{1,0:T(8,128)(2,1)S(1)}, u32[]{:S(2)}, u32[]{:S(2)}) collective-permute-start(bf16[96,512]{1,0:T(8,128)(2,1)S(1)} %get-tuple-element.45), channel_id=1, source_target_pairs={{0,6},{1,7},{2,0},{3,1},{4,2},{5,3},{6,4},{7,5},{8,14},{9,15},{10,... | collective-permute-start | bytes 294920 | tf_op jit(solution)/shard_map/ppermute | solution.py:330
  (9 other events, 19.2 us)

commit v11 on v10

--- a/solution.py
+++ b/solution.py
@@ -340,6 +340,7 @@
         [],
         0,
         6 * stacks * width * node_dev,
+        limit=TILES_VMEM_BYTES,
     )(
         turned,
         turned_in_trio(turned, -1),

time: 191 us -> 190 us (level)
  local copies, waits for them, and re-layouts: 6.93 us -> 4.83 us
  starting transfers between devices: 103 us -> 101 us
    unnamed x28 -> x24, local copies, waits for them, and re-layouts: 5.6 us -> 3.51 us
where the time goes in v11:
time: 190 us; the launch traced here: 188 us
  starting transfers between devices  101 us (53%)
  waiting for transfers between devices  46 us (24%)
  Pallas kernels  20.6 us (11%)
  blocking collectives  14.5 us (8%)
  local copies, waits for them, and re-layouts  4.83 us (3%)
    all_to_all x2, starting transfers between devices, over_stacks(): return lax.all_to_all(value, 'feat', 0, 0, axis_index_groups=same_core)  24.1 us
    ppermute x4, starting transfers between devices, shifted(): return lax.ppermute(value, 'rows', pairs)  17.8 us
    ppermute x3, starting transfers between devices, to_stack(): return lax.ppermute(value, 'feat', pairs)  16 us
    all_to_all x2, waiting for transfers between devices, over_stacks(): return lax.all_to_all(value, 'feat', 0, 0, axis_index_groups=same_core)  14.7 us
    all_to_all x1, blocking collectives, on_device(): lax.all_to_all(weight_part, 'rows', 0, 0, axis_index_groups=same_column)  14.5 us
    ppermute x4, starting transfers between devices, turned_in_trio(): return lax.ppermute(value, 'rows', pairs)  11.2 us
    all_to_all x1, starting transfers between devices, on_device(): pieces = lax.all_to_all(pieces, 'feat', 0, 0)  11.1 us
    ppermute x3, waiting for transfers between devices, to_stack(): return lax.ppermute(value, 'feat', pairs)  11 us
  transfers between devices with their start and end apart: 19, of which 11 were waited for; matrix products, arithmetic and copies ran while one was open for 1% of the time, Pallas kernels for 4%

profile of v11, /device:TPU:65, one launch (start us, length us, event | category | flops | bytes accessed | tf_op | source)
XLA Modules:
  0.0 188.5 jit_solution(15479881272051308364)
XLA Ops:
  0.6 4.0 %collective-permute-start.1 = (bf16[96,512]{1,0:T(8,128)(2,1)}, bf16[96,512]{1,0:T(8,128)(2,1)S(1)}, u32[]{:S(2)}, u32[]{:S(2)}) collective-permute-start(bf16[96,512]{1,0:T(8,128)(2,1)} %bitcast.15), channel_id=1, source_target_pairs={{0,8},{8,16},{16,0},{24,32},{32,40},{40,24},{48,56},{56,64},{64,48... | collective-permute-start | bytes 294920 | tf_op jit(solution)/shard_map/ppermute | solution.py:292
  6.6 3.6 %collective-permute-done.first_ref = bf16[96,512]{1,0:T(8,128)(2,1)S(1)} collective-permute-done((bf16[96,512]{1,0:T(8,128)(2,1)}, bf16[96,512]{1,0:T(8,128)(2,1)S(1)}, u32[]{:S(2)}, u32[]{:S(2)}) %collective-permute-start) | collective-permute-done | bytes 98336 | tf_op jit(solution)/shard_map/ppermute | solution.py:292
  13.1 13.6 %all-to-all-start = ((bf16[4,192,512]{2,1,0:T(8,128)(2,1)}), bf16[4,192,512]{2,1,0:T(8,128)(2,1)S(1)}, u32[]{:S(2)}, u32[]{:S(2)}) async-start(bf16[4,192,512]{2,1,0:T(8,128)(2,1)} %get-tuple-element.28), calls=%async_computation | async-start | bytes 1572864 | tf_op jit(solution)/shard_map/all_to_all | solution.py:326
  26.7 7.3 %collective-permute-start.4 = (bf16[3,96,512]{2,1,0:T(8,128)(2,1)}, bf16[3,96,512]{2,1,0:T(8,128)(2,1)S(1)}, u32[]{:S(2)}, u32[]{:S(2)}) collective-permute-start(bf16[3,96,512]{2,1,0:T(8,128)(2,1)} %get-tuple-element.29.level_ref), channel_id=1, source_target_pairs={{0,744},{8,752},{16,760},{24,0},{32,8},{40,16},{48,24},{56,32},{64... | collective-permute-start | bytes 884744 | tf_op jit(solution)/shard_map/ppermute | solution.py:284
  38.2 6.9 %collective-permute-done.3.below_ref = bf16[3,96,512]{2,1,0:T(8,128)(2,1)S(1)} collective-permute-done((bf16[3,96,512]{2,1,0:T(8,128)(2,1)}, bf16[3,96,512]{2,1,0:T(8,128)(2,1)S(1)}, u32[]{:S(2)}, u32[]{:S(2)}) %collective-permute-start.3) | collective-permute-done | bytes 294944 | tf_op jit(solution)/shard_map/ppermute | solution.py:284
  45.9 6.8 %shard_map.138 = bf16[4,96,512]{2,1,0:T(8,128)(2,1)} custom-call(s32[1]{0:T(128)} %bitcast.place_ref, s32[7]{0:T(128)} %count_ref.3, s32[112]{0:T(128)} %dest_ref.3, s32[112]{0:T(128)} %source_ref.3, bf16[112,128,128]{2,1,0:T(8,128)(2,1)} %tiles_hbm.3, s32[1,512]{1,0:T(1,128)} %bitcast.18, bf16[3,96,512]{2,1,0:T(8,128)(2,1)} %copy-done.9, ...), custom_call_target="tpu_custom_call" | custom-call | flops 469762048 | bytes 3670016 | tf_op jit(solution)/shard_map/pallas_call | solution.py:359
  52.7 10.4 %all-to-all-start.1 = ((bf16[4,96,512]{2,1,0:T(8,128)(2,1)}), bf16[4,96,512]{2,1,0:T(8,128)(2,1)S(1)}, u32[]{:S(2)}, u32[]{:S(2)}) async-start(bf16[4,96,512]{2,1,0:T(8,128)(2,1)} %shard_map.138), calls=%async_computation.1 | async-start | bytes 786432 | tf_op jit(solution)/shard_map/all_to_all | solution.py:326
  63.2 4.7 %collective-permute-start.2 = (bf16[4,192,512]{2,1,0:T(8,128)(2,1)S(1)}, bf16[4,192,512]{2,1,0:T(8,128)(2,1)S(1)}, u32[]{:S(2)}, u32[]{:S(2)}) collective-permute-start(bf16[4,192,512]{2,1,0:T(8,128)(2,1)S(1)} %all-to-all-done.refs_0_), channel_id=1, source_target_pairs={{0,1},{1,0},{2,3},{3,2},{4,5},{5,4},{6,7},{7,6},{8,9},{9,8},{10,11... | collective-permute-start | bytes 2359304 | tf_op jit(solution)/shard_map/ppermute | solution.py:354
  67.9 14.6 %all-to-all-done.1.refs_2_ = bf16[4,96,512]{2,1,0:T(8,128)(2,1)S(1)} async-done(((bf16[4,96,512]{2,1,0:T(8,128)(2,1)}), bf16[4,96,512]{2,1,0:T(8,128)(2,1)S(1)}, u32[]{:S(2)}, u32[]{:S(2)}) %all-to-all-start.1) | async-done | bytes 393248 | tf_op jit(solution)/shard_map/all_to_all | solution.py:326
  82.5 2.9 %collective-permute-start.5 = (bf16[4,96,512]{2,1,0:T(8,128)(2,1)S(1)}, bf16[4,96,512]{2,1,0:T(8,128)(2,1)S(1)}, u32[]{:S(2)}, u32[]{:S(2)}) collective-permute-start(bf16[4,96,512]{2,1,0:T(8,128)(2,1)S(1)} %all-to-all-done.1.refs_2_), channel_id=1, source_target_pairs={{0,1},{1,0},{2,3},{3,2},{4,5},{5,4},{6,7},{7,6},{8,9},{9,8},{10,11... | collective-permute-start | bytes 1179656 | tf_op jit(solution)/shard_map/ppermute | solution.py:374
  87.7 8.4 %shard_map.139 = (bf16[512,128]{1,0:T(8,128)(2,1)}, bf16[128,512]{1,0:T(8,128)(2,1)}, bf16[12,9,16,128]{3,2,1,0:T(8,128)(2,1)}, bf16[768,128]{1,0:T(8,128)(2,1)}...) custom-call(s32[1]{0:T(128)} %bitcast.place_ref, ...), custom_call_target="tpu_custom_call" | custom-call | flops 939524096 | bytes 3670016 | tf_op jit(solution)/shard_map/pallas_call | solution.py:382
  96.2 14.5 %all_to_all.30.got_ref = bf16[12,9,16,128]{3,2,1,0:T(8,128)(2,1)S(1)} all-to-all(bf16[12,9,16,128]{3,2,1,0:T(8,128)(2,1)} %get-tuple-element.46), channel_id=1, replica_groups={{0,8,16,192,200,208,384,392,400,576,584,592},{24,32,40,216,224,232,408,..., dimensions={0} | all-to-all | bytes 884736 | tf_op jit(solution)/shard_map/all_to_all | solution.py:431
  111.4 6.1 %all-to-all-start.3 = ((bf16[8,9,16,128]{3,2,1,0:T(8,128)(2,1)}), bf16[8,9,16,128]{3,2,1,0:T(8,128)(2,1)S(1)}, u32[]{:S(2)}, u32[]{:S(2)}) async-start(bf16[8,9,16,128]{3,2,1,0:T(8,128)(2,1)} %shard_map.143), calls=%async_computation.3 | async-start | bytes 589824 | tf_op jit(solution)/shard_map/all_to_all | solution.py:445
  117.5 3.4 %collective-permute-start.6 = (bf16[3,128,512]{2,1,0:T(8,128)(2,1)}, bf16[3,128,512]{2,1,0:T(8,128)(2,1)S(1)}, u32[]{:S(2)}, u32[]{:S(2)}) collective-permute-start(bf16[3,128,512]{2,1,0:T(8,128)(2,1)} %get-tuple-element.32), channel_id=1, source_target_pairs={{0,24},{8,32},{16,40},{24,48},{32,56},{40,64},{48,72},{56,80},{64,... | collective-permute-start | bytes 1179656 | tf_op jit(solution)/shard_map/ppermute | solution.py:284
  120.9 5.2 %collective-permute-start.7 = (bf16[3,128,512]{2,1,0:T(8,128)(2,1)}, bf16[3,128,512]{2,1,0:T(8,128)(2,1)S(1)}, u32[]{:S(2)}, u32[]{:S(2)}) collective-permute-start(bf16[3,128,512]{2,1,0:T(8,128)(2,1)} %get-tuple-element.33), channel_id=1, source_target_pairs={{0,744},{8,752},{16,760},{24,0},{32,8},{40,16},{48,24},{56,32},{64... | collective-permute-start | bytes 1179656 | tf_op jit(solution)/shard_map/ppermute | solution.py:284
  128.4 11.1 %all-to-all-start.4 = ((bf16[8,16,128]{2,1,0:T(8,128)(2,1)}), bf16[8,16,128]{2,1,0:T(8,128)(2,1)S(1)}, u32[]{:S(2)}, u32[]{:S(2)}) async-start(bf16[8,16,128]{2,1,0:T(8,128)(2,1)} %get-tuple-element.47), calls=%async_computation.4 | async-start | bytes 65536 | tf_op jit(solution)/shard_map/all_to_all | solution.py:447
  142.7 3.3 %collective-permute-start.9 = (bf16[128,512]{1,0:T(8,128)(2,1)S(1)}, bf16[128,512]{1,0:T(8,128)(2,1)S(1)}, u32[]{:S(2)}, u32[]{:S(2)}) collective-permute-start(bf16[128,512]{1,0:T(8,128)(2,1)S(1)} %get-tuple-element.36), channel_id=1, source_target_pairs={{0,16},{8,0},{16,8},{24,40},{32,24},{40,32},{48,64},{56,48},{64,56... | collective-permute-start | bytes 393224 | tf_op jit(solution)/shard_map/ppermute | solution.py:292
  146.0 3.3 %all-to-all-done.4 = bf16[8,16,128]{2,1,0:T(8,128)(2,1)S(1)} async-done(((bf16[8,16,128]{2,1,0:T(8,128)(2,1)}), bf16[8,16,128]{2,1,0:T(8,128)(2,1)S(1)}, u32[]{:S(2)}, u32[]{:S(2)}) %all-to-all-start.4) | async-done | bytes 32800 | tf_op jit(solution)/shard_map/all_to_all | solution.py:447
  150.1 4.2 %all-to-all-start.5 = ((bf16[12,8,16,128]{3,2,1,0:T(8,128)(2,1)}), bf16[12,8,16,128]{3,2,1,0:T(8,128)(2,1)S(1)}, u32[]{:S(2)}, u32[]{:S(2)}) async-start(bf16[12,8,16,128]{3,2,1,0:T(8,128)(2,1)} %broadcast_in_dim.2), calls=%async_computation.5 | async-start | bytes 786432 | tf_op jit(solution)/shard_map/all_to_all | solution.py:448
  155.0 2.9 %collective-permute-start.10 = (bf16[384,512]{1,0:T(8,128)(2,1)S(1)}, bf16[384,512]{1,0:T(8,128)(2,1)S(1)}, u32[]{:S(2)}, u32[]{:S(2)}) collective-permute-start(bf16[384,512]{1,0:T(8,128)(2,1)S(1)} %get-tuple-element.41), channel_id=1, source_target_pairs={{0,1},{1,0},{2,3},{3,2},{4,5},{5,4},{6,7},{7,6},{8,9},{9,8},{10,11... | collective-permute-start | bytes 1179656 | tf_op jit(solution)/shard_map/ppermute | solution.py:482
  159.3 5.7 %collective-permute-start.11 = (bf16[96,512]{1,0:T(8,128)(2,1)S(1)}, bf16[96,512]{1,0:T(8,128)(2,1)S(1)}, u32[]{:S(2)}, u32[]{:S(2)}) collective-permute-start(bf16[96,512]{1,0:T(8,128)(2,1)S(1)} %get-tuple-element.43), channel_id=1, source_target_pairs={{0,2},{1,3},{2,4},{3,5},{4,6},{5,7},{6,0},{7,1},{8,10},{9,11},{10,... | collective-permute-start | bytes 294920 | tf_op jit(solution)/shard_map/ppermute | solution.py:330
  165.0 4.6 %collective-permute-start.12 = (bf16[96,512]{1,0:T(8,128)(2,1)S(1)}, bf16[96,512]{1,0:T(8,128)(2,1)S(1)}, u32[]{:S(2)}, u32[]{:S(2)}) collective-permute-start(bf16[96,512]{1,0:T(8,128)(2,1)S(1)} %get-tuple-element.44), channel_id=1, source_target_pairs={{0,4},{1,5},{2,6},{3,7},{4,0},{5,1},{6,2},{7,3},{8,12},{9,13},{10,... | collective-permute-start | bytes 294920 | tf_op jit(solution)/shard_map/ppermute | solution.py:330
  169.6 5.8 %collective-permute-start.13 = (bf16[96,512]{1,0:T(8,128)(2,1)S(1)}, bf16[96,512]{1,0:T(8,128)(2,1)S(1)}, u32[]{:S(2)}, u32[]{:S(2)}) collective-permute-start(bf16[96,512]{1,0:T(8,128)(2,1)S(1)} %get-tuple-element.45), channel_id=1, source_target_pairs={{0,6},{1,7},{2,0},{3,1},{4,2},{5,3},{6,4},{7,5},{8,14},{9,15},{10,... | collective-permute-start | bytes 294920 | tf_op jit(solution)/shard_map/ppermute | solution.py:330
  176.7 9.7 %collective-permute-done.13 = bf16[96,512]{1,0:T(8,128)(2,1)S(1)} collective-permute-done((bf16[96,512]{1,0:T(8,128)(2,1)S(1)}, bf16[96,512]{1,0:T(8,128)(2,1)S(1)}, u32[]{:S(2)}, u32[]{:S(2)}) %collective-permute-start.13) | collective-permute-done | bytes 98336 | tf_op jit(solution)/shard_map/ppermute | solution.py:330
  (51 shorter events, 24.6 us)
Async XLA Ops:
  0.6 5.9 %collective-permute-start.1 = (bf16[96,512]{1,0:T(8,128)(2,1)}, bf16[96,512]{1,0:T(8,128)(2,1)S(1)}, u32[]{:S(2)}, u32[]{:S(2)}) collective-permute-start(bf16[96,512]{1,0:T(8,128)(2,1)} %bitcast.15), channel_id=1, source_target_pairs={{0,8},{8,16},{16,0},{24,32},{32,40},{40,24},{48,56},{56,64},{64,48... | collective-permute-start | bytes 294920 | tf_op jit(solution)/shard_map/ppermute | solution.py:292
  4.6 5.6 %collective-permute-start = (bf16[96,512]{1,0:T(8,128)(2,1)}, bf16[96,512]{1,0:T(8,128)(2,1)S(1)}, u32[]{:S(2)}, u32[]{:S(2)}) collective-permute-start(bf16[96,512]{1,0:T(8,128)(2,1)} %bitcast.16), channel_id=1, source_target_pairs={{0,16},{8,0},{16,8},{24,40},{32,24},{40,32},{48,64},{56,48},{64,56... | collective-permute-start | bytes 294920 | tf_op jit(solution)/shard_map/ppermute | solution.py:292
  13.1 39.6 %all-to-all-start = ((bf16[4,192,512]{2,1,0:T(8,128)(2,1)}), bf16[4,192,512]{2,1,0:T(8,128)(2,1)S(1)}, u32[]{:S(2)}, u32[]{:S(2)}) async-start(bf16[4,192,512]{2,1,0:T(8,128)(2,1)} %get-tuple-element.28), calls=%async_computation | async-start | bytes 1572864 | tf_op jit(solution)/shard_map/all_to_all | solution.py:326
  26.7 11.5 %collective-permute-start.4 = (bf16[3,96,512]{2,1,0:T(8,128)(2,1)}, bf16[3,96,512]{2,1,0:T(8,128)(2,1)S(1)}, u32[]{:S(2)}, u32[]{:S(2)}) collective-permute-start(bf16[3,96,512]{2,1,0:T(8,128)(2,1)} %get-tuple-element.29.level_ref), channel_id=1, source_target_pairs={{0,744},{8,752},{16,760},{24,0},{32,8},{40,16},{48,24},{56,32},{64... | collective-permute-start | bytes 884744 | tf_op jit(solution)/shard_map/ppermute | solution.py:284
  34.0 11.1 %collective-permute-start.3 = (bf16[3,96,512]{2,1,0:T(8,128)(2,1)}, bf16[3,96,512]{2,1,0:T(8,128)(2,1)S(1)}, u32[]{:S(2)}, u32[]{:S(2)}) collective-permute-start(bf16[3,96,512]{2,1,0:T(8,128)(2,1)} %get-tuple-element.29.level_ref), channel_id=1, source_target_pairs={{0,24},{8,32},{16,40},{24,48},{32,56},{40,64},{48,72},{56,80},{64,... | collective-permute-start | bytes 884744 | tf_op jit(solution)/shard_map/ppermute | solution.py:284
  38.2 6.9 %copy-start.8 = (bf16[3,96,512]{2,1,0:T(8,128)(2,1)}, bf16[3,96,512]{2,1,0:T(8,128)(2,1)S(1)}, u32[]{:S(2)}) copy-start(bf16[3,96,512]{2,1,0:T(8,128)(2,1)S(1)} %collective-permute-done.4.above_ref) | copy-start | bytes 884740
  52.7 34.0 %copy-start.4 = (bf16[4,192,512]{2,1,0:T(8,128)(2,1)}, bf16[4,192,512]{2,1,0:T(8,128)(2,1)S(1)}, u32[]{:S(2)}) copy-start(bf16[4,192,512]{2,1,0:T(8,128)(2,1)S(1)} %all-to-all-done.refs_0_) | copy-start | bytes 2359300
  52.7 29.7 %all-to-all-start.1 = ((bf16[4,96,512]{2,1,0:T(8,128)(2,1)}), bf16[4,96,512]{2,1,0:T(8,128)(2,1)S(1)}, u32[]{:S(2)}, u32[]{:S(2)}) async-start(bf16[4,96,512]{2,1,0:T(8,128)(2,1)} %shard_map.138), calls=%async_computation.1 | async-start | bytes 786432 | tf_op jit(solution)/shard_map/all_to_all | solution.py:326
  63.2 23.5 %collective-permute-start.2 = (bf16[4,192,512]{2,1,0:T(8,128)(2,1)S(1)}, bf16[4,192,512]{2,1,0:T(8,128)(2,1)S(1)}, u32[]{:S(2)}, u32[]{:S(2)}) collective-permute-start(bf16[4,192,512]{2,1,0:T(8,128)(2,1)S(1)} %all-to-all-done.refs_0_), channel_id=1, source_target_pairs={{0,1},{1,0},{2,3},{3,2},{4,5},{5,4},{6,7},{7,6},{8,9},{9,8},{10,11... | collective-permute-start | bytes 2359304 | tf_op jit(solution)/shard_map/ppermute | solution.py:354
  82.5 4.2 %collective-permute-start.5 = (bf16[4,96,512]{2,1,0:T(8,128)(2,1)S(1)}, bf16[4,96,512]{2,1,0:T(8,128)(2,1)S(1)}, u32[]{:S(2)}, u32[]{:S(2)}) collective-permute-start(bf16[4,96,512]{2,1,0:T(8,128)(2,1)S(1)} %all-to-all-done.1.refs_2_), channel_id=1, source_target_pairs={{0,1},{1,0},{2,3},{3,2},{4,5},{5,4},{6,7},{7,6},{8,9},{9,8},{10,11... | collective-permute-start | bytes 1179656 | tf_op jit(solution)/shard_map/ppermute | solution.py:374
  96.2 58.2 %copy-start.1 = (bf16[768,128]{1,0:T(8,128)(2,1)S(1)}, bf16[768,128]{1,0:T(8,128)(2,1)}, u32[]{:S(2)}) copy-start(bf16[768,128]{1,0:T(8,128)(2,1)} %get-tuple-element.38.self_ref) | copy-start | bytes 589828
  96.2 58.2 %copy-start.2 = (bf16[768,128]{1,0:T(8,128)(2,1)S(1)}, bf16[768,128]{1,0:T(8,128)(2,1)}, u32[]{:S(2)}) copy-start(bf16[768,128]{1,0:T(8,128)(2,1)} %get-tuple-element.39.neighbour_ref) | copy-start | bytes 589828
  96.2 58.2 %copy-start.3 = (bf16[128,512]{1,0:T(8,128)(2,1)S(1)}, bf16[128,512]{1,0:T(8,128)(2,1)}, u32[]{:S(2)}) copy-start(bf16[128,512]{1,0:T(8,128)(2,1)} %get-tuple-element.37.grad_ref) | copy-start | bytes 393220
  111.4 16.3 %all-to-all-start.3 = ((bf16[8,9,16,128]{3,2,1,0:T(8,128)(2,1)}), bf16[8,9,16,128]{3,2,1,0:T(8,128)(2,1)S(1)}, u32[]{:S(2)}, u32[]{:S(2)}) async-start(bf16[8,9,16,128]{3,2,1,0:T(8,128)(2,1)} %shard_map.143), calls=%async_computation.3 | async-start | bytes 589824 | tf_op jit(solution)/shard_map/all_to_all | solution.py:445
  117.5 21.9 %collective-permute-start.6 = (bf16[3,128,512]{2,1,0:T(8,128)(2,1)}, bf16[3,128,512]{2,1,0:T(8,128)(2,1)S(1)}, u32[]{:S(2)}, u32[]{:S(2)}) collective-permute-start(bf16[3,128,512]{2,1,0:T(8,128)(2,1)} %get-tuple-element.32), channel_id=1, source_target_pairs={{0,24},{8,32},{16,40},{24,48},{32,56},{40,64},{48,72},{56,80},{64,... | collective-permute-start | bytes 1179656 | tf_op jit(solution)/shard_map/ppermute | solution.py:284
  120.9 18.6 %collective-permute-start.7 = (bf16[3,128,512]{2,1,0:T(8,128)(2,1)}, bf16[3,128,512]{2,1,0:T(8,128)(2,1)S(1)}, u32[]{:S(2)}, u32[]{:S(2)}) collective-permute-start(bf16[3,128,512]{2,1,0:T(8,128)(2,1)} %get-tuple-element.33), channel_id=1, source_target_pairs={{0,744},{8,752},{16,760},{24,0},{32,8},{40,16},{48,24},{56,32},{64... | collective-permute-start | bytes 1179656 | tf_op jit(solution)/shard_map/ppermute | solution.py:284
  128.4 20.9 %all-to-all-start.4 = ((bf16[8,16,128]{2,1,0:T(8,128)(2,1)}), bf16[8,16,128]{2,1,0:T(8,128)(2,1)S(1)}, u32[]{:S(2)}, u32[]{:S(2)}) async-start(bf16[8,16,128]{2,1,0:T(8,128)(2,1)} %get-tuple-element.47), calls=%async_computation.4 | async-start | bytes 65536 | tf_op jit(solution)/shard_map/all_to_all | solution.py:447
  140.7 13.6 %collective-permute-start.8 = (bf16[128,512]{1,0:T(8,128)(2,1)S(1)}, bf16[128,512]{1,0:T(8,128)(2,1)S(1)}, u32[]{:S(2)}, u32[]{:S(2)}) collective-permute-start(bf16[128,512]{1,0:T(8,128)(2,1)S(1)} %get-tuple-element.35), channel_id=1, source_target_pairs={{0,8},{8,16},{16,0},{24,32},{32,40},{40,24},{48,56},{56,64},{64,48... | collective-permute-start | bytes 393224 | tf_op jit(solution)/shard_map/ppermute | solution.py:292
  142.7 11.6 %collective-permute-start.9 = (bf16[128,512]{1,0:T(8,128)(2,1)S(1)}, bf16[128,512]{1,0:T(8,128)(2,1)S(1)}, u32[]{:S(2)}, u32[]{:S(2)}) collective-permute-start(bf16[128,512]{1,0:T(8,128)(2,1)S(1)} %get-tuple-element.36), channel_id=1, source_target_pairs={{0,16},{8,0},{16,8},{24,40},{32,24},{40,32},{48,64},{56,48},{64,56... | collective-permute-start | bytes 393224 | tf_op jit(solution)/shard_map/ppermute | solution.py:292
  150.1 37.5 %all-to-all-start.5 = ((bf16[12,8,16,128]{3,2,1,0:T(8,128)(2,1)}), bf16[12,8,16,128]{3,2,1,0:T(8,128)(2,1)S(1)}, u32[]{:S(2)}, u32[]{:S(2)}) async-start(bf16[12,8,16,128]{3,2,1,0:T(8,128)(2,1)} %broadcast_in_dim.2), calls=%async_computation.5 | async-start | bytes 786432 | tf_op jit(solution)/shard_map/all_to_all | solution.py:448
  155.0 4.3 %collective-permute-start.10 = (bf16[384,512]{1,0:T(8,128)(2,1)S(1)}, bf16[384,512]{1,0:T(8,128)(2,1)S(1)}, u32[]{:S(2)}, u32[]{:S(2)}) collective-permute-start(bf16[384,512]{1,0:T(8,128)(2,1)S(1)} %get-tuple-element.41), channel_id=1, source_target_pairs={{0,1},{1,0},{2,3},{3,2},{4,5},{5,4},{6,7},{7,6},{8,9},{9,8},{10,11... | collective-permute-start | bytes 1179656 | tf_op jit(solution)/shard_map/ppermute | solution.py:482
  159.3 16.1 %collective-permute-start.11 = (bf16[96,512]{1,0:T(8,128)(2,1)S(1)}, bf16[96,512]{1,0:T(8,128)(2,1)S(1)}, u32[]{:S(2)}, u32[]{:S(2)}) collective-permute-start(bf16[96,512]{1,0:T(8,128)(2,1)S(1)} %get-tuple-element.43), channel_id=1, source_target_pairs={{0,2},{1,3},{2,4},{3,5},{4,6},{5,7},{6,0},{7,1},{8,10},{9,11},{10,... | collective-permute-start | bytes 294920 | tf_op jit(solution)/shard_map/ppermute | solution.py:330
  165.0 11.7 %collective-permute-start.12 = (bf16[96,512]{1,0:T(8,128)(2,1)S(1)}, bf16[96,512]{1,0:T(8,128)(2,1)S(1)}, u32[]{:S(2)}, u32[]{:S(2)}) collective-permute-start(bf16[96,512]{1,0:T(8,128)(2,1)S(1)} %get-tuple-element.44), channel_id=1, source_target_pairs={{0,4},{1,5},{2,6},{3,7},{4,0},{5,1},{6,2},{7,3},{8,12},{9,13},{10,... | collective-permute-start | bytes 294920 | tf_op jit(solution)/shard_map/ppermute | solution.py:330
  169.6 16.8 %collective-permute-start.13 = (bf16[96,512]{1,0:T(8,128)(2,1)S(1)}, bf16[96,512]{1,0:T(8,128)(2,1)S(1)}, u32[]{:S(2)}, u32[]{:S(2)}) collective-permute-start(bf16[96,512]{1,0:T(8,128)(2,1)S(1)} %get-tuple-element.45), channel_id=1, source_target_pairs={{0,6},{1,7},{2,0},{3,1},{4,2},{5,3},{6,4},{7,5},{8,14},{9,15},{10,... | collective-permute-start | bytes 294920 | tf_op jit(solution)/shard_map/ppermute | solution.py:330
  (7 other events, 12.1 us)
